TPU v7x, 32 devices: a whole 2x2x4 slice. The times are simulated.
32 devices in a mesh: ctx: 16 (over z, y, x), head: 2 (over core).
Axes of the slice: x: 2, y: 2, z: 4, core: 2. Of those that a mesh axis runs over, the one named last changes fastest.
Arguments:
- hidden: bfloat16 [8192, 4096], P('ctx', 'head'), may hold values from -6 to 6
- w_query: bfloat16 [4096, 2048], P(None, 'head'), may hold values from -0.09375 to 0.09375
- keys: bfloat16 [8192, 2048], P('ctx', 'head'), may hold values from -6 to 6
- values: bfloat16 [8192, 2048], P('ctx', 'head'), may hold values from -6 to 6
- d_out: bfloat16 [8192, 2048], P('ctx', 'head'), may hold values from -6 to 6
- log_decay: float32 [8192, 16], P('ctx', 'head'), may hold values from -1.5 to 0, as said below
Outputs:
- d_hidden: bfloat16 [8192, 4096], P('ctx', 'head')
- d_keys: bfloat16 [8192, 2048], P('ctx', 'head')
- d_values: bfloat16 [8192, 2048], P('ctx', 'head')
Inputs may be any that keep to these rules, and one draw needn't show every extreme that they name: `log_decay`: every entry is negative.
All inputs are finite; a program needn't handle non-finite values.
Results may differ from a plain program's by a relative error of at most 0.013.
Values may be sent and summed in bfloat16 or wider, within the bound.
No kernel may reach another device: no remote copies, remote signals or barrier semaphores. Data moves between devices by JAX's collectives and lax.ppermute only.
A program may use at most 128 MiB of HBM per device.

v0:
```python
import jax
import jax.numpy as jnp
from jax import lax
from jax.sharding import PartitionSpec as P

HDIM = 128


highest = lax.Precision.HIGHEST


def summaries(query_heads, scaled_keys, value_heads, grad_heads, cumulative, block_total, scaling):
    keep_share = jnp.exp(block_total[None] - cumulative)[:, :, None]
    decayed_keys = (keep_share * scaled_keys).astype(jnp.bfloat16)
    local_state = jnp.einsum(
        "bhe,bhf->hef", decayed_keys, value_heads, preferred_element_type=jnp.float32
    )
    decayed_queries = (scaling * jnp.exp(cumulative)[:, :, None] * query_heads).astype(jnp.bfloat16)
    local_adjoint = jnp.einsum(
        "bhe,bhf->hef", decayed_queries, grad_heads, preferred_element_type=jnp.float32
    )
    return (local_state, local_adjoint)


def gradients(
    query_heads,
    scaled_keys,
    value_heads,
    grad_heads,
    gate_gain,
    cumulative,
    block_total,
    state_in,
    adjoint_in,
    scaling,
):
    row_count = query_heads.shape[0]
    places = jnp.arange(row_count)
    causal = (places[:, None] >= places[None, :])[None]
    cumul_heads = cumulative.T
    spread = cumul_heads[:, :, None] - cumul_heads[:, None, :]
    decays = jnp.where(causal, jnp.exp(jnp.where(causal, spread, 0.0)), 0.0) * scaling
    weight_dv = (
        decays
        * jnp.einsum("the,she->hts", grad_heads, value_heads, preferred_element_type=jnp.float32)
    ).astype(jnp.bfloat16)
    weight_kq = (
        decays
        * jnp.einsum("the,she->hts", query_heads, scaled_keys, preferred_element_type=jnp.float32)
    ).astype(jnp.bfloat16)
    carry_query = jnp.einsum(
        "thf,hef->the", grad_heads.astype(jnp.float32), state_in, precision=highest
    )
    d_query = (
        jnp.einsum("hts,she->the", weight_dv, scaled_keys, preferred_element_type=jnp.float32)
        + scaling * jnp.exp(cumulative)[:, :, None] * carry_query
    )
    tail_decay = jnp.exp(block_total[None] - cumulative)[:, :, None]
    carry_keys = jnp.einsum(
        "shf,hef->she", value_heads.astype(jnp.float32), adjoint_in, precision=highest
    )
    carry_values = jnp.einsum(
        "she,hef->shf", scaled_keys.astype(jnp.float32), adjoint_in, precision=highest
    )
    d_scaled = (
        jnp.einsum("hts,the->she", weight_dv, query_heads, preferred_element_type=jnp.float32)
        + tail_decay * carry_keys
    )
    d_values = (
        jnp.einsum("hts,the->she", weight_kq, grad_heads, preferred_element_type=jnp.float32)
        + tail_decay * carry_values
    )
    d_keys = gate_gain[:, :, None] * d_scaled
    return (
        d_query.astype(jnp.bfloat16),
        d_keys.astype(jnp.bfloat16),
        d_values.astype(jnp.bfloat16),
    )


def body(hidden, w_query, keys, values, d_out, log_decay):
    row_count = hidden.shape[0]
    head_count = log_decay.shape[1]
    width = w_query.shape[1]
    scaling = HDIM ** (-0.5)
    head_shape = (row_count, head_count, HDIM)
    weight_rows = w_query
    projected = jnp.dot(
        lax.all_gather(hidden, "head", axis=1, tiled=True),
        weight_rows,
        preferred_element_type=jnp.float32,
    )
    query_heads = projected.astype(jnp.bfloat16).reshape(head_shape)
    gate_gain = jnp.sqrt(-jnp.expm1(2.0 * log_decay))
    scaled_keys = (gate_gain[:, :, None] * keys.reshape(head_shape)).astype(jnp.bfloat16)
    value_heads = values.reshape(head_shape)
    grad_heads = d_out.reshape(head_shape)
    cumulative = jnp.cumsum(log_decay, axis=0)
    block_total = cumulative[-1]
    local_state, local_adjoint = summaries(
        query_heads, scaled_keys, value_heads, grad_heads, cumulative, block_total, scaling
    )
    all_logs = lax.all_gather(block_total[None], "ctx", axis=0, tiled=True)
    inclusive = jnp.cumsum(all_logs, axis=0)
    my_place = lax.axis_index("ctx")
    mine_inclusive = lax.dynamic_index_in_dim(inclusive, my_place, 0, keepdims=False)
    before_me = mine_inclusive - lax.dynamic_index_in_dim(all_logs, my_place, 0, keepdims=False)
    state_piece = lax.all_gather(local_state[None], "ctx", axis=0, tiled=True)
    adjoint_piece = lax.all_gather(local_adjoint[None], "ctx", axis=0, tiled=True)
    piece_rows = state_piece.shape[0]
    sources = jnp.arange(piece_rows)
    earlier = (sources < my_place)[:, None]
    later = (sources > my_place)[:, None]
    early_exp = jnp.where(earlier, before_me[None] - inclusive, 0.0)
    late_exp = jnp.where(later, inclusive - all_logs - mine_inclusive[None], 0.0)
    early_factor = jnp.where(earlier, jnp.exp(early_exp), 0.0)
    late_factor = jnp.where(later, jnp.exp(late_exp), 0.0)
    new_state = jnp.einsum("nh,nhef->hef", early_factor, state_piece, precision=highest)
    new_adjoint = jnp.einsum("nh,nhef->hef", late_factor, adjoint_piece, precision=highest)
    d_query, d_keys, d_values = gradients(
        query_heads,
        scaled_keys,
        value_heads,
        grad_heads,
        gate_gain,
        cumulative,
        block_total,
        new_state,
        new_adjoint,
        scaling,
    )
    d_flat = d_query.reshape(row_count, width)
    weight_rows = w_query
    reduced = lax.psum_scatter(
        lax.dot_general(
            weight_rows, d_flat, (((1,), (1,)), ((), ())), preferred_element_type=jnp.float32
        ).astype(jnp.bfloat16),
        "head",
        scatter_dimension=0,
        tiled=True,
    ).astype(jnp.float32)
    d_hidden = reduced.T.astype(jnp.bfloat16)
    return (d_hidden, d_keys.reshape(row_count, width), d_values.reshape(row_count, width))


def solution(mesh):
    return jax.shard_map(
        body,
        mesh=mesh,
        in_specs=(
            P("ctx", "head"),
            P(None, "head"),
            P("ctx", "head"),
            P("ctx", "head"),
            P("ctx", "head"),
            P("ctx", "head"),
        ),
        out_specs=(P("ctx", "head"), P("ctx", "head"), P("ctx", "head")),
        check_vma=False,
    )
```

profile of v0, /device:TPU:0, one launch (start us, length us, event | category | flops | bytes accessed | tf_op | source)
XLA Modules:
  0.0 277.2 jit_solution(12329096914835954702)
XLA Ops:
  7.2 0.7 all-gather.7.cloned.1.call-update
  8.0 2.2 reduce-window.6
  10.2 0.2 slice_reduce_fusion
  10.4 2.6 copy.63
  13.0 0.1 exponential_multiply_fusion
  13.0 0.2 slice_reduce_fusion.1
  13.3 0.1 subtract_exponential_fusion
  13.3 1.9 multiply_convert_fusion.5
  15.2 1.3 fusion.14
  16.6 1.3 copy.97
  17.9 8.1 %all-gather.7.cloned.1.call-done = bf16[512,4096]{1,0:T(8,128)(2,1)} async-done(((bf16[512,2048]{1,0:T(8,128)(2,1)}), bf16[512,4096]{1,0:T(8,128)(2,1)}) %all-gather.7.cloned.1.call-update) | async-done | bytes 4194320 | tf_op jit(solution)/shard_map/all_gather | solution.py:89
  26.0 10.1 %convolution_convert_fusion.1 = bf16[512,1024]{1,0:T(8,128)(2,1)} fusion(bf16[512,4096]{1,0:T(8,128)(2,1)} %all-gather.7.cloned.1.call-done, bf16[4096,1024]{1,0:T(8,128)(2,1)} %param.7), kind=kOutput, calls=%fused_computation.24 | convolution fusion | flops 4295491584 | bytes 13631488 | tf_op jit(solution)/shard_map/dot_general | solution.py:88
  36.1 1.5 copy.70
  37.6 2.6 fusion.15
  40.3 41.0 %all-gather.2 = f32[16,1,8]{2,1,0:T(1,128)S(1)} all-gather(f32[1,1,8]{2,1,0:T(1,128)S(1)} %bitcast.121), channel_id=1, replica_groups=mesh['ctx'=16,'head'=2] {'ctx'}, dimensions={0}, use_global_device_ids=true | all-gather | bytes 544 | tf_op jit(solution)/shard_map/all_gather | solution.py:103
  81.4 0.1 select_bitcast_fusion
  81.5 0.1 iota_compare_fusion
  81.7 4.5 %multiply_convert_fusion.1 = bf16[8,512,512]{2,1,0:T(8,128)(2,1)S(1)} fusion(f32[8,512]{1,0:T(8,128)S(1)} %add_bitcast_fusion.1, pred[512,512]{1,0:T(8,128)(4,1)S(1)} %iota_compare_fusion, bf16[512,8,128]{0,2,1:T(8,128)(2,1)} %bitcast.108, bf16[512,1024]{1,0:T(8,128)(2,1)S(1)} %copy-done), kind=kOutput, calls=%fused_computation.4 | convolution fusion | flops 549453824 | bytes 6569984 | tf_op jit(solution)/shard_map/the,she->hts/dot_general | solution.py:45
  86.2 1.9 copy-done.1
  88.1 2.8 %fusion.28 = f32[8,128,512]{2,1,0:T(8,128)} fusion(bf16[512,8,128]{0,2,1:T(8,128)(2,1)S(1)} %multiply_convert_fusion.5, bf16[8,512,512]{2,1,0:T(8,128)(2,1)S(1)} %multiply_convert_fusion.1), kind=kOutput, calls=%fused_computation.53 | convolution fusion | flops 536870912 | bytes 7340032 | tf_op jit(solution)/shard_map/hts,she->the/dot_general | solution.py:55
  90.9 52.0 %all-gather.9.cloned.1.call-done = f32[128,128,128]{2,1,0:T(8,128)} async-done(((f32[8,128,128]{2,1,0:T(8,128)}), f32[128,128,128]{2,1,0:T(8,128)}) %all-gather.9.cloned.1.call-update) | async-done | bytes 8388624 | tf_op jit(solution)/shard_map/all_gather | solution.py:108
  142.9 12.5 %fusion = f32[8,1,128,128]{3,1,2,0:T(1,128)S(1)} fusion(f32[16,8,1,1]{0,2,3,1:T(1,128)S(1)} %copy.81, f32[16,8,128,128]{3,2,1,0:T(8,128)} %bitcast.113), kind=kOutput, calls=%fused_computation.1 | convolution fusion | flops 25165824 | bytes 8913408 | tf_op jit(solution)/shard_map/nh,nhef->hef/dot_general | solution.py:118
  155.4 1.2 fusion.13
  156.6 9.7 %fusion.2 = bf16[4096,512]{0,1:T(8,128)(2,1)} fusion(bf16[512,1024]{0,1:T(8,128)(2,1)S(1)} %bitcast.117, bf16[4096,1024]{1,0:T(8,128)(2,1)} %param.7), kind=kOutput, calls=%fused_computation.7 | convolution fusion | flops 4297064448 | bytes 13631488 | tf_op jit(solution)/shard_map/dot_general | solution.py:135
  166.3 4.2 %fusion.29 = f32[8,128,512]{2,1,0:T(8,128)} fusion(bf16[512,8,128]{0,2,1:T(8,128)(2,1)S(1)} %bitcast.105, bf16[8,512,512]{2,1,0:T(8,128)(2,1)} %copy-done.1), kind=kOutput, calls=%fused_computation.54 | convolution fusion | flops 536870912 | bytes 7340032 | tf_op jit(solution)/shard_map/hts,the->she/dot_general | solution.py:66
  170.5 6.3 %fusion.3 = f32[8,512,128]{1,2,0:T(8,128)} fusion(bf16[512,8,128]{0,2,1:T(8,128)(2,1)} %bitcast.109, f32[8,512]{1,0:T(8,128)S(1)} %add_bitcast_fusion.1, pred[512,512]{1,0:T(8,128)(4,1)S(1)} %iota_compare_fusion, bf16[512,8,128]{0,2,1:T(8,128)(2,1)S(1)} %bitcast.106, bf16[512,8,128]{0,2,1:T(8,128)(2,1)S(1)} %multiply_convert_fusion.5), kind=kOutput, calls=%fused_computation.8 | convolution fusion | flops 1086324736 | bytes 5521408 | tf_op jit(solution)/shard_map/hts,the->she/dot_general | solution.py:70
  176.8 80.5 %all-gather.11.cloned.1.call-done = f32[128,128,128]{2,1,0:T(8,128)} async-done(((f32[8,128,128]{2,1,0:T(8,128)}), f32[128,128,128]{2,1,0:T(8,128)}) %all-gather.11.cloned.1.call-update) | async-done | bytes 8388624 | tf_op jit(solution)/shard_map/all_gather | solution.py:109
  257.3 4.2 %multiply_reduce_fusion = f32[8,128,128]{2,1,0:T(8,128)S(1)} fusion(f32[8,16,128,128]{3,2,0,1:T(8,128)} %bitcast.111, f32[8,16]{0,1:T(8,128)S(1)} %get-tuple-element.17), kind=kLoop, calls=%fused_computation | loop fusion | flops 4063232 | bytes 8913408 | tf_op jit(solution)/shard_map/nh,nhef->hef/dot_general | solution.py:119
  261.5 2.2 fusion.8
  263.7 2.4 copy.80
  266.1 3.3 %fusion.11 = bf16[512,8,128]{0,2,1:T(8,128)(2,1)S(1)} fusion(f32[8,128,512]{2,1,0:T(8,128)} %fusion.29, f32[8,128,128]{2,1,0:T(8,128)S(1)} %multiply_reduce_fusion, f32[512,8]{0,1:T(8,128)S(1)} %subtract_exponential_fusion, f32[512,8]{0,1:T(8,128)S(1)} %negate_sqrt_fusion, bf16[512,1024]{1,0:T(8,128)(2,1)S(1)} %copy-done), kind=kOutput, calls=%fused_computation.17 | convolution fusion | flops 807403520 | bytes 4751360 | tf_op jit(solution)/shard_map/shf,hef->she/dot_general | solution.py:59
  269.4 1.3 copy.79
  (29 shorter events, 0.5 us)
Async XLA Ops:
  7.2 8.0 %copy-start = (bf16[512,1024]{1,0:T(8,128)(2,1)S(1)}, bf16[512,1024]{1,0:T(8,128)(2,1)}, u32[]{:S(2)}) copy-start(bf16[512,1024]{1,0:T(8,128)(2,1)} %param.9) | copy-start | bytes 3145732
  7.2 6.0 %copy-start.6 = (f32[512,8]{0,1:T(8,128)S(1)}, f32[512,8]{0,1:T(8,128)}, u32[]{:S(2)}) copy-start(f32[512,8]{0,1:T(8,128)} %param.11) | copy-start | bytes 49156
  7.2 18.8 %all-gather.7.cloned.1.call-start = ((), (), s32[]{:S(2)}) async-start(), calls=%async_computation.2 | async-start | bytes 6291456 | tf_op jit(solution)/shard_map/all_gather | solution.py:89
  7.9 135.0 %all-gather.9.cloned.1.call-start = ((), (), s32[]{:S(2)}) async-start(), calls=%async_computation.3 | async-start | bytes 8912896 | tf_op jit(solution)/shard_map/all_gather | solution.py:108
  13.0 3.6 %copy-start.5 = (bf16[512,1024]{1,0:T(8,128)(2,1)S(1)}, bf16[512,1024]{1,0:T(8,128)(2,1)}, u32[]{:S(2)}) copy-start(bf16[512,1024]{1,0:T(8,128)(2,1)} %param.10) | copy-start | bytes 3145732
  16.5 240.8 %all-gather.11.cloned.1.call-start = ((), (), s32[]{:S(2)}) async-start(), calls=%async_computation.4 | async-start | bytes 8912896 | tf_op jit(solution)/shard_map/all_gather | solution.py:109
  40.2 230.5 %reduce-scatter.2.cloned.1.call-start = ((), (), s32[]{:S(2)}) async-start(), calls=%async_computation.1 | async-start | bytes 6291456 | tf_op jit(solution)/shard_map/reduce_scatter | solution.py:134
  86.2 1.9 copy-start.1
  142.9 12.5 %copy-start.2 = (bf16[512,1024]{0,1:T(8,128)(2,1)S(1)}, bf16[512,1024]{0,1:T(8,128)(2,1)}, u32[]{:S(2)}) copy-start(bf16[512,1024]{0,1:T(8,128)(2,1)} %copy.97) | copy-start | bytes 3145732
  142.9 12.5 %copy-start.3 = (f32[8,128,512]{2,1,0:T(8,128)S(1)}, f32[8,128,512]{2,1,0:T(8,128)}, u32[]{:S(2)}) copy-start(f32[8,128,512]{2,1,0:T(8,128)} %fusion.28) | copy-start | bytes 6291460
  257.3 4.2 %copy-start.4 = (f32[8,512,128]{1,2,0:T(8,128)S(1)}, f32[8,512,128]{1,2,0:T(8,128)}, u32[]{:S(2)}) copy-start(f32[8,512,128]{1,2,0:T(8,128)} %fusion.3) | copy-start | bytes 6291460
Sparse Core Ops, SparseCore 0:
  9.6 16.4 all-gather.6
  28.8 114.0 all-gather.8
  146.2 111.0 all-gather.10
  260.0 10.2 reduce-scatter.1
where the time goes:
time: 278 us; the launch traced here: 277 us
  waiting for transfers between devices  141 us (51%)
  matrix products  60.5 us (22%)
  blocking collectives  41 us (15%)
  between operations  13.9 us (5%)
  local copies, waits for them, and re-layouts  11.5 us (4%)
  other arithmetic  8.77 us (3%)
    all_gather x1, waiting for transfers between devices, body(): lax.all_gather(local_adjoint[None], 'ctx', axis=0, tiled=True)  80.5 us
    all_gather x1, waiting for transfers between devices, body(): state_piece = lax.all_gather(local_state[None], 'ctx', axis=0, tiled=True)  52 us
    all_gather x1, blocking collectives, body(): all_logs = lax.all_gather(block_total[None], 'ctx', axis=0, tiled=True)  41 us
    dot_general x1, matrix products, body(): jnp.einsum('nh,nhef->hef', early_factor, state_piece, precision=highest)  12.5 us
    dot_general x1, matrix products, body(): jnp.dot(lax.all_gather(hidden, 'head', axis=1, tiled=True), weight_rows,...  10.1 us
    dot_general x1, matrix products, body(): lax.dot_general(weight_rows, d_flat, (((1,), (1,)), ((), ())), preferred_...  9.65 us
    all_gather x1, waiting for transfers between devices, body(): lax.all_gather(hidden, 'head', axis=1, tiled=True)  8.12 us
    dot_general x1, matrix products, gradients(): jnp.einsum('hts,the->she', weight_kq, grad_heads, preferred_element_type=...  6.32 us
  transfers between devices with their start and end apart: 4, of which 3 were waited for; matrix products, arithmetic and copies ran while one was open for 28% of the time, Pallas kernels for 0%

commit v1 on v0

v1 whole, which is shorter than its diff:
```python
import functools

import jax
import jax.numpy as jnp
from jax import lax
from jax.experimental import pallas as pl
from jax.experimental.pallas import tpu as pltpu
from jax.sharding import PartitionSpec as P

HDIM = 128
LANES = 128
F32, BF16 = jnp.float32, jnp.bfloat16
MIB = 1 << 20

NN = (((1,), (0,)), ((), ()))
NT = (((1,), (1,)), ((), ()))
TN = (((0,), (0,)), ((), ()))


def dot(a, b, dims):
    return lax.dot_general(a, b, dims, preferred_element_type=F32)


def params(mib, **kw):
    return pltpu.CompilerParams(vmem_limit_bytes=mib * MIB, **kw)


def cost(flops, nbytes):
    return pl.CostEstimate(flops=int(flops), bytes_accessed=int(nbytes), transcendentals=0)


def sublanes(count):
    return -(-count // 8) * 8


def expm1_negative(z):
    series = jnp.full_like(z, 1.0)
    for order in range(10, 1, -1):
        series = 1.0 + z * series * (1.0 / order)
    return jnp.where(z > -0.5, z * series, jnp.exp(z) - 1.0)


def column(table, lane, width=LANES):
    return jnp.broadcast_to(table[:, lane : lane + 1], (table.shape[0], width))


def prepare_kernel(heads, hp, scaling, ld_ref, k_ref, v_ref, ks_ref, table_ref, cumt_ref, msg_ref, state_ref, wide):
    rows = ld_ref.shape[0]
    wide[...] = jnp.zeros_like(wide)
    wide[:, :heads] = ld_ref[...]
    logs = wide[...].T[:hp]
    lane = lax.broadcasted_iota(jnp.int32, logs.shape, 1)
    cumulative = logs
    step = 1
    while step < rows:
        moved = pltpu.roll(cumulative, step, 1)
        cumulative = cumulative + jnp.where(lane >= step, moved, 0.0)
        step *= 2
    cumt_ref[...] = cumulative
    total = cumulative[:, rows - 1 :]
    gain = jnp.sqrt(-expm1_negative(2.0 * logs))
    tail = jnp.exp(total - cumulative)
    lead = scaling * jnp.exp(cumulative)
    spare = jnp.zeros((LANES - 4 * hp, rows), F32)
    table = jnp.concatenate([cumulative, gain, tail, lead, spare], axis=0).T
    table_ref[...] = table
    share = jnp.broadcast_to(jnp.exp(total), (hp, LANES))
    high = share.astype(BF16)
    low = (share - high.astype(F32)).astype(BF16)
    base = heads * HDIM
    msg_ref[base:, :] = jnp.concatenate([high.astype(F32), low.astype(F32)], axis=0).astype(BF16)
    for h in range(heads):
        cols = slice(h * HDIM, (h + 1) * HDIM)
        scaled = (column(table, hp + h) * k_ref[:, cols].astype(F32)).astype(BF16)
        ks_ref[:, cols] = scaled
        decayed = (column(table, 2 * hp + h) * scaled.astype(F32)).astype(BF16)
        local = dot(decayed, v_ref[:, cols], TN)
        state_ref[cols, :] = local
        msg_ref[cols, :] = local.astype(BF16)


def prepare(log_decay, keys, values, heads, hp, scaling):
    rows, width = keys.shape
    vm = pl.BlockSpec(memory_space=pltpu.VMEM)
    return pl.pallas_call(
        functools.partial(prepare_kernel, heads, hp, scaling),
        out_shape=(
            jax.ShapeDtypeStruct((rows, width), BF16),
            jax.ShapeDtypeStruct((rows, LANES), F32),
            jax.ShapeDtypeStruct((hp, rows), F32),
            jax.ShapeDtypeStruct((width + 2 * hp, HDIM), BF16),
            jax.ShapeDtypeStruct((width, HDIM), F32),
        ),
        in_specs=[vm] * 3,
        out_specs=(vm,) * 5,
        scratch_shapes=[pltpu.VMEM((rows, LANES), F32)],
        compiler_params=params(24),
        cost_estimate=cost(2 * rows * width * HDIM, 8 * rows * width),
        name="prepare",
    )(log_decay, keys, values)


def project_kernel(places, hp, nparts, place_ref, *refs):
    parts, (w_ref, do_ref, table_ref, q_ref, adj_ref, msg_ref) = refs[:nparts], refs[nparts:]
    step = pl.program_id(0)
    rows, feat = parts[0].shape
    total = None
    for part, ref in enumerate(parts):
        start = pl.multiple_of(place_ref[part] * feat, feat)
        term = dot(ref[...], w_ref[pl.ds(start, feat), :], NN)
        total = term if total is None else total + term
    query = total.astype(BF16)
    q_ref[...] = query
    table = pltpu.roll(table_ref[...], LANES - step * places, 1)
    for h in range(places):
        cols = slice(h * HDIM, (h + 1) * HDIM)
        decayed = (column(table, 3 * hp + h) * query[:, cols].astype(F32)).astype(BF16)
        local = dot(decayed, do_ref[:, cols], TN)
        adj_ref[cols, :] = local
        msg_ref[cols, :] = local.astype(BF16)


def project(parts, owners, w_query, d_out, table, hp):
    rows, feat = parts[0].shape
    depth, width = w_query.shape
    block = min(256, width)
    whole = lambda shape: pl.BlockSpec(shape, lambda j, s: (0, 0))
    tall = lambda r: pl.BlockSpec((r, block), lambda j, s: (0, j))
    flat = pl.BlockSpec((block, HDIM), lambda j, s: (j, 0))
    return pl.pallas_call(
        functools.partial(project_kernel, block // HDIM, hp, len(parts)),
        grid_spec=pltpu.PrefetchScalarGridSpec(
            num_scalar_prefetch=1,
            grid=(width // block,),
            in_specs=[whole((rows, feat))] * len(parts) + [tall(depth), tall(rows), whole((rows, LANES))],
            out_specs=(tall(rows), flat, flat),
        ),
        out_shape=(
            jax.ShapeDtypeStruct((rows, width), BF16),
            jax.ShapeDtypeStruct((width, HDIM), F32),
            jax.ShapeDtypeStruct((width, HDIM), BF16),
        ),
        compiler_params=params(40),
        cost_estimate=cost(2 * rows * width * depth, 2 * (depth * width + rows * depth)),
        name="project",
    )(owners, *parts, w_query, d_out, table)


def inner_kernel(hp, scaling, q_ref, ks_ref, v_ref, do_ref, table_ref, cumt_ref, dq_ref, dk_ref, dv_ref):
    head = pl.program_id(0)
    rows = q_ref.shape[0]
    size = min(256, rows)
    table = pltpu.roll(table_ref[...], LANES - head, 1)
    cum_col = column(table, 0)
    cum_row = cumt_ref[pl.ds(head, 1), :]
    dq = [None] * (rows // size)
    dk = [None] * (rows // size)
    dv = [None] * (rows // size)
    plus = lambda a, b: b if a is None else a + b
    for i in range(rows // size):
        ti = slice(i * size, (i + 1) * size)
        here = jnp.concatenate([cum_col[ti]] * (size // LANES), axis=1)
        for j in range(i + 1):
            sj = slice(j * size, (j + 1) * size)
            gap = here - cum_row[:, sj]
            if i == j:
                keep = lax.broadcasted_iota(jnp.int32, gap.shape, 0) >= lax.broadcasted_iota(
                    jnp.int32, gap.shape, 1
                )
                decays = jnp.where(keep, jnp.exp(jnp.where(keep, gap, 0.0)) * scaling, 0.0)
            else:
                decays = jnp.exp(gap) * scaling
            wdv = (decays * dot(do_ref[ti, :], v_ref[sj, :], NT)).astype(BF16)
            wkq = (decays * dot(q_ref[ti, :], ks_ref[sj, :], NT)).astype(BF16)
            dq[i] = plus(dq[i], dot(wdv, ks_ref[sj, :], NN))
            dk[j] = plus(dk[j], dot(wdv, q_ref[ti, :], TN))
            dv[j] = plus(dv[j], dot(wkq, do_ref[ti, :], TN))
    for i in range(rows // size):
        ti = slice(i * size, (i + 1) * size)
        dq_ref[ti, :] = dq[i]
        dk_ref[ti, :] = dk[i]
        dv_ref[ti, :] = dv[i]


def inner(query, scaled_keys, values, d_out, table, cumt, heads, hp, scaling):
    rows, width = query.shape
    tall = pl.BlockSpec((rows, HDIM), lambda h: (0, h))
    whole = lambda a: pl.BlockSpec(a.shape, lambda h: (0, 0))
    return pl.pallas_call(
        functools.partial(inner_kernel, hp, scaling),
        grid=(heads,),
        in_specs=[tall] * 4 + [whole(table), whole(cumt)],
        out_specs=(tall,) * 3,
        out_shape=(jax.ShapeDtypeStruct((rows, width), F32),) * 3,
        compiler_params=params(32),
        cost_estimate=cost(10 * rows * rows * width, 20 * rows * width),
        name="inner",
    )(query, scaled_keys, values, d_out, table, cumt)


def mix(coef_ref, pieces, heads, h):
    cols = slice(h * HDIM, (h + 1) * HDIM)
    total = None
    for stage, piece in enumerate(pieces):
        row = stage * heads + h
        term = coef_ref[row : row + 1, :] * piece[cols, :].astype(F32)
        total = term if total is None else total + term
    return total.astype(BF16)


def query_kernel(heads, hp, stages, place_ref, *refs):
    pieces = refs[:stages]
    coef_ref, inner_ref, do_ref, table_ref, w_ref, dq_ref, out_ref, held = refs[stages:]

    @pl.when(pl.program_id(0) == 0)
    def _():
        for h in range(heads):
            cols = slice(h * HDIM, (h + 1) * HDIM)
            state = mix(coef_ref, pieces, heads, h)
            carry = dot(do_ref[:, cols], state, NT)
            full = inner_ref[:, cols] + column(table_ref[...], 3 * hp + h) * carry
            held[:, cols] = full.astype(BF16)
        dq_ref[...] = held[...]

    out_ref[...] = dot(held[...], w_ref[...], NT).astype(BF16)


def query_term(pieces, coefs, inner_dq, d_out, table, w_query, place, feat, heads, hp):
    rows, width = d_out.shape
    block = min(512, feat)
    whole = lambda a: pl.BlockSpec(a.shape, lambda j, s: (0,) * a.ndim)
    args = (*pieces, coefs, inner_dq, d_out, table)
    return pl.pallas_call(
        functools.partial(query_kernel, heads, hp, len(pieces)),
        grid_spec=pltpu.PrefetchScalarGridSpec(
            num_scalar_prefetch=1,
            grid=(feat // block,),
            in_specs=[whole(a) for a in args]
            + [pl.BlockSpec((block, width), lambda j, s: (s[0] * (feat // block) + j, 0))],
            out_specs=(
                pl.BlockSpec((rows, width), lambda j, s: (0, 0)),
                pl.BlockSpec((rows, block), lambda j, s: (0, j)),
            ),
            scratch_shapes=[pltpu.VMEM((rows, width), BF16)],
        ),
        out_shape=(
            jax.ShapeDtypeStruct((rows, width), BF16),
            jax.ShapeDtypeStruct((rows, feat), BF16),
        ),
        compiler_params=params(40),
        cost_estimate=cost(2 * rows * width * feat, 2 * (width + rows) * feat + 10 * rows * width),
        name="query_term",
    )(place, *args, w_query)


def term_kernel(place_ref, dq_ref, w_ref, out_ref):
    out_ref[...] = dot(dq_ref[...], w_ref[...], NT).astype(BF16)


def plain_term(d_query, w_query, place, feat):
    rows, width = d_query.shape
    block = min(512, feat)
    return pl.pallas_call(
        term_kernel,
        grid_spec=pltpu.PrefetchScalarGridSpec(
            num_scalar_prefetch=1,
            grid=(feat // block,),
            in_specs=[
                pl.BlockSpec((rows, width), lambda j, s: (0, 0)),
                pl.BlockSpec((block, width), lambda j, s: (s[0] * (feat // block) + j, 0)),
            ],
            out_specs=pl.BlockSpec((rows, block), lambda j, s: (0, j)),
        ),
        out_shape=jax.ShapeDtypeStruct((rows, feat), BF16),
        compiler_params=params(24),
        cost_estimate=cost(2 * rows * width * feat, 2 * (width + rows) * feat),
        name="term",
    )(place, d_query, w_query)


def close_kernel(heads, hp, stages, *refs):
    pieces = refs[:stages]
    coef_ref, dk_ref, dv_ref, ks_ref, v_ref, table_ref, out_k, out_v = refs[stages:]
    for h in range(heads):
        cols = slice(h * HDIM, (h + 1) * HDIM)
        adjoint = mix(coef_ref, pieces, heads, h)
        table = table_ref[...]
        tail, gain = column(table, 2 * hp + h), column(table, hp + h)
        carry_k = dot(v_ref[:, cols], adjoint, NT)
        out_k[:, cols] = (gain * (dk_ref[:, cols] + tail * carry_k)).astype(BF16)
        carry_v = dot(ks_ref[:, cols], adjoint, NN)
        out_v[:, cols] = (dv_ref[:, cols] + tail * carry_v).astype(BF16)


def close(pieces, coefs, dk, dv, scaled_keys, values, table, heads, hp):
    rows, width = dk.shape
    vm = pl.BlockSpec(memory_space=pltpu.VMEM)
    return pl.pallas_call(
        functools.partial(close_kernel, heads, hp, len(pieces)),
        out_shape=(jax.ShapeDtypeStruct((rows, width), BF16),) * 2,
        in_specs=[vm] * (len(pieces) + 6),
        out_specs=(vm,) * 2,
        compiler_params=params(32),
        cost_estimate=cost(4 * rows * width * HDIM, 16 * rows * width),
        name="close",
    )(*pieces, coefs, dk, dv, scaled_keys, values, table)


def body(ctx_size, head_size, hidden, w_query, keys, values, d_out, log_decay):
    rows, feat = hidden.shape
    heads = log_decay.shape[1]
    width = w_query.shape[1]
    hp = sublanes(heads)
    scaling = HDIM ** (-0.5)
    me = lax.axis_index("ctx")
    mine = lax.axis_index("head")

    parts = [hidden]
    for shift in range(1, head_size):
        ring = [(i, (i + shift) % head_size) for i in range(head_size)]
        parts.append(lax.ppermute(hidden, "head", ring))
    owners = jnp.stack([(mine + head_size - s) % head_size for s in range(head_size)]).astype(jnp.int32)

    scaled_keys, table, cumt, state_msg, state = prepare(log_decay, keys, values, heads, hp, scaling)
    query, adjoint, adjoint_msg = project(parts, owners, w_query, d_out, table, hp)

    wide = lambda factor: factor[:heads, None, :]
    cube = lambda flat: flat.reshape(heads, HDIM, HDIM)
    msg = state_msg
    tail_rows = msg[width:]
    share = tail_rows[:hp].astype(F32) + tail_rows[hp:].astype(F32)
    before = jnp.ones_like(share)
    after = jnp.ones_like(share)
    state_pieces, state_coefs, adjoint_pieces, adjoint_coefs = [], [], [], []
    amsg = adjoint_msg
    dist = 1
    while dist < ctx_size:
        upper = (me & dist) != 0
        last = 2 * dist >= ctx_size
        state_coefs.append(jnp.where(upper, before, 0.0)[:heads])
        adjoint_coefs.append(jnp.where(upper, 0.0, after)[:heads])
        if last:
            up = [(i, i + dist) for i in range(ctx_size) if not i & dist]
            down = [(j, i) for i, j in up]
            got = lax.ppermute(msg[:width], "ctx", up)
            agot = lax.ppermute(amsg, "ctx", down)
        else:
            pairs = [(i, i ^ dist) for i in range(ctx_size)]
            got = lax.ppermute(msg, "ctx", pairs)
            agot = lax.ppermute(amsg, "ctx", pairs)
            theirs = got[width : width + hp].astype(F32) + got[width + hp :].astype(F32)
            arrived = cube(got[:width]).astype(F32)
            state = (
                wide(jnp.where(upper, 1.0, theirs)) * cube(state) + wide(jnp.where(upper, share, 1.0)) * arrived
            ).reshape(width, HDIM)
            aarrived = cube(agot).astype(F32)
            adjoint = (
                wide(jnp.where(upper, theirs, 1.0)) * cube(adjoint) + wide(jnp.where(upper, 1.0, share)) * aarrived
            ).reshape(width, HDIM)
            before = jnp.where(upper, before * theirs, before)
            after = jnp.where(upper, after, after * theirs)
            share = share * theirs
            high = share.astype(BF16)
            low = (share - high.astype(F32)).astype(BF16)
            msg = state.astype(BF16)
            if 4 * dist < ctx_size:
                msg = jnp.concatenate([msg, high, low], axis=0)
            amsg = adjoint.astype(BF16)
        state_pieces.append(got)
        adjoint_pieces.append(agot)
        dist *= 2
    state_coefs = jnp.concatenate(state_coefs, axis=0)
    adjoint_coefs = jnp.concatenate(adjoint_coefs, axis=0)

    inner_dq, inner_dk, inner_dv = inner(query, scaled_keys, values, d_out, table, cumt, heads, hp, scaling)

    place = lambda shift: ((mine + shift) % head_size).astype(jnp.int32).reshape(1)
    d_query, term = query_term(
        state_pieces, state_coefs, inner_dq, d_out, table, w_query, place(1), feat, heads, hp
    )
    arrived = []
    for shift in range(1, head_size):
        if shift > 1:
            term = plain_term(d_query, w_query, place(shift), feat)
        ring = [(i, (i + shift) % head_size) for i in range(head_size)]
        arrived.append(lax.ppermute(term, "head", ring))
    summed = plain_term(d_query, w_query, place(0), feat).astype(F32)
    d_keys, d_values = close(
        adjoint_pieces, adjoint_coefs, inner_dk, inner_dv, scaled_keys, values, table, heads, hp
    )
    for piece in arrived:
        summed = summed + piece.astype(F32)
    return (summed.astype(BF16), d_keys, d_values)


def solution(mesh):
    return jax.shard_map(
        functools.partial(body, mesh.shape["ctx"], mesh.shape["head"]),
        mesh=mesh,
        in_specs=(
            P("ctx", "head"),
            P(None, "head"),
            P("ctx", "head"),
            P("ctx", "head"),
            P("ctx", "head"),
            P("ctx", "head"),
        ),
        out_specs=(P("ctx", "head"), P("ctx", "head"), P("ctx", "head")),
        check_vma=False,
    )
```

time: 278 us -> 114 us (0.41)
  waiting for transfers between devices: 141 us -> 43.2 us
  matrix products: 60.5 us -> 0 us
  blocking collectives: 41 us -> 0 us
  Pallas kernels: 0 us -> 35.7 us
  starting transfers between devices: 0.16 us -> 16.5 us
  between operations: 13.9 us -> 0.86 us
  other arithmetic: 8.77 us -> 5.69 us
    all_gather x3 -> x0, waiting for transfers between devices: 141 us -> none  [the longest x1 80.5 us: body(): lax.all_gather(local_adjoint[None], 'ctx', axis=0, tiled=True)]
    dot_general x12 -> x0, matrix products: 60.5 us -> none  [the longest x1 12.5 us: body(): jnp.einsum('nh,nhef->hef', early_factor, state_piece, precision=highest)]
    ppermute x0 -> x10, waiting for transfers between devices: none -> 43.2 us  [the longest x3 19.3 us: body(): agot = lax.ppermute(amsg, 'ctx', pairs)]
    all_gather x1 -> x0, blocking collectives: 41 us -> none  [body(): all_logs = lax.all_gather(block_total[None], 'ctx', axis=0, tiled=True)]
    pallas_call x0 -> x6, Pallas kernels: none -> 35.7 us  [the longest x1 10.2 us: inner(): pl.pallas_call(functools.partial(inner_kernel, hp, scaling), grid=(heads,...]
    ppermute x0 -> x10, starting transfers between devices: none -> 16.5 us  [the longest x3 6.35 us: body(): got = lax.ppermute(msg, 'ctx', pairs)]
    unnamed x16 -> x39, local copies, waits for them, and re-layouts: 5.69 us -> 12 us
    dot_general x1 -> x0, other arithmetic: 4.18 us -> none  [body(): jnp.einsum('nh,nhef->hef', late_factor, adjoint_piece, precision=highest)]
  transfers between devices with their start and end apart: 4 -> 10, of which waited for: 3 -> 7; matrix products, arithmetic and copies ran while one was open for 28% -> 2% of each run, Pallas kernels for 0% -> 23%
where the time goes in v1:
time: 114 us
  waiting for transfers between devices  43.2 us (38%)
  Pallas kernels  35.7 us (31%)
  starting transfers between devices  16.5 us (14%)
  local copies, waits for them, and re-layouts  12 us (11%)
  other arithmetic  5.69 us (5%)
    ppermute x3, waiting for transfers between devices, body(): agot = lax.ppermute(amsg, 'ctx', pairs)  19.3 us
    ppermute x3, waiting for transfers between devices, body(): got = lax.ppermute(msg, 'ctx', pairs)  17.3 us
    unnamed x39, local copies, waits for them, and re-layouts  12 us
    pallas_call x1, Pallas kernels, inner(): pl.pallas_call(functools.partial(inner_kernel, hp, scaling), grid=(heads,...  10.2 us
    pallas_call x1, Pallas kernels, project(): pl.pallas_call(functools.partial(project_kernel, block // HDIM, hp, len(p...  10.1 us
    pallas_call x1, Pallas kernels, query_term(): pl.pallas_call(functools.partial(query_kernel, heads, hp, len(pieces)), g...  6.63 us
    ppermute x1, waiting for transfers between devices, body(): agot = lax.ppermute(amsg, 'ctx', down)  6.61 us
    ppermute x3, starting transfers between devices, body(): got = lax.ppermute(msg, 'ctx', pairs)  6.35 us
  transfers between devices with their start and end apart: 10, of which 7 were waited for; matrix products, arithmetic and copies ran while one was open for 2% of the time, Pallas kernels for 23%

profile of v1, /device:TPU:0, one launch (start us, length us, event | category | flops | bytes accessed | tf_op | source)
XLA Modules:
  0.0 114.0 jit_solution(7041547402291836675)
XLA Ops:
  0.6 0.8 copy.9.ld_ref
  1.5 1.2 %copy-done.1 = bf16[512,1024]{1,0:T(8,128)(2,1)S(1)} copy-done((bf16[512,1024]{1,0:T(8,128)(2,1)S(1)}, bf16[512,1024]{1,0:T(8,128)(2,1)}, u32[]{:S(2)}) %copy-start.1) | copy-done | bytes 1048600
  2.7 1.2 %copy-done.7 = bf16[512,1024]{1,0:T(8,128)(2,1)S(1)} copy-done((bf16[512,1024]{1,0:T(8,128)(2,1)S(1)}, bf16[512,1024]{1,0:T(8,128)(2,1)}, u32[]{:S(2)}) %copy-start.7) | copy-done | bytes 1048600
  3.9 2.7 %prepare.1 = (bf16[512,1024]{1,0:T(8,128)(2,1)S(1)}, f32[512,128]{1,0:T(8,128)S(1)}, f32[8,512]{1,0:T(8,128)S(1)}, bf16[1040,128]{1,0:T(8,128)(2,1)S(1)}, f32[1024,128]{1,0:T(8,128)S(1)}) custom-call(f32[512,8]{1,0:T(8,128)S(1)} %copy.9.ld_ref, bf16[512,1024]{1,0:T(8,128)(2,1)S(1)} %copy-done.7, bf16[512,1024]{1,0:T(8,128)(2,1)S(1)} %copy-done.1), custom_call_target="tpu_custom_call" | custom-call | flops 134217728 | bytes 4194304 | tf_op jit(solution)/shard_map/prepare/pallas_call | solution.py:85
  6.6 1.0 copy-done.10
  7.6 0.7 copy-done.13
  8.3 2.9 %collective-permute-start = (bf16[1040,128]{1,0:T(8,128)(2,1)S(1)}, bf16[1040,128]{1,0:T(8,128)(2,1)S(1)}, u32[]{:S(2)}, u32[]{:S(2)}) collective-permute-start(bf16[1040,128]{1,0:T(8,128)(2,1)S(1)} %get-tuple-element.18), channel_id=1, source_target_pairs={{0,2},{2,0},{4,6},{6,4},{8,10},{10,8},{12,14},{14,12},{16,18},{18,... | collective-permute-start | bytes 798728 | tf_op jit(solution)/shard_map/ppermute | solution.py:349
  11.3 6.4 %collective-permute-done.refs_0_ = bf16[1040,128]{1,0:T(8,128)(2,1)S(1)} collective-permute-done((bf16[1040,128]{1,0:T(8,128)(2,1)S(1)}, bf16[1040,128]{1,0:T(8,128)(2,1)S(1)}, u32[]{:S(2)}, u32[]{:S(2)}) %collective-permute-start) | collective-permute-done | bytes 266272 | tf_op jit(solution)/shard_map/ppermute | solution.py:349
  17.8 1.8 %collective-permute-start.1 = (bf16[1040,128]{1,0:T(8,128)(2,1)S(1)}, bf16[1040,128]{1,0:T(8,128)(2,1)S(1)}, u32[]{:S(2)}, u32[]{:S(2)}) collective-permute-start(bf16[1040,128]{1,0:T(8,128)(2,1)S(1)} %pad_maximum_fusion), channel_id=1, source_target_pairs={{0,4},{2,6},{4,0},{6,2},{8,12},{10,14},{12,8},{14,10},{16,20},{18,... | collective-permute-start | bytes 798728 | tf_op jit(solution)/shard_map/ppermute | solution.py:349
  19.6 5.8 %collective-permute-done.1.refs_1_ = bf16[1040,128]{1,0:T(8,128)(2,1)S(1)} collective-permute-done((bf16[1040,128]{1,0:T(8,128)(2,1)S(1)}, bf16[1040,128]{1,0:T(8,128)(2,1)S(1)}, u32[]{:S(2)}, u32[]{:S(2)}) %collective-permute-start.1) | collective-permute-done | bytes 266272 | tf_op jit(solution)/shard_map/ppermute | solution.py:349
  25.7 1.6 %collective-permute-start.2 = (bf16[1040,128]{1,0:T(8,128)(2,1)S(1)}, bf16[1040,128]{1,0:T(8,128)(2,1)S(1)}, u32[]{:S(2)}, u32[]{:S(2)}) collective-permute-start(bf16[1040,128]{1,0:T(8,128)(2,1)S(1)} %pad_maximum_fusion.1), channel_id=1, source_target_pairs={{0,8},{2,10},{4,12},{6,14},{8,0},{10,2},{12,4},{14,6},{16,24},{18,... | collective-permute-start | bytes 798728 | tf_op jit(solution)/shard_map/ppermute | solution.py:349
  27.3 5.1 %collective-permute-done.2.refs_2_ = bf16[1040,128]{1,0:T(8,128)(2,1)S(1)} collective-permute-done((bf16[1040,128]{1,0:T(8,128)(2,1)S(1)}, bf16[1040,128]{1,0:T(8,128)(2,1)S(1)}, u32[]{:S(2)}, u32[]{:S(2)}) %collective-permute-start.2) | collective-permute-done | bytes 266272 | tf_op jit(solution)/shard_map/ppermute | solution.py:349
  32.6 4.2 %collective-permute-start.3 = (bf16[1024,128]{1,0:T(8,128)(2,1)S(1)}, bf16[1024,128]{1,0:T(8,128)(2,1)S(1)}, u32[]{:S(2)}, u32[]{:S(2)}) collective-permute-start(bf16[1024,128]{1,0:T(8,128)(2,1)S(1)} %fusion.5), channel_id=1, source_target_pairs={{0,16},{2,18},{4,20},{6,22},{8,24},{10,26},{12,28},{14,30},{1,17},... | collective-permute-start | bytes 786440 | tf_op jit(solution)/shard_map/ppermute | solution.py:345
  37.0 0.9 copy-done.14
  37.9 10.1 %project.1 = (bf16[512,1024]{1,0:T(8,128)(2,1)S(1)}, f32[1024,128]{1,0:T(8,128)S(1)}, bf16[1024,128]{1,0:T(8,128)(2,1)S(1)}) custom-call(s32[2]{0:T(128)S(1)} %pad_add_fusion.place_ref, bf16[512,2048]{1,0:T(8,128)(2,1)} %refs_0_.1, bf16[512,2048]{1,0:T(8,128)(2,1)} %collective-permute-done.4.refs_1_, bf16[4096,1024]{1,0:T(8,128)(2,1)} %w_ref.1, ...), custom_call_target="tpu_custom_call" | custom-call | flops 4294967296 | bytes 12582912 | tf_op jit(solution)/shard_map/project/pallas_call | solution.py:130
  48.1 10.2 %inner.1 = (f32[512,1024]{1,0:T(8,128)S(1)}, f32[512,1024]{1,0:T(8,128)S(1)}, f32[512,1024]{1,0:T(8,128)S(1)}) custom-call(bf16[512,1024]{1,0:T(8,128)(2,1)S(1)} %get-tuple-element.21.q_ref, bf16[512,1024]{1,0:T(8,128)(2,1)S(1)} %copy-done.11, bf16[512,1024]{1,0:T(8,128)(2,1)S(1)} %copy-done.2, bf16[512,1024]{1,0:T(8,128)(2,1)S(1)} %copy-done.8, ...), custom_call_target="tpu_custom_call" | custom-call | flops 2684354560 | bytes 10485760 | tf_op jit(solution)/shard_map/inner/pallas_call | solution.py:189
  58.3 1.3 %copy-done.3 = f32[512,1024]{1,0:T(8,128)} copy-done((f32[512,1024]{1,0:T(8,128)}, f32[512,1024]{1,0:T(8,128)S(1)}, u32[]{:S(2)}) %copy-start.3) | copy-done | bytes 2097176
  59.6 1.4 %copy-done.5 = f32[512,1024]{1,0:T(8,128)} copy-done((f32[512,1024]{1,0:T(8,128)}, f32[512,1024]{1,0:T(8,128)S(1)}, u32[]{:S(2)}) %copy-start.5) | copy-done | bytes 2097176
  61.0 6.6 %query_term.1 = (bf16[512,1024]{1,0:T(8,128)(2,1)S(1)}, bf16[512,2048]{1,0:T(8,128)(2,1)}) custom-call(s32[1]{0:T(128)} %bitcast.1.place_ref, bf16[1040,128]{1,0:T(8,128)(2,1)S(1)} %collective-permute-done.refs_0_, bf16[1040,128]{1,0:T(8,128)(2,1)S(1)} %collective-permute-done.1.refs_1_, bf16[1040,128]{1,0:T(8,128)(2,1)S(1)} %collective-permute-done.2.refs_2_, ...), custom_call_target="tpu_custom_call" | custom-call | flops 2147483648 | bytes 11534336 | tf_op jit(solution)/shard_map/query_term/pallas_call | solution.py:233
  67.6 1.5 %collective-permute-start.6 = (bf16[1024,128]{1,0:T(8,128)(2,1)S(1)}, bf16[1024,128]{1,0:T(8,128)(2,1)S(1)}, u32[]{:S(2)}, u32[]{:S(2)}) collective-permute-start(bf16[1024,128]{1,0:T(8,128)(2,1)S(1)} %get-tuple-element.27), channel_id=1, source_target_pairs={{0,2},{2,0},{4,6},{6,4},{8,10},{10,8},{12,14},{14,12},{16,18},{18,... | collective-permute-start | bytes 786440 | tf_op jit(solution)/shard_map/ppermute | solution.py:350
  69.1 7.2 %collective-permute-done.6.refs_0_ = bf16[1024,128]{1,0:T(8,128)(2,1)S(1)} collective-permute-done((bf16[1024,128]{1,0:T(8,128)(2,1)S(1)}, bf16[1024,128]{1,0:T(8,128)(2,1)S(1)}, u32[]{:S(2)}, u32[]{:S(2)}) %collective-permute-start.6) | collective-permute-done | bytes 262176 | tf_op jit(solution)/shard_map/ppermute | solution.py:350
  76.5 1.6 %collective-permute-start.7 = (bf16[1024,128]{1,0:T(8,128)(2,1)S(1)}, bf16[1024,128]{1,0:T(8,128)(2,1)S(1)}, u32[]{:S(2)}, u32[]{:S(2)}) collective-permute-start(bf16[1024,128]{1,0:T(8,128)(2,1)S(1)} %fusion.9), channel_id=1, source_target_pairs={{0,4},{2,6},{4,0},{6,2},{8,12},{10,14},{12,8},{14,10},{16,20},{18,... | collective-permute-start | bytes 786440 | tf_op jit(solution)/shard_map/ppermute | solution.py:350
  78.0 6.4 %collective-permute-done.7.refs_1_ = bf16[1024,128]{1,0:T(8,128)(2,1)S(1)} collective-permute-done((bf16[1024,128]{1,0:T(8,128)(2,1)S(1)}, bf16[1024,128]{1,0:T(8,128)(2,1)S(1)}, u32[]{:S(2)}, u32[]{:S(2)}) %collective-permute-start.7) | collective-permute-done | bytes 262176 | tf_op jit(solution)/shard_map/ppermute | solution.py:350
  84.5 0.9 fusion.10
  85.3 1.6 %collective-permute-start.8 = (bf16[1024,128]{1,0:T(8,128)(2,1)}, bf16[1024,128]{1,0:T(8,128)(2,1)S(1)}, u32[]{:S(2)}, u32[]{:S(2)}) collective-permute-start(bf16[1024,128]{1,0:T(8,128)(2,1)} %fusion.10), channel_id=1, source_target_pairs={{0,8},{2,10},{4,12},{6,14},{8,0},{10,2},{12,4},{14,6},{16,24},{18,... | collective-permute-start | bytes 786440 | tf_op jit(solution)/shard_map/ppermute | solution.py:350
  86.9 5.7 %collective-permute-done.8.refs_2_ = bf16[1024,128]{1,0:T(8,128)(2,1)S(1)} collective-permute-done((bf16[1024,128]{1,0:T(8,128)(2,1)}, bf16[1024,128]{1,0:T(8,128)(2,1)S(1)}, u32[]{:S(2)}, u32[]{:S(2)}) %collective-permute-start.8) | collective-permute-done | bytes 262176 | tf_op jit(solution)/shard_map/ppermute | solution.py:350
  92.8 1.3 %collective-permute-start.9 = (bf16[1024,128]{1,0:T(8,128)(2,1)S(1)}, bf16[1024,128]{1,0:T(8,128)(2,1)S(1)}, u32[]{:S(2)}, u32[]{:S(2)}) collective-permute-start(bf16[1024,128]{1,0:T(8,128)(2,1)S(1)} %fusion.1), channel_id=1, source_target_pairs={{16,0},{18,2},{20,4},{22,6},{24,8},{26,10},{28,12},{30,14},{17,1},... | collective-permute-start | bytes 786440 | tf_op jit(solution)/shard_map/ppermute | solution.py:346
  94.2 3.4 %copy-done = bf16[4096,1024]{1,0:T(8,128)(2,1)S(1)} copy-done((bf16[4096,1024]{1,0:T(8,128)(2,1)S(1)}, bf16[4096,1024]{1,0:T(8,128)(2,1)}, u32[]{:S(2)}) %copy-start) | copy-done | bytes 8388632
  97.6 3.1 %term.1 = bf16[512,2048]{1,0:T(8,128)(2,1)S(1)} custom-call(s32[1]{0:T(128)} %bitcast.place_ref, bf16[512,1024]{1,0:T(8,128)(2,1)S(1)} %get-tuple-element.25.dq_ref, bf16[4096,1024]{1,0:T(8,128)(2,1)S(1)} %copy-done), custom_call_target="tpu_custom_call" | custom-call | flops 2147483648 | bytes 6291456 | tf_op jit(solution)/shard_map/term/pallas_call | solution.py:263
  100.7 6.6 %collective-permute-done.9.refs_3_ = bf16[1024,128]{1,0:T(8,128)(2,1)S(1)} collective-permute-done((bf16[1024,128]{1,0:T(8,128)(2,1)S(1)}, bf16[1024,128]{1,0:T(8,128)(2,1)S(1)}, u32[]{:S(2)}, u32[]{:S(2)}) %collective-permute-start.9) | collective-permute-done | bytes 262176 | tf_op jit(solution)/shard_map/ppermute | solution.py:346
  107.4 2.9 %close.1 = (bf16[512,1024]{1,0:T(8,128)(2,1)}, bf16[512,1024]{1,0:T(8,128)(2,1)}) custom-call(bf16[1024,128]{1,0:T(8,128)(2,1)S(1)} %collective-permute-done.6.refs_0_, bf16[1024,128]{1,0:T(8,128)(2,1)S(1)} %collective-permute-done.7.refs_1_, bf16[1024,128]{1,0:T(8,128)(2,1)S(1)} %copy-done.18, bf16[1024,128]{1,0:T(8,128)(2,1)S(1)} %collective-permute-done.9.refs_3_, ...), custom_call_target="tpu_custom_call" | custom-call | flops 268435456 | bytes 8388608 | tf_op jit(solution)/shard_map/close/pallas_call | solution.py:298
  110.3 3.7 %add_convert_fusion = bf16[512,2048]{1,0:T(8,128)(2,1)} fusion(bf16[512,2048]{1,0:T(8,128)(2,1)} %collective-permute-done.5, bf16[512,2048]{1,0:T(8,128)(2,1)S(1)} %term.1), kind=kLoop, calls=%fused_computation | loop fusion | flops 4194304 | bytes 6291456 | tf_op jit(solution)/shard_map/convert_element_type | solution.py:393
  (55 shorter events, 1.2 us)
Async XLA Ops:
  1.5 1.2 %copy-start.1 = (bf16[512,1024]{1,0:T(8,128)(2,1)S(1)}, bf16[512,1024]{1,0:T(8,128)(2,1)}, u32[]{:S(2)}) copy-start(bf16[512,1024]{1,0:T(8,128)(2,1)} %refs_8_.3) | copy-start | bytes 3145732
  2.7 1.2 %copy-start.7 = (bf16[512,1024]{1,0:T(8,128)(2,1)S(1)}, bf16[512,1024]{1,0:T(8,128)(2,1)}, u32[]{:S(2)}) copy-start(bf16[512,1024]{1,0:T(8,128)(2,1)} %k_ref.1) | copy-start | bytes 3145732
  6.6 1.0 copy-start.10
  7.6 0.7 copy-start.13
  8.3 9.3 %collective-permute-start = (bf16[1040,128]{1,0:T(8,128)(2,1)S(1)}, bf16[1040,128]{1,0:T(8,128)(2,1)S(1)}, u32[]{:S(2)}, u32[]{:S(2)}) collective-permute-start(bf16[1040,128]{1,0:T(8,128)(2,1)S(1)} %get-tuple-element.18), channel_id=1, source_target_pairs={{0,2},{2,0},{4,6},{6,4},{8,10},{10,8},{12,14},{14,12},{16,18},{18,... | collective-permute-start | bytes 798728 | tf_op jit(solution)/shard_map/ppermute | solution.py:349
  11.2 25.7 %collective-permute-start.4 = (bf16[512,2048]{1,0:T(8,128)(2,1)}, bf16[512,2048]{1,0:T(8,128)(2,1)}, u32[]{:S(2)}, u32[]{:S(2)}) collective-permute-start(bf16[512,2048]{1,0:T(8,128)(2,1)} %refs_0_.1), channel_id=1, source_target_pairs={{0,1},{1,0},{2,3},{3,2},{4,5},{5,4},{6,7},{7,6},{8,9},{9,8},{10,11... | collective-permute-start | bytes 6291464 | tf_op jit(solution)/shard_map/ppermute | solution.py:321
  17.8 19.2 %copy-start.8 = (bf16[512,1024]{1,0:T(8,128)(2,1)S(1)}, bf16[512,1024]{1,0:T(8,128)(2,1)}, u32[]{:S(2)}) copy-start(bf16[512,1024]{1,0:T(8,128)(2,1)} %refs_6_.1) | copy-start | bytes 3145732
  17.8 7.6 %collective-permute-start.1 = (bf16[1040,128]{1,0:T(8,128)(2,1)S(1)}, bf16[1040,128]{1,0:T(8,128)(2,1)S(1)}, u32[]{:S(2)}, u32[]{:S(2)}) collective-permute-start(bf16[1040,128]{1,0:T(8,128)(2,1)S(1)} %pad_maximum_fusion), channel_id=1, source_target_pairs={{0,4},{2,6},{4,0},{6,2},{8,12},{10,14},{12,8},{14,10},{16,20},{18,... | collective-permute-start | bytes 798728 | tf_op jit(solution)/shard_map/ppermute | solution.py:349
  25.7 6.7 %collective-permute-start.2 = (bf16[1040,128]{1,0:T(8,128)(2,1)S(1)}, bf16[1040,128]{1,0:T(8,128)(2,1)S(1)}, u32[]{:S(2)}, u32[]{:S(2)}) collective-permute-start(bf16[1040,128]{1,0:T(8,128)(2,1)S(1)} %pad_maximum_fusion.1), channel_id=1, source_target_pairs={{0,8},{2,10},{4,12},{6,14},{8,0},{10,2},{12,4},{14,6},{16,24},{18,... | collective-permute-start | bytes 798728 | tf_op jit(solution)/shard_map/ppermute | solution.py:349
  32.6 28.4 %collective-permute-start.3 = (bf16[1024,128]{1,0:T(8,128)(2,1)S(1)}, bf16[1024,128]{1,0:T(8,128)(2,1)S(1)}, u32[]{:S(2)}, u32[]{:S(2)}) collective-permute-start(bf16[1024,128]{1,0:T(8,128)(2,1)S(1)} %fusion.5), channel_id=1, source_target_pairs={{0,16},{2,18},{4,20},{6,22},{8,24},{10,26},{12,28},{14,30},{1,17},... | collective-permute-start | bytes 786440 | tf_op jit(solution)/shard_map/ppermute | solution.py:345
  37.0 1.0 copy-start.14
  37.9 10.2 %copy-start.2 = (bf16[512,1024]{1,0:T(8,128)(2,1)S(1)}, bf16[512,1024]{1,0:T(8,128)(2,1)}, u32[]{:S(2)}) copy-start(bf16[512,1024]{1,0:T(8,128)(2,1)} %refs_8_.3) | copy-start | bytes 3145732
  37.9 10.2 %copy-start.11 = (bf16[512,1024]{1,0:T(8,128)(2,1)S(1)}, bf16[512,1024]{1,0:T(8,128)(2,1)}, u32[]{:S(2)}) copy-start(bf16[512,1024]{1,0:T(8,128)(2,1)} %copy-done.10) | copy-start | bytes 3145732
  37.9 10.2 %copy-start.15 = (f32[512,128]{1,0:T(8,128)S(1)}, f32[512,128]{1,0:T(8,128)}, u32[]{:S(2)}) copy-start(f32[512,128]{1,0:T(8,128)} %copy-done.13) | copy-start | bytes 786436
  48.1 12.9 %copy-start.9 = (bf16[512,1024]{1,0:T(8,128)(2,1)S(1)}, bf16[512,1024]{1,0:T(8,128)(2,1)}, u32[]{:S(2)}) copy-start(bf16[512,1024]{1,0:T(8,128)(2,1)} %refs_6_.1) | copy-start | bytes 3145732
  58.3 1.3 %copy-start.3 = (f32[512,1024]{1,0:T(8,128)}, f32[512,1024]{1,0:T(8,128)S(1)}, u32[]{:S(2)}) copy-start(f32[512,1024]{1,0:T(8,128)S(1)} %get-tuple-element.29.refs_5_) | copy-start | bytes 6291460
  59.6 1.4 %copy-start.5 = (f32[512,1024]{1,0:T(8,128)}, f32[512,1024]{1,0:T(8,128)S(1)}, u32[]{:S(2)}) copy-start(f32[512,1024]{1,0:T(8,128)S(1)} %get-tuple-element.30.refs_6_) | copy-start | bytes 6291460
  67.6 42.6 %collective-permute-start.5 = (bf16[512,2048]{1,0:T(8,128)(2,1)}, bf16[512,2048]{1,0:T(8,128)(2,1)}, u32[]{:S(2)}, u32[]{:S(2)}) collective-permute-start(bf16[512,2048]{1,0:T(8,128)(2,1)} %get-tuple-element.26), channel_id=1, source_target_pairs={{0,1},{1,0},{2,3},{3,2},{4,5},{5,4},{6,7},{7,6},{8,9},{9,8},{10,11... | collective-permute-start | bytes 6291464 | tf_op jit(solution)/shard_map/ppermute | solution.py:386
  67.6 8.7 %collective-permute-start.6 = (bf16[1024,128]{1,0:T(8,128)(2,1)S(1)}, bf16[1024,128]{1,0:T(8,128)(2,1)S(1)}, u32[]{:S(2)}, u32[]{:S(2)}) collective-permute-start(bf16[1024,128]{1,0:T(8,128)(2,1)S(1)} %get-tuple-element.27), channel_id=1, source_target_pairs={{0,2},{2,0},{4,6},{6,4},{8,10},{10,8},{12,14},{14,12},{16,18},{18,... | collective-permute-start | bytes 786440 | tf_op jit(solution)/shard_map/ppermute | solution.py:350
  76.5 8.0 %collective-permute-start.7 = (bf16[1024,128]{1,0:T(8,128)(2,1)S(1)}, bf16[1024,128]{1,0:T(8,128)(2,1)S(1)}, u32[]{:S(2)}, u32[]{:S(2)}) collective-permute-start(bf16[1024,128]{1,0:T(8,128)(2,1)S(1)} %fusion.9), channel_id=1, source_target_pairs={{0,4},{2,6},{4,0},{6,2},{8,12},{10,14},{12,8},{14,10},{16,20},{18,... | collective-permute-start | bytes 786440 | tf_op jit(solution)/shard_map/ppermute | solution.py:350
  85.3 7.3 %collective-permute-start.8 = (bf16[1024,128]{1,0:T(8,128)(2,1)}, bf16[1024,128]{1,0:T(8,128)(2,1)S(1)}, u32[]{:S(2)}, u32[]{:S(2)}) collective-permute-start(bf16[1024,128]{1,0:T(8,128)(2,1)} %fusion.10), channel_id=1, source_target_pairs={{0,8},{2,10},{4,12},{6,14},{8,0},{10,2},{12,4},{14,6},{16,24},{18,... | collective-permute-start | bytes 786440 | tf_op jit(solution)/shard_map/ppermute | solution.py:350
  92.6 1.6 %copy-start.17 = (bf16[1024,128]{1,0:T(8,128)(2,1)}, bf16[1024,128]{1,0:T(8,128)(2,1)S(1)}, u32[]{:S(2)}) copy-start(bf16[1024,128]{1,0:T(8,128)(2,1)S(1)} %collective-permute-done.8.refs_2_) | copy-start | bytes 786436
  92.8 14.5 %collective-permute-start.9 = (bf16[1024,128]{1,0:T(8,128)(2,1)S(1)}, bf16[1024,128]{1,0:T(8,128)(2,1)S(1)}, u32[]{:S(2)}, u32[]{:S(2)}) collective-permute-start(bf16[1024,128]{1,0:T(8,128)(2,1)S(1)} %fusion.1), channel_id=1, source_target_pairs={{16,0},{18,2},{20,4},{22,6},{24,8},{26,10},{28,12},{30,14},{17,1},... | collective-permute-start | bytes 786440 | tf_op jit(solution)/shard_map/ppermute | solution.py:346
  94.2 3.4 %copy-start = (bf16[4096,1024]{1,0:T(8,128)(2,1)S(1)}, bf16[4096,1024]{1,0:T(8,128)(2,1)}, u32[]{:S(2)}) copy-start(bf16[4096,1024]{1,0:T(8,128)(2,1)} %w_ref.1) | copy-start | bytes 25165828
  97.6 9.8 %copy-start.4 = (f32[512,1024]{1,0:T(8,128)S(1)}, f32[512,1024]{1,0:T(8,128)}, u32[]{:S(2)}) copy-start(f32[512,1024]{1,0:T(8,128)} %copy-done.3) | copy-start | bytes 6291460
  97.6 9.8 %copy-start.6 = (f32[512,1024]{1,0:T(8,128)S(1)}, f32[512,1024]{1,0:T(8,128)}, u32[]{:S(2)}) copy-start(f32[512,1024]{1,0:T(8,128)} %copy-done.5) | copy-start | bytes 6291460
  97.6 9.8 %copy-start.12 = (bf16[512,1024]{1,0:T(8,128)(2,1)S(1)}, bf16[512,1024]{1,0:T(8,128)(2,1)}, u32[]{:S(2)}) copy-start(bf16[512,1024]{1,0:T(8,128)(2,1)} %copy-done.10) | copy-start | bytes 3145732
  97.6 9.8 %copy-start.16 = (f32[512,128]{1,0:T(8,128)S(1)}, f32[512,128]{1,0:T(8,128)}, u32[]{:S(2)}) copy-start(f32[512,128]{1,0:T(8,128)} %copy-done.13) | copy-start | bytes 786436
  97.6 9.8 %copy-start.18 = (bf16[1024,128]{1,0:T(8,128)(2,1)S(1)}, bf16[1024,128]{1,0:T(8,128)(2,1)}, u32[]{:S(2)}) copy-start(bf16[1024,128]{1,0:T(8,128)(2,1)} %copy-done.17) | copy-start | bytes 786436

commit v2 on v1

v2 whole, which is shorter than its diff:
```python
import functools
import math

import jax
import jax.numpy as jnp
from jax import lax
from jax.experimental import pallas as pl
from jax.experimental.pallas import tpu as pltpu
from jax.sharding import PartitionSpec as P

HDIM = 128
LANES = 128
F32, BF16 = jnp.float32, jnp.bfloat16
MIB = 1 << 20
VM = pl.BlockSpec(memory_space=pltpu.VMEM)

NN = (((1,), (0,)), ((), ()))
NT = (((1,), (1,)), ((), ()))
TN = (((0,), (0,)), ((), ()))


def dot(a, b, dims):
    return lax.dot_general(a, b, dims, preferred_element_type=F32)


def params(mib, **kw):
    return pltpu.CompilerParams(vmem_limit_bytes=mib * MIB, **kw)


def cost(flops, nbytes):
    return pl.CostEstimate(flops=int(flops), bytes_accessed=int(nbytes), transcendentals=0)


def sublanes(count):
    return -(-count // 8) * 8


def expm1_negative(z):
    series = jnp.full_like(z, 1.0)
    for order in range(10, 1, -1):
        series = 1.0 + z * series * (1.0 / order)
    return jnp.where(z > -0.5, z * series, jnp.exp(z) - 1.0)


def column(table, lane, width=LANES):
    return jnp.broadcast_to(table[:, lane : lane + 1], (table.shape[0], width))


def prepare_kernel(
    heads, hp, scaling, ld_hbm, k_hbm, v_hbm, ks_ref, table_ref, cumt_ref, msg_ref, state_ref, ld, kbuf, vbuf, sems
):
    rows = kbuf.shape[0]
    copies = [pltpu.make_async_copy(ld_hbm, ld, sems.at[0])]
    for h in range(heads):
        cols = pl.ds(h * HDIM, HDIM)
        copies.append(pltpu.make_async_copy(k_hbm.at[:, cols], kbuf.at[:, cols], sems.at[1 + 2 * h]))
        copies.append(pltpu.make_async_copy(v_hbm.at[:, cols], vbuf.at[:, cols], sems.at[2 + 2 * h]))
    for copy in copies:
        copy.start()
    copies[0].wait()
    logs = ld[...]
    if heads < hp:
        logs = jnp.concatenate([logs, jnp.zeros((hp - heads, rows), F32)], axis=0)
    lane = lax.broadcasted_iota(jnp.int32, logs.shape, 1)
    cumulative = logs
    step = 1
    while step < rows:
        moved = pltpu.roll(cumulative, step, 1)
        cumulative = cumulative + jnp.where(lane >= step, moved, 0.0)
        step *= 2
    cumt_ref[...] = cumulative
    total = cumulative[:, rows - 1 :]
    gain = jnp.sqrt(-expm1_negative(2.0 * logs))
    tail = jnp.exp(total - cumulative)
    lead = scaling * jnp.exp(cumulative)
    spare = jnp.zeros((LANES - 4 * hp, rows), F32)
    table = jnp.concatenate([cumulative, gain, tail, lead, spare], axis=0).T
    table_ref[...] = table
    share = jnp.broadcast_to(jnp.exp(total), (hp, LANES))
    high = share.astype(BF16)
    low = (share - high.astype(F32)).astype(BF16)
    base = heads * HDIM
    msg_ref[base:, :] = jnp.concatenate([high.astype(F32), low.astype(F32)], axis=0).astype(BF16)
    for h in range(heads):
        cols = slice(h * HDIM, (h + 1) * HDIM)
        copies[1 + 2 * h].wait()
        scaled = (column(table, hp + h) * kbuf[:, cols].astype(F32)).astype(BF16)
        ks_ref[:, cols] = scaled
        decayed = (column(table, 2 * hp + h) * scaled.astype(F32)).astype(BF16)
        copies[2 + 2 * h].wait()
        local = dot(decayed, vbuf[:, cols], TN)
        state_ref[cols, :] = local
        msg_ref[cols, :] = local.astype(BF16)


def prepare(logs, keys, values, heads, hp, scaling):
    rows, width = keys.shape
    return pl.pallas_call(
        functools.partial(prepare_kernel, heads, hp, scaling),
        out_shape=(
            jax.ShapeDtypeStruct((rows, width), BF16),
            jax.ShapeDtypeStruct((rows, LANES), F32),
            jax.ShapeDtypeStruct((hp, rows), F32),
            jax.ShapeDtypeStruct((width + 2 * hp, HDIM), BF16),
            jax.ShapeDtypeStruct((width, HDIM), F32),
        ),
        in_specs=[pl.BlockSpec(memory_space=pl.ANY)] * 3,
        out_specs=(VM,) * 5,
        scratch_shapes=[
            pltpu.VMEM((heads, rows), F32),
            pltpu.VMEM((rows, width), BF16),
            pltpu.VMEM((rows, width), BF16),
            pltpu.SemaphoreType.DMA((1 + 2 * heads,)),
        ],
        compiler_params=params(8),
        cost_estimate=cost(2 * rows * width * HDIM, 8 * rows * width),
        name="prepare",
    )(logs, keys, values)


def project_kernel(hp, nparts, place_ref, *refs):
    parts, (w_ref, do_ref, table_ref, q_ref, adj_ref, msg_ref) = refs[:nparts], refs[nparts:]
    rows, feat = parts[0].shape
    width = w_ref.shape[1]
    block = min(256, width)
    starts = [pl.multiple_of(place_ref[part] * feat, feat) for part in range(nparts)]
    for first in range(0, width, block):
        wide = slice(first, first + block)
        total = None
        for start, ref in zip(starts, parts):
            term = dot(ref[...], w_ref[pl.ds(start, feat), wide], NN)
            total = term if total is None else total + term
        query = total.astype(BF16)
        q_ref[:, wide] = query
        for h in range(first // HDIM, (first + block) // HDIM):
            cols = slice(h * HDIM, (h + 1) * HDIM)
            lead = column(table_ref[...], 3 * hp + h)
            decayed = (lead * query[:, h * HDIM - first : (h + 1) * HDIM - first].astype(F32)).astype(BF16)
            local = dot(decayed, do_ref[:, cols], TN)
            adj_ref[cols, :] = local
            msg_ref[cols, :] = local.astype(BF16)


def project(parts, owners, w_query, d_out, table, hp):
    rows, feat = parts[0].shape
    depth, width = w_query.shape
    return pl.pallas_call(
        functools.partial(project_kernel, hp, len(parts)),
        in_specs=[pl.BlockSpec(memory_space=pltpu.SMEM)] + [VM] * (len(parts) + 3),
        out_specs=(VM,) * 3,
        out_shape=(
            jax.ShapeDtypeStruct((rows, width), BF16),
            jax.ShapeDtypeStruct((width, HDIM), F32),
            jax.ShapeDtypeStruct((width, HDIM), BF16),
        ),
        compiler_params=params(10),
        cost_estimate=cost(2 * rows * width * depth, 2 * (depth * width + rows * depth)),
        name="project",
    )(owners, *parts, w_query, d_out, table)


def inner_kernel(first, last, q_ref, ks_ref, v_ref, do_ref, table_ref, cumt_ref, dq_ref, dk_ref, dv_ref):
    rows = q_ref.shape[0]
    row = lax.broadcasted_iota(jnp.int32, (rows, rows), 0)
    keep = row >= lax.broadcasted_iota(jnp.int32, (rows, rows), 1)
    shift = -0.5 * math.log2(HDIM)
    turn = math.log2(math.e)
    for h in range(first, last):
        cols = slice(h * HDIM, (h + 1) * HDIM)
        outs = slice((h - first) * HDIM, (h - first + 1) * HDIM)
        later = column(table_ref[...], h) * turn + shift
        sooner = cumt_ref[h : h + 1, :] * turn
        gap = jnp.concatenate([later] * (rows // LANES), axis=1) - sooner
        decays = jnp.exp2(jnp.where(keep, gap, -1e30))
        query, scaled, grad = q_ref[:, cols], ks_ref[:, cols], do_ref[:, cols]
        wdv = (decays * dot(grad, v_ref[:, cols], NT)).astype(BF16)
        wkq = (decays * dot(query, scaled, NT)).astype(BF16)
        dq_ref[:, outs] = dot(wdv, scaled, NN)
        dk_ref[:, outs] = dot(query, wdv, TN).T
        dv_ref[:, outs] = dot(grad, wkq, TN).T


def inner(first, last, query, scaled_keys, values, d_out, table, cumt):
    rows = query.shape[0]
    width = (last - first) * HDIM
    return pl.pallas_call(
        functools.partial(inner_kernel, first, last),
        in_specs=[VM] * 6,
        out_specs=(VM,) * 3,
        out_shape=(jax.ShapeDtypeStruct((rows, width), F32),) * 3,
        compiler_params=params(16),
        cost_estimate=cost(10 * rows * rows * width, 20 * rows * width),
        name="inner",
    )(query, scaled_keys, values, d_out, table, cumt)


def mix(coef_ref, pieces, heads, h):
    cols = slice(h * HDIM, (h + 1) * HDIM)
    total = None
    for stage, piece in enumerate(pieces):
        row = stage * heads + h
        term = coef_ref[row : row + 1, :] * piece[cols, :].astype(F32)
        total = term if total is None else total + term
    return total.astype(BF16)


def query_kernel(heads, hp, stages, place_ref, *refs):
    pieces = refs[:stages]
    coef_ref, do_ref, table_ref, w_ref = refs[stages : stages + 4]
    inner_refs, (dq_ref, out_ref) = refs[stages + 4 : -2], refs[-2:]
    each = heads // len(inner_refs)
    for h in range(heads):
        cols = slice(h * HDIM, (h + 1) * HDIM)
        state = mix(coef_ref, pieces, heads, h)
        carry = dot(do_ref[:, cols], state, NT)
        local = inner_refs[h // each][:, (h % each) * HDIM : (h % each + 1) * HDIM]
        dq_ref[:, cols] = (local + column(table_ref[...], 3 * hp + h) * carry).astype(BF16)
    term_kernel(place_ref, dq_ref, w_ref, out_ref)


def query_term(pieces, coefs, inner_dq, d_out, table, w_query, place, feat, heads, hp):
    rows, width = d_out.shape
    args = (*pieces, coefs, d_out, table, w_query, *inner_dq)
    return pl.pallas_call(
        functools.partial(query_kernel, heads, hp, len(pieces)),
        in_specs=[pl.BlockSpec(memory_space=pltpu.SMEM)] + [VM] * len(args),
        out_specs=(VM,) * 2,
        out_shape=(
            jax.ShapeDtypeStruct((rows, width), BF16),
            jax.ShapeDtypeStruct((rows, feat), BF16),
        ),
        compiler_params=params(10),
        cost_estimate=cost(2 * rows * width * feat, 2 * (width + rows) * feat + 10 * rows * width),
        name="query_term",
    )(place, *args)


def term_kernel(place_ref, dq_ref, w_ref, out_ref):
    feat = out_ref.shape[1]
    block = min(512, feat)
    for first in range(0, feat, block):
        start = pl.multiple_of(place_ref[0] * feat + first, block)
        out_ref[:, first : first + block] = dot(dq_ref[...], w_ref[pl.ds(start, block), :], NT).astype(BF16)


def plain_term(d_query, w_query, place, feat):
    rows, width = d_query.shape
    return pl.pallas_call(
        term_kernel,
        in_specs=[pl.BlockSpec(memory_space=pltpu.SMEM), VM, VM],
        out_specs=VM,
        out_shape=jax.ShapeDtypeStruct((rows, feat), BF16),
        compiler_params=params(10),
        cost_estimate=cost(2 * rows * width * feat, 2 * (width + rows) * feat),
        name="term",
    )(place, d_query, w_query)


def close_kernel(heads, hp, stages, *refs):
    pieces = refs[:stages]
    coef_ref, ks_ref, v_ref, table_ref = refs[stages : stages + 4]
    rest, (out_k, out_v) = refs[stages + 4 : -2], refs[-2:]
    dks, dvs = rest[: len(rest) // 2], rest[len(rest) // 2 :]
    each = heads // len(dks)
    for h in range(heads):
        cols = slice(h * HDIM, (h + 1) * HDIM)
        part = slice((h % each) * HDIM, (h % each + 1) * HDIM)
        adjoint = mix(coef_ref, pieces, heads, h)
        table = table_ref[...]
        tail, gain = column(table, 2 * hp + h), column(table, hp + h)
        carry_k = dot(v_ref[:, cols], adjoint, NT)
        out_k[:, cols] = (gain * (dks[h // each][:, part] + tail * carry_k)).astype(BF16)
        carry_v = dot(ks_ref[:, cols], adjoint, NN)
        out_v[:, cols] = (dvs[h // each][:, part] + tail * carry_v).astype(BF16)


def close(pieces, coefs, dks, dvs, scaled_keys, values, table, heads, hp):
    rows, width = values.shape
    args = (*pieces, coefs, scaled_keys, values, table, *dks, *dvs)
    return pl.pallas_call(
        functools.partial(close_kernel, heads, hp, len(pieces)),
        out_shape=(jax.ShapeDtypeStruct((rows, width), BF16),) * 2,
        in_specs=[VM] * len(args),
        out_specs=(VM,) * 2,
        compiler_params=params(8),
        cost_estimate=cost(4 * rows * width * HDIM, 16 * rows * width),
        name="close",
    )(*args)


def body(ctx_size, head_size, hidden, w_query, keys, values, d_out, log_decay):
    rows, feat = hidden.shape
    heads = log_decay.shape[1]
    width = w_query.shape[1]
    hp = sublanes(heads)
    scaling = HDIM ** (-0.5)
    me = lax.axis_index("ctx")
    mine = lax.axis_index("head")

    parts = [hidden]
    for shift in range(1, head_size):
        ring = [(i, (i + shift) % head_size) for i in range(head_size)]
        parts.append(lax.ppermute(hidden, "head", ring))
    owners = jnp.stack([(mine + head_size - s) % head_size for s in range(head_size)]).astype(jnp.int32)

    scaled_keys, table, cumt, msg, state = prepare(log_decay.T, keys, values, heads, hp, scaling)
    query, adjoint, amsg = project(parts, owners, w_query, d_out, table, hp)

    wide = lambda factor: factor[:heads, None, :]
    cube = lambda flat: flat.reshape(heads, HDIM, HDIM)
    split = lambda f: (f.astype(BF16), (f - f.astype(BF16).astype(F32)).astype(BF16))
    joined = lambda pair: pair[:hp].astype(F32) + pair[hp:].astype(F32)
    stages = (ctx_size - 1).bit_length()

    def send(array, stage, up):
        dist = 1 << stage
        if stage < stages - 1:
            pairs = [(i, i ^ dist) for i in range(ctx_size)]
        else:
            pairs = [(i, i + dist) if up else (i + dist, i) for i in range(ctx_size) if not i & dist]
        return lax.ppermute(array, "ctx", pairs)

    uppers = [(me & (1 << stage)) != 0 for stage in range(stages)]
    shares, others = [joined(msg[width:])], []
    got, agot = [], []
    before, after = [jnp.ones_like(shares[0])], [jnp.ones_like(shares[0])]

    def fold_state(stage, state):
        upper, arrived = uppers[stage], cube(got[stage][:width]).astype(F32)
        theirs = joined(got[stage][width:])
        others.append(theirs)
        own, other = jnp.where(upper, 1.0, theirs), jnp.where(upper, shares[stage], 1.0)
        state = (wide(own) * cube(state) + wide(other) * arrived).reshape(width, HDIM)
        shares.append(shares[stage] * theirs)
        before.append(jnp.where(upper, before[stage] * theirs, before[stage]))
        after.append(jnp.where(upper, after[stage], after[stage] * theirs))
        msg = state.astype(BF16)
        if stage + 2 < stages:
            msg = jnp.concatenate([msg, *split(shares[-1])], axis=0)
        return msg, state

    def fold_adjoint(stage, adjoint):
        upper, arrived = uppers[stage], cube(agot[stage]).astype(F32)
        own, other = jnp.where(upper, others[stage], 1.0), jnp.where(upper, 1.0, shares[stage])
        adjoint = (wide(own) * cube(adjoint) + wide(other) * arrived).reshape(width, HDIM)
        return adjoint.astype(BF16), adjoint

    half = max(1, heads // 2)
    pending = [(first, first + half) for first in range(0, heads, half)]
    inner_parts = []

    def next_inner():
        return inner(*pending.pop(0), query, scaled_keys, values, d_out, table, cumt)

    barrier = lax.optimization_barrier
    for stage in range(stages):
        arrived = send(msg if stage < stages - 1 else msg[:width], stage, True)
        if stage == 0:
            arrived, query, adjoint, amsg = barrier((arrived, query, adjoint, amsg))
        else:
            agot.append(send(amsg, stage - 1, False))
            if pending and (stage == 1 or stage == stages - 1):
                part = next_inner()
                arrived, *part = barrier((arrived, *part))
                inner_parts.append(part)
        got.append(arrived)
        if stage < stages - 1:
            msg, state = fold_state(stage, state)
        if stage >= 1:
            amsg, adjoint = fold_adjoint(stage - 1, adjoint)
    while pending:
        inner_parts.append(next_inner())
    agot.append(send(amsg, stages - 1, False))
    got[-1], _ = barrier((got[-1], amsg))

    state_coefs = [jnp.where(u, f, 0.0)[:heads] for u, f in zip(uppers, before)]
    adjoint_coefs = [jnp.where(u, 0.0, f)[:heads] for u, f in zip(uppers, after)]
    state_coefs = jnp.concatenate(state_coefs, axis=0)
    adjoint_coefs = jnp.concatenate(adjoint_coefs, axis=0)
    dqs, dks, dvs = zip(*inner_parts)

    place = lambda shift: ((mine + shift) % head_size).astype(jnp.int32).reshape(1)
    d_query, term = query_term(got, state_coefs, dqs, d_out, table, w_query, place(1), feat, heads, hp)
    arrived = []
    for shift in range(1, head_size):
        if shift > 1:
            term = plain_term(d_query, w_query, place(shift), feat)
        ring = [(i, (i + shift) % head_size) for i in range(head_size)]
        arrived.append(lax.ppermute(term, "head", ring))
    summed = plain_term(d_query, w_query, place(0), feat).astype(F32)
    d_keys, d_values = close(agot, adjoint_coefs, dks, dvs, scaled_keys, values, table, heads, hp)
    for piece in arrived:
        summed = summed + piece.astype(F32)
    return (summed.astype(BF16), d_keys, d_values)


def solution(mesh):
    return jax.shard_map(
        functools.partial(body, mesh.shape["ctx"], mesh.shape["head"]),
        mesh=mesh,
        in_specs=(
            P("ctx", "head"),
            P(None, "head"),
            P("ctx", "head"),
            P("ctx", "head"),
            P("ctx", "head"),
            P("ctx", "head"),
        ),
        out_specs=(P("ctx", "head"), P("ctx", "head"), P("ctx", "head")),
        check_vma=False,
    )
```

time: 114 us -> 97.5 us (0.86)
  the two profiles are of different devices: /device:TPU:0 before, /device:TPU:4 now
where the time goes in v2:
time: 97.5 us; the launch traced here: 96.7 us
  Pallas kernels  31.7 us (33%)
  local copies, waits for them, and re-layouts  28.9 us (30%)
  waiting for transfers between devices  14.9 us (15%)
  starting transfers between devices  12.2 us (13%)
  other arithmetic  8.13 us (8%)
    unnamed x76, local copies, waits for them, and re-layouts  28.8 us
    ppermute x8, waiting for transfers between devices, send(): return lax.ppermute(array, 'ctx', pairs)  14.9 us
    ppermute x8, starting transfers between devices, send(): return lax.ppermute(array, 'ctx', pairs)  12.1 us
    pallas_call x1, Pallas kernels, project(): pl.pallas_call(functools.partial(project_kernel, hp, len(parts)), in_spec...  11.3 us
    pallas_call x1, Pallas kernels, prepare(): pl.pallas_call(functools.partial(prepare_kernel, heads, hp, scaling), out...  5.67 us
    pallas_call x2, Pallas kernels, inner(): pl.pallas_call(functools.partial(inner_kernel, first, last), in_specs=[VM...  5.33 us
    pallas_call x1, Pallas kernels, query_term(): pl.pallas_call(functools.partial(query_kernel, heads, hp, len(pieces)), i...  4.15 us
    convert_element_type x1, other arithmetic, body(): return (summed.astype(BF16), d_keys, d_values)  3.69 us
  transfers between devices with their start and end apart: 10, of which 3 were waited for; matrix products, arithmetic and copies ran while one was open for 4% of the time, Pallas kernels for 29%

profile of v2, /device:TPU:4, one launch (start us, length us, event | category | flops | bytes accessed | tf_op | source)
XLA Modules:
  0.0 96.7 jit_solution(3782035087268915604)
XLA Ops:
  0.7 1.2 %copy-done.3 = bf16[512,1024]{1,0:T(8,128)(2,1)S(1)} copy-done((bf16[512,1024]{1,0:T(8,128)(2,1)S(1)}, bf16[512,1024]{1,0:T(8,128)(2,1)}, u32[]{:S(2)}) %copy-start.3) | copy-done | bytes 1048600
  1.9 1.2 %copy-done.5 = bf16[512,1024]{1,0:T(8,128)(2,1)S(1)} copy-done((bf16[512,1024]{1,0:T(8,128)(2,1)S(1)}, bf16[512,1024]{1,0:T(8,128)(2,1)}, u32[]{:S(2)}) %copy-start.5) | copy-done | bytes 1048600
  3.9 5.7 %prepare.1 = (bf16[512,1024]{1,0:T(8,128)(2,1)S(1)}, f32[512,128]{1,0:T(8,128)S(1)}, f32[8,512]{1,0:T(8,128)S(1)}, bf16[1040,128]{1,0:T(8,128)(2,1)}, f32[1024,128]{1,0:T(8,128)S(1)}) custom-call(f32[8,512]{1,0:T(8,128)S(1)} %bitcast.104, bf16[512,1024]{1,0:T(8,128)(2,1)S(1)} %copy-done.5, bf16[512,1024]{1,0:T(8,128)(2,1)S(1)} %copy-done.3), custom_call_target="tpu_custom_call" | custom-call | flops 134217728 | bytes 4194304 | tf_op jit(solution)/shard_map/prepare/pallas_call | solution.py:98
  9.6 1.0 copy-done.10
  11.2 1.5 %collective-permute-start = (bf16[1040,128]{1,0:T(8,128)(2,1)}, bf16[1040,128]{1,0:T(8,128)(2,1)S(1)}, u32[]{:S(2)}, u32[]{:S(2)}) collective-permute-start(bf16[1040,128]{1,0:T(8,128)(2,1)} %get-tuple-element.34), channel_id=1, source_target_pairs={{0,2},{2,0},{4,6},{6,4},{8,10},{10,8},{12,14},{14,12},{16,18},{18,... | collective-permute-start | bytes 798728 | tf_op jit(solution)/shard_map/ppermute | solution.py:321
  12.8 3.4 %copy-done = bf16[4096,1024]{1,0:T(8,128)(2,1)S(1)} copy-done((bf16[4096,1024]{1,0:T(8,128)(2,1)S(1)}, bf16[4096,1024]{1,0:T(8,128)(2,1)}, u32[]{:S(2)}) %copy-start) | copy-done | bytes 8388632
  17.1 1.6 %copy-done.33 = bf16[512,2048]{1,0:T(8,128)(2,1)S(1)} copy-done((bf16[512,2048]{1,0:T(8,128)(2,1)S(1)}, bf16[512,2048]{1,0:T(8,128)(2,1)}, u32[]{:S(2)}) %copy-start.33) | copy-done | bytes 2097176
  18.7 11.3 %project.1 = (bf16[512,1024]{1,0:T(8,128)(2,1)S(1)}, f32[1024,128]{1,0:T(8,128)S(1)}, bf16[1024,128]{1,0:T(8,128)(2,1)S(1)}) custom-call(s32[2]{0:T(128)S(1)} %pad_add_fusion.place_ref, bf16[512,2048]{1,0:T(8,128)(2,1)S(1)} %copy-done.33, bf16[512,2048]{1,0:T(8,128)(2,1)} %collective-permute-done.1.refs_1_, bf16[4096,1024]{1,0:T(8,128)(2,1)S(1)} %copy-done, ...), custom_call_target="tpu_custom_call" | custom-call | flops 4294967296 | bytes 12582912 | tf_op jit(solution)/shard_map/project/pallas_call | solution.py:147
  31.7 1.2 %copy-done.7 = bf16[512,1024]{1,0:T(8,128)(2,1)S(1)} copy-done((bf16[512,1024]{1,0:T(8,128)(2,1)S(1)}, bf16[512,1024]{1,0:T(8,128)(2,1)}, u32[]{:S(2)}) %copy-start.7) | copy-done | bytes 1048600
  32.9 1.2 %copy-done.11 = bf16[512,1024]{1,0:T(8,128)(2,1)S(1)} copy-done((bf16[512,1024]{1,0:T(8,128)(2,1)S(1)}, bf16[512,1024]{1,0:T(8,128)(2,1)}, u32[]{:S(2)}) %copy-start.11) | copy-done | bytes 1048600
  35.1 1.2 %copy-done.36 = bf16[512,1024]{1,0:T(8,128)(2,1)S(1)} copy-done((bf16[512,1024]{1,0:T(8,128)(2,1)S(1)}, bf16[512,1024]{1,0:T(8,128)(2,1)}, u32[]{:S(2)}) %copy-start.36) | copy-done | bytes 1048600
  36.3 2.6 %inner.2 = (f32[512,512]{1,0:T(8,128)S(1)}, f32[512,512]{1,0:T(8,128)S(1)}, f32[512,512]{1,0:T(8,128)S(1)}) custom-call(bf16[512,1024]{1,0:T(8,128)(2,1)S(1)} %copy-done.36, bf16[512,1024]{1,0:T(8,128)(2,1)S(1)} %copy-done.11, bf16[512,1024]{1,0:T(8,128)(2,1)S(1)} %copy-done.4, bf16[512,1024]{1,0:T(8,128)(2,1)S(1)} %copy-done.7, f32[512,128]{1,0:T(8,128)S(1)} %copy-done.26, ...), custom_call_target="tpu_custom_call" | custom-call | flops 1342177280 | bytes 5242880 | tf_op jit(solution)/shard_map/inner/pallas_call | solution.py:186
  38.9 1.0 copy-done.22
  41.0 2.0 %collective-permute-start.3 = (bf16[1040,128]{1,0:T(8,128)(2,1)}, bf16[1040,128]{1,0:T(8,128)(2,1)S(1)}, u32[]{:S(2)}, u32[]{:S(2)}) collective-permute-start(bf16[1040,128]{1,0:T(8,128)(2,1)} %pad_maximum_fusion.1), channel_id=1, source_target_pairs={{0,8},{2,10},{4,12},{6,14},{8,0},{10,2},{12,4},{14,6},{16,24},{18,... | collective-permute-start | bytes 798728 | tf_op jit(solution)/shard_map/ppermute | solution.py:321
  43.8 1.5 %collective-permute-start.6 = (bf16[1024,128]{1,0:T(8,128)(2,1)}, bf16[1024,128]{1,0:T(8,128)(2,1)S(1)}, u32[]{:S(2)}, u32[]{:S(2)}) collective-permute-start(bf16[1024,128]{1,0:T(8,128)(2,1)} %fusion.9), channel_id=1, source_target_pairs={{0,4},{2,6},{4,0},{6,2},{8,12},{10,14},{12,8},{14,10},{16,20},{18,... | collective-permute-start | bytes 786440 | tf_op jit(solution)/shard_map/ppermute | solution.py:321
  45.4 1.2 %copy-done.8 = bf16[512,1024]{1,0:T(8,128)(2,1)S(1)} copy-done((bf16[512,1024]{1,0:T(8,128)(2,1)S(1)}, bf16[512,1024]{1,0:T(8,128)(2,1)}, u32[]{:S(2)}) %copy-start.8) | copy-done | bytes 1048600
  46.6 1.2 %copy-done.12 = bf16[512,1024]{1,0:T(8,128)(2,1)S(1)} copy-done((bf16[512,1024]{1,0:T(8,128)(2,1)S(1)}, bf16[512,1024]{1,0:T(8,128)(2,1)}, u32[]{:S(2)}) %copy-start.12) | copy-done | bytes 1048600
  48.8 1.2 %copy-done.37 = bf16[512,1024]{1,0:T(8,128)(2,1)S(1)} copy-done((bf16[512,1024]{1,0:T(8,128)(2,1)S(1)}, bf16[512,1024]{1,0:T(8,128)(2,1)}, u32[]{:S(2)}) %copy-start.37) | copy-done | bytes 1048600
  50.0 2.8 %inner.3 = (f32[512,512]{1,0:T(8,128)S(1)}, f32[512,512]{1,0:T(8,128)S(1)}, f32[512,512]{1,0:T(8,128)S(1)}) custom-call(bf16[512,1024]{1,0:T(8,128)(2,1)S(1)} %copy-done.37, bf16[512,1024]{1,0:T(8,128)(2,1)S(1)} %copy-done.12, bf16[512,1024]{1,0:T(8,128)(2,1)S(1)} %copy-done.4, bf16[512,1024]{1,0:T(8,128)(2,1)S(1)} %copy-done.8, f32[512,128]{1,0:T(8,128)S(1)} %copy-done.27, ...), custom_call_target="tpu_custom_call" | custom-call | flops 1342177280 | bytes 5242880 | tf_op jit(solution)/shard_map/inner/pallas_call | solution.py:186
  52.8 1.0 copy-done.18
  54.7 4.6 %collective-permute-start.4 = (bf16[1024,128]{1,0:T(8,128)(2,1)S(1)}, bf16[1024,128]{1,0:T(8,128)(2,1)S(1)}, u32[]{:S(2)}, u32[]{:S(2)}) collective-permute-start(bf16[1024,128]{1,0:T(8,128)(2,1)S(1)} %fusion.5), channel_id=1, source_target_pairs={{0,16},{2,18},{4,20},{6,22},{8,24},{10,26},{12,28},{14,30},{1,17},... | collective-permute-start | bytes 786440 | tf_op jit(solution)/shard_map/ppermute | solution.py:321
  59.5 1.8 %collective-permute-done.7.refs_2_ = bf16[1024,128]{1,0:T(8,128)(2,1)S(1)} collective-permute-done((bf16[1024,128]{1,0:T(8,128)(2,1)S(1)}, bf16[1024,128]{1,0:T(8,128)(2,1)S(1)}, u32[]{:S(2)}, u32[]{:S(2)}) %collective-permute-start.7) | collective-permute-done | bytes 262176 | tf_op jit(solution)/shard_map/ppermute | solution.py:321
  61.3 0.9 fusion.1
  62.3 2.7 %collective-permute-done.4.refs_3_ = bf16[1024,128]{1,0:T(8,128)(2,1)S(1)} collective-permute-done((bf16[1024,128]{1,0:T(8,128)(2,1)S(1)}, bf16[1024,128]{1,0:T(8,128)(2,1)S(1)}, u32[]{:S(2)}, u32[]{:S(2)}) %collective-permute-start.4) | collective-permute-done | bytes 262176 | tf_op jit(solution)/shard_map/ppermute | solution.py:321
  65.0 3.4 %copy-done.1 = bf16[4096,1024]{1,0:T(8,128)(2,1)S(1)} copy-done((bf16[4096,1024]{1,0:T(8,128)(2,1)S(1)}, bf16[4096,1024]{1,0:T(8,128)(2,1)}, u32[]{:S(2)}) %copy-start.1) | copy-done | bytes 8388632
  68.4 4.2 %query_term.1 = (bf16[512,1024]{1,0:T(8,128)(2,1)S(1)}, bf16[512,2048]{1,0:T(8,128)(2,1)}) custom-call(s32[1]{0:T(128)} %bitcast.1.place_ref, bf16[1040,128]{1,0:T(8,128)(2,1)S(1)} %collective-permute-done.refs_0_, bf16[1040,128]{1,0:T(8,128)(2,1)S(1)} %collective-permute-done.2.refs_1_, bf16[1040,128]{1,0:T(8,128)(2,1)S(1)} %collective-permute-done.3.refs_2_, ...), custom_call_target="tpu_custom_call" | custom-call | flops 2147483648 | bytes 11534336 | tf_op jit(solution)/shard_map/query_term/pallas_call | solution.py:224
  72.5 1.3 %collective-permute-start.9 = (bf16[1024,128]{1,0:T(8,128)(2,1)}, bf16[1024,128]{1,0:T(8,128)(2,1)S(1)}, u32[]{:S(2)}, u32[]{:S(2)}) collective-permute-start(bf16[1024,128]{1,0:T(8,128)(2,1)} %fusion.1), channel_id=1, source_target_pairs={{16,0},{18,2},{20,4},{22,6},{24,8},{26,10},{28,12},{30,14},{17,1},... | collective-permute-start | bytes 786440 | tf_op jit(solution)/shard_map/ppermute | solution.py:321
  73.9 3.4 %copy-done.2 = bf16[4096,1024]{1,0:T(8,128)(2,1)S(1)} copy-done((bf16[4096,1024]{1,0:T(8,128)(2,1)S(1)}, bf16[4096,1024]{1,0:T(8,128)(2,1)}, u32[]{:S(2)}) %copy-start.2) | copy-done | bytes 8388632
  77.3 2.4 %term.1 = bf16[512,2048]{1,0:T(8,128)(2,1)S(1)} custom-call(s32[1]{0:T(128)} %bitcast.place_ref, bf16[512,1024]{1,0:T(8,128)(2,1)S(1)} %get-tuple-element.57.dq_ref, bf16[4096,1024]{1,0:T(8,128)(2,1)S(1)} %copy-done.2), custom_call_target="tpu_custom_call" | custom-call | flops 2147483648 | bytes 6291456 | tf_op jit(solution)/shard_map/term/pallas_call | solution.py:248
  79.7 10.3 %collective-permute-done.9.refs_3_ = bf16[1024,128]{1,0:T(8,128)(2,1)S(1)} collective-permute-done((bf16[1024,128]{1,0:T(8,128)(2,1)}, bf16[1024,128]{1,0:T(8,128)(2,1)S(1)}, u32[]{:S(2)}, u32[]{:S(2)}) %collective-permute-start.9) | collective-permute-done | bytes 262176 | tf_op jit(solution)/shard_map/ppermute | solution.py:321
  90.1 2.9 %close.1 = (bf16[512,1024]{1,0:T(8,128)(2,1)}, bf16[512,1024]{1,0:T(8,128)(2,1)}) custom-call(bf16[1024,128]{1,0:T(8,128)(2,1)S(1)} %collective-permute-done.5.refs_0_, bf16[1024,128]{1,0:T(8,128)(2,1)S(1)} %collective-permute-done.6.refs_1_, bf16[1024,128]{1,0:T(8,128)(2,1)S(1)} %copy-done.31, bf16[1024,128]{1,0:T(8,128)(2,1)S(1)} %collective-permute-done.9.refs_3_, ...), custom_call_target="tpu_custom_call" | custom-call | flops 268435456 | bytes 8388608 | tf_op jit(solution)/shard_map/close/pallas_call | solution.py:280
  93.0 3.7 %add_convert_fusion = bf16[512,2048]{1,0:T(8,128)(2,1)} fusion(bf16[512,2048]{1,0:T(8,128)(2,1)} %collective-permute-done.8, bf16[512,2048]{1,0:T(8,128)(2,1)S(1)} %term.1), kind=kLoop, calls=%fused_computation | loop fusion | flops 4194304 | bytes 6291456 | tf_op jit(solution)/shard_map/convert_element_type | solution.py:394
  (93 shorter events, 9.2 us)
Async XLA Ops:
  0.6 12.2 %collective-permute-start.1 = (bf16[512,2048]{1,0:T(8,128)(2,1)}, bf16[512,2048]{1,0:T(8,128)(2,1)}, u32[]{:S(2)}, u32[]{:S(2)}) collective-permute-start(bf16[512,2048]{1,0:T(8,128)(2,1)} %refs_0_.1), channel_id=1, source_target_pairs={{0,1},{1,0},{2,3},{3,2},{4,5},{5,4},{6,7},{7,6},{8,9},{9,8},{10,11... | collective-permute-start | bytes 6291464 | tf_op jit(solution)/shard_map/ppermute | solution.py:303
  0.7 1.2 %copy-start.3 = (bf16[512,1024]{1,0:T(8,128)(2,1)S(1)}, bf16[512,1024]{1,0:T(8,128)(2,1)}, u32[]{:S(2)}) copy-start(bf16[512,1024]{1,0:T(8,128)(2,1)} %refs_6_.1) | copy-start | bytes 3145732
  3.9 8.9 %copy-start.6 = (bf16[512,1024]{1,0:T(8,128)(2,1)S(1)}, bf16[512,1024]{1,0:T(8,128)(2,1)}, u32[]{:S(2)}) copy-start(bf16[512,1024]{1,0:T(8,128)(2,1)} %refs_5_.1) | copy-start | bytes 3145732
  11.2 18.8 %collective-permute-start = (bf16[1040,128]{1,0:T(8,128)(2,1)}, bf16[1040,128]{1,0:T(8,128)(2,1)S(1)}, u32[]{:S(2)}, u32[]{:S(2)}) collective-permute-start(bf16[1040,128]{1,0:T(8,128)(2,1)} %get-tuple-element.34), channel_id=1, source_target_pairs={{0,2},{2,0},{4,6},{6,4},{8,10},{10,8},{12,14},{14,12},{16,18},{18,... | collective-permute-start | bytes 798728 | tf_op jit(solution)/shard_map/ppermute | solution.py:321
  12.8 3.4 %copy-start = (bf16[4096,1024]{1,0:T(8,128)(2,1)S(1)}, bf16[4096,1024]{1,0:T(8,128)(2,1)}, u32[]{:S(2)}) copy-start(bf16[4096,1024]{1,0:T(8,128)(2,1)} %w_ref.1) | copy-start | bytes 25165828
  17.1 1.6 %copy-start.33 = (bf16[512,2048]{1,0:T(8,128)(2,1)S(1)}, bf16[512,2048]{1,0:T(8,128)(2,1)}, u32[]{:S(2)}) copy-start(bf16[512,2048]{1,0:T(8,128)(2,1)} %refs_0_.1) | copy-start | bytes 6291460
  18.7 13.0 %copy-start.4 = (bf16[512,1024]{1,0:T(8,128)(2,1)S(1)}, bf16[512,1024]{1,0:T(8,128)(2,1)}, u32[]{:S(2)}) copy-start(bf16[512,1024]{1,0:T(8,128)(2,1)} %refs_6_.1) | copy-start | bytes 3145732
  31.1 8.8 %collective-permute-start.2 = (bf16[1040,128]{1,0:T(8,128)(2,1)S(1)}, bf16[1040,128]{1,0:T(8,128)(2,1)S(1)}, u32[]{:S(2)}, u32[]{:S(2)}) collective-permute-start(bf16[1040,128]{1,0:T(8,128)(2,1)S(1)} %pad_maximum_fusion), channel_id=1, source_target_pairs={{0,4},{2,6},{4,0},{6,2},{8,12},{10,14},{12,8},{14,10},{16,20},{18,... | collective-permute-start | bytes 798728 | tf_op jit(solution)/shard_map/ppermute | solution.py:321
  31.6 11.4 %collective-permute-start.5 = (bf16[1024,128]{1,0:T(8,128)(2,1)}, bf16[1024,128]{1,0:T(8,128)(2,1)S(1)}, u32[]{:S(2)}, u32[]{:S(2)}) collective-permute-start(bf16[1024,128]{1,0:T(8,128)(2,1)} %copy-done.34), channel_id=1, source_target_pairs={{0,2},{2,0},{4,6},{6,4},{8,10},{10,8},{12,14},{14,12},{16,18},{18,... | collective-permute-start | bytes 786440 | tf_op jit(solution)/shard_map/ppermute | solution.py:321
  31.7 1.2 %copy-start.7 = (bf16[512,1024]{1,0:T(8,128)(2,1)S(1)}, bf16[512,1024]{1,0:T(8,128)(2,1)}, u32[]{:S(2)}) copy-start(bf16[512,1024]{1,0:T(8,128)(2,1)} %refs_5_.1) | copy-start | bytes 3145732
  39.9 3.2 %copy-start.14 = (f32[512,512]{1,0:T(8,128)}, f32[512,512]{1,0:T(8,128)S(1)}, u32[]{:S(2)}) copy-start(f32[512,512]{1,0:T(8,128)S(1)} %get-tuple-element.59.refs_8_) | copy-start | bytes 3145732
  39.9 4.0 %copy-start.16 = (f32[512,512]{1,0:T(8,128)}, f32[512,512]{1,0:T(8,128)S(1)}, u32[]{:S(2)}) copy-start(f32[512,512]{1,0:T(8,128)S(1)} %get-tuple-element.61.refs_10_) | copy-start | bytes 3145732
  41.0 13.5 %collective-permute-start.3 = (bf16[1040,128]{1,0:T(8,128)(2,1)}, bf16[1040,128]{1,0:T(8,128)(2,1)S(1)}, u32[]{:S(2)}, u32[]{:S(2)}) collective-permute-start(bf16[1040,128]{1,0:T(8,128)(2,1)} %pad_maximum_fusion.1), channel_id=1, source_target_pairs={{0,8},{2,10},{4,12},{6,14},{8,0},{10,2},{12,4},{14,6},{16,24},{18,... | collective-permute-start | bytes 798728 | tf_op jit(solution)/shard_map/ppermute | solution.py:321
  43.8 9.9 %collective-permute-start.6 = (bf16[1024,128]{1,0:T(8,128)(2,1)}, bf16[1024,128]{1,0:T(8,128)(2,1)S(1)}, u32[]{:S(2)}, u32[]{:S(2)}) collective-permute-start(bf16[1024,128]{1,0:T(8,128)(2,1)} %fusion.9), channel_id=1, source_target_pairs={{0,4},{2,6},{4,0},{6,2},{8,12},{10,14},{12,8},{14,10},{16,20},{18,... | collective-permute-start | bytes 786440 | tf_op jit(solution)/shard_map/ppermute | solution.py:321
  53.7 8.5 %copy-start.20 = (f32[512,512]{1,0:T(8,128)}, f32[512,512]{1,0:T(8,128)S(1)}, u32[]{:S(2)}) copy-start(f32[512,512]{1,0:T(8,128)S(1)} %get-tuple-element.62.refs_11_) | copy-start | bytes 3145732
  53.7 11.2 %copy-start.9 = (bf16[512,1024]{1,0:T(8,128)(2,1)S(1)}, bf16[512,1024]{1,0:T(8,128)(2,1)}, u32[]{:S(2)}) copy-start(bf16[512,1024]{1,0:T(8,128)(2,1)} %refs_5_.1) | copy-start | bytes 3145732
  53.8 11.2 %copy-start.23 = (f32[512,512]{1,0:T(8,128)S(1)}, f32[512,512]{1,0:T(8,128)}, u32[]{:S(2)}) copy-start(f32[512,512]{1,0:T(8,128)} %copy-done.22) | copy-start | bytes 3145732
  53.8 11.2 %copy-start.28 = (f32[512,128]{1,0:T(8,128)S(1)}, f32[512,128]{1,0:T(8,128)}, u32[]{:S(2)}) copy-start(f32[512,128]{1,0:T(8,128)} %copy-done.24) | copy-start | bytes 786436
  54.0 7.4 %collective-permute-start.7 = (bf16[1024,128]{1,0:T(8,128)(2,1)S(1)}, bf16[1024,128]{1,0:T(8,128)(2,1)S(1)}, u32[]{:S(2)}, u32[]{:S(2)}) collective-permute-start(bf16[1024,128]{1,0:T(8,128)(2,1)S(1)} %fusion.10), channel_id=1, source_target_pairs={{0,8},{2,10},{4,12},{6,14},{8,0},{10,2},{12,4},{14,6},{16,24},{18,... | collective-permute-start | bytes 786440 | tf_op jit(solution)/shard_map/ppermute | solution.py:321
  54.7 10.2 %collective-permute-start.4 = (bf16[1024,128]{1,0:T(8,128)(2,1)S(1)}, bf16[1024,128]{1,0:T(8,128)(2,1)S(1)}, u32[]{:S(2)}, u32[]{:S(2)}) collective-permute-start(bf16[1024,128]{1,0:T(8,128)(2,1)S(1)} %fusion.5), channel_id=1, source_target_pairs={{0,16},{2,18},{4,20},{6,22},{8,24},{10,26},{12,28},{14,30},{1,17},... | collective-permute-start | bytes 786440 | tf_op jit(solution)/shard_map/ppermute | solution.py:321
  61.3 11.2 %copy-start.30 = (bf16[1024,128]{1,0:T(8,128)(2,1)}, bf16[1024,128]{1,0:T(8,128)(2,1)S(1)}, u32[]{:S(2)}) copy-start(bf16[1024,128]{1,0:T(8,128)(2,1)S(1)} %collective-permute-done.7.refs_2_) | copy-start | bytes 786436
  65.0 3.4 %copy-start.1 = (bf16[4096,1024]{1,0:T(8,128)(2,1)S(1)}, bf16[4096,1024]{1,0:T(8,128)(2,1)}, u32[]{:S(2)}) copy-start(bf16[4096,1024]{1,0:T(8,128)(2,1)} %w_ref.1) | copy-start | bytes 25165828
  72.5 20.5 %collective-permute-start.8 = (bf16[512,2048]{1,0:T(8,128)(2,1)}, bf16[512,2048]{1,0:T(8,128)(2,1)}, u32[]{:S(2)}, u32[]{:S(2)}) collective-permute-start(bf16[512,2048]{1,0:T(8,128)(2,1)} %get-tuple-element.58), channel_id=1, source_target_pairs={{0,1},{1,0},{2,3},{3,2},{4,5},{5,4},{6,7},{7,6},{8,9},{9,8},{10,11... | collective-permute-start | bytes 6291464 | tf_op jit(solution)/shard_map/ppermute | solution.py:389
  72.5 17.5 %collective-permute-start.9 = (bf16[1024,128]{1,0:T(8,128)(2,1)}, bf16[1024,128]{1,0:T(8,128)(2,1)S(1)}, u32[]{:S(2)}, u32[]{:S(2)}) collective-permute-start(bf16[1024,128]{1,0:T(8,128)(2,1)} %fusion.1), channel_id=1, source_target_pairs={{16,0},{18,2},{20,4},{22,6},{24,8},{26,10},{28,12},{30,14},{17,1},... | collective-permute-start | bytes 786440 | tf_op jit(solution)/shard_map/ppermute | solution.py:321
  73.9 3.4 %copy-start.2 = (bf16[4096,1024]{1,0:T(8,128)(2,1)S(1)}, bf16[4096,1024]{1,0:T(8,128)(2,1)}, u32[]{:S(2)}) copy-start(bf16[4096,1024]{1,0:T(8,128)(2,1)} %w_ref.1) | copy-start | bytes 25165828
  77.3 12.7 %copy-start.13 = (bf16[512,1024]{1,0:T(8,128)(2,1)S(1)}, bf16[512,1024]{1,0:T(8,128)(2,1)}, u32[]{:S(2)}) copy-start(bf16[512,1024]{1,0:T(8,128)(2,1)} %copy-done.10) | copy-start | bytes 3145732
  77.3 12.7 %copy-start.15 = (f32[512,512]{1,0:T(8,128)S(1)}, f32[512,512]{1,0:T(8,128)}, u32[]{:S(2)}) copy-start(f32[512,512]{1,0:T(8,128)} %copy-done.14) | copy-start | bytes 3145732
  77.3 12.7 %copy-start.17 = (f32[512,512]{1,0:T(8,128)S(1)}, f32[512,512]{1,0:T(8,128)}, u32[]{:S(2)}) copy-start(f32[512,512]{1,0:T(8,128)} %copy-done.16) | copy-start | bytes 3145732
  77.3 12.8 %copy-start.19 = (f32[512,512]{1,0:T(8,128)S(1)}, f32[512,512]{1,0:T(8,128)}, u32[]{:S(2)}) copy-start(f32[512,512]{1,0:T(8,128)} %copy-done.18) | copy-start | bytes 3145732
  77.3 12.8 %copy-start.21 = (f32[512,512]{1,0:T(8,128)S(1)}, f32[512,512]{1,0:T(8,128)}, u32[]{:S(2)}) copy-start(f32[512,512]{1,0:T(8,128)} %copy-done.20) | copy-start | bytes 3145732
  77.3 12.8 %copy-start.29 = (f32[512,128]{1,0:T(8,128)S(1)}, f32[512,128]{1,0:T(8,128)}, u32[]{:S(2)}) copy-start(f32[512,128]{1,0:T(8,128)} %copy-done.24) | copy-start | bytes 786436
  77.3 12.8 %copy-start.31 = (bf16[1024,128]{1,0:T(8,128)(2,1)S(1)}, bf16[1024,128]{1,0:T(8,128)(2,1)}, u32[]{:S(2)}) copy-start(bf16[1024,128]{1,0:T(8,128)(2,1)} %copy-done.30) | copy-start | bytes 786436
  (16 other events, 16.5 us)

commit v3 on v2

v3 whole, which is shorter than its diff:
```python
import functools
import math

import jax
import jax.numpy as jnp
from jax import lax
from jax.experimental import pallas as pl
from jax.experimental.pallas import tpu as pltpu
from jax.sharding import PartitionSpec as P

HDIM = 128
LANES = 128
F32, BF16 = jnp.float32, jnp.bfloat16
MIB = 1 << 20
VM = pl.BlockSpec(memory_space=pltpu.VMEM)
SM = pl.BlockSpec(memory_space=pltpu.SMEM)
HB = pl.BlockSpec(memory_space=pltpu.HBM)

NN = (((1,), (0,)), ((), ()))
NT = (((1,), (1,)), ((), ()))
TN = (((0,), (0,)), ((), ()))


def dot(a, b, dims):
    return lax.dot_general(a, b, dims, preferred_element_type=F32)


def params(mib, **kw):
    return pltpu.CompilerParams(vmem_limit_bytes=mib * MIB, **kw)


def pinned(array):
    return pltpu.with_memory_space_constraint(array, pltpu.HBM)


def cost(flops, nbytes):
    return pl.CostEstimate(flops=int(flops), bytes_accessed=int(nbytes), transcendentals=0)


def sublanes(count):
    return -(-count // 8) * 8


def expm1_negative(z):
    series = jnp.full_like(z, 1.0)
    for order in range(10, 1, -1):
        series = 1.0 + z * series * (1.0 / order)
    return jnp.where(z > -0.5, z * series, jnp.exp(z) - 1.0)


def column(table, lane, width=LANES):
    return jnp.broadcast_to(table[:, lane : lane + 1], (table.shape[0], width))


class Copies:
    def __init__(self, sems):
        self.sems, self.count, self.out = sems, 0, []

    def start(self, src, dst):
        copy = pltpu.make_async_copy(src, dst, self.sems.at[self.count])
        self.count += 1
        copy.start()
        return copy

    def store(self, src, dst):
        self.out.append(self.start(src, dst))

    def finish(self):
        for copy in self.out:
            copy.wait()


def groups(heads):
    size = min(4, heads)
    return [(f, f + size, slice(f * HDIM, (f + size) * HDIM)) for f in range(0, heads, size)]


def turned(facts):
    spare = jnp.zeros((LANES - facts.shape[0], facts.shape[1]), F32)
    return jnp.concatenate([facts, spare], axis=0).T


def prepare_kernel(
    heads, hp, scaling, ld_hbm, k_hbm, v_hbm, ks_hbm, facts_hbm, msg_ref, state_ref, ld, facts_ref, kbuf, vbuf, ksbuf, sems
):
    rows = kbuf.shape[0]
    copies = Copies(sems)
    ld_in = copies.start(ld_hbm, ld)
    parts = [pl.ds(f, rows // 2) for f in (0, rows // 2)]
    k_in = [copies.start(k_hbm.at[p, :], kbuf.at[p, :]) for p in parts]
    v_in = [copies.start(v_hbm.at[p, :], vbuf.at[p, :]) for p in parts]
    ld_in.wait()
    logs = ld[...]
    if heads < hp:
        logs = jnp.concatenate([logs, jnp.zeros((hp - heads, rows), F32)], axis=0)
    lane = lax.broadcasted_iota(jnp.int32, logs.shape, 1)
    cumulative = logs
    step = 1
    while step < rows:
        moved = pltpu.roll(cumulative, step, 1)
        cumulative = cumulative + jnp.where(lane >= step, moved, 0.0)
        step *= 2
    total = cumulative[:, rows - 1 :]
    gain = jnp.sqrt(-expm1_negative(2.0 * logs))
    tail = jnp.exp(total - cumulative)
    lead = scaling * jnp.exp(cumulative)
    facts = jnp.concatenate([cumulative, gain, tail, lead], axis=0)
    facts_ref[...] = facts
    copies.store(facts_ref, facts_hbm)
    table = turned(facts)
    share = jnp.broadcast_to(jnp.exp(total), (hp, LANES))
    high = share.astype(BF16)
    low = (share - high.astype(F32)).astype(BF16)
    base = heads * HDIM
    msg_ref[base:, :] = jnp.concatenate([high.astype(F32), low.astype(F32)], axis=0).astype(BF16)
    for copy in k_in + v_in:
        copy.wait()
    for first, last, wide in groups(heads):
        for h in range(first, last):
            cols = slice(h * HDIM, (h + 1) * HDIM)
            scaled = (column(table, hp + h) * kbuf[:, cols].astype(F32)).astype(BF16)
            ksbuf[:, cols] = scaled
            decayed = (column(table, 2 * hp + h) * scaled.astype(F32)).astype(BF16)
            local = dot(decayed, vbuf[:, cols], TN)
            state_ref[cols, :] = local
            msg_ref[cols, :] = local.astype(BF16)
        copies.store(ksbuf.at[:, wide], ks_hbm.at[:, wide])
    copies.finish()


def prepare(logs, keys, values, heads, hp, scaling):
    rows, width = keys.shape
    buf = pltpu.VMEM((rows, width), BF16)
    return pl.pallas_call(
        functools.partial(prepare_kernel, heads, hp, scaling),
        out_shape=(
            jax.ShapeDtypeStruct((rows, width), BF16),
            jax.ShapeDtypeStruct((4 * hp, rows), F32),
            jax.ShapeDtypeStruct((width + 2 * hp, HDIM), BF16),
            jax.ShapeDtypeStruct((width, HDIM), F32),
        ),
        in_specs=[HB] * 3,
        out_specs=(HB, HB, VM, VM),
        scratch_shapes=[
            pltpu.VMEM((heads, rows), F32),
            pltpu.VMEM((4 * hp, rows), F32),
            buf,
            buf,
            buf,
            pltpu.SemaphoreType.DMA((6 + len(groups(heads)),)),
        ],
        compiler_params=params(12),
        cost_estimate=cost(2 * rows * width * HDIM, 8 * rows * width),
        name="prepare",
    )(pinned(logs), pinned(keys), pinned(values))


def project_kernel(hp, nparts, chunk, place_ref, *refs):
    parts, (w_hbm, do_hbm, facts_hbm, q_hbm, adj_ref, msg_ref) = refs[:nparts], refs[nparts : nparts + 6]
    hbuf, wbuf, dobuf, facts_ref, qbuf, total, sems = refs[nparts + 6 :]
    rows, feat = parts[0].shape
    width = wbuf.shape[1]
    heads = width // HDIM
    copies = Copies(sems)
    loads = []
    for part, ref in enumerate(parts):
        for first in range(0, feat, chunk):
            here = pl.ds(part * feat + first, chunk)
            start = pl.multiple_of(place_ref[part] * feat + first, chunk)
            loads.append(
                (
                    slice(part * feat + first, part * feat + first + chunk),
                    copies.start(ref.at[:, pl.ds(first, chunk)], hbuf.at[:, here]),
                    copies.start(w_hbm.at[pl.ds(start, chunk), :], wbuf.at[here, :]),
                )
            )
    late = [copies.start(facts_hbm, facts_ref), copies.start(do_hbm, dobuf)]
    block = min(256, width)
    for order, (here, h_in, w_in) in enumerate(loads):
        h_in.wait()
        w_in.wait()
        for first in range(0, width, block):
            wide = slice(first, first + block)
            term = dot(hbuf[:, here], wbuf[here, wide], NN)
            if order == 0:
                total[:, wide] = term
            elif order < len(loads) - 1:
                total[:, wide] += term
            else:
                qbuf[:, wide] = (total[:, wide] + term).astype(BF16)
    for copy in late:
        copy.wait()
    copies.store(qbuf, q_hbm)
    table = turned(facts_ref[...])
    for h in range(heads):
        cols = slice(h * HDIM, (h + 1) * HDIM)
        decayed = (column(table, 3 * hp + h) * qbuf[:, cols].astype(F32)).astype(BF16)
        local = dot(decayed, dobuf[:, cols], TN)
        adj_ref[cols, :] = local
        msg_ref[cols, :] = local.astype(BF16)
    copies.finish()


def project(parts, owners, w_query, d_out, facts, hp):
    rows, feat = parts[0].shape
    depth, width = w_query.shape
    chunk = min(512, feat)
    return pl.pallas_call(
        functools.partial(project_kernel, hp, len(parts), chunk),
        in_specs=[SM] + [HB] * (len(parts) + 3),
        out_specs=(HB, VM, VM),
        out_shape=(
            jax.ShapeDtypeStruct((rows, width), BF16),
            jax.ShapeDtypeStruct((width, HDIM), F32),
            jax.ShapeDtypeStruct((width, HDIM), BF16),
        ),
        scratch_shapes=[
            pltpu.VMEM((rows, depth), BF16),
            pltpu.VMEM((depth, width), BF16),
            pltpu.VMEM((rows, width), BF16),
            pltpu.VMEM(facts.shape, F32),
            pltpu.VMEM((rows, width), BF16),
            pltpu.VMEM((rows, width), F32),
            pltpu.SemaphoreType.DMA((2 * len(parts) * (feat // chunk) + 3,)),
        ],
        compiler_params=params(28),
        cost_estimate=cost(2 * rows * width * depth, 2 * (depth * width + rows * depth)),
        name="project",
    )(owners, pinned(parts[0]), *parts[1:], pinned(w_query), d_out, facts)


def inner_kernel(first, last, hp, *refs):
    ins, facts_hbm, outs = refs[:4], refs[4], refs[5:8]
    bufs, facts_ref, sides, sems = refs[8:12], refs[12], refs[13:16], refs[16]
    rows = ins[0].shape[0]
    wide = pl.ds(first * HDIM, (last - first) * HDIM)
    copies = Copies(sems)
    facts_in = copies.start(facts_hbm, facts_ref)
    loads = [copies.start(src.at[:, wide], dst) for src, dst in zip(ins, bufs)]
    facts_in.wait()
    table = turned(facts_ref[...])
    row = lax.broadcasted_iota(jnp.int32, (rows, rows), 0)
    keep = row >= lax.broadcasted_iota(jnp.int32, (rows, rows), 1)
    shift = -0.5 * math.log2(HDIM)
    turn = math.log2(math.e)
    for copy in loads:
        copy.wait()
    q_ref, ks_ref, v_ref, do_ref = bufs
    for h in range(first, last):
        cols = slice((h - first) * HDIM, (h - first + 1) * HDIM)
        later = column(table, h) * turn + shift
        sooner = facts_ref[h : h + 1, :] * turn
        gap = jnp.concatenate([later] * (rows // LANES), axis=1) - sooner
        decays = jnp.exp2(jnp.where(keep, gap, -1e30))
        query, scaled, grad = q_ref[:, cols], ks_ref[:, cols], do_ref[:, cols]
        wdv = (decays * dot(grad, v_ref[:, cols], NT)).astype(BF16)
        wkq = (decays * dot(query, scaled, NT)).astype(BF16)
        sides[0][:, cols] = dot(wdv, scaled, NN)
        sides[1][:, cols] = dot(query, wdv, TN).T
        sides[2][:, cols] = dot(grad, wkq, TN).T
    for side, out in zip(sides, outs):
        copies.store(side, out)
    copies.finish()


def inner(first, last, query, scaled_keys, values, d_out, facts, hp):
    rows = query.shape[0]
    width = (last - first) * HDIM
    return pl.pallas_call(
        functools.partial(inner_kernel, first, last, hp),
        in_specs=[HB] * 5,
        out_specs=(HB,) * 3,
        out_shape=(jax.ShapeDtypeStruct((rows, width), F32),) * 3,
        scratch_shapes=[
            *[pltpu.VMEM((rows, width), BF16)] * 4,
            pltpu.VMEM(facts.shape, F32),
            *[pltpu.VMEM((rows, width), F32)] * 3,
            pltpu.SemaphoreType.DMA((8,)),
        ],
        compiler_params=params(24),
        cost_estimate=cost(10 * rows * rows * width, 20 * rows * width),
        name="inner",
    )(query, scaled_keys, values, d_out, facts)


def mix(coef_ref, pieces, heads, h):
    cols = slice(h * HDIM, (h + 1) * HDIM)
    total = None
    for stage, piece in enumerate(pieces):
        row = stage * heads + h
        term = coef_ref[row : row + 1, :] * piece[cols, :].astype(F32)
        total = term if total is None else total + term
    return total.astype(BF16)


def load_weight(copies, place_ref, first, w_hbm, wbuf, feat, block):
    loads = []
    for at in range(0, wbuf.shape[0], block):
        start = pl.multiple_of(place_ref[0] * feat + first + at, block)
        loads.append((at, copies.start(w_hbm.at[pl.ds(start, block), :], wbuf.at[pl.ds(at, block), :])))
    return loads


def query_kernel(heads, hp, stages, feat, block, place_ref, *refs):
    pieces = refs[:stages]
    coef_ref, do_hbm, facts_hbm, w_hbm = refs[stages : stages + 4]
    inner_hbm = refs[stages + 4 : -9]
    dq_hbm, out_hbm, dobuf, facts_ref, wbuf, local, held, sent, sems = refs[-9:]
    copies = Copies(sems)
    each = heads // len(inner_hbm)
    facts_in = copies.start(facts_hbm, facts_ref)
    loads = []
    for part, src in enumerate(inner_hbm):
        wide = pl.ds(part * each * HDIM, each * HDIM)
        loads.append(
            (copies.start(do_hbm.at[:, wide], dobuf.at[:, wide]), copies.start(src, local.at[:, wide]))
        )
    w_in = load_weight(copies, place_ref, 0, w_hbm, wbuf, feat, block)
    facts_in.wait()
    table = turned(facts_ref[...])
    for h in range(heads):
        if h % each == 0:
            for copy in loads[h // each]:
                copy.wait()
        cols = slice(h * HDIM, (h + 1) * HDIM)
        state = mix(coef_ref, pieces, heads, h)
        carry = dot(dobuf[:, cols], state, NT)
        held[:, cols] = (local[:, cols] + column(table, 3 * hp + h) * carry).astype(BF16)
    copies.store(held, dq_hbm)
    send_terms(copies, w_in, held, wbuf, sent, out_hbm, block)
    copies.finish()


def send_terms(copies, w_in, dq_ref, wbuf, sent, out_hbm, block):
    for at, copy in w_in:
        copy.wait()
        wide = slice(at, at + block)
        sent[:, wide] = dot(dq_ref[...], wbuf[wide, :], NT).astype(BF16)
        copies.store(sent.at[:, wide], out_hbm.at[:, wide])


def query_term(pieces, coefs, inner_dq, d_out, facts, w_query, place, feat, count, heads, hp):
    rows, width = d_out.shape
    block = min(512, count)
    args = (coefs, d_out, facts, w_query, *inner_dq)
    return pl.pallas_call(
        functools.partial(query_kernel, heads, hp, len(pieces), feat, block),
        in_specs=[SM] + [VM] * (len(pieces) + 1) + [HB] * (len(args) - 1),
        out_specs=(HB, HB),
        out_shape=(
            jax.ShapeDtypeStruct((rows, width), BF16),
            jax.ShapeDtypeStruct((rows, count), BF16),
        ),
        scratch_shapes=[
            pltpu.VMEM((rows, width), BF16),
            pltpu.VMEM(facts.shape, F32),
            pltpu.VMEM((count, width), BF16),
            pltpu.VMEM((rows, width), F32),
            pltpu.VMEM((rows, width), BF16),
            pltpu.VMEM((rows, count), BF16),
            pltpu.SemaphoreType.DMA((2 + 2 * len(inner_dq) + 2 * (count // block),)),
        ],
        compiler_params=params(20),
        cost_estimate=cost(2 * rows * width * count, 2 * (width + rows) * count + 10 * rows * width),
        name="query_term",
    )(place, *pieces, *args)


def term_kernel(feat, first, block, place_ref, dq_hbm, w_hbm, out_hbm, held, wbuf, sent, sems):
    copies = Copies(sems)
    dq_in = copies.start(dq_hbm, held)
    w_in = load_weight(copies, place_ref, first, w_hbm, wbuf, feat, block)
    dq_in.wait()
    send_terms(copies, w_in, held, wbuf, sent, out_hbm, block)
    copies.finish()


def plain_term(d_query, w_query, place, feat, first, count):
    rows, width = d_query.shape
    block = min(512, count)
    return pl.pallas_call(
        functools.partial(term_kernel, feat, first, block),
        in_specs=[SM, HB, HB],
        out_specs=HB,
        out_shape=jax.ShapeDtypeStruct((rows, count), BF16),
        scratch_shapes=[
            pltpu.VMEM((rows, width), BF16),
            pltpu.VMEM((count, width), BF16),
            pltpu.VMEM((rows, count), BF16),
            pltpu.SemaphoreType.DMA((1 + 2 * (count // block),)),
        ],
        compiler_params=params(16),
        cost_estimate=cost(2 * rows * width * count, 2 * (width + rows) * count),
        name="term",
    )(place, d_query, w_query)


def finish_kernel(count, block, place_ref, *refs):
    dq_hbm, w_hbm = refs[:2]
    arrived, (out_hbm, held, wbuf, extra, sent, sems) = refs[2:-6], refs[-6:]
    feat = sent.shape[1]
    copies = Copies(sems)
    dq_in = copies.start(dq_hbm, held)
    w_in = load_weight(copies, place_ref, 0, w_hbm, wbuf, feat, block)
    per = feat // count
    others = []
    for index, src in enumerate(arrived):
        shift, first = divmod(index, per)
        others.append(copies.start(src, extra.at[shift, :, pl.ds(first * count, count)]))
    dq_in.wait()
    for at, copy in w_in:
        copy.wait()
        wide = slice(at, at + block)
        total = dot(held[...], wbuf[wide, :], NT).astype(BF16).astype(F32)
        for index, other in enumerate(others):
            if at == index % per * count:
                other.wait()
        for shift in range(extra.shape[0]):
            total = total + extra[shift, :, wide].astype(F32)
        sent[:, wide] = total.astype(BF16)
        copies.store(sent.at[:, wide], out_hbm.at[:, wide])
    copies.finish()


def finish(d_query, w_query, place, arrived, feat):
    rows, width = d_query.shape
    count = arrived[0].shape[1]
    block = min(512, count)
    return pl.pallas_call(
        functools.partial(finish_kernel, count, block),
        in_specs=[SM] + [HB] * (2 + len(arrived)),
        out_specs=HB,
        out_shape=jax.ShapeDtypeStruct((rows, feat), BF16),
        scratch_shapes=[
            pltpu.VMEM((rows, width), BF16),
            pltpu.VMEM((feat, width), BF16),
            pltpu.VMEM((len(arrived) * count // feat, rows, feat), BF16),
            pltpu.VMEM((rows, feat), BF16),
            pltpu.SemaphoreType.DMA((1 + 2 * (feat // block) + len(arrived),)),
        ],
        compiler_params=params(24),
        cost_estimate=cost(2 * rows * width * feat, 2 * (width + 3 * rows) * feat),
        name="finish",
    )(place, d_query, w_query, *arrived)


def close_kernel(heads, hp, stages, *refs):
    pieces = refs[:stages]
    coef_ref, ks_hbm, v_hbm, facts_hbm = refs[stages : stages + 4]
    rest = refs[stages + 4 : -10]
    k_hbm, dv_hbm, ksbuf, vbuf, facts_ref, dkbuf, dvbuf, kside, vside, sems = refs[-10:]
    dks, dvs = rest[: len(rest) // 2], rest[len(rest) // 2 :]
    each = heads // len(dks)
    copies = Copies(sems)
    facts_in = copies.start(facts_hbm, facts_ref)
    loads = []
    for part, (dk, dv) in enumerate(zip(dks, dvs)):
        wide = pl.ds(part * each * HDIM, each * HDIM)
        loads.append(
            (
                copies.start(v_hbm.at[:, wide], vbuf.at[:, wide]),
                copies.start(dk, dkbuf.at[:, wide]),
                copies.start(ks_hbm.at[:, wide], ksbuf.at[:, wide]),
                copies.start(dv, dvbuf.at[:, wide]),
            )
        )
    facts_in.wait()
    table = turned(facts_ref[...])
    for h in range(heads):
        if h % each == 0:
            for copy in loads[h // each]:
                copy.wait()
        cols = slice(h * HDIM, (h + 1) * HDIM)
        adjoint = mix(coef_ref, pieces, heads, h)
        tail, gain = column(table, 2 * hp + h), column(table, hp + h)
        carry_k = dot(vbuf[:, cols], adjoint, NT)
        kside[:, cols] = (gain * (dkbuf[:, cols] + tail * carry_k)).astype(BF16)
        carry_v = dot(ksbuf[:, cols], adjoint, NN)
        vside[:, cols] = (dvbuf[:, cols] + tail * carry_v).astype(BF16)
        if (h + 1) % each == 0:
            wide = slice((h + 1 - each) * HDIM, (h + 1) * HDIM)
            copies.store(kside.at[:, wide], k_hbm.at[:, wide])
            copies.store(vside.at[:, wide], dv_hbm.at[:, wide])
    copies.finish()


def close(pieces, coefs, dks, dvs, scaled_keys, values, facts, heads, hp):
    rows, width = values.shape
    args = (coefs, scaled_keys, values, facts, *dks, *dvs)
    buf, wide = pltpu.VMEM((rows, width), BF16), pltpu.VMEM((rows, width), F32)
    return pl.pallas_call(
        functools.partial(close_kernel, heads, hp, len(pieces)),
        out_shape=(jax.ShapeDtypeStruct((rows, width), BF16),) * 2,
        in_specs=[VM] * (len(pieces) + 1) + [HB] * (len(args) - 1),
        out_specs=(HB,) * 2,
        scratch_shapes=[
            buf,
            buf,
            pltpu.VMEM(facts.shape, F32),
            wide,
            wide,
            buf,
            buf,
            pltpu.SemaphoreType.DMA((1 + 6 * len(dks),)),
        ],
        compiler_params=params(20),
        cost_estimate=cost(4 * rows * width * HDIM, 16 * rows * width),
        name="close",
    )(*pieces, *args)


def body(ctx_size, head_size, hidden, w_query, keys, values, d_out, log_decay):
    rows, feat = hidden.shape
    heads = log_decay.shape[1]
    width = w_query.shape[1]
    hp = sublanes(heads)
    scaling = HDIM ** (-0.5)
    me = lax.axis_index("ctx")
    mine = lax.axis_index("head")

    parts = [hidden]
    for shift in range(1, head_size):
        ring = [(i, (i + shift) % head_size) for i in range(head_size)]
        parts.append(lax.ppermute(hidden, "head", ring))
    owners = jnp.stack([(mine + head_size - s) % head_size for s in range(head_size)]).astype(jnp.int32)

    scaled_keys, facts, msg, state = prepare(log_decay.T, keys, values, heads, hp, scaling)
    query, adjoint, amsg = project(parts, owners, w_query, d_out, facts, hp)

    wide = lambda factor: factor[:heads, None, :]
    cube = lambda flat: flat.reshape(heads, HDIM, HDIM)
    split = lambda f: (f.astype(BF16), (f - f.astype(BF16).astype(F32)).astype(BF16))
    joined = lambda pair: pair[:hp].astype(F32) + pair[hp:].astype(F32)
    stages = (ctx_size - 1).bit_length()

    def send(array, stage, up):
        dist = 1 << stage
        if stage < stages - 1:
            pairs = [(i, i ^ dist) for i in range(ctx_size)]
        else:
            pairs = [(i, i + dist) if up else (i + dist, i) for i in range(ctx_size) if not i & dist]
        return lax.ppermute(array, "ctx", pairs)

    uppers = [(me & (1 << stage)) != 0 for stage in range(stages)]
    shares, others = [joined(msg[width:])], []
    got, agot = [], []
    before, after = [jnp.ones_like(shares[0])], [jnp.ones_like(shares[0])]

    def fold_state(stage, state):
        upper, arrived = uppers[stage], cube(got[stage][:width]).astype(F32)
        theirs = joined(got[stage][width:])
        others.append(theirs)
        own, other = jnp.where(upper, 1.0, theirs), jnp.where(upper, shares[stage], 1.0)
        state = (wide(own) * cube(state) + wide(other) * arrived).reshape(width, HDIM)
        shares.append(shares[stage] * theirs)
        before.append(jnp.where(upper, before[stage] * theirs, before[stage]))
        after.append(jnp.where(upper, after[stage], after[stage] * theirs))
        msg = state.astype(BF16)
        if stage + 2 < stages:
            msg = jnp.concatenate([msg, *split(shares[-1])], axis=0)
        return msg, state

    def fold_adjoint(stage, adjoint):
        upper, arrived = uppers[stage], cube(agot[stage]).astype(F32)
        own, other = jnp.where(upper, others[stage], 1.0), jnp.where(upper, 1.0, shares[stage])
        adjoint = (wide(own) * cube(adjoint) + wide(other) * arrived).reshape(width, HDIM)
        return adjoint.astype(BF16), adjoint

    half = max(1, heads // 2)
    pending = [(first, first + half) for first in range(0, heads, half)]
    inner_parts = []

    def next_inner():
        return inner(*pending.pop(0), query, scaled_keys, values, d_out, facts, hp)

    barrier = lax.optimization_barrier
    for stage in range(stages):
        arrived = send(msg if stage < stages - 1 else msg[:width], stage, True)
        if stage == 0:
            arrived, query, adjoint, amsg = barrier((arrived, query, adjoint, amsg))
        else:
            agot.append(send(amsg, stage - 1, False))
            if pending and (stage == 1 or stage == stages - 1):
                part = next_inner()
                arrived, *part = barrier((arrived, *part))
                inner_parts.append(part)
        got.append(arrived)
        if stage < stages - 1:
            msg, state = fold_state(stage, state)
        if stage >= 1:
            amsg, adjoint = fold_adjoint(stage - 1, adjoint)
    while pending:
        inner_parts.append(next_inner())
    agot.append(send(amsg, stages - 1, False))
    got[-1], _ = barrier((got[-1], amsg))

    state_coefs = [jnp.where(u, f, 0.0)[:heads] for u, f in zip(uppers, before)]
    adjoint_coefs = [jnp.where(u, 0.0, f)[:heads] for u, f in zip(uppers, after)]
    state_coefs = jnp.concatenate(state_coefs, axis=0)
    adjoint_coefs = jnp.concatenate(adjoint_coefs, axis=0)
    dqs, dks, dvs = zip(*inner_parts)

    place = lambda shift: ((mine + shift) % head_size).astype(jnp.int32).reshape(1)
    count = feat // 2 if feat >= 1024 else feat
    arrived = []
    for shift in range(1, head_size):
        ring = [(i, (i + shift) % head_size) for i in range(head_size)]
        for first in range(0, feat, count):
            if shift == 1 and first == 0:
                d_query, term = query_term(
                    got, state_coefs, dqs, d_out, facts, w_query, place(1), feat, count, heads, hp
                )
            else:
                term = plain_term(d_query, w_query, place(shift), feat, first, count)
            arrived.append(lax.ppermute(term, "head", ring))
    d_keys, d_values = close(agot, adjoint_coefs, dks, dvs, scaled_keys, values, facts, heads, hp)
    d_hidden = finish(d_query, w_query, place(0), arrived, feat)
    return (d_hidden, d_keys, d_values)


def solution(mesh):
    return jax.shard_map(
        functools.partial(body, mesh.shape["ctx"], mesh.shape["head"]),
        mesh=mesh,
        in_specs=(
            P("ctx", "head"),
            P(None, "head"),
            P("ctx", "head"),
            P("ctx", "head"),
            P("ctx", "head"),
            P("ctx", "head"),
        ),
        out_specs=(P("ctx", "head"), P("ctx", "head"), P("ctx", "head")),
        check_vma=False,
    )
```

time: 97.5 us -> 96.9 us (level)
  the two profiles are of different devices: /device:TPU:4 before, /device:TPU:6 now
where the time goes in v3:
time: 96.9 us; the launch traced here: 96.2 us
  Pallas kernels  35.3 us (36%)
  local copies, waits for them, and re-layouts  22.3 us (23%)
  waiting for transfers between devices  20.1 us (21%)
  starting transfers between devices  12.7 us (13%)
  other arithmetic  4.49 us (5%)
  between operations  1.14 us (1%)
    unnamed x58, local copies, waits for them, and re-layouts  22.3 us
    ppermute x8, waiting for transfers between devices, send(): return lax.ppermute(array, 'ctx', pairs)  20.1 us
    ppermute x8, starting transfers between devices, send(): return lax.ppermute(array, 'ctx', pairs)  12.1 us
    pallas_call x1, Pallas kernels, project(): pl.pallas_call(functools.partial(project_kernel, hp, len(parts), chunk),...  8.52 us
    pallas_call x2, Pallas kernels, inner(): pl.pallas_call(functools.partial(inner_kernel, first, last, hp), in_specs...  6.62 us
    pallas_call x1, Pallas kernels, finish(): pl.pallas_call(functools.partial(finish_kernel, count, block), in_specs=[...  4.97 us
    pallas_call x1, Pallas kernels, prepare(): pl.pallas_call(functools.partial(prepare_kernel, heads, hp, scaling), out...  4.67 us
    pallas_call x1, Pallas kernels, query_term(): pl.pallas_call(functools.partial(query_kernel, heads, hp, len(pieces), fe...  4.07 us
  transfers between devices with their start and end apart: 11, of which 3 were waited for; matrix products, arithmetic and copies ran while one was open for 4% of the time, Pallas kernels for 27%

profile of v3, /device:TPU:6, one launch (start us, length us, event | category | flops | bytes accessed | tf_op | source)
XLA Modules:
  0.0 96.2 jit_solution(1881346943012873853)
XLA Ops:
  0.7 4.7 %prepare.1 = (bf16[512,1024]{1,0:T(8,128)(2,1)S(1)}, f32[32,512]{1,0:T(8,128)S(1)}, bf16[1040,128]{1,0:T(8,128)(2,1)}, f32[1024,128]{1,0:T(8,128)S(1)}) custom-call(f32[8,512]{1,0:T(8,128)} %bitcast.106, bf16[512,1024]{1,0:T(8,128)(2,1)} %k_hbm.1, bf16[512,1024]{1,0:T(8,128)(2,1)} %refs_6_.1), custom_call_target="tpu_custom_call" | custom-call | flops 134217728 | bytes 4194304 | tf_op jit(solution)/shard_map/prepare/pallas_call | solution.py:134
  5.4 1.0 copy-done.3
  7.0 8.5 %project.1 = (bf16[512,1024]{1,0:T(8,128)(2,1)S(1)}, f32[1024,128]{1,0:T(8,128)S(1)}, bf16[1024,128]{1,0:T(8,128)(2,1)S(1)}) custom-call(s32[2]{0:T(128)S(1)} %pad_add_fusion.place_ref, bf16[512,2048]{1,0:T(8,128)(2,1)} %refs_0_.1, bf16[512,2048]{1,0:T(8,128)(2,1)} %collective-permute-done.1.refs_1_, bf16[4096,1024]{1,0:T(8,128)(2,1)} %refs_1_.1, ...), custom_call_target="tpu_custom_call" | custom-call | flops 4294967296 | bytes 12582912 | tf_op jit(solution)/shard_map/project/pallas_call | solution.py:208
  16.8 1.8 %collective-permute-start.5 = (bf16[1024,128]{1,0:T(8,128)(2,1)}, bf16[1024,128]{1,0:T(8,128)(2,1)S(1)}, u32[]{:S(2)}, u32[]{:S(2)}) collective-permute-start(bf16[1024,128]{1,0:T(8,128)(2,1)} %copy-done.23), channel_id=1, source_target_pairs={{0,2},{2,0},{4,6},{6,4},{8,10},{10,8},{12,14},{14,12},{16,18},{18,... | collective-permute-start | bytes 786440 | tf_op jit(solution)/shard_map/ppermute | solution.py:542
  18.6 1.2 %copy-done.4 = bf16[512,1024]{1,0:T(8,128)(2,1)S(1)} copy-done((bf16[512,1024]{1,0:T(8,128)(2,1)S(1)}, bf16[512,1024]{1,0:T(8,128)(2,1)}, u32[]{:S(2)}) %copy-start.4) | copy-done | bytes 1048600
  19.8 1.2 %copy-done.18 = bf16[512,1024]{1,0:T(8,128)(2,1)S(1)} copy-done((bf16[512,1024]{1,0:T(8,128)(2,1)S(1)}, bf16[512,1024]{1,0:T(8,128)(2,1)}, u32[]{:S(2)}) %copy-start.18) | copy-done | bytes 1048600
  21.0 1.2 %copy-done.25 = bf16[512,1024]{1,0:T(8,128)(2,1)S(1)} copy-done((bf16[512,1024]{1,0:T(8,128)(2,1)S(1)}, bf16[512,1024]{1,0:T(8,128)(2,1)}, u32[]{:S(2)}) %copy-start.25) | copy-done | bytes 1048600
  22.3 3.2 %inner.2 = (f32[512,512]{1,0:T(8,128)S(1)}, f32[512,512]{1,0:T(8,128)S(1)}, f32[512,512]{1,0:T(8,128)S(1)}) custom-call(bf16[512,1024]{1,0:T(8,128)(2,1)S(1)} %copy-done.25, bf16[512,1024]{1,0:T(8,128)(2,1)S(1)} %copy-done.4, bf16[512,1024]{1,0:T(8,128)(2,1)S(1)} %copy-done.2, bf16[512,1024]{1,0:T(8,128)(2,1)S(1)} %copy-done.18, ...), custom_call_target="tpu_custom_call" | custom-call | flops 1342177280 | bytes 5242880 | tf_op jit(solution)/shard_map/inner/pallas_call | solution.py:269
  25.5 1.0 copy-done.21
  26.7 1.0 %pad_maximum_fusion.1 = bf16[1040,128]{1,0:T(8,128)(2,1)} fusion(bf16[8,128]{1,0:T(8,128)(2,1)S(1)} %get-tuple-element.71, bf16[8,128]{1,0:T(8,128)(2,1)S(1)} %get-tuple-element.72, bf16[1024,128]{1,0:T(8,128)(2,1)S(1)} %fusion.11), kind=kLoop, calls=%fused_computation.23 | loop fusion | flops 798720 | bytes 532480 | tf_op jit(solution)/shard_map/concatenate | solution.py:560
  27.6 1.6 %collective-permute-start.3 = (bf16[1040,128]{1,0:T(8,128)(2,1)}, bf16[1040,128]{1,0:T(8,128)(2,1)S(1)}, u32[]{:S(2)}, u32[]{:S(2)}) collective-permute-start(bf16[1040,128]{1,0:T(8,128)(2,1)} %pad_maximum_fusion.1), channel_id=1, source_target_pairs={{0,8},{2,10},{4,12},{6,14},{8,0},{10,2},{12,4},{14,6},{16,24},{18,... | collective-permute-start | bytes 798728 | tf_op jit(solution)/shard_map/ppermute | solution.py:542
  30.0 1.5 %collective-permute-start.6 = (bf16[1024,128]{1,0:T(8,128)(2,1)}, bf16[1024,128]{1,0:T(8,128)(2,1)S(1)}, u32[]{:S(2)}, u32[]{:S(2)}) collective-permute-start(bf16[1024,128]{1,0:T(8,128)(2,1)} %fusion.9), channel_id=1, source_target_pairs={{0,4},{2,6},{4,0},{6,2},{8,12},{10,14},{12,8},{14,10},{16,20},{18,... | collective-permute-start | bytes 786440 | tf_op jit(solution)/shard_map/ppermute | solution.py:542
  31.6 1.2 %copy-done.5 = bf16[512,1024]{1,0:T(8,128)(2,1)S(1)} copy-done((bf16[512,1024]{1,0:T(8,128)(2,1)S(1)}, bf16[512,1024]{1,0:T(8,128)(2,1)}, u32[]{:S(2)}) %copy-start.5) | copy-done | bytes 1048600
  32.8 1.2 %copy-done.19 = bf16[512,1024]{1,0:T(8,128)(2,1)S(1)} copy-done((bf16[512,1024]{1,0:T(8,128)(2,1)S(1)}, bf16[512,1024]{1,0:T(8,128)(2,1)}, u32[]{:S(2)}) %copy-start.19) | copy-done | bytes 1048600
  34.0 1.2 %copy-done.26 = bf16[512,1024]{1,0:T(8,128)(2,1)S(1)} copy-done((bf16[512,1024]{1,0:T(8,128)(2,1)S(1)}, bf16[512,1024]{1,0:T(8,128)(2,1)}, u32[]{:S(2)}) %copy-start.26) | copy-done | bytes 1048600
  35.2 3.4 %inner.3 = (f32[512,512]{1,0:T(8,128)S(1)}, f32[512,512]{1,0:T(8,128)S(1)}, f32[512,512]{1,0:T(8,128)S(1)}) custom-call(bf16[512,1024]{1,0:T(8,128)(2,1)S(1)} %copy-done.26, bf16[512,1024]{1,0:T(8,128)(2,1)S(1)} %copy-done.5, bf16[512,1024]{1,0:T(8,128)(2,1)S(1)} %copy-done.2, bf16[512,1024]{1,0:T(8,128)(2,1)S(1)} %copy-done.19, ...), custom_call_target="tpu_custom_call" | custom-call | flops 1342177280 | bytes 5242880 | tf_op jit(solution)/shard_map/inner/pallas_call | solution.py:269
  39.7 4.6 %collective-permute-start.4 = (bf16[1024,128]{1,0:T(8,128)(2,1)S(1)}, bf16[1024,128]{1,0:T(8,128)(2,1)S(1)}, u32[]{:S(2)}, u32[]{:S(2)}) collective-permute-start(bf16[1024,128]{1,0:T(8,128)(2,1)S(1)} %fusion.5), channel_id=1, source_target_pairs={{0,16},{2,18},{4,20},{6,22},{8,24},{10,26},{12,28},{14,30},{1,17},... | collective-permute-start | bytes 786440 | tf_op jit(solution)/shard_map/ppermute | solution.py:542
  44.4 1.8 %collective-permute-done.7.refs_2_ = bf16[1024,128]{1,0:T(8,128)(2,1)S(1)} collective-permute-done((bf16[1024,128]{1,0:T(8,128)(2,1)S(1)}, bf16[1024,128]{1,0:T(8,128)(2,1)S(1)}, u32[]{:S(2)}, u32[]{:S(2)}) %collective-permute-start.7) | collective-permute-done | bytes 262176 | tf_op jit(solution)/shard_map/ppermute | solution.py:542
  47.2 2.7 %collective-permute-done.4.refs_3_ = bf16[1024,128]{1,0:T(8,128)(2,1)S(1)} collective-permute-done((bf16[1024,128]{1,0:T(8,128)(2,1)S(1)}, bf16[1024,128]{1,0:T(8,128)(2,1)S(1)}, u32[]{:S(2)}, u32[]{:S(2)}) %collective-permute-start.4) | collective-permute-done | bytes 262176 | tf_op jit(solution)/shard_map/ppermute | solution.py:542
  49.9 3.4 %copy-done = bf16[4096,1024]{1,0:T(8,128)(2,1)S(1)} copy-done((bf16[4096,1024]{1,0:T(8,128)(2,1)S(1)}, bf16[4096,1024]{1,0:T(8,128)(2,1)}, u32[]{:S(2)}) %copy-start) | copy-done | bytes 8388632
  53.2 4.1 %query_term.1 = (bf16[512,1024]{1,0:T(8,128)(2,1)S(1)}, bf16[512,1024]{1,0:T(8,128)(2,1)}) custom-call(s32[1]{0:T(128)} %bitcast.1.place_ref, bf16[1040,128]{1,0:T(8,128)(2,1)S(1)} %collective-permute-done.refs_0_, bf16[1040,128]{1,0:T(8,128)(2,1)S(1)} %collective-permute-done.2.refs_1_, bf16[1040,128]{1,0:T(8,128)(2,1)S(1)} %collective-permute-done.3.refs_2_, ...), custom_call_target="tpu_custom_call" | custom-call | flops 1073741824 | bytes 8388608 | tf_op jit(solution)/shard_map/query_term/pallas_call | solution.py:346
  57.4 2.6 %term.1 = bf16[512,1024]{1,0:T(8,128)(2,1)} custom-call(s32[1]{0:T(128)} %bitcast.1.place_ref, bf16[512,1024]{1,0:T(8,128)(2,1)S(1)} %get-tuple-element.55.dq_hbm.refs_0_, bf16[4096,1024]{1,0:T(8,128)(2,1)S(1)} %bitcast.105), custom_call_target="tpu_custom_call" | custom-call | flops 1073741824 | bytes 3145728 | tf_op jit(solution)/shard_map/term/pallas_call | solution.py:381
  60.6 1.3 %collective-permute-start.10 = (bf16[1024,128]{1,0:T(8,128)(2,1)}, bf16[1024,128]{1,0:T(8,128)(2,1)S(1)}, u32[]{:S(2)}, u32[]{:S(2)}) collective-permute-start(bf16[1024,128]{1,0:T(8,128)(2,1)} %fusion.1), channel_id=1, source_target_pairs={{16,0},{18,2},{20,4},{22,6},{24,8},{26,10},{28,12},{30,14},{17,1},... | collective-permute-start | bytes 786440 | tf_op jit(solution)/shard_map/ppermute | solution.py:542
  62.0 15.6 %collective-permute-done.10.refs_3_ = bf16[1024,128]{1,0:T(8,128)(2,1)S(1)} collective-permute-done((bf16[1024,128]{1,0:T(8,128)(2,1)}, bf16[1024,128]{1,0:T(8,128)(2,1)S(1)}, u32[]{:S(2)}, u32[]{:S(2)}) %collective-permute-start.10) | collective-permute-done | bytes 262176 | tf_op jit(solution)/shard_map/ppermute | solution.py:542
  77.7 1.2 %copy-done.6 = bf16[512,1024]{1,0:T(8,128)(2,1)S(1)} copy-done((bf16[512,1024]{1,0:T(8,128)(2,1)S(1)}, bf16[512,1024]{1,0:T(8,128)(2,1)}, u32[]{:S(2)}) %copy-start.6) | copy-done | bytes 1048600
  78.9 1.2 %copy-done.8 = f32[512,512]{1,0:T(8,128)S(1)} copy-done((f32[512,512]{1,0:T(8,128)S(1)}, f32[512,512]{1,0:T(8,128)}, u32[]{:S(2)}) %copy-start.8) | copy-done | bytes 1048600
  80.1 1.2 %copy-done.10 = f32[512,512]{1,0:T(8,128)S(1)} copy-done((f32[512,512]{1,0:T(8,128)S(1)}, f32[512,512]{1,0:T(8,128)}, u32[]{:S(2)}) %copy-start.10) | copy-done | bytes 1048600
  81.3 1.2 %copy-done.12 = f32[512,512]{1,0:T(8,128)S(1)} copy-done((f32[512,512]{1,0:T(8,128)S(1)}, f32[512,512]{1,0:T(8,128)}, u32[]{:S(2)}) %copy-start.12) | copy-done | bytes 1048600
  82.6 1.2 %copy-done.14 = f32[512,512]{1,0:T(8,128)S(1)} copy-done((f32[512,512]{1,0:T(8,128)S(1)}, f32[512,512]{1,0:T(8,128)}, u32[]{:S(2)}) %copy-start.14) | copy-done | bytes 1048600
  83.8 3.8 %close.1 = (bf16[512,1024]{1,0:T(8,128)(2,1)}, bf16[512,1024]{1,0:T(8,128)(2,1)}) custom-call(bf16[1024,128]{1,0:T(8,128)(2,1)S(1)} %collective-permute-done.5.refs_0_, bf16[1024,128]{1,0:T(8,128)(2,1)S(1)} %collective-permute-done.6.refs_1_, bf16[1024,128]{1,0:T(8,128)(2,1)S(1)} %copy-done.16, bf16[1024,128]{1,0:T(8,128)(2,1)S(1)} %collective-permute-done.10.refs_3_, ...), custom_call_target="tpu_custom_call" | custom-call | flops 268435456 | bytes 8388608 | tf_op jit(solution)/shard_map/close/pallas_call | solution.py:491
  87.7 3.4 %copy-done.1 = bf16[4096,1024]{1,0:T(8,128)(2,1)S(1)} copy-done((bf16[4096,1024]{1,0:T(8,128)(2,1)S(1)}, bf16[4096,1024]{1,0:T(8,128)(2,1)}, u32[]{:S(2)}) %copy-start.1) | copy-done | bytes 8388632
  91.0 5.0 %finish.1 = bf16[512,2048]{1,0:T(8,128)(2,1)} custom-call(s32[1]{0:T(128)} %bitcast.place_ref, bf16[512,1024]{1,0:T(8,128)(2,1)S(1)} %get-tuple-element.55.dq_hbm.refs_0_, bf16[4096,1024]{1,0:T(8,128)(2,1)S(1)} %copy-done.1, bf16[512,1024]{1,0:T(8,128)(2,1)} %collective-permute-done.8.refs_2_, bf16[512,1024]{1,0:T(8,128)(2,1)} %collective-permute-done.9.refs_3_), custom_call_target="tpu_custom_call" | custom-call | flops 2147483648 | bytes 10485760 | tf_op jit(solution)/shard_map/finish/pallas_call | solution.py:429
  (78 shorter events, 5.7 us)
Async XLA Ops:
  0.6 6.4 %copy-start.17 = (bf16[512,1024]{1,0:T(8,128)(2,1)S(1)}, bf16[512,1024]{1,0:T(8,128)(2,1)}, u32[]{:S(2)}) copy-start(bf16[512,1024]{1,0:T(8,128)(2,1)} %refs_5_.1) | copy-start | bytes 3145732
  0.6 6.3 %collective-permute-start.1 = (bf16[512,2048]{1,0:T(8,128)(2,1)}, bf16[512,2048]{1,0:T(8,128)(2,1)}, u32[]{:S(2)}, u32[]{:S(2)}) collective-permute-start(bf16[512,2048]{1,0:T(8,128)(2,1)} %refs_0_.1), channel_id=1, source_target_pairs={{0,1},{1,0},{2,3},{3,2},{4,5},{5,4},{6,7},{7,6},{8,9},{9,8},{10,11... | collective-permute-start | bytes 6291464 | tf_op jit(solution)/shard_map/ppermute | solution.py:524
  6.4 9.2 %collective-permute-start = (bf16[1040,128]{1,0:T(8,128)(2,1)}, bf16[1040,128]{1,0:T(8,128)(2,1)S(1)}, u32[]{:S(2)}, u32[]{:S(2)}) collective-permute-start(bf16[1040,128]{1,0:T(8,128)(2,1)} %get-tuple-element.33), channel_id=1, source_target_pairs={{0,2},{2,0},{4,6},{6,4},{8,10},{10,8},{12,14},{14,12},{16,18},{18,... | collective-permute-start | bytes 798728 | tf_op jit(solution)/shard_map/ppermute | solution.py:542
  7.0 11.6 %copy-start.2 = (bf16[512,1024]{1,0:T(8,128)(2,1)S(1)}, bf16[512,1024]{1,0:T(8,128)(2,1)}, u32[]{:S(2)}) copy-start(bf16[512,1024]{1,0:T(8,128)(2,1)} %refs_6_.1) | copy-start | bytes 3145732
  16.6 9.9 %collective-permute-start.2 = (bf16[1040,128]{1,0:T(8,128)(2,1)S(1)}, bf16[1040,128]{1,0:T(8,128)(2,1)S(1)}, u32[]{:S(2)}, u32[]{:S(2)}) collective-permute-start(bf16[1040,128]{1,0:T(8,128)(2,1)S(1)} %pad_maximum_fusion), channel_id=1, source_target_pairs={{0,4},{2,6},{4,0},{6,2},{8,12},{10,14},{12,8},{14,10},{16,20},{18,... | collective-permute-start | bytes 798728 | tf_op jit(solution)/shard_map/ppermute | solution.py:542
  16.8 12.4 %collective-permute-start.5 = (bf16[1024,128]{1,0:T(8,128)(2,1)}, bf16[1024,128]{1,0:T(8,128)(2,1)S(1)}, u32[]{:S(2)}, u32[]{:S(2)}) collective-permute-start(bf16[1024,128]{1,0:T(8,128)(2,1)} %copy-done.23), channel_id=1, source_target_pairs={{0,2},{2,0},{4,6},{6,4},{8,10},{10,8},{12,14},{14,12},{16,18},{18,... | collective-permute-start | bytes 786440 | tf_op jit(solution)/shard_map/ppermute | solution.py:542
  18.6 1.2 %copy-start.4 = (bf16[512,1024]{1,0:T(8,128)(2,1)S(1)}, bf16[512,1024]{1,0:T(8,128)(2,1)}, u32[]{:S(2)}) copy-start(bf16[512,1024]{1,0:T(8,128)(2,1)} %copy-done.3) | copy-start | bytes 3145732
  19.8 1.2 %copy-start.18 = (bf16[512,1024]{1,0:T(8,128)(2,1)S(1)}, bf16[512,1024]{1,0:T(8,128)(2,1)}, u32[]{:S(2)}) copy-start(bf16[512,1024]{1,0:T(8,128)(2,1)} %refs_5_.1) | copy-start | bytes 3145732
  21.0 1.2 %copy-start.25 = (bf16[512,1024]{1,0:T(8,128)(2,1)S(1)}, bf16[512,1024]{1,0:T(8,128)(2,1)}, u32[]{:S(2)}) copy-start(bf16[512,1024]{1,0:T(8,128)(2,1)} %copy-done.24) | copy-start | bytes 3145732
  26.5 2.8 %copy-start.7 = (f32[512,512]{1,0:T(8,128)}, f32[512,512]{1,0:T(8,128)S(1)}, u32[]{:S(2)}) copy-start(f32[512,512]{1,0:T(8,128)S(1)} %get-tuple-element.57.refs_8_) | copy-start | bytes 3145732
  26.5 3.6 %copy-start.9 = (f32[512,512]{1,0:T(8,128)}, f32[512,512]{1,0:T(8,128)S(1)}, u32[]{:S(2)}) copy-start(f32[512,512]{1,0:T(8,128)S(1)} %get-tuple-element.59.refs_10_) | copy-start | bytes 3145732
  27.6 11.8 %collective-permute-start.3 = (bf16[1040,128]{1,0:T(8,128)(2,1)}, bf16[1040,128]{1,0:T(8,128)(2,1)S(1)}, u32[]{:S(2)}, u32[]{:S(2)}) collective-permute-start(bf16[1040,128]{1,0:T(8,128)(2,1)} %pad_maximum_fusion.1), channel_id=1, source_target_pairs={{0,8},{2,10},{4,12},{6,14},{8,0},{10,2},{12,4},{14,6},{16,24},{18,... | collective-permute-start | bytes 798728 | tf_op jit(solution)/shard_map/ppermute | solution.py:542
  30.0 8.7 %collective-permute-start.6 = (bf16[1024,128]{1,0:T(8,128)(2,1)}, bf16[1024,128]{1,0:T(8,128)(2,1)S(1)}, u32[]{:S(2)}, u32[]{:S(2)}) collective-permute-start(bf16[1024,128]{1,0:T(8,128)(2,1)} %fusion.9), channel_id=1, source_target_pairs={{0,4},{2,6},{4,0},{6,2},{8,12},{10,14},{12,8},{14,10},{16,20},{18,... | collective-permute-start | bytes 786440 | tf_op jit(solution)/shard_map/ppermute | solution.py:542
  31.6 1.2 %copy-start.5 = (bf16[512,1024]{1,0:T(8,128)(2,1)S(1)}, bf16[512,1024]{1,0:T(8,128)(2,1)}, u32[]{:S(2)}) copy-start(bf16[512,1024]{1,0:T(8,128)(2,1)} %copy-done.3) | copy-start | bytes 3145732
  32.8 1.2 %copy-start.19 = (bf16[512,1024]{1,0:T(8,128)(2,1)S(1)}, bf16[512,1024]{1,0:T(8,128)(2,1)}, u32[]{:S(2)}) copy-start(bf16[512,1024]{1,0:T(8,128)(2,1)} %refs_5_.1) | copy-start | bytes 3145732
  34.0 1.2 %copy-start.26 = (bf16[512,1024]{1,0:T(8,128)(2,1)S(1)}, bf16[512,1024]{1,0:T(8,128)(2,1)}, u32[]{:S(2)}) copy-start(bf16[512,1024]{1,0:T(8,128)(2,1)} %copy-done.24) | copy-start | bytes 3145732
  35.2 22.2 %slice-start = ((s8[8388608]{0:T(1024)(128)(4,1)}), s8[4194304]{0:T(1024)(128)(4,1)S(1)}, s32[]{:S(2)}) async-start(s8[8388608]{0:T(1024)(128)(4,1)} %bitcast.104), calls=%async_computation | async-start | bytes 8388608
  38.7 8.5 %copy-start.11 = (f32[512,512]{1,0:T(8,128)}, f32[512,512]{1,0:T(8,128)S(1)}, u32[]{:S(2)}) copy-start(f32[512,512]{1,0:T(8,128)S(1)} %get-tuple-element.58.refs_9_) | copy-start | bytes 3145732
  38.7 8.5 %copy-start.13 = (f32[512,512]{1,0:T(8,128)}, f32[512,512]{1,0:T(8,128)S(1)}, u32[]{:S(2)}) copy-start(f32[512,512]{1,0:T(8,128)S(1)} %get-tuple-element.60.refs_11_) | copy-start | bytes 3145732
  38.7 11.2 %copy-start.20 = (bf16[512,1024]{1,0:T(8,128)(2,1)S(1)}, bf16[512,1024]{1,0:T(8,128)(2,1)}, u32[]{:S(2)}) copy-start(bf16[512,1024]{1,0:T(8,128)(2,1)} %refs_5_.1) | copy-start | bytes 3145732
  38.7 11.2 %copy-start.22 = (f32[512,512]{1,0:T(8,128)S(1)}, f32[512,512]{1,0:T(8,128)}, u32[]{:S(2)}) copy-start(f32[512,512]{1,0:T(8,128)} %copy-done.21) | copy-start | bytes 3145732
  38.9 7.3 %collective-permute-start.7 = (bf16[1024,128]{1,0:T(8,128)(2,1)S(1)}, bf16[1024,128]{1,0:T(8,128)(2,1)S(1)}, u32[]{:S(2)}, u32[]{:S(2)}) collective-permute-start(bf16[1024,128]{1,0:T(8,128)(2,1)S(1)} %fusion.10), channel_id=1, source_target_pairs={{0,8},{2,10},{4,12},{6,14},{8,0},{10,2},{12,4},{14,6},{16,24},{18,... | collective-permute-start | bytes 786440 | tf_op jit(solution)/shard_map/ppermute | solution.py:542
  39.7 10.2 %collective-permute-start.4 = (bf16[1024,128]{1,0:T(8,128)(2,1)S(1)}, bf16[1024,128]{1,0:T(8,128)(2,1)S(1)}, u32[]{:S(2)}, u32[]{:S(2)}) collective-permute-start(bf16[1024,128]{1,0:T(8,128)(2,1)S(1)} %fusion.5), channel_id=1, source_target_pairs={{0,16},{2,18},{4,20},{6,22},{8,24},{10,26},{12,28},{14,30},{1,17},... | collective-permute-start | bytes 786440 | tf_op jit(solution)/shard_map/ppermute | solution.py:542
  46.2 3.6 %copy-start.15 = (bf16[1024,128]{1,0:T(8,128)(2,1)}, bf16[1024,128]{1,0:T(8,128)(2,1)S(1)}, u32[]{:S(2)}) copy-start(bf16[1024,128]{1,0:T(8,128)(2,1)S(1)} %collective-permute-done.7.refs_2_) | copy-start | bytes 786436
  49.9 3.4 %copy-start = (bf16[4096,1024]{1,0:T(8,128)(2,1)S(1)}, bf16[4096,1024]{1,0:T(8,128)(2,1)}, u32[]{:S(2)}) copy-start(bf16[4096,1024]{1,0:T(8,128)(2,1)} %refs_1_.1) | copy-start | bytes 25165828
  53.2 4.2 %slice-start.1 = ((s8[8388608]{0:T(1024)(128)(4,1)}), s8[4194304]{0:T(1024)(128)(4,1)S(1)}, s32[]{:S(2)}) async-start(s8[8388608]{0:T(1024)(128)(4,1)} %bitcast.104), calls=%async_computation.1 | async-start | bytes 8388608
  57.3 30.3 %collective-permute-start.8 = (bf16[512,1024]{1,0:T(8,128)(2,1)}, bf16[512,1024]{1,0:T(8,128)(2,1)}, u32[]{:S(2)}, u32[]{:S(2)}) collective-permute-start(bf16[512,1024]{1,0:T(8,128)(2,1)} %get-tuple-element.56), channel_id=1, source_target_pairs={{0,1},{1,0},{2,3},{3,2},{4,5},{5,4},{6,7},{7,6},{8,9},{9,8},{10,11... | collective-permute-start | bytes 3145736 | tf_op jit(solution)/shard_map/ppermute | solution.py:615
  57.4 20.2 %copy-start.16 = (bf16[1024,128]{1,0:T(8,128)(2,1)S(1)}, bf16[1024,128]{1,0:T(8,128)(2,1)}, u32[]{:S(2)}) copy-start(bf16[1024,128]{1,0:T(8,128)(2,1)} %copy-done.15) | copy-start | bytes 786436
  60.1 27.6 %collective-permute-start.9 = (bf16[512,1024]{1,0:T(8,128)(2,1)}, bf16[512,1024]{1,0:T(8,128)(2,1)}, u32[]{:S(2)}, u32[]{:S(2)}) collective-permute-start(bf16[512,1024]{1,0:T(8,128)(2,1)} %term.1), channel_id=1, source_target_pairs={{0,1},{1,0},{2,3},{3,2},{4,5},{5,4},{6,7},{7,6},{8,9},{9,8},{10,11... | collective-permute-start | bytes 3145736 | tf_op jit(solution)/shard_map/ppermute | solution.py:615
  60.6 17.0 %collective-permute-start.10 = (bf16[1024,128]{1,0:T(8,128)(2,1)}, bf16[1024,128]{1,0:T(8,128)(2,1)S(1)}, u32[]{:S(2)}, u32[]{:S(2)}) collective-permute-start(bf16[1024,128]{1,0:T(8,128)(2,1)} %fusion.1), channel_id=1, source_target_pairs={{16,0},{18,2},{20,4},{22,6},{24,8},{26,10},{28,12},{30,14},{17,1},... | collective-permute-start | bytes 786440 | tf_op jit(solution)/shard_map/ppermute | solution.py:542
  77.7 1.2 %copy-start.6 = (bf16[512,1024]{1,0:T(8,128)(2,1)S(1)}, bf16[512,1024]{1,0:T(8,128)(2,1)}, u32[]{:S(2)}) copy-start(bf16[512,1024]{1,0:T(8,128)(2,1)} %copy-done.3) | copy-start | bytes 3145732
  87.6 3.4 %copy-start.1 = (bf16[4096,1024]{1,0:T(8,128)(2,1)S(1)}, bf16[4096,1024]{1,0:T(8,128)(2,1)}, u32[]{:S(2)}) copy-start(bf16[4096,1024]{1,0:T(8,128)(2,1)} %refs_1_.1) | copy-start | bytes 25165828
  (8 other events, 8.8 us)

commit v4 on v3

--- a/solution.py
+++ b/solution.py
@@ -15,6 +15,7 @@
 VM = pl.BlockSpec(memory_space=pltpu.VMEM)
 SM = pl.BlockSpec(memory_space=pltpu.SMEM)
 HB = pl.BlockSpec(memory_space=pltpu.HBM)
+AN = pl.BlockSpec(memory_space=pl.ANY)
 
 NN = (((1,), (0,)), ((), ()))
 NT = (((1,), (1,)), ((), ()))
@@ -25,16 +26,21 @@
     return lax.dot_general(a, b, dims, preferred_element_type=F32)
 
 
-def params(mib, **kw):
-    return pltpu.CompilerParams(vmem_limit_bytes=mib * MIB, **kw)
-
-
-def pinned(array):
-    return pltpu.with_memory_space_constraint(array, pltpu.HBM)
-
-
-def cost(flops, nbytes):
-    return pl.CostEstimate(flops=int(flops), bytes_accessed=int(nbytes), transcendentals=0)
+def kernel_call(kernel, args, specs, outs, out_specs, scratch, mib, name):
+    pinned = [pltpu.with_memory_space_constraint(a, pltpu.HBM) if s is HB else a for a, s in zip(args, specs)]
+    placed = tuple(
+        (pltpu.HBM if s is HB else jax.ShapeDtypeStruct)(shape, dtype) for (shape, dtype), s in zip(outs, out_specs)
+    )
+    return pl.pallas_call(
+        kernel,
+        in_specs=specs,
+        out_specs=tuple(out_specs),
+        out_shape=placed,
+        scratch_shapes=scratch,
+        compiler_params=pltpu.CompilerParams(vmem_limit_bytes=mib * MIB),
+        cost_estimate=pl.CostEstimate(flops=1, bytes_accessed=1, transcendentals=0),
+        name=name,
+    )(*pinned)
 
 
 def sublanes(count):
@@ -131,17 +137,13 @@
 def prepare(logs, keys, values, heads, hp, scaling):
     rows, width = keys.shape
     buf = pltpu.VMEM((rows, width), BF16)
-    return pl.pallas_call(
+    return kernel_call(
         functools.partial(prepare_kernel, heads, hp, scaling),
-        out_shape=(
-            jax.ShapeDtypeStruct((rows, width), BF16),
-            jax.ShapeDtypeStruct((4 * hp, rows), F32),
-            jax.ShapeDtypeStruct((width + 2 * hp, HDIM), BF16),
-            jax.ShapeDtypeStruct((width, HDIM), F32),
-        ),
-        in_specs=[HB] * 3,
-        out_specs=(HB, HB, VM, VM),
-        scratch_shapes=[
+        (logs, keys, values),
+        [HB] * 3,
+        [((rows, width), BF16), ((4 * hp, rows), F32), ((width + 2 * hp, HDIM), BF16), ((width, HDIM), F32)],
+        (HB, HB, VM, VM),
+        [
             pltpu.VMEM((heads, rows), F32),
             pltpu.VMEM((4 * hp, rows), F32),
             buf,
@@ -149,10 +151,9 @@
             buf,
             pltpu.SemaphoreType.DMA((6 + len(groups(heads)),)),
         ],
-        compiler_params=params(12),
-        cost_estimate=cost(2 * rows * width * HDIM, 8 * rows * width),
-        name="prepare",
-    )(pinned(logs), pinned(keys), pinned(values))
+        12,
+        "prepare",
+    )
 
 
 def project_kernel(hp, nparts, chunk, place_ref, *refs):
@@ -205,16 +206,13 @@
     rows, feat = parts[0].shape
     depth, width = w_query.shape
     chunk = min(512, feat)
-    return pl.pallas_call(
+    return kernel_call(
         functools.partial(project_kernel, hp, len(parts), chunk),
-        in_specs=[SM] + [HB] * (len(parts) + 3),
-        out_specs=(HB, VM, VM),
-        out_shape=(
-            jax.ShapeDtypeStruct((rows, width), BF16),
-            jax.ShapeDtypeStruct((width, HDIM), F32),
-            jax.ShapeDtypeStruct((width, HDIM), BF16),
-        ),
-        scratch_shapes=[
+        (owners, *parts, w_query, d_out, facts),
+        [SM, HB] + [AN] * (len(parts) - 1) + [HB] * 3,
+        [((rows, width), BF16), ((width, HDIM), F32), ((width, HDIM), BF16)],
+        (HB, VM, VM),
+        [
             pltpu.VMEM((rows, depth), BF16),
             pltpu.VMEM((depth, width), BF16),
             pltpu.VMEM((rows, width), BF16),
@@ -223,10 +221,9 @@
             pltpu.VMEM((rows, width), F32),
             pltpu.SemaphoreType.DMA((2 * len(parts) * (feat // chunk) + 3,)),
         ],
-        compiler_params=params(28),
-        cost_estimate=cost(2 * rows * width * depth, 2 * (depth * width + rows * depth)),
-        name="project",
-    )(owners, pinned(parts[0]), *parts[1:], pinned(w_query), d_out, facts)
+        28,
+        "project",
+    )
 
 
 def inner_kernel(first, last, hp, *refs):
@@ -266,21 +263,21 @@
 def inner(first, last, query, scaled_keys, values, d_out, facts, hp):
     rows = query.shape[0]
     width = (last - first) * HDIM
-    return pl.pallas_call(
+    return kernel_call(
         functools.partial(inner_kernel, first, last, hp),
-        in_specs=[HB] * 5,
-        out_specs=(HB,) * 3,
-        out_shape=(jax.ShapeDtypeStruct((rows, width), F32),) * 3,
-        scratch_shapes=[
+        (query, scaled_keys, values, d_out, facts),
+        [HB] * 5,
+        [((rows, width), F32)] * 3,
+        (HB,) * 3,
+        [
             *[pltpu.VMEM((rows, width), BF16)] * 4,
             pltpu.VMEM(facts.shape, F32),
             *[pltpu.VMEM((rows, width), F32)] * 3,
             pltpu.SemaphoreType.DMA((8,)),
         ],
-        compiler_params=params(24),
-        cost_estimate=cost(10 * rows * rows * width, 20 * rows * width),
-        name="inner",
-    )(query, scaled_keys, values, d_out, facts)
+        24,
+        "inner",
+    )
 
 
 def mix(coef_ref, pieces, heads, h):
@@ -343,15 +340,13 @@
     rows, width = d_out.shape
     block = min(512, count)
     args = (coefs, d_out, facts, w_query, *inner_dq)
-    return pl.pallas_call(
+    return kernel_call(
         functools.partial(query_kernel, heads, hp, len(pieces), feat, block),
-        in_specs=[SM] + [VM] * (len(pieces) + 1) + [HB] * (len(args) - 1),
-        out_specs=(HB, HB),
-        out_shape=(
-            jax.ShapeDtypeStruct((rows, width), BF16),
-            jax.ShapeDtypeStruct((rows, count), BF16),
-        ),
-        scratch_shapes=[
+        (place, *pieces, *args),
+        [SM] + [VM] * (len(pieces) + 1) + [HB] * (len(args) - 1),
+        [((rows, width), BF16), ((rows, count), BF16)],
+        (HB, HB),
+        [
             pltpu.VMEM((rows, width), BF16),
             pltpu.VMEM(facts.shape, F32),
             pltpu.VMEM((count, width), BF16),
@@ -360,10 +355,9 @@
             pltpu.VMEM((rows, count), BF16),
             pltpu.SemaphoreType.DMA((2 + 2 * len(inner_dq) + 2 * (count // block),)),
         ],
-        compiler_params=params(20),
-        cost_estimate=cost(2 * rows * width * count, 2 * (width + rows) * count + 10 * rows * width),
-        name="query_term",
-    )(place, *pieces, *args)
+        20,
+        "query_term",
+    )
 
 
 def term_kernel(feat, first, block, place_ref, dq_hbm, w_hbm, out_hbm, held, wbuf, sent, sems):
@@ -378,21 +372,21 @@
 def plain_term(d_query, w_query, place, feat, first, count):
     rows, width = d_query.shape
     block = min(512, count)
-    return pl.pallas_call(
+    return kernel_call(
         functools.partial(term_kernel, feat, first, block),
-        in_specs=[SM, HB, HB],
-        out_specs=HB,
-        out_shape=jax.ShapeDtypeStruct((rows, count), BF16),
-        scratch_shapes=[
+        (place, d_query, w_query),
+        [SM, HB, HB],
+        [((rows, count), BF16)],
+        (HB,),
+        [
             pltpu.VMEM((rows, width), BF16),
             pltpu.VMEM((count, width), BF16),
             pltpu.VMEM((rows, count), BF16),
             pltpu.SemaphoreType.DMA((1 + 2 * (count // block),)),
         ],
-        compiler_params=params(16),
-        cost_estimate=cost(2 * rows * width * count, 2 * (width + rows) * count),
-        name="term",
-    )(place, d_query, w_query)
+        16,
+        "term",
+    )[0]
 
 
 def finish_kernel(count, block, place_ref, *refs):
@@ -426,22 +420,22 @@
     rows, width = d_query.shape
     count = arrived[0].shape[1]
     block = min(512, count)
-    return pl.pallas_call(
+    return kernel_call(
         functools.partial(finish_kernel, count, block),
-        in_specs=[SM] + [HB] * (2 + len(arrived)),
-        out_specs=HB,
-        out_shape=jax.ShapeDtypeStruct((rows, feat), BF16),
-        scratch_shapes=[
+        (place, d_query, w_query, *arrived),
+        [SM, HB, HB] + [AN] * len(arrived),
+        [((rows, feat), BF16)],
+        (HB,),
+        [
             pltpu.VMEM((rows, width), BF16),
             pltpu.VMEM((feat, width), BF16),
             pltpu.VMEM((len(arrived) * count // feat, rows, feat), BF16),
             pltpu.VMEM((rows, feat), BF16),
             pltpu.SemaphoreType.DMA((1 + 2 * (feat // block) + len(arrived),)),
         ],
-        compiler_params=params(24),
-        cost_estimate=cost(2 * rows * width * feat, 2 * (width + 3 * rows) * feat),
-        name="finish",
-    )(place, d_query, w_query, *arrived)
+        24,
+        "finish",
+    )[0]
 
 
 def close_kernel(heads, hp, stages, *refs):
@@ -488,12 +482,13 @@
     rows, width = values.shape
     args = (coefs, scaled_keys, values, facts, *dks, *dvs)
     buf, wide = pltpu.VMEM((rows, width), BF16), pltpu.VMEM((rows, width), F32)
-    return pl.pallas_call(
+    return kernel_call(
         functools.partial(close_kernel, heads, hp, len(pieces)),
-        out_shape=(jax.ShapeDtypeStruct((rows, width), BF16),) * 2,
-        in_specs=[VM] * (len(pieces) + 1) + [HB] * (len(args) - 1),
-        out_specs=(HB,) * 2,
-        scratch_shapes=[
+        (*pieces, *args),
+        [VM] * (len(pieces) + 1) + [HB] * (len(args) - 1),
+        [((rows, width), BF16)] * 2,
+        (HB,) * 2,
+        [
             buf,
             buf,
             pltpu.VMEM(facts.shape, F32),
@@ -503,10 +498,9 @@
             buf,
             pltpu.SemaphoreType.DMA((1 + 6 * len(dks),)),
         ],
-        compiler_params=params(20),
-        cost_estimate=cost(4 * rows * width * HDIM, 16 * rows * width),
-        name="close",
-    )(*pieces, *args)
+        20,
+        "close",
+    )
 
 
 def body(ctx_size, head_size, hidden, w_query, keys, values, d_out, log_decay):

time: 96.9 us -> 83.8 us (0.86)
  the two profiles are of different devices: /device:TPU:6 before, /device:TPU:0 now
where the time goes in v4:
time: 83.8 us; the launch traced here: 83.5 us
  Pallas kernels  43.6 us (52%)
  waiting for transfers between devices  20.6 us (25%)
  starting transfers between devices  16.1 us (19%)
  other arithmetic  2.13 us (3%)
  between operations  1 us (1%)
    pallas_call x8, Pallas kernels, kernel_call(): pl.pallas_call(kernel, in_specs=specs, out_specs=tuple(out_specs), out_sh...  43.6 us
    ppermute x8, waiting for transfers between devices, send(): return lax.ppermute(array, 'ctx', pairs)  20.6 us
    ppermute x8, starting transfers between devices, send(): return lax.ppermute(array, 'ctx', pairs)  15 us
  transfers between devices with their start and end apart: 11, of which 5 were waited for; matrix products, arithmetic and copies ran while one was open for 1% of the time, Pallas kernels for 40%

profile of v4, /device:TPU:0, one launch (start us, length us, event | category | flops | bytes accessed | tf_op | source)
XLA Modules:
  0.0 83.5 jit_solution(8135092632738264795)
XLA Ops:
  0.6 0.5 collective-permute-start.1
  1.1 4.8 %prepare.1 = (bf16[512,1024]{1,0:T(8,128)(2,1)}, f32[32,512]{1,0:T(8,128)}, bf16[1040,128]{1,0:T(8,128)(2,1)}, f32[1024,128]{1,0:T(8,128)S(1)}) custom-call(f32[8,512]{1,0:T(8,128)} %bitcast.104, bf16[512,1024]{1,0:T(8,128)(2,1)} %k_hbm.1, bf16[512,1024]{1,0:T(8,128)(2,1)} %refs_6_.1), custom_call_target="tpu_custom_call" | custom-call | flops 1 | bytes 1 | tf_op jit(solution)/shard_map/prepare/pallas_call | solution.py:34
  6.0 2.6 %collective-permute-start = (bf16[1040,128]{1,0:T(8,128)(2,1)}, bf16[1040,128]{1,0:T(8,128)(2,1)S(1)}, u32[]{:S(2)}, u32[]{:S(2)}) collective-permute-start(bf16[1040,128]{1,0:T(8,128)(2,1)} %get-tuple-element.33), channel_id=1, source_target_pairs={{0,2},{2,0},{4,6},{6,4},{8,10},{10,8},{12,14},{14,12},{16,18},{18,... | collective-permute-start | bytes 798728 | tf_op jit(solution)/shard_map/ppermute | solution.py:536
  8.5 0.1 pad_add_fusion.place_ref
  8.6 8.5 %project.1 = (bf16[512,1024]{1,0:T(8,128)(2,1)}, f32[1024,128]{1,0:T(8,128)S(1)}, bf16[1024,128]{1,0:T(8,128)(2,1)S(1)}) custom-call(s32[2]{0:T(128)S(1)} %pad_add_fusion.place_ref, bf16[512,2048]{1,0:T(8,128)(2,1)} %refs_0_.1, bf16[512,2048]{1,0:T(8,128)(2,1)S(1)} %collective-permute-done.1.refs_1_, bf16[4096,1024]{1,0:T(8,128)(2,1)} %refs_1_.1, ...), custom_call_target="tpu_custom_call" | custom-call | flops 1 | bytes 1 | tf_op jit(solution)/shard_map/project/pallas_call | solution.py:34
  17.1 0.8 broadcast_select_fusion.3
  17.9 0.1 fusion.8
  18.0 1.6 %collective-permute-start.2 = (bf16[1040,128]{1,0:T(8,128)(2,1)S(1)}, bf16[1040,128]{1,0:T(8,128)(2,1)S(1)}, u32[]{:S(2)}, u32[]{:S(2)}) collective-permute-start(bf16[1040,128]{1,0:T(8,128)(2,1)S(1)} %pad_maximum_fusion), channel_id=1, source_target_pairs={{0,4},{2,6},{4,0},{6,2},{8,12},{10,14},{12,8},{14,10},{16,20},{18,... | collective-permute-start | bytes 798728 | tf_op jit(solution)/shard_map/ppermute | solution.py:536
  19.6 0.5 collective-permute-start.5
  20.2 5.7 %inner.2 = (f32[512,512]{1,0:T(8,128)}, f32[512,512]{1,0:T(8,128)}, f32[512,512]{1,0:T(8,128)}) custom-call(bf16[512,1024]{1,0:T(8,128)(2,1)} %get-tuple-element.40.refs_0_, bf16[512,1024]{1,0:T(8,128)(2,1)} %get-tuple-element.41.refs_1_.refs_5_, bf16[512,1024]{1,0:T(8,128)(2,1)} %refs_6_.1, bf16[512,1024]{1,0:T(8,128)(2,1)} %refs_5_.1, ...), custom_call_target="tpu_custom_call" | custom-call | flops 1 | bytes 1 | tf_op jit(solution)/shard_map/inner/pallas_call | solution.py:34
  25.8 0.8 collective-permute-done.2.refs_1_
  26.6 0.2 fusion.11
  26.8 1.6 %collective-permute-start.3 = (bf16[1040,128]{1,0:T(8,128)(2,1)S(1)}, bf16[1040,128]{1,0:T(8,128)(2,1)S(1)}, u32[]{:S(2)}, u32[]{:S(2)}) collective-permute-start(bf16[1040,128]{1,0:T(8,128)(2,1)S(1)} %pad_maximum_fusion.1), channel_id=1, source_target_pairs={{0,8},{2,10},{4,12},{6,14},{8,0},{10,2},{12,4},{14,6},{16,24},{18,... | collective-permute-start | bytes 798728 | tf_op jit(solution)/shard_map/ppermute | solution.py:536
  28.5 0.1 fusion.9
  28.6 1.6 %collective-permute-start.6 = (bf16[1024,128]{1,0:T(8,128)(2,1)S(1)}, bf16[1024,128]{1,0:T(8,128)(2,1)S(1)}, u32[]{:S(2)}, u32[]{:S(2)}) collective-permute-start(bf16[1024,128]{1,0:T(8,128)(2,1)S(1)} %fusion.9), channel_id=1, source_target_pairs={{0,4},{2,6},{4,0},{6,2},{8,12},{10,14},{12,8},{14,10},{16,20},{18,... | collective-permute-start | bytes 786440 | tf_op jit(solution)/shard_map/ppermute | solution.py:536
  30.2 5.7 %inner.3 = (f32[512,512]{1,0:T(8,128)}, f32[512,512]{1,0:T(8,128)}, f32[512,512]{1,0:T(8,128)}) custom-call(bf16[512,1024]{1,0:T(8,128)(2,1)} %get-tuple-element.40.refs_0_, bf16[512,1024]{1,0:T(8,128)(2,1)} %get-tuple-element.41.refs_1_.refs_5_, bf16[512,1024]{1,0:T(8,128)(2,1)} %refs_6_.1, bf16[512,1024]{1,0:T(8,128)(2,1)} %refs_5_.1, ...), custom_call_target="tpu_custom_call" | custom-call | flops 1 | bytes 1 | tf_op jit(solution)/shard_map/inner/pallas_call | solution.py:34
  35.9 0.1 collective-permute-done.6.refs_1_
  36.0 0.2 fusion.10
  36.2 1.1 %collective-permute-start.7 = (bf16[1024,128]{1,0:T(8,128)(2,1)S(1)}, bf16[1024,128]{1,0:T(8,128)(2,1)S(1)}, u32[]{:S(2)}, u32[]{:S(2)}) collective-permute-start(bf16[1024,128]{1,0:T(8,128)(2,1)S(1)} %fusion.10), channel_id=1, source_target_pairs={{0,8},{2,10},{4,12},{6,14},{8,0},{10,2},{12,4},{14,6},{16,24},{18,... | collective-permute-start | bytes 786440 | tf_op jit(solution)/shard_map/ppermute | solution.py:536
  37.3 0.2 fusion.5
  37.5 4.7 %collective-permute-start.4 = (bf16[1024,128]{1,0:T(8,128)(2,1)S(1)}, bf16[1024,128]{1,0:T(8,128)(2,1)S(1)}, u32[]{:S(2)}, u32[]{:S(2)}) collective-permute-start(bf16[1024,128]{1,0:T(8,128)(2,1)S(1)} %fusion.5), channel_id=1, source_target_pairs={{0,16},{2,18},{4,20},{6,22},{8,24},{10,26},{12,28},{14,30},{1,17},... | collective-permute-start | bytes 786440 | tf_op jit(solution)/shard_map/ppermute | solution.py:536
  42.2 0.1 pad_maximum_fusion.2.refs_4_
  42.3 0.9 %collective-permute-done.7.refs_2_ = bf16[1024,128]{1,0:T(8,128)(2,1)S(1)} collective-permute-done((bf16[1024,128]{1,0:T(8,128)(2,1)S(1)}, bf16[1024,128]{1,0:T(8,128)(2,1)S(1)}, u32[]{:S(2)}, u32[]{:S(2)}) %collective-permute-start.7) | collective-permute-done | bytes 262176 | tf_op jit(solution)/shard_map/ppermute | solution.py:536
  43.2 0.2 fusion.1
  43.4 3.4 %collective-permute-done.4.refs_3_ = bf16[1024,128]{1,0:T(8,128)(2,1)S(1)} collective-permute-done((bf16[1024,128]{1,0:T(8,128)(2,1)S(1)}, bf16[1024,128]{1,0:T(8,128)(2,1)S(1)}, u32[]{:S(2)}, u32[]{:S(2)}) %collective-permute-start.4) | collective-permute-done | bytes 262176 | tf_op jit(solution)/shard_map/ppermute | solution.py:536
  46.8 4.7 %query_term.1 = (bf16[512,1024]{1,0:T(8,128)(2,1)}, bf16[512,1024]{1,0:T(8,128)(2,1)}) custom-call(s32[1]{0:T(128)} %bitcast.1.place_ref, bf16[1040,128]{1,0:T(8,128)(2,1)S(1)} %collective-permute-done.refs_0_, bf16[1040,128]{1,0:T(8,128)(2,1)S(1)} %collective-permute-done.2.refs_1_, bf16[1040,128]{1,0:T(8,128)(2,1)S(1)} %collective-permute-done.3.refs_2_, ...), custom_call_target="tpu_custom_call" | custom-call | flops 1 | bytes 1 | tf_op jit(solution)/shard_map/query_term/pallas_call | solution.py:34
  51.7 3.9 %term.1 = bf16[512,1024]{1,0:T(8,128)(2,1)} custom-call(s32[1]{0:T(128)} %bitcast.1.place_ref, bf16[512,1024]{1,0:T(8,128)(2,1)} %get-tuple-element.55.dq_hbm.refs_0_, bf16[4096,1024]{1,0:T(8,128)(2,1)} %refs_1_.1), custom_call_target="tpu_custom_call" | custom-call | flops 1 | bytes 1 | tf_op jit(solution)/shard_map/term/pallas_call | solution.py:34
  55.6 0.6 collective-permute-start.9
  56.2 1.3 %collective-permute-start.10 = (bf16[1024,128]{1,0:T(8,128)(2,1)S(1)}, bf16[1024,128]{1,0:T(8,128)(2,1)S(1)}, u32[]{:S(2)}, u32[]{:S(2)}) collective-permute-start(bf16[1024,128]{1,0:T(8,128)(2,1)S(1)} %fusion.1), channel_id=1, source_target_pairs={{16,0},{18,2},{20,4},{22,6},{24,8},{26,10},{28,12},{30,14},{17,1},... | collective-permute-start | bytes 786440 | tf_op jit(solution)/shard_map/ppermute | solution.py:536
  57.6 15.4 %collective-permute-done.10.refs_3_ = bf16[1024,128]{1,0:T(8,128)(2,1)S(1)} collective-permute-done((bf16[1024,128]{1,0:T(8,128)(2,1)S(1)}, bf16[1024,128]{1,0:T(8,128)(2,1)S(1)}, u32[]{:S(2)}, u32[]{:S(2)}) %collective-permute-start.10) | collective-permute-done | bytes 262176 | tf_op jit(solution)/shard_map/ppermute | solution.py:536
  73.0 4.7 %close.1 = (bf16[512,1024]{1,0:T(8,128)(2,1)}, bf16[512,1024]{1,0:T(8,128)(2,1)}) custom-call(bf16[1024,128]{1,0:T(8,128)(2,1)S(1)} %collective-permute-done.5.refs_0_, bf16[1024,128]{1,0:T(8,128)(2,1)S(1)} %collective-permute-done.6.refs_1_, bf16[1024,128]{1,0:T(8,128)(2,1)S(1)} %collective-permute-done.7.refs_2_, ...), custom_call_target="tpu_custom_call" | custom-call | flops 1 | bytes 1 | tf_op jit(solution)/shard_map/close/pallas_call | solution.py:34
  77.6 5.7 %finish.1 = bf16[512,2048]{1,0:T(8,128)(2,1)} custom-call(s32[1]{0:T(128)} %bitcast.place_ref, bf16[512,1024]{1,0:T(8,128)(2,1)} %get-tuple-element.55.dq_hbm.refs_0_, bf16[4096,1024]{1,0:T(8,128)(2,1)} %refs_1_.1, bf16[512,1024]{1,0:T(8,128)(2,1)S(1)} %collective-permute-done.8.refs_2_, bf16[512,1024]{1,0:T(8,128)(2,1)} %collective-permute-done.9.refs_3_), custom_call_target="tpu_custom_call" | custom-call | flops 1 | bytes 1 | tf_op jit(solution)/shard_map/finish/pallas_call | solution.py:34
  (21 shorter events, 0.3 us)
Async XLA Ops:
  0.6 8.0 %collective-permute-start.1 = (bf16[512,2048]{1,0:T(8,128)(2,1)}, bf16[512,2048]{1,0:T(8,128)(2,1)S(1)}, u32[]{:S(2)}, u32[]{:S(2)}) collective-permute-start(bf16[512,2048]{1,0:T(8,128)(2,1)} %refs_0_.1), channel_id=1, source_target_pairs={{0,1},{1,0},{2,3},{3,2},{4,5},{5,4},{6,7},{7,6},{8,9},{9,8},{10,11... | collective-permute-start | bytes 6291464 | tf_op jit(solution)/shard_map/ppermute | solution.py:518
  6.0 11.1 %collective-permute-start = (bf16[1040,128]{1,0:T(8,128)(2,1)}, bf16[1040,128]{1,0:T(8,128)(2,1)S(1)}, u32[]{:S(2)}, u32[]{:S(2)}) collective-permute-start(bf16[1040,128]{1,0:T(8,128)(2,1)} %get-tuple-element.33), channel_id=1, source_target_pairs={{0,2},{2,0},{4,6},{6,4},{8,10},{10,8},{12,14},{14,12},{16,18},{18,... | collective-permute-start | bytes 798728 | tf_op jit(solution)/shard_map/ppermute | solution.py:536
  17.1 0.9 %copy-start = (bf16[1024,128]{1,0:T(8,128)(2,1)}, bf16[1024,128]{1,0:T(8,128)(2,1)S(1)}, u32[]{:S(2)}) copy-start(bf16[1024,128]{1,0:T(8,128)(2,1)S(1)} %get-tuple-element.51) | copy-start | bytes 786436
  18.0 8.6 %collective-permute-start.2 = (bf16[1040,128]{1,0:T(8,128)(2,1)S(1)}, bf16[1040,128]{1,0:T(8,128)(2,1)S(1)}, u32[]{:S(2)}, u32[]{:S(2)}) collective-permute-start(bf16[1040,128]{1,0:T(8,128)(2,1)S(1)} %pad_maximum_fusion), channel_id=1, source_target_pairs={{0,4},{2,6},{4,0},{6,2},{8,12},{10,14},{12,8},{14,10},{16,20},{18,... | collective-permute-start | bytes 798728 | tf_op jit(solution)/shard_map/ppermute | solution.py:536
  19.6 8.9 %collective-permute-start.5 = (bf16[1024,128]{1,0:T(8,128)(2,1)}, bf16[1024,128]{1,0:T(8,128)(2,1)S(1)}, u32[]{:S(2)}, u32[]{:S(2)}) collective-permute-start(bf16[1024,128]{1,0:T(8,128)(2,1)} %copy-done), channel_id=1, source_target_pairs={{0,2},{2,0},{4,6},{6,4},{8,10},{10,8},{12,14},{14,12},{16,18},{18,... | collective-permute-start | bytes 786440 | tf_op jit(solution)/shard_map/ppermute | solution.py:536
  26.8 10.4 %collective-permute-start.3 = (bf16[1040,128]{1,0:T(8,128)(2,1)S(1)}, bf16[1040,128]{1,0:T(8,128)(2,1)S(1)}, u32[]{:S(2)}, u32[]{:S(2)}) collective-permute-start(bf16[1040,128]{1,0:T(8,128)(2,1)S(1)} %pad_maximum_fusion.1), channel_id=1, source_target_pairs={{0,8},{2,10},{4,12},{6,14},{8,0},{10,2},{12,4},{14,6},{16,24},{18,... | collective-permute-start | bytes 798728 | tf_op jit(solution)/shard_map/ppermute | solution.py:536
  28.6 7.4 %collective-permute-start.6 = (bf16[1024,128]{1,0:T(8,128)(2,1)S(1)}, bf16[1024,128]{1,0:T(8,128)(2,1)S(1)}, u32[]{:S(2)}, u32[]{:S(2)}) collective-permute-start(bf16[1024,128]{1,0:T(8,128)(2,1)S(1)} %fusion.9), channel_id=1, source_target_pairs={{0,4},{2,6},{4,0},{6,2},{8,12},{10,14},{12,8},{14,10},{16,20},{18,... | collective-permute-start | bytes 786440 | tf_op jit(solution)/shard_map/ppermute | solution.py:536
  36.2 7.0 %collective-permute-start.7 = (bf16[1024,128]{1,0:T(8,128)(2,1)S(1)}, bf16[1024,128]{1,0:T(8,128)(2,1)S(1)}, u32[]{:S(2)}, u32[]{:S(2)}) collective-permute-start(bf16[1024,128]{1,0:T(8,128)(2,1)S(1)} %fusion.10), channel_id=1, source_target_pairs={{0,8},{2,10},{4,12},{6,14},{8,0},{10,2},{12,4},{14,6},{16,24},{18,... | collective-permute-start | bytes 786440 | tf_op jit(solution)/shard_map/ppermute | solution.py:536
  37.5 9.3 %collective-permute-start.4 = (bf16[1024,128]{1,0:T(8,128)(2,1)S(1)}, bf16[1024,128]{1,0:T(8,128)(2,1)S(1)}, u32[]{:S(2)}, u32[]{:S(2)}) collective-permute-start(bf16[1024,128]{1,0:T(8,128)(2,1)S(1)} %fusion.5), channel_id=1, source_target_pairs={{0,16},{2,18},{4,20},{6,22},{8,24},{10,26},{12,28},{14,30},{1,17},... | collective-permute-start | bytes 786440 | tf_op jit(solution)/shard_map/ppermute | solution.py:536
  51.6 26.0 %collective-permute-start.8 = (bf16[512,1024]{1,0:T(8,128)(2,1)}, bf16[512,1024]{1,0:T(8,128)(2,1)S(1)}, u32[]{:S(2)}, u32[]{:S(2)}) collective-permute-start(bf16[512,1024]{1,0:T(8,128)(2,1)} %get-tuple-element.56), channel_id=1, source_target_pairs={{0,1},{1,0},{2,3},{3,2},{4,5},{5,4},{6,7},{7,6},{8,9},{9,8},{10,11... | collective-permute-start | bytes 3145736 | tf_op jit(solution)/shard_map/ppermute | solution.py:609
  55.6 22.0 %collective-permute-start.9 = (bf16[512,1024]{1,0:T(8,128)(2,1)}, bf16[512,1024]{1,0:T(8,128)(2,1)}, u32[]{:S(2)}, u32[]{:S(2)}) collective-permute-start(bf16[512,1024]{1,0:T(8,128)(2,1)} %term.1), channel_id=1, source_target_pairs={{0,1},{1,0},{2,3},{3,2},{4,5},{5,4},{6,7},{7,6},{8,9},{9,8},{10,11... | collective-permute-start | bytes 3145736 | tf_op jit(solution)/shard_map/ppermute | solution.py:609
  56.2 16.8 %collective-permute-start.10 = (bf16[1024,128]{1,0:T(8,128)(2,1)S(1)}, bf16[1024,128]{1,0:T(8,128)(2,1)S(1)}, u32[]{:S(2)}, u32[]{:S(2)}) collective-permute-start(bf16[1024,128]{1,0:T(8,128)(2,1)S(1)} %fusion.1), channel_id=1, source_target_pairs={{16,0},{18,2},{20,4},{22,6},{24,8},{26,10},{28,12},{30,14},{17,1},... | collective-permute-start | bytes 786440 | tf_op jit(solution)/shard_map/ppermute | solution.py:536

commit v5 on v4

--- a/solution.py
+++ b/solution.py
@@ -26,7 +26,7 @@
     return lax.dot_general(a, b, dims, preferred_element_type=F32)
 
 
-def kernel_call(kernel, args, specs, outs, out_specs, scratch, mib, name):
+def kernel_call(kernel, args, specs, outs, out_specs, scratch, mib, name, flops=1):
     pinned = [pltpu.with_memory_space_constraint(a, pltpu.HBM) if s is HB else a for a, s in zip(args, specs)]
     placed = tuple(
         (pltpu.HBM if s is HB else jax.ShapeDtypeStruct)(shape, dtype) for (shape, dtype), s in zip(outs, out_specs)
@@ -38,7 +38,7 @@
         out_shape=placed,
         scratch_shapes=scratch,
         compiler_params=pltpu.CompilerParams(vmem_limit_bytes=mib * MIB),
-        cost_estimate=pl.CostEstimate(flops=1, bytes_accessed=1, transcendentals=0),
+        cost_estimate=pl.CostEstimate(flops=flops, bytes_accessed=1, transcendentals=0),
         name=name,
     )(*pinned)
 
@@ -500,6 +500,7 @@
         ],
         20,
         "close",
+        flops=10**11,
     )
 
 

time: 83.8 us -> 70.9 us (0.85)
  the two profiles are of different devices: /device:TPU:0 before, /device:TPU:25 now
where the time goes in v5:
time: 70.9 us; the launch traced here: 70.6 us
  Pallas kernels  43.6 us (61%)
  waiting for transfers between devices  12.1 us (17%)
  starting transfers between devices  11.7 us (17%)
  other arithmetic  2.13 us (3%)
  between operations  0.97 us (1%)
    pallas_call x8, Pallas kernels, kernel_call(): pl.pallas_call(kernel, in_specs=specs, out_specs=tuple(out_specs), out_sh...  43.6 us
    ppermute x8, waiting for transfers between devices, send(): return lax.ppermute(array, 'ctx', pairs)  12.1 us
    ppermute x8, starting transfers between devices, send(): return lax.ppermute(array, 'ctx', pairs)  9.18 us
    ppermute x2, starting transfers between devices, body(): arrived.append(lax.ppermute(term, 'head', ring))  1.78 us
  transfers between devices with their start and end apart: 11, of which 4 were waited for; matrix products, arithmetic and copies ran while one was open for 2% of the time, Pallas kernels for 54%

profile of v5, /device:TPU:25, one launch (start us, length us, event | category | flops | bytes accessed | tf_op | source)
XLA Modules:
  0.0 70.6 jit_solution(9154394359531965921)
XLA Ops:
  0.6 0.7 %collective-permute-start.1 = (bf16[512,2048]{1,0:T(8,128)(2,1)}, bf16[512,2048]{1,0:T(8,128)(2,1)S(1)}, u32[]{:S(2)}, u32[]{:S(2)}) collective-permute-start(bf16[512,2048]{1,0:T(8,128)(2,1)} %refs_0_.1), channel_id=1, source_target_pairs={{0,1},{1,0},{2,3},{3,2},{4,5},{5,4},{6,7},{7,6},{8,9},{9,8},{10,11... | collective-permute-start | bytes 6291464 | tf_op jit(solution)/shard_map/ppermute | solution.py:519
  1.4 4.8 %prepare.1 = (bf16[512,1024]{1,0:T(8,128)(2,1)}, f32[32,512]{1,0:T(8,128)}, bf16[1040,128]{1,0:T(8,128)(2,1)}, f32[1024,128]{1,0:T(8,128)S(1)}) custom-call(f32[8,512]{1,0:T(8,128)} %bitcast.104, bf16[512,1024]{1,0:T(8,128)(2,1)} %k_hbm.1, bf16[512,1024]{1,0:T(8,128)(2,1)} %refs_6_.1), custom_call_target="tpu_custom_call" | custom-call | flops 1 | bytes 1 | tf_op jit(solution)/shard_map/prepare/pallas_call | solution.py:34
  6.2 1.3 %collective-permute-start = (bf16[1040,128]{1,0:T(8,128)(2,1)}, bf16[1040,128]{1,0:T(8,128)(2,1)S(1)}, u32[]{:S(2)}, u32[]{:S(2)}) collective-permute-start(bf16[1040,128]{1,0:T(8,128)(2,1)} %get-tuple-element.33), channel_id=1, source_target_pairs={{0,2},{2,0},{4,6},{6,4},{8,10},{10,8},{12,14},{14,12},{16,18},{18,... | collective-permute-start | bytes 798728 | tf_op jit(solution)/shard_map/ppermute | solution.py:537
  7.5 0.1 pad_add_fusion.place_ref
  7.5 8.5 %project.1 = (bf16[512,1024]{1,0:T(8,128)(2,1)}, f32[1024,128]{1,0:T(8,128)S(1)}, bf16[1024,128]{1,0:T(8,128)(2,1)S(1)}) custom-call(s32[2]{0:T(128)S(1)} %pad_add_fusion.place_ref, bf16[512,2048]{1,0:T(8,128)(2,1)} %refs_0_.1, bf16[512,2048]{1,0:T(8,128)(2,1)S(1)} %collective-permute-done.1.refs_1_, bf16[4096,1024]{1,0:T(8,128)(2,1)} %refs_1_.1, ...), custom_call_target="tpu_custom_call" | custom-call | flops 1 | bytes 1 | tf_op jit(solution)/shard_map/project/pallas_call | solution.py:34
  16.0 0.8 %broadcast_select_fusion.3 = (f32[8,128]{1,0:T(8,128)S(1)}, f32[8,128]{1,0:T(8,128)S(1)}, f32[8,128]{1,0:T(8,128)S(1)}, f32[8,128]{1,0:T(8,128)S(1)}, f32[8,128]...) fusion(pred[]{:T(512)S(6)} %ne.34, ...), kind=kLoop, calls=%fused_computation.53 | loop fusion | flops 14336 | bytes 40962 | tf_op jit(solution)/shard_map/jit(_where)/select_n | solution.py:592
  16.8 0.1 fusion.8
  17.0 1.3 %collective-permute-start.2 = (bf16[1040,128]{1,0:T(8,128)(2,1)S(1)}, bf16[1040,128]{1,0:T(8,128)(2,1)S(1)}, u32[]{:S(2)}, u32[]{:S(2)}) collective-permute-start(bf16[1040,128]{1,0:T(8,128)(2,1)S(1)} %pad_maximum_fusion), channel_id=1, source_target_pairs={{0,4},{2,6},{4,0},{6,2},{8,12},{10,14},{12,8},{14,10},{16,20},{18,... | collective-permute-start | bytes 798728 | tf_op jit(solution)/shard_map/ppermute | solution.py:537
  18.3 0.3 collective-permute-start.5
  18.5 5.7 %inner.2 = (f32[512,512]{1,0:T(8,128)}, f32[512,512]{1,0:T(8,128)}, f32[512,512]{1,0:T(8,128)}) custom-call(bf16[512,1024]{1,0:T(8,128)(2,1)} %get-tuple-element.40.refs_0_, bf16[512,1024]{1,0:T(8,128)(2,1)} %get-tuple-element.41.refs_1_.refs_5_, bf16[512,1024]{1,0:T(8,128)(2,1)} %refs_6_.1, bf16[512,1024]{1,0:T(8,128)(2,1)} %refs_5_.1, ...), custom_call_target="tpu_custom_call" | custom-call | flops 1 | bytes 1 | tf_op jit(solution)/shard_map/inner/pallas_call | solution.py:34
  24.2 0.5 collective-permute-done.2.refs_1_
  24.7 0.2 fusion.11
  24.9 0.2 collective-permute-start.3
  25.2 0.6 collective-permute-done.5.refs_0_
  25.8 0.1 fusion.9
  25.9 0.7 %collective-permute-start.6 = (bf16[1024,128]{1,0:T(8,128)(2,1)S(1)}, bf16[1024,128]{1,0:T(8,128)(2,1)S(1)}, u32[]{:S(2)}, u32[]{:S(2)}) collective-permute-start(bf16[1024,128]{1,0:T(8,128)(2,1)S(1)} %fusion.9), channel_id=1, source_target_pairs={{0,4},{2,6},{4,0},{6,2},{8,12},{10,14},{12,8},{14,10},{16,20},{18,... | collective-permute-start | bytes 786440 | tf_op jit(solution)/shard_map/ppermute | solution.py:537
  26.6 5.7 %inner.3 = (f32[512,512]{1,0:T(8,128)}, f32[512,512]{1,0:T(8,128)}, f32[512,512]{1,0:T(8,128)}) custom-call(bf16[512,1024]{1,0:T(8,128)(2,1)} %get-tuple-element.40.refs_0_, bf16[512,1024]{1,0:T(8,128)(2,1)} %get-tuple-element.41.refs_1_.refs_5_, bf16[512,1024]{1,0:T(8,128)(2,1)} %refs_6_.1, bf16[512,1024]{1,0:T(8,128)(2,1)} %refs_5_.1, ...), custom_call_target="tpu_custom_call" | custom-call | flops 1 | bytes 1 | tf_op jit(solution)/shard_map/inner/pallas_call | solution.py:34
  32.3 0.2 fusion.10
  32.5 1.3 %collective-permute-start.7 = (bf16[1024,128]{1,0:T(8,128)(2,1)S(1)}, bf16[1024,128]{1,0:T(8,128)(2,1)S(1)}, u32[]{:S(2)}, u32[]{:S(2)}) collective-permute-start(bf16[1024,128]{1,0:T(8,128)(2,1)S(1)} %fusion.10), channel_id=1, source_target_pairs={{0,8},{2,10},{4,12},{6,14},{8,0},{10,2},{12,4},{14,6},{16,24},{18,... | collective-permute-start | bytes 786440 | tf_op jit(solution)/shard_map/ppermute | solution.py:537
  33.9 0.2 fusion.5
  34.1 1.3 %collective-permute-start.4 = (bf16[1024,128]{1,0:T(8,128)(2,1)S(1)}, bf16[1024,128]{1,0:T(8,128)(2,1)S(1)}, u32[]{:S(2)}, u32[]{:S(2)}) collective-permute-start(bf16[1024,128]{1,0:T(8,128)(2,1)S(1)} %fusion.5), channel_id=1, source_target_pairs={{0,16},{2,18},{4,20},{6,22},{8,24},{10,26},{12,28},{14,30},{1,17},... | collective-permute-start | bytes 786440 | tf_op jit(solution)/shard_map/ppermute | solution.py:537
  35.5 2.4 %collective-permute-done.7.refs_2_ = bf16[1024,128]{1,0:T(8,128)(2,1)S(1)} collective-permute-done((bf16[1024,128]{1,0:T(8,128)(2,1)S(1)}, bf16[1024,128]{1,0:T(8,128)(2,1)S(1)}, u32[]{:S(2)}, u32[]{:S(2)}) %collective-permute-start.7) | collective-permute-done | bytes 262176 | tf_op jit(solution)/shard_map/ppermute | solution.py:537
  37.8 0.2 fusion.1
  38.1 2.7 %collective-permute-start.10 = (bf16[1024,128]{1,0:T(8,128)(2,1)S(1)}, bf16[1024,128]{1,0:T(8,128)(2,1)S(1)}, u32[]{:S(2)}, u32[]{:S(2)}) collective-permute-start(bf16[1024,128]{1,0:T(8,128)(2,1)S(1)} %fusion.1), channel_id=1, source_target_pairs={{16,0},{18,2},{20,4},{22,6},{24,8},{26,10},{28,12},{30,14},{17,1},... | collective-permute-start | bytes 786440 | tf_op jit(solution)/shard_map/ppermute | solution.py:537
  40.8 0.1 pad_maximum_fusion.2.refs_4_
  41.0 8.6 %collective-permute-done.4.refs_3_ = bf16[1024,128]{1,0:T(8,128)(2,1)S(1)} collective-permute-done((bf16[1024,128]{1,0:T(8,128)(2,1)S(1)}, bf16[1024,128]{1,0:T(8,128)(2,1)S(1)}, u32[]{:S(2)}, u32[]{:S(2)}) %collective-permute-start.4) | collective-permute-done | bytes 262176 | tf_op jit(solution)/shard_map/ppermute | solution.py:537
  49.6 4.7 %query_term.1 = (bf16[512,1024]{1,0:T(8,128)(2,1)}, bf16[512,1024]{1,0:T(8,128)(2,1)}) custom-call(s32[1]{0:T(128)} %bitcast.1.place_ref, bf16[1040,128]{1,0:T(8,128)(2,1)S(1)} %collective-permute-done.refs_0_, bf16[1040,128]{1,0:T(8,128)(2,1)S(1)} %collective-permute-done.2.refs_1_, bf16[1040,128]{1,0:T(8,128)(2,1)S(1)} %collective-permute-done.3.refs_2_, ...), custom_call_target="tpu_custom_call" | custom-call | flops 1 | bytes 1 | tf_op jit(solution)/shard_map/query_term/pallas_call | solution.py:34
  54.4 1.7 %collective-permute-start.8 = (bf16[512,1024]{1,0:T(8,128)(2,1)}, bf16[512,1024]{1,0:T(8,128)(2,1)S(1)}, u32[]{:S(2)}, u32[]{:S(2)}) collective-permute-start(bf16[512,1024]{1,0:T(8,128)(2,1)} %get-tuple-element.56), channel_id=1, source_target_pairs={{0,1},{1,0},{2,3},{3,2},{4,5},{5,4},{6,7},{7,6},{8,9},{9,8},{10,11... | collective-permute-start | bytes 3145736 | tf_op jit(solution)/shard_map/ppermute | solution.py:610
  56.1 3.9 %term.1 = bf16[512,1024]{1,0:T(8,128)(2,1)} custom-call(s32[1]{0:T(128)} %bitcast.1.place_ref, bf16[512,1024]{1,0:T(8,128)(2,1)} %get-tuple-element.55.dq_hbm.refs_0_, bf16[4096,1024]{1,0:T(8,128)(2,1)} %refs_1_.1), custom_call_target="tpu_custom_call" | custom-call | flops 1 | bytes 1 | tf_op jit(solution)/shard_map/term/pallas_call | solution.py:34
  60.0 0.1 collective-permute-start.9
  60.1 4.7 %close.1 = (bf16[512,1024]{1,0:T(8,128)(2,1)}, bf16[512,1024]{1,0:T(8,128)(2,1)}) custom-call(bf16[1024,128]{1,0:T(8,128)(2,1)S(1)} %collective-permute-done.5.refs_0_, bf16[1024,128]{1,0:T(8,128)(2,1)S(1)} %collective-permute-done.6.refs_1_, bf16[1024,128]{1,0:T(8,128)(2,1)S(1)} %collective-permute-done.7.refs_2_, ...), custom_call_target="tpu_custom_call" | custom-call | flops 99999997952 | bytes 1 | tf_op jit(solution)/shard_map/close/pallas_call | solution.py:34
  64.8 5.7 %finish.1 = bf16[512,2048]{1,0:T(8,128)(2,1)} custom-call(s32[1]{0:T(128)} %bitcast.place_ref, bf16[512,1024]{1,0:T(8,128)(2,1)} %get-tuple-element.55.dq_hbm.refs_0_, bf16[4096,1024]{1,0:T(8,128)(2,1)} %refs_1_.1, bf16[512,1024]{1,0:T(8,128)(2,1)S(1)} %collective-permute-done.8.refs_2_, bf16[512,1024]{1,0:T(8,128)(2,1)S(1)} %collective-permute-done.9.refs_3_), custom_call_target="tpu_custom_call" | custom-call | flops 1 | bytes 1 | tf_op jit(solution)/shard_map/finish/pallas_call | solution.py:34
  (21 shorter events, 0.2 us)
Async XLA Ops:
  0.6 6.9 %collective-permute-start.1 = (bf16[512,2048]{1,0:T(8,128)(2,1)}, bf16[512,2048]{1,0:T(8,128)(2,1)S(1)}, u32[]{:S(2)}, u32[]{:S(2)}) collective-permute-start(bf16[512,2048]{1,0:T(8,128)(2,1)} %refs_0_.1), channel_id=1, source_target_pairs={{0,1},{1,0},{2,3},{3,2},{4,5},{5,4},{6,7},{7,6},{8,9},{9,8},{10,11... | collective-permute-start | bytes 6291464 | tf_op jit(solution)/shard_map/ppermute | solution.py:519
  6.2 9.8 %collective-permute-start = (bf16[1040,128]{1,0:T(8,128)(2,1)}, bf16[1040,128]{1,0:T(8,128)(2,1)S(1)}, u32[]{:S(2)}, u32[]{:S(2)}) collective-permute-start(bf16[1040,128]{1,0:T(8,128)(2,1)} %get-tuple-element.33), channel_id=1, source_target_pairs={{0,2},{2,0},{4,6},{6,4},{8,10},{10,8},{12,14},{14,12},{16,18},{18,... | collective-permute-start | bytes 798728 | tf_op jit(solution)/shard_map/ppermute | solution.py:537
  16.0 0.9 %copy-start = (bf16[1024,128]{1,0:T(8,128)(2,1)}, bf16[1024,128]{1,0:T(8,128)(2,1)S(1)}, u32[]{:S(2)}) copy-start(bf16[1024,128]{1,0:T(8,128)(2,1)S(1)} %get-tuple-element.51) | copy-start | bytes 786436
  17.0 7.7 %collective-permute-start.2 = (bf16[1040,128]{1,0:T(8,128)(2,1)S(1)}, bf16[1040,128]{1,0:T(8,128)(2,1)S(1)}, u32[]{:S(2)}, u32[]{:S(2)}) collective-permute-start(bf16[1040,128]{1,0:T(8,128)(2,1)S(1)} %pad_maximum_fusion), channel_id=1, source_target_pairs={{0,4},{2,6},{4,0},{6,2},{8,12},{10,14},{12,8},{14,10},{16,20},{18,... | collective-permute-start | bytes 798728 | tf_op jit(solution)/shard_map/ppermute | solution.py:537
  18.3 7.5 %collective-permute-start.5 = (bf16[1024,128]{1,0:T(8,128)(2,1)}, bf16[1024,128]{1,0:T(8,128)(2,1)S(1)}, u32[]{:S(2)}, u32[]{:S(2)}) collective-permute-start(bf16[1024,128]{1,0:T(8,128)(2,1)} %copy-done), channel_id=1, source_target_pairs={{0,2},{2,0},{4,6},{6,4},{8,10},{10,8},{12,14},{14,12},{16,18},{18,... | collective-permute-start | bytes 786440 | tf_op jit(solution)/shard_map/ppermute | solution.py:537
  24.9 9.0 %collective-permute-start.3 = (bf16[1040,128]{1,0:T(8,128)(2,1)S(1)}, bf16[1040,128]{1,0:T(8,128)(2,1)S(1)}, u32[]{:S(2)}, u32[]{:S(2)}) collective-permute-start(bf16[1040,128]{1,0:T(8,128)(2,1)S(1)} %pad_maximum_fusion.1), channel_id=1, source_target_pairs={{0,8},{2,10},{4,12},{6,14},{8,0},{10,2},{12,4},{14,6},{16,24},{18,... | collective-permute-start | bytes 798728 | tf_op jit(solution)/shard_map/ppermute | solution.py:537
  25.9 6.5 %collective-permute-start.6 = (bf16[1024,128]{1,0:T(8,128)(2,1)S(1)}, bf16[1024,128]{1,0:T(8,128)(2,1)S(1)}, u32[]{:S(2)}, u32[]{:S(2)}) collective-permute-start(bf16[1024,128]{1,0:T(8,128)(2,1)S(1)} %fusion.9), channel_id=1, source_target_pairs={{0,4},{2,6},{4,0},{6,2},{8,12},{10,14},{12,8},{14,10},{16,20},{18,... | collective-permute-start | bytes 786440 | tf_op jit(solution)/shard_map/ppermute | solution.py:537
  32.5 5.3 %collective-permute-start.7 = (bf16[1024,128]{1,0:T(8,128)(2,1)S(1)}, bf16[1024,128]{1,0:T(8,128)(2,1)S(1)}, u32[]{:S(2)}, u32[]{:S(2)}) collective-permute-start(bf16[1024,128]{1,0:T(8,128)(2,1)S(1)} %fusion.10), channel_id=1, source_target_pairs={{0,8},{2,10},{4,12},{6,14},{8,0},{10,2},{12,4},{14,6},{16,24},{18,... | collective-permute-start | bytes 786440 | tf_op jit(solution)/shard_map/ppermute | solution.py:537
  34.1 15.5 %collective-permute-start.4 = (bf16[1024,128]{1,0:T(8,128)(2,1)S(1)}, bf16[1024,128]{1,0:T(8,128)(2,1)S(1)}, u32[]{:S(2)}, u32[]{:S(2)}) collective-permute-start(bf16[1024,128]{1,0:T(8,128)(2,1)S(1)} %fusion.5), channel_id=1, source_target_pairs={{0,16},{2,18},{4,20},{6,22},{8,24},{10,26},{12,28},{14,30},{1,17},... | collective-permute-start | bytes 786440 | tf_op jit(solution)/shard_map/ppermute | solution.py:537
  38.1 22.0 %collective-permute-start.10 = (bf16[1024,128]{1,0:T(8,128)(2,1)S(1)}, bf16[1024,128]{1,0:T(8,128)(2,1)S(1)}, u32[]{:S(2)}, u32[]{:S(2)}) collective-permute-start(bf16[1024,128]{1,0:T(8,128)(2,1)S(1)} %fusion.1), channel_id=1, source_target_pairs={{16,0},{18,2},{20,4},{22,6},{24,8},{26,10},{28,12},{30,14},{17,1},... | collective-permute-start | bytes 786440 | tf_op jit(solution)/shard_map/ppermute | solution.py:537
  54.4 10.4 %collective-permute-start.8 = (bf16[512,1024]{1,0:T(8,128)(2,1)}, bf16[512,1024]{1,0:T(8,128)(2,1)S(1)}, u32[]{:S(2)}, u32[]{:S(2)}) collective-permute-start(bf16[512,1024]{1,0:T(8,128)(2,1)} %get-tuple-element.56), channel_id=1, source_target_pairs={{0,1},{1,0},{2,3},{3,2},{4,5},{5,4},{6,7},{7,6},{8,9},{9,8},{10,11... | collective-permute-start | bytes 3145736 | tf_op jit(solution)/shard_map/ppermute | solution.py:610
  60.0 4.8 %collective-permute-start.9 = (bf16[512,1024]{1,0:T(8,128)(2,1)}, bf16[512,1024]{1,0:T(8,128)(2,1)S(1)}, u32[]{:S(2)}, u32[]{:S(2)}) collective-permute-start(bf16[512,1024]{1,0:T(8,128)(2,1)} %term.1), channel_id=1, source_target_pairs={{0,1},{1,0},{2,3},{3,2},{4,5},{5,4},{6,7},{7,6},{8,9},{9,8},{10,11... | collective-permute-start | bytes 3145736 | tf_op jit(solution)/shard_map/ppermute | solution.py:610

commit v6 on v5

--- a/solution.py
+++ b/solution.py
@@ -86,15 +86,13 @@
     return jnp.concatenate([facts, spare], axis=0).T
 
 
-def prepare_kernel(
-    heads, hp, scaling, ld_hbm, k_hbm, v_hbm, ks_hbm, facts_hbm, msg_ref, state_ref, ld, facts_ref, kbuf, vbuf, ksbuf, sems
-):
+def prepare_kernel(heads, hp, scaling, ld_hbm, k_hbm, v_hbm, facts_hbm, msg_ref, state_ref, ld, facts_ref, kbuf, vbuf, sems):
     rows = kbuf.shape[0]
     copies = Copies(sems)
     ld_in = copies.start(ld_hbm, ld)
-    parts = [pl.ds(f, rows // 2) for f in (0, rows // 2)]
-    k_in = [copies.start(k_hbm.at[p, :], kbuf.at[p, :]) for p in parts]
-    v_in = [copies.start(v_hbm.at[p, :], vbuf.at[p, :]) for p in parts]
+    loads = []
+    for _, _, wide in groups(heads):
+        loads.append([copies.start(src.at[:, wide], dst.at[:, wide]) for src, dst in ((k_hbm, kbuf), (v_hbm, vbuf))])
     ld_in.wait()
     logs = ld[...]
     if heads < hp:
@@ -119,19 +117,21 @@
     low = (share - high.astype(F32)).astype(BF16)
     base = heads * HDIM
     msg_ref[base:, :] = jnp.concatenate([high.astype(F32), low.astype(F32)], axis=0).astype(BF16)
-    for copy in k_in + v_in:
-        copy.wait()
-    for first, last, wide in groups(heads):
+    for (first, last, _), load in zip(groups(heads), loads):
+        for copy in load:
+            copy.wait()
         for h in range(first, last):
             cols = slice(h * HDIM, (h + 1) * HDIM)
-            scaled = (column(table, hp + h) * kbuf[:, cols].astype(F32)).astype(BF16)
-            ksbuf[:, cols] = scaled
+            scaled = scaled_keys(table, hp, h, kbuf[:, cols])
             decayed = (column(table, 2 * hp + h) * scaled.astype(F32)).astype(BF16)
             local = dot(decayed, vbuf[:, cols], TN)
             state_ref[cols, :] = local
             msg_ref[cols, :] = local.astype(BF16)
-        copies.store(ksbuf.at[:, wide], ks_hbm.at[:, wide])
     copies.finish()
+
+
+def scaled_keys(table, hp, h, keys):
+    return (column(table, hp + h) * keys.astype(F32)).astype(BF16)
 
 
 def prepare(logs, keys, values, heads, hp, scaling):
@@ -141,15 +141,14 @@
         functools.partial(prepare_kernel, heads, hp, scaling),
         (logs, keys, values),
         [HB] * 3,
-        [((rows, width), BF16), ((4 * hp, rows), F32), ((width + 2 * hp, HDIM), BF16), ((width, HDIM), F32)],
-        (HB, HB, VM, VM),
+        [((4 * hp, rows), F32), ((width + 2 * hp, HDIM), BF16), ((width, HDIM), F32)],
+        (HB, VM, VM),
         [
             pltpu.VMEM((heads, rows), F32),
             pltpu.VMEM((4 * hp, rows), F32),
             buf,
             buf,
-            buf,
-            pltpu.SemaphoreType.DMA((6 + len(groups(heads)),)),
+            pltpu.SemaphoreType.DMA((2 + 2 * len(groups(heads)),)),
         ],
         12,
         "prepare",
@@ -230,50 +229,58 @@
     ins, facts_hbm, outs = refs[:4], refs[4], refs[5:8]
     bufs, facts_ref, sides, sems = refs[8:12], refs[12], refs[13:16], refs[16]
     rows = ins[0].shape[0]
-    wide = pl.ds(first * HDIM, (last - first) * HDIM)
     copies = Copies(sems)
     facts_in = copies.start(facts_hbm, facts_ref)
-    loads = [copies.start(src.at[:, wide], dst) for src, dst in zip(ins, bufs)]
+    loads = {}
+    for h in range(first, last, 2):
+        count = min(2, last - h)
+        src, dst = pl.ds(h * HDIM, count * HDIM), pl.ds((h - first) * HDIM, count * HDIM)
+        loads[h] = [copies.start(ref.at[:, src], buf.at[:, dst]) for ref, buf in zip(ins, bufs)]
     facts_in.wait()
     table = turned(facts_ref[...])
     row = lax.broadcasted_iota(jnp.int32, (rows, rows), 0)
     keep = row >= lax.broadcasted_iota(jnp.int32, (rows, rows), 1)
     shift = -0.5 * math.log2(HDIM)
     turn = math.log2(math.e)
-    for copy in loads:
-        copy.wait()
-    q_ref, ks_ref, v_ref, do_ref = bufs
+    q_ref, k_ref, v_ref, do_ref = bufs
     for h in range(first, last):
+        for copy in loads.get(h, ()):
+            copy.wait()
         cols = slice((h - first) * HDIM, (h - first + 1) * HDIM)
         later = column(table, h) * turn + shift
         sooner = facts_ref[h : h + 1, :] * turn
         gap = jnp.concatenate([later] * (rows // LANES), axis=1) - sooner
         decays = jnp.exp2(jnp.where(keep, gap, -1e30))
-        query, scaled, grad = q_ref[:, cols], ks_ref[:, cols], do_ref[:, cols]
+        query, grad = q_ref[:, cols], do_ref[:, cols]
+        scaled = scaled_keys(table, hp, h, k_ref[:, cols])
         wdv = (decays * dot(grad, v_ref[:, cols], NT)).astype(BF16)
         wkq = (decays * dot(query, scaled, NT)).astype(BF16)
-        sides[0][:, cols] = dot(wdv, scaled, NN)
-        sides[1][:, cols] = dot(query, wdv, TN).T
-        sides[2][:, cols] = dot(grad, wkq, TN).T
-    for side, out in zip(sides, outs):
-        copies.store(side, out)
+        sides[0][:, cols] = dot(wdv, scaled, NN).astype(BF16)
+        sides[1][:, cols] = dot(query, wdv, TN).T.astype(BF16)
+        sides[2][:, cols] = dot(grad, wkq, TN).T.astype(BF16)
+        if h + 1 == last or h + 1 in loads:
+            from_head = h if h in loads else h - 1
+            done = slice((from_head - first) * HDIM, (h + 1 - first) * HDIM)
+            for side, out in zip(sides, outs):
+                copies.store(side.at[:, done], out.at[:, done])
     copies.finish()
 
 
-def inner(first, last, query, scaled_keys, values, d_out, facts, hp):
+def inner(first, last, query, keys, values, d_out, facts, hp):
     rows = query.shape[0]
     width = (last - first) * HDIM
+    pairs = -(-(last - first) // 2)
     return kernel_call(
         functools.partial(inner_kernel, first, last, hp),
-        (query, scaled_keys, values, d_out, facts),
+        (query, keys, values, d_out, facts),
         [HB] * 5,
-        [((rows, width), F32)] * 3,
+        [((rows, width), BF16)] * 3,
         (HB,) * 3,
         [
             *[pltpu.VMEM((rows, width), BF16)] * 4,
             pltpu.VMEM(facts.shape, F32),
-            *[pltpu.VMEM((rows, width), F32)] * 3,
-            pltpu.SemaphoreType.DMA((8,)),
+            *[pltpu.VMEM((rows, width), BF16)] * 3,
+            pltpu.SemaphoreType.DMA((1 + 7 * pairs,)),
         ],
         24,
         "inner",
@@ -322,7 +329,7 @@
         cols = slice(h * HDIM, (h + 1) * HDIM)
         state = mix(coef_ref, pieces, heads, h)
         carry = dot(dobuf[:, cols], state, NT)
-        held[:, cols] = (local[:, cols] + column(table, 3 * hp + h) * carry).astype(BF16)
+        held[:, cols] = (local[:, cols].astype(F32) + column(table, 3 * hp + h) * carry).astype(BF16)
     copies.store(held, dq_hbm)
     send_terms(copies, w_in, held, wbuf, sent, out_hbm, block)
     copies.finish()
@@ -350,7 +357,7 @@
             pltpu.VMEM((rows, width), BF16),
             pltpu.VMEM(facts.shape, F32),
             pltpu.VMEM((count, width), BF16),
-            pltpu.VMEM((rows, width), F32),
+            pltpu.VMEM((rows, width), BF16),
             pltpu.VMEM((rows, width), BF16),
             pltpu.VMEM((rows, count), BF16),
             pltpu.SemaphoreType.DMA((2 + 2 * len(inner_dq) + 2 * (count // block),)),
@@ -440,9 +447,9 @@
 
 def close_kernel(heads, hp, stages, *refs):
     pieces = refs[:stages]
-    coef_ref, ks_hbm, v_hbm, facts_hbm = refs[stages : stages + 4]
+    coef_ref, in_hbm, v_hbm, facts_hbm = refs[stages : stages + 4]
     rest = refs[stages + 4 : -10]
-    k_hbm, dv_hbm, ksbuf, vbuf, facts_ref, dkbuf, dvbuf, kside, vside, sems = refs[-10:]
+    dk_hbm, dv_hbm, kbuf, vbuf, facts_ref, dkbuf, dvbuf, kside, vside, sems = refs[-10:]
     dks, dvs = rest[: len(rest) // 2], rest[len(rest) // 2 :]
     each = heads // len(dks)
     copies = Copies(sems)
@@ -454,7 +461,7 @@
             (
                 copies.start(v_hbm.at[:, wide], vbuf.at[:, wide]),
                 copies.start(dk, dkbuf.at[:, wide]),
-                copies.start(ks_hbm.at[:, wide], ksbuf.at[:, wide]),
+                copies.start(in_hbm.at[:, wide], kbuf.at[:, wide]),
                 copies.start(dv, dvbuf.at[:, wide]),
             )
         )
@@ -468,20 +475,20 @@
         adjoint = mix(coef_ref, pieces, heads, h)
         tail, gain = column(table, 2 * hp + h), column(table, hp + h)
         carry_k = dot(vbuf[:, cols], adjoint, NT)
-        kside[:, cols] = (gain * (dkbuf[:, cols] + tail * carry_k)).astype(BF16)
-        carry_v = dot(ksbuf[:, cols], adjoint, NN)
-        vside[:, cols] = (dvbuf[:, cols] + tail * carry_v).astype(BF16)
+        kside[:, cols] = (gain * (dkbuf[:, cols].astype(F32) + tail * carry_k)).astype(BF16)
+        carry_v = dot(scaled_keys(table, hp, h, kbuf[:, cols]), adjoint, NN)
+        vside[:, cols] = (dvbuf[:, cols].astype(F32) + tail * carry_v).astype(BF16)
         if (h + 1) % each == 0:
             wide = slice((h + 1 - each) * HDIM, (h + 1) * HDIM)
-            copies.store(kside.at[:, wide], k_hbm.at[:, wide])
+            copies.store(kside.at[:, wide], dk_hbm.at[:, wide])
             copies.store(vside.at[:, wide], dv_hbm.at[:, wide])
     copies.finish()
 
 
-def close(pieces, coefs, dks, dvs, scaled_keys, values, facts, heads, hp):
+def close(pieces, coefs, dks, dvs, keys, values, facts, heads, hp):
     rows, width = values.shape
-    args = (coefs, scaled_keys, values, facts, *dks, *dvs)
-    buf, wide = pltpu.VMEM((rows, width), BF16), pltpu.VMEM((rows, width), F32)
+    args = (coefs, keys, values, facts, *dks, *dvs)
+    buf = pltpu.VMEM((rows, width), BF16)
     return kernel_call(
         functools.partial(close_kernel, heads, hp, len(pieces)),
         (*pieces, *args),
@@ -492,8 +499,8 @@
             buf,
             buf,
             pltpu.VMEM(facts.shape, F32),
-            wide,
-            wide,
+            buf,
+            buf,
             buf,
             buf,
             pltpu.SemaphoreType.DMA((1 + 6 * len(dks),)),
@@ -519,7 +526,7 @@
         parts.append(lax.ppermute(hidden, "head", ring))
     owners = jnp.stack([(mine + head_size - s) % head_size for s in range(head_size)]).astype(jnp.int32)
 
-    scaled_keys, facts, msg, state = prepare(log_decay.T, keys, values, heads, hp, scaling)
+    facts, msg, state = prepare(log_decay.T, keys, values, heads, hp, scaling)
     query, adjoint, amsg = project(parts, owners, w_query, d_out, facts, hp)
 
     wide = lambda factor: factor[:heads, None, :]
@@ -566,10 +573,12 @@
     inner_parts = []
 
     def next_inner():
-        return inner(*pending.pop(0), query, scaled_keys, values, d_out, facts, hp)
+        return inner(*pending.pop(0), query, keys, values, d_out, facts, hp)
 
     barrier = lax.optimization_barrier
     for stage in range(stages):
+        if stage == stages - 1:
+            msg, query = barrier((msg, query))
         arrived = send(msg if stage < stages - 1 else msg[:width], stage, True)
         if stage == 0:
             arrived, query, adjoint, amsg = barrier((arrived, query, adjoint, amsg))
@@ -596,7 +605,7 @@
     dqs, dks, dvs = zip(*inner_parts)
 
     place = lambda shift: ((mine + shift) % head_size).astype(jnp.int32).reshape(1)
-    count = feat // 2 if feat >= 1024 else feat
+    count = feat
     arrived = []
     for shift in range(1, head_size):
         ring = [(i, (i + shift) % head_size) for i in range(head_size)]
@@ -608,7 +617,7 @@
             else:
                 term = plain_term(d_query, w_query, place(shift), feat, first, count)
             arrived.append(lax.ppermute(term, "head", ring))
-    d_keys, d_values = close(agot, adjoint_coefs, dks, dvs, scaled_keys, values, facts, heads, hp)
+    d_keys, d_values = close(agot, adjoint_coefs, dks, dvs, keys, values, facts, heads, hp)
     d_hidden = finish(d_query, w_query, place(0), arrived, feat)
     return (d_hidden, d_keys, d_values)
 

time: 70.9 us -> 71.2 us (level)
  the two profiles are of different devices: /device:TPU:25 before, /device:TPU:0 now
where the time goes in v6:
time: 71.2 us; the launch traced here: 70.9 us
  Pallas kernels  38.5 us (54%)
  starting transfers between devices  15.2 us (21%)
  waiting for transfers between devices  14.1 us (20%)
  other arithmetic  2.13 us (3%)
  between operations  0.96 us (1%)
    pallas_call x7, Pallas kernels, kernel_call(): pl.pallas_call(kernel, in_specs=specs, out_specs=tuple(out_specs), out_sh...  38.5 us
    ppermute x8, starting transfers between devices, send(): return lax.ppermute(array, 'ctx', pairs)  14.6 us
    ppermute x8, waiting for transfers between devices, send(): return lax.ppermute(array, 'ctx', pairs)  14.1 us
  transfers between devices with their start and end apart: 10, of which 5 were waited for; matrix products, arithmetic and copies ran while one was open for 2% of the time, Pallas kernels for 46%

profile of v6, /device:TPU:0, one launch (start us, length us, event | category | flops | bytes accessed | tf_op | source)
XLA Modules:
  0.0 70.9 jit_solution(13997920235546368523)
XLA Ops:
  0.6 0.5 collective-permute-start.1
  1.1 4.4 %prepare.1 = (f32[32,512]{1,0:T(8,128)}, bf16[1040,128]{1,0:T(8,128)(2,1)}, f32[1024,128]{1,0:T(8,128)S(1)}) custom-call(f32[8,512]{1,0:T(8,128)} %bitcast.104, bf16[512,1024]{1,0:T(8,128)(2,1)} %refs_5_.3, bf16[512,1024]{1,0:T(8,128)(2,1)} %refs_6_.1), custom_call_target="tpu_custom_call" | custom-call | flops 1 | bytes 1 | tf_op jit(solution)/shard_map/prepare/pallas_call | solution.py:34
  5.5 2.6 %collective-permute-start = (bf16[1040,128]{1,0:T(8,128)(2,1)}, bf16[1040,128]{1,0:T(8,128)(2,1)S(1)}, u32[]{:S(2)}, u32[]{:S(2)}) collective-permute-start(bf16[1040,128]{1,0:T(8,128)(2,1)} %get-tuple-element.34), channel_id=1, source_target_pairs={{0,2},{2,0},{4,6},{6,4},{8,10},{10,8},{12,14},{14,12},{16,18},{18,... | collective-permute-start | bytes 798728 | tf_op jit(solution)/shard_map/ppermute | solution.py:544
  8.1 0.1 pad_add_fusion.place_ref
  8.2 8.5 %project.1 = (bf16[512,1024]{1,0:T(8,128)(2,1)}, f32[1024,128]{1,0:T(8,128)S(1)}, bf16[1024,128]{1,0:T(8,128)(2,1)S(1)}) custom-call(s32[2]{0:T(128)S(1)} %pad_add_fusion.place_ref, bf16[512,2048]{1,0:T(8,128)(2,1)} %refs_0_.1, bf16[512,2048]{1,0:T(8,128)(2,1)S(1)} %collective-permute-done.1.refs_1_, bf16[4096,1024]{1,0:T(8,128)(2,1)} %refs_1_.5, ...), custom_call_target="tpu_custom_call" | custom-call | flops 1 | bytes 1 | tf_op jit(solution)/shard_map/project/pallas_call | solution.py:34
  16.7 0.8 %broadcast_select_fusion.3 = (f32[8,128]{1,0:T(8,128)S(1)}, f32[8,128]{1,0:T(8,128)S(1)}, f32[8,128]{1,0:T(8,128)S(1)}, f32[8,128]{1,0:T(8,128)S(1)}, f32[8,128]...) fusion(pred[]{:T(512)S(6)} %ne.32, ...), kind=kLoop, calls=%fused_computation.53 | loop fusion | flops 14336 | bytes 40962 | tf_op jit(solution)/shard_map/jit(_where)/select_n | solution.py:601
  17.5 0.1 fusion.8
  17.6 1.6 %collective-permute-start.2 = (bf16[1040,128]{1,0:T(8,128)(2,1)S(1)}, bf16[1040,128]{1,0:T(8,128)(2,1)S(1)}, u32[]{:S(2)}, u32[]{:S(2)}) collective-permute-start(bf16[1040,128]{1,0:T(8,128)(2,1)S(1)} %pad_maximum_fusion), channel_id=1, source_target_pairs={{0,4},{2,6},{4,0},{6,2},{8,12},{10,14},{12,8},{14,10},{16,20},{18,... | collective-permute-start | bytes 798728 | tf_op jit(solution)/shard_map/ppermute | solution.py:544
  19.2 5.0 %inner.2 = (bf16[512,512]{1,0:T(8,128)(2,1)}, bf16[512,512]{1,0:T(8,128)(2,1)}, bf16[512,512]{1,0:T(8,128)(2,1)}) custom-call(bf16[512,1024]{1,0:T(8,128)(2,1)} %get-tuple-element.47.refs_0_, bf16[512,1024]{1,0:T(8,128)(2,1)} %refs_5_.3, bf16[512,1024]{1,0:T(8,128)(2,1)} %refs_6_.1, bf16[512,1024]{1,0:T(8,128)(2,1)} %refs_5_.2, ...), custom_call_target="tpu_custom_call" | custom-call | flops 1 | bytes 1 | tf_op jit(solution)/shard_map/inner/pallas_call | solution.py:34
  24.2 0.6 collective-permute-start.5
  24.8 1.4 %collective-permute-done.2.refs_1_ = bf16[1040,128]{1,0:T(8,128)(2,1)S(1)} collective-permute-done((bf16[1040,128]{1,0:T(8,128)(2,1)S(1)}, bf16[1040,128]{1,0:T(8,128)(2,1)S(1)}, u32[]{:S(2)}, u32[]{:S(2)}) %collective-permute-start.2) | collective-permute-done | bytes 266272 | tf_op jit(solution)/shard_map/ppermute | solution.py:544
  26.2 0.2 fusion.11
  26.4 1.6 %collective-permute-start.3 = (bf16[1040,128]{1,0:T(8,128)(2,1)S(1)}, bf16[1040,128]{1,0:T(8,128)(2,1)S(1)}, u32[]{:S(2)}, u32[]{:S(2)}) collective-permute-start(bf16[1040,128]{1,0:T(8,128)(2,1)S(1)} %pad_maximum_fusion.1), channel_id=1, source_target_pairs={{0,8},{2,10},{4,12},{6,14},{8,0},{10,2},{12,4},{14,6},{16,24},{18,... | collective-permute-start | bytes 798728 | tf_op jit(solution)/shard_map/ppermute | solution.py:544
  28.0 4.4 %collective-permute-done.5.refs_0_ = bf16[1024,128]{1,0:T(8,128)(2,1)S(1)} collective-permute-done((bf16[1024,128]{1,0:T(8,128)(2,1)S(1)}, bf16[1024,128]{1,0:T(8,128)(2,1)S(1)}, u32[]{:S(2)}, u32[]{:S(2)}) %collective-permute-start.5) | collective-permute-done | bytes 262176 | tf_op jit(solution)/shard_map/ppermute | solution.py:544
  32.4 0.1 fusion.9
  32.5 0.6 collective-permute-start.6
  33.1 6.7 %collective-permute-done.6.refs_1_ = bf16[1024,128]{1,0:T(8,128)(2,1)S(1)} collective-permute-done((bf16[1024,128]{1,0:T(8,128)(2,1)S(1)}, bf16[1024,128]{1,0:T(8,128)(2,1)S(1)}, u32[]{:S(2)}, u32[]{:S(2)}) %collective-permute-start.6) | collective-permute-done | bytes 262176 | tf_op jit(solution)/shard_map/ppermute | solution.py:544
  39.9 0.2 fusion.10
  40.0 1.6 %collective-permute-start.7 = (bf16[1024,128]{1,0:T(8,128)(2,1)S(1)}, bf16[1024,128]{1,0:T(8,128)(2,1)S(1)}, u32[]{:S(2)}, u32[]{:S(2)}) collective-permute-start(bf16[1024,128]{1,0:T(8,128)(2,1)S(1)} %fusion.10), channel_id=1, source_target_pairs={{0,8},{2,10},{4,12},{6,14},{8,0},{10,2},{12,4},{14,6},{16,24},{18,... | collective-permute-start | bytes 786440 | tf_op jit(solution)/shard_map/ppermute | solution.py:544
  41.7 0.2 fusion.5
  41.9 4.5 %collective-permute-start.4 = (bf16[1024,128]{1,0:T(8,128)(2,1)S(1)}, bf16[1024,128]{1,0:T(8,128)(2,1)S(1)}, u32[]{:S(2)}, u32[]{:S(2)}) collective-permute-start(bf16[1024,128]{1,0:T(8,128)(2,1)S(1)} %fusion.5), channel_id=1, source_target_pairs={{0,16},{2,18},{4,20},{6,22},{8,24},{10,26},{12,28},{14,30},{1,17},... | collective-permute-start | bytes 786440 | tf_op jit(solution)/shard_map/ppermute | solution.py:544
  46.5 0.2 collective-permute-done.7.refs_2_
  46.7 0.2 fusion.1
  46.9 1.5 %collective-permute-start.9 = (bf16[1024,128]{1,0:T(8,128)(2,1)S(1)}, bf16[1024,128]{1,0:T(8,128)(2,1)S(1)}, u32[]{:S(2)}, u32[]{:S(2)}) collective-permute-start(bf16[1024,128]{1,0:T(8,128)(2,1)S(1)} %fusion.1), channel_id=1, source_target_pairs={{16,0},{18,2},{20,4},{22,6},{24,8},{26,10},{28,12},{30,14},{17,1},... | collective-permute-start | bytes 786440 | tf_op jit(solution)/shard_map/ppermute | solution.py:544
  48.4 0.1 pad_maximum_fusion.3.refs_4_
  48.5 5.0 %inner.3 = (bf16[512,512]{1,0:T(8,128)(2,1)}, bf16[512,512]{1,0:T(8,128)(2,1)}, bf16[512,512]{1,0:T(8,128)(2,1)}) custom-call(bf16[512,1024]{1,0:T(8,128)(2,1)} %get-tuple-element.47.refs_0_, bf16[512,1024]{1,0:T(8,128)(2,1)} %refs_5_.3, bf16[512,1024]{1,0:T(8,128)(2,1)} %refs_6_.1, bf16[512,1024]{1,0:T(8,128)(2,1)} %refs_5_.2, ...), custom_call_target="tpu_custom_call" | custom-call | flops 1 | bytes 1 | tf_op jit(solution)/shard_map/inner/pallas_call | solution.py:34
  53.5 0.1 pad_maximum_fusion.2.refs_4_
  53.5 5.9 %query_term.1 = (bf16[512,1024]{1,0:T(8,128)(2,1)}, bf16[512,2048]{1,0:T(8,128)(2,1)}) custom-call(s32[1]{0:T(128)} %bitcast.1.place_ref, bf16[1040,128]{1,0:T(8,128)(2,1)S(1)} %collective-permute-done.refs_0_, bf16[1040,128]{1,0:T(8,128)(2,1)S(1)} %collective-permute-done.2.refs_1_, bf16[1040,128]{1,0:T(8,128)(2,1)S(1)} %collective-permute-done.3.refs_2_, ...), custom_call_target="tpu_custom_call" | custom-call | flops 1 | bytes 1 | tf_op jit(solution)/shard_map/query_term/pallas_call | solution.py:34
  59.4 0.1 collective-permute-start.8
  59.5 1.4 %collective-permute-done.9.refs_3_ = bf16[1024,128]{1,0:T(8,128)(2,1)S(1)} collective-permute-done((bf16[1024,128]{1,0:T(8,128)(2,1)S(1)}, bf16[1024,128]{1,0:T(8,128)(2,1)S(1)}, u32[]{:S(2)}, u32[]{:S(2)}) %collective-permute-start.9) | collective-permute-done | bytes 262176 | tf_op jit(solution)/shard_map/ppermute | solution.py:544
  61.0 4.2 %close.1 = (bf16[512,1024]{1,0:T(8,128)(2,1)}, bf16[512,1024]{1,0:T(8,128)(2,1)}) custom-call(bf16[1024,128]{1,0:T(8,128)(2,1)S(1)} %collective-permute-done.5.refs_0_, bf16[1024,128]{1,0:T(8,128)(2,1)S(1)} %collective-permute-done.6.refs_1_, bf16[1024,128]{1,0:T(8,128)(2,1)S(1)} %collective-permute-done.7.refs_2_, ...), custom_call_target="tpu_custom_call" | custom-call | flops 99999997952 | bytes 1 | tf_op jit(solution)/shard_map/close/pallas_call | solution.py:34
  65.2 5.5 %finish.1 = bf16[512,2048]{1,0:T(8,128)(2,1)} custom-call(s32[1]{0:T(128)} %bitcast.place_ref, bf16[512,1024]{1,0:T(8,128)(2,1)} %get-tuple-element.57.refs_0_, bf16[4096,1024]{1,0:T(8,128)(2,1)} %refs_1_.5, bf16[512,2048]{1,0:T(8,128)(2,1)S(1)} %collective-permute-done.8.refs_2_), custom_call_target="tpu_custom_call" | custom-call | flops 1 | bytes 1 | tf_op jit(solution)/shard_map/finish/pallas_call | solution.py:34
  (20 shorter events, 0.1 us)
Async XLA Ops:
  0.6 7.5 %collective-permute-start.1 = (bf16[512,2048]{1,0:T(8,128)(2,1)}, bf16[512,2048]{1,0:T(8,128)(2,1)S(1)}, u32[]{:S(2)}, u32[]{:S(2)}) collective-permute-start(bf16[512,2048]{1,0:T(8,128)(2,1)} %refs_0_.1), channel_id=1, source_target_pairs={{0,1},{1,0},{2,3},{3,2},{4,5},{5,4},{6,7},{7,6},{8,9},{9,8},{10,11... | collective-permute-start | bytes 6291464 | tf_op jit(solution)/shard_map/ppermute | solution.py:526
  5.5 11.1 %collective-permute-start = (bf16[1040,128]{1,0:T(8,128)(2,1)}, bf16[1040,128]{1,0:T(8,128)(2,1)S(1)}, u32[]{:S(2)}, u32[]{:S(2)}) collective-permute-start(bf16[1040,128]{1,0:T(8,128)(2,1)} %get-tuple-element.34), channel_id=1, source_target_pairs={{0,2},{2,0},{4,6},{6,4},{8,10},{10,8},{12,14},{14,12},{16,18},{18,... | collective-permute-start | bytes 798728 | tf_op jit(solution)/shard_map/ppermute | solution.py:544
  16.6 0.9 %copy-start = (bf16[1024,128]{1,0:T(8,128)(2,1)}, bf16[1024,128]{1,0:T(8,128)(2,1)S(1)}, u32[]{:S(2)}) copy-start(bf16[1024,128]{1,0:T(8,128)(2,1)S(1)} %get-tuple-element.53) | copy-start | bytes 786436
  17.6 8.6 %collective-permute-start.2 = (bf16[1040,128]{1,0:T(8,128)(2,1)S(1)}, bf16[1040,128]{1,0:T(8,128)(2,1)S(1)}, u32[]{:S(2)}, u32[]{:S(2)}) collective-permute-start(bf16[1040,128]{1,0:T(8,128)(2,1)S(1)} %pad_maximum_fusion), channel_id=1, source_target_pairs={{0,4},{2,6},{4,0},{6,2},{8,12},{10,14},{12,8},{14,10},{16,20},{18,... | collective-permute-start | bytes 798728 | tf_op jit(solution)/shard_map/ppermute | solution.py:544
  19.2 5.0 %copy-start.1 = (bf16[1024,128]{1,0:T(8,128)(2,1)S(1)}, bf16[1024,128]{1,0:T(8,128)(2,1)}, u32[]{:S(2)}) copy-start(bf16[1024,128]{1,0:T(8,128)(2,1)} %copy-done) | copy-start | bytes 786436
  24.2 8.2 %collective-permute-start.5 = (bf16[1024,128]{1,0:T(8,128)(2,1)S(1)}, bf16[1024,128]{1,0:T(8,128)(2,1)S(1)}, u32[]{:S(2)}, u32[]{:S(2)}) collective-permute-start(bf16[1024,128]{1,0:T(8,128)(2,1)S(1)} %copy-done.1), channel_id=1, source_target_pairs={{0,2},{2,0},{4,6},{6,4},{8,10},{10,8},{12,14},{14,12},{16,18},{18,... | collective-permute-start | bytes 786440 | tf_op jit(solution)/shard_map/ppermute | solution.py:544
  26.4 15.3 %collective-permute-start.3 = (bf16[1040,128]{1,0:T(8,128)(2,1)S(1)}, bf16[1040,128]{1,0:T(8,128)(2,1)S(1)}, u32[]{:S(2)}, u32[]{:S(2)}) collective-permute-start(bf16[1040,128]{1,0:T(8,128)(2,1)S(1)} %pad_maximum_fusion.1), channel_id=1, source_target_pairs={{0,8},{2,10},{4,12},{6,14},{8,0},{10,2},{12,4},{14,6},{16,24},{18,... | collective-permute-start | bytes 798728 | tf_op jit(solution)/shard_map/ppermute | solution.py:544
  32.5 7.4 %collective-permute-start.6 = (bf16[1024,128]{1,0:T(8,128)(2,1)S(1)}, bf16[1024,128]{1,0:T(8,128)(2,1)S(1)}, u32[]{:S(2)}, u32[]{:S(2)}) collective-permute-start(bf16[1024,128]{1,0:T(8,128)(2,1)S(1)} %fusion.9), channel_id=1, source_target_pairs={{0,4},{2,6},{4,0},{6,2},{8,12},{10,14},{12,8},{14,10},{16,20},{18,... | collective-permute-start | bytes 786440 | tf_op jit(solution)/shard_map/ppermute | solution.py:544
  40.0 6.6 %collective-permute-start.7 = (bf16[1024,128]{1,0:T(8,128)(2,1)S(1)}, bf16[1024,128]{1,0:T(8,128)(2,1)S(1)}, u32[]{:S(2)}, u32[]{:S(2)}) collective-permute-start(bf16[1024,128]{1,0:T(8,128)(2,1)S(1)} %fusion.10), channel_id=1, source_target_pairs={{0,8},{2,10},{4,12},{6,14},{8,0},{10,2},{12,4},{14,6},{16,24},{18,... | collective-permute-start | bytes 786440 | tf_op jit(solution)/shard_map/ppermute | solution.py:544
  41.9 11.6 %collective-permute-start.4 = (bf16[1024,128]{1,0:T(8,128)(2,1)S(1)}, bf16[1024,128]{1,0:T(8,128)(2,1)S(1)}, u32[]{:S(2)}, u32[]{:S(2)}) collective-permute-start(bf16[1024,128]{1,0:T(8,128)(2,1)S(1)} %fusion.5), channel_id=1, source_target_pairs={{0,16},{2,18},{4,20},{6,22},{8,24},{10,26},{12,28},{14,30},{1,17},... | collective-permute-start | bytes 786440 | tf_op jit(solution)/shard_map/ppermute | solution.py:544
  46.9 14.0 %collective-permute-start.9 = (bf16[1024,128]{1,0:T(8,128)(2,1)S(1)}, bf16[1024,128]{1,0:T(8,128)(2,1)S(1)}, u32[]{:S(2)}, u32[]{:S(2)}) collective-permute-start(bf16[1024,128]{1,0:T(8,128)(2,1)S(1)} %fusion.1), channel_id=1, source_target_pairs={{16,0},{18,2},{20,4},{22,6},{24,8},{26,10},{28,12},{30,14},{17,1},... | collective-permute-start | bytes 786440 | tf_op jit(solution)/shard_map/ppermute | solution.py:544
  59.4 5.7 %collective-permute-start.8 = (bf16[512,2048]{1,0:T(8,128)(2,1)}, bf16[512,2048]{1,0:T(8,128)(2,1)S(1)}, u32[]{:S(2)}, u32[]{:S(2)}) collective-permute-start(bf16[512,2048]{1,0:T(8,128)(2,1)} %get-tuple-element.58), channel_id=1, source_target_pairs={{0,1},{1,0},{2,3},{3,2},{4,5},{5,4},{6,7},{7,6},{8,9},{9,8},{10,11... | collective-permute-start | bytes 6291464 | tf_op jit(solution)/shard_map/ppermute | solution.py:619

commit v7 on v6

--- a/solution.py
+++ b/solution.py
@@ -26,7 +26,7 @@
     return lax.dot_general(a, b, dims, preferred_element_type=F32)
 
 
-def kernel_call(kernel, args, specs, outs, out_specs, scratch, mib, name, flops=1):
+def kernel_call(kernel, args, specs, outs, out_specs, scratch, mib, name, micros):
     pinned = [pltpu.with_memory_space_constraint(a, pltpu.HBM) if s is HB else a for a, s in zip(args, specs)]
     placed = tuple(
         (pltpu.HBM if s is HB else jax.ShapeDtypeStruct)(shape, dtype) for (shape, dtype), s in zip(outs, out_specs)
@@ -38,7 +38,7 @@
         out_shape=placed,
         scratch_shapes=scratch,
         compiler_params=pltpu.CompilerParams(vmem_limit_bytes=mib * MIB),
-        cost_estimate=pl.CostEstimate(flops=flops, bytes_accessed=1, transcendentals=0),
+        cost_estimate=pl.CostEstimate(flops=int(micros * 1e9), bytes_accessed=1, transcendentals=0),
         name=name,
     )(*pinned)
 
@@ -152,6 +152,7 @@
         ],
         12,
         "prepare",
+        4,
     )
 
 
@@ -222,6 +223,7 @@
         ],
         28,
         "project",
+        8,
     )
 
 
@@ -284,6 +286,7 @@
         ],
         24,
         "inner",
+        2,
     )
 
 
@@ -364,6 +367,7 @@
         ],
         20,
         "query_term",
+        6,
     )
 
 
@@ -393,6 +397,7 @@
         ],
         16,
         "term",
+        4,
     )[0]
 
 
@@ -442,6 +447,7 @@
         ],
         24,
         "finish",
+        6,
     )[0]
 
 
@@ -507,7 +513,7 @@
         ],
         20,
         "close",
-        flops=10**11,
+        100,
     )
 
 
@@ -577,8 +583,6 @@
 
     barrier = lax.optimization_barrier
     for stage in range(stages):
-        if stage == stages - 1:
-            msg, query = barrier((msg, query))
         arrived = send(msg if stage < stages - 1 else msg[:width], stage, True)
         if stage == 0:
             arrived, query, adjoint, amsg = barrier((arrived, query, adjoint, amsg))
@@ -592,6 +596,7 @@
         if stage < stages - 1:
             msg, state = fold_state(stage, state)
         if stage >= 1:
+            agot[-1], _ = barrier((agot[-1], msg))
             amsg, adjoint = fold_adjoint(stage - 1, adjoint)
     while pending:
         inner_parts.append(next_inner())

time: 71.2 us -> 73.4 us (1.031)
  waiting for transfers between devices: 14.1 us -> 17.7 us
  other arithmetic: 2.13 us -> 1.23 us
    ppermute x8, waiting for transfers between devices: 14.1 us -> 17.7 us  [send(): return lax.ppermute(array, 'ctx', pairs)]
    select_n x1, other arithmetic: 0.8 us -> 0.01 us  [body(): state_coefs = [jnp.where(u, f, 0.0)[:heads] for u, f in zip(uppers, before)]]
  transfers between devices with their start and end apart: 10 -> 10, of which waited for: 5 -> 3; matrix products, arithmetic and copies ran while one was open for 2% -> 2% of each run, Pallas kernels for 46% -> 44%
where the time goes in v7:
time: 73.4 us; the launch traced here: 73.1 us
  Pallas kernels  38 us (52%)
  waiting for transfers between devices  17.7 us (24%)
  starting transfers between devices  15.2 us (21%)
  other arithmetic  1.23 us (2%)
  between operations  0.98 us (1%)
    pallas_call x7, Pallas kernels, kernel_call(): pl.pallas_call(kernel, in_specs=specs, out_specs=tuple(out_specs), out_sh...  38 us
    ppermute x8, waiting for transfers between devices, send(): return lax.ppermute(array, 'ctx', pairs)  17.7 us
    ppermute x8, starting transfers between devices, send(): return lax.ppermute(array, 'ctx', pairs)  14.7 us
  transfers between devices with their start and end apart: 10, of which 3 were waited for; matrix products, arithmetic and copies ran while one was open for 2% of the time, Pallas kernels for 44%

profile of v7, /device:TPU:0, one launch (start us, length us, event | category | flops | bytes accessed | tf_op | source)
XLA Modules:
  0.0 73.1 jit_solution(16736429778648222307)
XLA Ops:
  0.6 0.5 collective-permute-start.1
  1.1 3.7 %prepare.1 = (f32[32,512]{1,0:T(8,128)}, bf16[1040,128]{1,0:T(8,128)(2,1)S(1)}, f32[1024,128]{1,0:T(8,128)S(1)}) custom-call(f32[8,512]{1,0:T(8,128)} %bitcast.104, bf16[512,1024]{1,0:T(8,128)(2,1)} %refs_5_.3, bf16[512,1024]{1,0:T(8,128)(2,1)} %refs_6_.1), custom_call_target="tpu_custom_call" | custom-call | flops 4000000000 | bytes 1 | tf_op jit(solution)/shard_map/prepare/pallas_call | solution.py:34
  4.8 2.6 %collective-permute-start = (bf16[1040,128]{1,0:T(8,128)(2,1)S(1)}, bf16[1040,128]{1,0:T(8,128)(2,1)S(1)}, u32[]{:S(2)}, u32[]{:S(2)}) collective-permute-start(bf16[1040,128]{1,0:T(8,128)(2,1)S(1)} %get-tuple-element.35), channel_id=1, source_target_pairs={{0,2},{2,0},{4,6},{6,4},{8,10},{10,8},{12,14},{14,12},{16,18},{18,... | collective-permute-start | bytes 798728 | tf_op jit(solution)/shard_map/ppermute | solution.py:550
  7.4 0.1 pad_add_fusion.place_ref
  7.5 0.0 collective-permute-done.1.refs_1_
  7.5 8.5 %project.1 = (bf16[512,1024]{1,0:T(8,128)(2,1)}, f32[1024,128]{1,0:T(8,128)S(1)}, bf16[1024,128]{1,0:T(8,128)(2,1)S(1)}) custom-call(s32[2]{0:T(128)S(1)} %pad_add_fusion.place_ref, bf16[512,2048]{1,0:T(8,128)(2,1)} %refs_0_.1, bf16[512,2048]{1,0:T(8,128)(2,1)} %collective-permute-done.1.refs_1_, bf16[4096,1024]{1,0:T(8,128)(2,1)} %refs_1_.5, ...), custom_call_target="tpu_custom_call" | custom-call | flops 8000000000 | bytes 1 | tf_op jit(solution)/shard_map/project/pallas_call | solution.py:34
  15.9 0.0 collective-permute-done.refs_0_
  16.0 0.1 fusion.8
  16.1 1.6 %collective-permute-start.2 = (bf16[1040,128]{1,0:T(8,128)(2,1)S(1)}, bf16[1040,128]{1,0:T(8,128)(2,1)S(1)}, u32[]{:S(2)}, u32[]{:S(2)}) collective-permute-start(bf16[1040,128]{1,0:T(8,128)(2,1)S(1)} %pad_maximum_fusion), channel_id=1, source_target_pairs={{0,4},{2,6},{4,0},{6,2},{8,12},{10,14},{12,8},{14,10},{16,20},{18,... | collective-permute-start | bytes 798728 | tf_op jit(solution)/shard_map/ppermute | solution.py:550
  17.7 0.7 collective-permute-start.5
  18.4 4.9 %inner.2 = (bf16[512,512]{1,0:T(8,128)(2,1)}, bf16[512,512]{1,0:T(8,128)(2,1)}, bf16[512,512]{1,0:T(8,128)(2,1)}) custom-call(bf16[512,1024]{1,0:T(8,128)(2,1)} %get-tuple-element.42.refs_0_, bf16[512,1024]{1,0:T(8,128)(2,1)} %refs_5_.3, bf16[512,1024]{1,0:T(8,128)(2,1)} %refs_6_.1, bf16[512,1024]{1,0:T(8,128)(2,1)} %refs_5_.2, ...), custom_call_target="tpu_custom_call" | custom-call | flops 2000000000 | bytes 1 | tf_op jit(solution)/shard_map/inner/pallas_call | solution.py:34
  23.3 1.4 %collective-permute-done.2.refs_1_ = bf16[1040,128]{1,0:T(8,128)(2,1)S(1)} collective-permute-done((bf16[1040,128]{1,0:T(8,128)(2,1)S(1)}, bf16[1040,128]{1,0:T(8,128)(2,1)S(1)}, u32[]{:S(2)}, u32[]{:S(2)}) %collective-permute-start.2) | collective-permute-done | bytes 266272 | tf_op jit(solution)/shard_map/ppermute | solution.py:550
  24.7 0.2 fusion.11
  24.9 1.6 %collective-permute-start.3 = (bf16[1040,128]{1,0:T(8,128)(2,1)S(1)}, bf16[1040,128]{1,0:T(8,128)(2,1)S(1)}, u32[]{:S(2)}, u32[]{:S(2)}) collective-permute-start(bf16[1040,128]{1,0:T(8,128)(2,1)S(1)} %pad_maximum_fusion.1), channel_id=1, source_target_pairs={{0,8},{2,10},{4,12},{6,14},{8,0},{10,2},{12,4},{14,6},{16,24},{18,... | collective-permute-start | bytes 798728 | tf_op jit(solution)/shard_map/ppermute | solution.py:550
  26.6 0.0 collective-permute-done.5.refs_0_
  26.6 0.1 fusion.9
  26.7 1.6 %collective-permute-start.6 = (bf16[1024,128]{1,0:T(8,128)(2,1)S(1)}, bf16[1024,128]{1,0:T(8,128)(2,1)S(1)}, u32[]{:S(2)}, u32[]{:S(2)}) collective-permute-start(bf16[1024,128]{1,0:T(8,128)(2,1)S(1)} %fusion.9), channel_id=1, source_target_pairs={{0,4},{2,6},{4,0},{6,2},{8,12},{10,14},{12,8},{14,10},{16,20},{18,... | collective-permute-start | bytes 786440 | tf_op jit(solution)/shard_map/ppermute | solution.py:550
  28.3 5.2 %inner.3 = (bf16[512,512]{1,0:T(8,128)(2,1)}, bf16[512,512]{1,0:T(8,128)(2,1)}, bf16[512,512]{1,0:T(8,128)(2,1)}) custom-call(bf16[512,1024]{1,0:T(8,128)(2,1)} %get-tuple-element.42.refs_0_, bf16[512,1024]{1,0:T(8,128)(2,1)} %refs_5_.3, bf16[512,1024]{1,0:T(8,128)(2,1)} %refs_6_.1, bf16[512,1024]{1,0:T(8,128)(2,1)} %refs_5_.2, ...), custom_call_target="tpu_custom_call" | custom-call | flops 2000000000 | bytes 1 | tf_op jit(solution)/shard_map/inner/pallas_call | solution.py:34
  33.5 0.2 fusion.5
  33.7 4.5 %collective-permute-start.4 = (bf16[1024,128]{1,0:T(8,128)(2,1)S(1)}, bf16[1024,128]{1,0:T(8,128)(2,1)S(1)}, u32[]{:S(2)}, u32[]{:S(2)}) collective-permute-start(bf16[1024,128]{1,0:T(8,128)(2,1)S(1)} %fusion.5), channel_id=1, source_target_pairs={{0,16},{2,18},{4,20},{6,22},{8,24},{10,26},{12,28},{14,30},{1,17},... | collective-permute-start | bytes 786440 | tf_op jit(solution)/shard_map/ppermute | solution.py:550
  38.2 0.0 collective-permute-done.6.refs_1_
  38.2 0.2 fusion.10
  38.4 0.8 %collective-permute-start.7 = (bf16[1024,128]{1,0:T(8,128)(2,1)S(1)}, bf16[1024,128]{1,0:T(8,128)(2,1)S(1)}, u32[]{:S(2)}, u32[]{:S(2)}) collective-permute-start(bf16[1024,128]{1,0:T(8,128)(2,1)S(1)} %fusion.10), channel_id=1, source_target_pairs={{0,8},{2,10},{4,12},{6,14},{8,0},{10,2},{12,4},{14,6},{16,24},{18,... | collective-permute-start | bytes 786440 | tf_op jit(solution)/shard_map/ppermute | solution.py:550
  39.2 0.1 pad_maximum_fusion.2
  39.3 9.1 %collective-permute-done.7.refs_2_ = bf16[1024,128]{1,0:T(8,128)(2,1)S(1)} collective-permute-done((bf16[1024,128]{1,0:T(8,128)(2,1)S(1)}, bf16[1024,128]{1,0:T(8,128)(2,1)S(1)}, u32[]{:S(2)}, u32[]{:S(2)}) %collective-permute-start.7) | collective-permute-done | bytes 262176 | tf_op jit(solution)/shard_map/ppermute | solution.py:550
  48.4 0.2 fusion.1
  48.6 1.3 %collective-permute-start.9 = (bf16[1024,128]{1,0:T(8,128)(2,1)S(1)}, bf16[1024,128]{1,0:T(8,128)(2,1)S(1)}, u32[]{:S(2)}, u32[]{:S(2)}) collective-permute-start(bf16[1024,128]{1,0:T(8,128)(2,1)S(1)} %fusion.1), channel_id=1, source_target_pairs={{16,0},{18,2},{20,4},{22,6},{24,8},{26,10},{28,12},{30,14},{17,1},... | collective-permute-start | bytes 786440 | tf_op jit(solution)/shard_map/ppermute | solution.py:550
  49.9 5.9 %query_term.1 = (bf16[512,1024]{1,0:T(8,128)(2,1)}, bf16[512,2048]{1,0:T(8,128)(2,1)}) custom-call(s32[1]{0:T(128)} %bitcast.1.place_ref, bf16[1040,128]{1,0:T(8,128)(2,1)S(1)} %collective-permute-done.refs_0_, bf16[1040,128]{1,0:T(8,128)(2,1)S(1)} %collective-permute-done.2.refs_1_, bf16[1040,128]{1,0:T(8,128)(2,1)S(1)} %collective-permute-done.3.refs_2_, ...), custom_call_target="tpu_custom_call" | custom-call | flops 6000000000 | bytes 1 | tf_op jit(solution)/shard_map/query_term/pallas_call | solution.py:34
  55.9 0.1 collective-permute-start.8
  56.0 7.2 %collective-permute-done.9.refs_3_ = bf16[1024,128]{1,0:T(8,128)(2,1)S(1)} collective-permute-done((bf16[1024,128]{1,0:T(8,128)(2,1)S(1)}, bf16[1024,128]{1,0:T(8,128)(2,1)S(1)}, u32[]{:S(2)}, u32[]{:S(2)}) %collective-permute-start.9) | collective-permute-done | bytes 262176 | tf_op jit(solution)/shard_map/ppermute | solution.py:550
  63.2 4.2 %close.1 = (bf16[512,1024]{1,0:T(8,128)(2,1)}, bf16[512,1024]{1,0:T(8,128)(2,1)}) custom-call(bf16[1024,128]{1,0:T(8,128)(2,1)S(1)} %collective-permute-done.5.refs_0_, bf16[1024,128]{1,0:T(8,128)(2,1)S(1)} %collective-permute-done.6.refs_1_, bf16[1024,128]{1,0:T(8,128)(2,1)S(1)} %collective-permute-done.7.refs_2_, ...), custom_call_target="tpu_custom_call" | custom-call | flops 99999997952 | bytes 1 | tf_op jit(solution)/shard_map/close/pallas_call | solution.py:34
  67.4 5.5 %finish.1 = bf16[512,2048]{1,0:T(8,128)(2,1)} custom-call(s32[1]{0:T(128)} %bitcast.place_ref, bf16[512,1024]{1,0:T(8,128)(2,1)} %get-tuple-element.59.refs_0_, bf16[4096,1024]{1,0:T(8,128)(2,1)} %refs_1_.5, bf16[512,2048]{1,0:T(8,128)(2,1)S(1)} %collective-permute-done.8.refs_2_), custom_call_target="tpu_custom_call" | custom-call | flops 6000000000 | bytes 1 | tf_op jit(solution)/shard_map/finish/pallas_call | solution.py:34
  (15 shorter events, 0.1 us)
Async XLA Ops:
  0.6 6.8 %collective-permute-start.1 = (bf16[512,2048]{1,0:T(8,128)(2,1)}, bf16[512,2048]{1,0:T(8,128)(2,1)}, u32[]{:S(2)}, u32[]{:S(2)}) collective-permute-start(bf16[512,2048]{1,0:T(8,128)(2,1)} %refs_0_.1), channel_id=1, source_target_pairs={{0,1},{1,0},{2,3},{3,2},{4,5},{5,4},{6,7},{7,6},{8,9},{9,8},{10,11... | collective-permute-start | bytes 6291464 | tf_op jit(solution)/shard_map/ppermute | solution.py:532
  4.8 11.1 %collective-permute-start = (bf16[1040,128]{1,0:T(8,128)(2,1)S(1)}, bf16[1040,128]{1,0:T(8,128)(2,1)S(1)}, u32[]{:S(2)}, u32[]{:S(2)}) collective-permute-start(bf16[1040,128]{1,0:T(8,128)(2,1)S(1)} %get-tuple-element.35), channel_id=1, source_target_pairs={{0,2},{2,0},{4,6},{6,4},{8,10},{10,8},{12,14},{14,12},{16,18},{18,... | collective-permute-start | bytes 798728 | tf_op jit(solution)/shard_map/ppermute | solution.py:550
  16.1 8.6 %collective-permute-start.2 = (bf16[1040,128]{1,0:T(8,128)(2,1)S(1)}, bf16[1040,128]{1,0:T(8,128)(2,1)S(1)}, u32[]{:S(2)}, u32[]{:S(2)}) collective-permute-start(bf16[1040,128]{1,0:T(8,128)(2,1)S(1)} %pad_maximum_fusion), channel_id=1, source_target_pairs={{0,4},{2,6},{4,0},{6,2},{8,12},{10,14},{12,8},{14,10},{16,20},{18,... | collective-permute-start | bytes 798728 | tf_op jit(solution)/shard_map/ppermute | solution.py:550
  17.7 8.9 %collective-permute-start.5 = (bf16[1024,128]{1,0:T(8,128)(2,1)S(1)}, bf16[1024,128]{1,0:T(8,128)(2,1)S(1)}, u32[]{:S(2)}, u32[]{:S(2)}) collective-permute-start(bf16[1024,128]{1,0:T(8,128)(2,1)S(1)} %get-tuple-element.52), channel_id=1, source_target_pairs={{0,2},{2,0},{4,6},{6,4},{8,10},{10,8},{12,14},{14,12},{16,18},{18,... | collective-permute-start | bytes 786440 | tf_op jit(solution)/shard_map/ppermute | solution.py:550
  24.9 8.5 %collective-permute-start.3 = (bf16[1040,128]{1,0:T(8,128)(2,1)S(1)}, bf16[1040,128]{1,0:T(8,128)(2,1)S(1)}, u32[]{:S(2)}, u32[]{:S(2)}) collective-permute-start(bf16[1040,128]{1,0:T(8,128)(2,1)S(1)} %pad_maximum_fusion.1), channel_id=1, source_target_pairs={{0,8},{2,10},{4,12},{6,14},{8,0},{10,2},{12,4},{14,6},{16,24},{18,... | collective-permute-start | bytes 798728 | tf_op jit(solution)/shard_map/ppermute | solution.py:550
  26.7 11.6 %collective-permute-start.6 = (bf16[1024,128]{1,0:T(8,128)(2,1)S(1)}, bf16[1024,128]{1,0:T(8,128)(2,1)S(1)}, u32[]{:S(2)}, u32[]{:S(2)}) collective-permute-start(bf16[1024,128]{1,0:T(8,128)(2,1)S(1)} %fusion.9), channel_id=1, source_target_pairs={{0,4},{2,6},{4,0},{6,2},{8,12},{10,14},{12,8},{14,10},{16,20},{18,... | collective-permute-start | bytes 786440 | tf_op jit(solution)/shard_map/ppermute | solution.py:550
  33.7 16.2 %collective-permute-start.4 = (bf16[1024,128]{1,0:T(8,128)(2,1)S(1)}, bf16[1024,128]{1,0:T(8,128)(2,1)S(1)}, u32[]{:S(2)}, u32[]{:S(2)}) collective-permute-start(bf16[1024,128]{1,0:T(8,128)(2,1)S(1)} %fusion.5), channel_id=1, source_target_pairs={{0,16},{2,18},{4,20},{6,22},{8,24},{10,26},{12,28},{14,30},{1,17},... | collective-permute-start | bytes 786440 | tf_op jit(solution)/shard_map/ppermute | solution.py:550
  38.4 10.0 %collective-permute-start.7 = (bf16[1024,128]{1,0:T(8,128)(2,1)S(1)}, bf16[1024,128]{1,0:T(8,128)(2,1)S(1)}, u32[]{:S(2)}, u32[]{:S(2)}) collective-permute-start(bf16[1024,128]{1,0:T(8,128)(2,1)S(1)} %fusion.10), channel_id=1, source_target_pairs={{0,8},{2,10},{4,12},{6,14},{8,0},{10,2},{12,4},{14,6},{16,24},{18,... | collective-permute-start | bytes 786440 | tf_op jit(solution)/shard_map/ppermute | solution.py:550
  48.6 14.6 %collective-permute-start.9 = (bf16[1024,128]{1,0:T(8,128)(2,1)S(1)}, bf16[1024,128]{1,0:T(8,128)(2,1)S(1)}, u32[]{:S(2)}, u32[]{:S(2)}) collective-permute-start(bf16[1024,128]{1,0:T(8,128)(2,1)S(1)} %fusion.1), channel_id=1, source_target_pairs={{16,0},{18,2},{20,4},{22,6},{24,8},{26,10},{28,12},{30,14},{17,1},... | collective-permute-start | bytes 786440 | tf_op jit(solution)/shard_map/ppermute | solution.py:550
  55.9 11.6 %collective-permute-start.8 = (bf16[512,2048]{1,0:T(8,128)(2,1)}, bf16[512,2048]{1,0:T(8,128)(2,1)S(1)}, u32[]{:S(2)}, u32[]{:S(2)}) collective-permute-start(bf16[512,2048]{1,0:T(8,128)(2,1)} %get-tuple-element.60), channel_id=1, source_target_pairs={{0,1},{1,0},{2,3},{3,2},{4,5},{5,4},{6,7},{7,6},{8,9},{9,8},{10,11... | collective-permute-start | bytes 6291464 | tf_op jit(solution)/shard_map/ppermute | solution.py:624

commit v8 on v7

--- a/solution.py
+++ b/solution.py
@@ -86,7 +86,17 @@
     return jnp.concatenate([facts, spare], axis=0).T
 
 
-def prepare_kernel(heads, hp, scaling, ld_hbm, k_hbm, v_hbm, facts_hbm, msg_ref, state_ref, ld, facts_ref, kbuf, vbuf, sems):
+def put_halves(upper, h, local, kept_ref, sent_ref):
+    half = HDIM // 2
+    at = slice(h * half, (h + 1) * half)
+    kept_ref[at, :] = jnp.where(upper, local[half:], local[:half]).astype(BF16)
+    sent_ref[at, :] = jnp.where(upper, local[:half], local[half:]).astype(BF16)
+
+
+def prepare_kernel(
+    heads, hp, scaling, ld_hbm, k_hbm, v_hbm, facts_hbm, kept_ref, sent_ref, share_ref, ld, facts_ref, kbuf, vbuf, sems
+):
+    upper = lax.axis_index("ctx") % 2 == 1
     rows = kbuf.shape[0]
     copies = Copies(sems)
     ld_in = copies.start(ld_hbm, ld)
@@ -115,8 +125,9 @@
     share = jnp.broadcast_to(jnp.exp(total), (hp, LANES))
     high = share.astype(BF16)
     low = (share - high.astype(F32)).astype(BF16)
-    base = heads * HDIM
-    msg_ref[base:, :] = jnp.concatenate([high.astype(F32), low.astype(F32)], axis=0).astype(BF16)
+    share_ref[...] = share
+    base = heads * HDIM // 2
+    sent_ref[base:, :] = jnp.concatenate([high.astype(F32), low.astype(F32)], axis=0).astype(BF16)
     for (first, last, _), load in zip(groups(heads), loads):
         for copy in load:
             copy.wait()
@@ -124,9 +135,7 @@
             cols = slice(h * HDIM, (h + 1) * HDIM)
             scaled = scaled_keys(table, hp, h, kbuf[:, cols])
             decayed = (column(table, 2 * hp + h) * scaled.astype(F32)).astype(BF16)
-            local = dot(decayed, vbuf[:, cols], TN)
-            state_ref[cols, :] = local
-            msg_ref[cols, :] = local.astype(BF16)
+            put_halves(upper, h, dot(decayed, vbuf[:, cols], TN), kept_ref, sent_ref)
     copies.finish()
 
 
@@ -141,8 +150,8 @@
         functools.partial(prepare_kernel, heads, hp, scaling),
         (logs, keys, values),
         [HB] * 3,
-        [((4 * hp, rows), F32), ((width + 2 * hp, HDIM), BF16), ((width, HDIM), F32)],
-        (HB, VM, VM),
+        [((4 * hp, rows), F32), ((width // 2, HDIM), BF16), ((width // 2 + 2 * hp, HDIM), BF16), ((hp, LANES), F32)],
+        (HB, VM, VM, VM),
         [
             pltpu.VMEM((heads, rows), F32),
             pltpu.VMEM((4 * hp, rows), F32),
@@ -157,11 +166,12 @@
 
 
 def project_kernel(hp, nparts, chunk, place_ref, *refs):
-    parts, (w_hbm, do_hbm, facts_hbm, q_hbm, adj_ref, msg_ref) = refs[:nparts], refs[nparts : nparts + 6]
+    parts, (w_hbm, do_hbm, facts_hbm, q_hbm, kept_ref, sent_ref) = refs[:nparts], refs[nparts : nparts + 6]
     hbuf, wbuf, dobuf, facts_ref, qbuf, total, sems = refs[nparts + 6 :]
     rows, feat = parts[0].shape
     width = wbuf.shape[1]
     heads = width // HDIM
+    upper = lax.axis_index("ctx") % 2 == 1
     copies = Copies(sems)
     loads = []
     for part, ref in enumerate(parts):
@@ -196,9 +206,7 @@
     for h in range(heads):
         cols = slice(h * HDIM, (h + 1) * HDIM)
         decayed = (column(table, 3 * hp + h) * qbuf[:, cols].astype(F32)).astype(BF16)
-        local = dot(decayed, dobuf[:, cols], TN)
-        adj_ref[cols, :] = local
-        msg_ref[cols, :] = local.astype(BF16)
+        put_halves(upper, h, dot(decayed, dobuf[:, cols], TN), kept_ref, sent_ref)
     copies.finish()
 
 
@@ -210,7 +218,7 @@
         functools.partial(project_kernel, hp, len(parts), chunk),
         (owners, *parts, w_query, d_out, facts),
         [SM, HB] + [AN] * (len(parts) - 1) + [HB] * 3,
-        [((rows, width), BF16), ((width, HDIM), F32), ((width, HDIM), BF16)],
+        [((rows, width), BF16), ((width // 2, HDIM), BF16), ((width // 2, HDIM), BF16)],
         (HB, VM, VM),
         [
             pltpu.VMEM((rows, depth), BF16),
@@ -286,18 +294,15 @@
         ],
         24,
         "inner",
-        2,
+        3,
     )
 
 
-def mix(coef_ref, pieces, heads, h):
-    cols = slice(h * HDIM, (h + 1) * HDIM)
-    total = None
-    for stage, piece in enumerate(pieces):
-        row = stage * heads + h
-        term = coef_ref[row : row + 1, :] * piece[cols, :].astype(F32)
-        total = term if total is None else total + term
-    return total.astype(BF16)
+def whole_head(upper, h, mine_ref, theirs_ref):
+    half = HDIM // 2
+    at = slice(h * half, (h + 1) * half)
+    mine, theirs = mine_ref[at, :], theirs_ref[at, :]
+    return jnp.concatenate([jnp.where(upper, theirs, mine), jnp.where(upper, mine, theirs)], axis=0)
 
 
 def load_weight(copies, place_ref, first, w_hbm, wbuf, feat, block):
@@ -308,11 +313,11 @@
     return loads
 
 
-def query_kernel(heads, hp, stages, feat, block, place_ref, *refs):
-    pieces = refs[:stages]
-    coef_ref, do_hbm, facts_hbm, w_hbm = refs[stages : stages + 4]
-    inner_hbm = refs[stages + 4 : -9]
+def query_kernel(heads, hp, feat, block, place_ref, *refs):
+    mine_ref, theirs_ref, do_hbm, facts_hbm, w_hbm = refs[:5]
+    inner_hbm = refs[5:-9]
     dq_hbm, out_hbm, dobuf, facts_ref, wbuf, local, held, sent, sems = refs[-9:]
+    upper = lax.axis_index("ctx") % 2 == 1
     copies = Copies(sems)
     each = heads // len(inner_hbm)
     facts_in = copies.start(facts_hbm, facts_ref)
@@ -330,7 +335,7 @@
             for copy in loads[h // each]:
                 copy.wait()
         cols = slice(h * HDIM, (h + 1) * HDIM)
-        state = mix(coef_ref, pieces, heads, h)
+        state = whole_head(upper, h, mine_ref, theirs_ref)
         carry = dot(dobuf[:, cols], state, NT)
         held[:, cols] = (local[:, cols].astype(F32) + column(table, 3 * hp + h) * carry).astype(BF16)
     copies.store(held, dq_hbm)
@@ -346,14 +351,14 @@
         copies.store(sent.at[:, wide], out_hbm.at[:, wide])
 
 
-def query_term(pieces, coefs, inner_dq, d_out, facts, w_query, place, feat, count, heads, hp):
+def query_term(halves, inner_dq, d_out, facts, w_query, place, feat, count, heads, hp):
     rows, width = d_out.shape
     block = min(512, count)
-    args = (coefs, d_out, facts, w_query, *inner_dq)
+    args = (d_out, facts, w_query, *inner_dq)
     return kernel_call(
-        functools.partial(query_kernel, heads, hp, len(pieces), feat, block),
-        (place, *pieces, *args),
-        [SM] + [VM] * (len(pieces) + 1) + [HB] * (len(args) - 1),
+        functools.partial(query_kernel, heads, hp, feat, block),
+        (place, *halves, *args),
+        [SM, VM, VM] + [HB] * len(args),
         [((rows, width), BF16), ((rows, count), BF16)],
         (HB, HB),
         [
@@ -451,10 +456,10 @@
     )[0]
 
 
-def close_kernel(heads, hp, stages, *refs):
-    pieces = refs[:stages]
-    coef_ref, in_hbm, v_hbm, facts_hbm = refs[stages : stages + 4]
-    rest = refs[stages + 4 : -10]
+def close_kernel(heads, hp, *refs):
+    mine_ref, theirs_ref, in_hbm, v_hbm, facts_hbm = refs[:5]
+    rest = refs[5:-10]
+    upper = lax.axis_index("ctx") % 2 == 1
     dk_hbm, dv_hbm, kbuf, vbuf, facts_ref, dkbuf, dvbuf, kside, vside, sems = refs[-10:]
     dks, dvs = rest[: len(rest) // 2], rest[len(rest) // 2 :]
     each = heads // len(dks)
@@ -478,7 +483,7 @@
             for copy in loads[h // each]:
                 copy.wait()
         cols = slice(h * HDIM, (h + 1) * HDIM)
-        adjoint = mix(coef_ref, pieces, heads, h)
+        adjoint = whole_head(upper, h, mine_ref, theirs_ref)
         tail, gain = column(table, 2 * hp + h), column(table, hp + h)
         carry_k = dot(vbuf[:, cols], adjoint, NT)
         kside[:, cols] = (gain * (dkbuf[:, cols].astype(F32) + tail * carry_k)).astype(BF16)
@@ -491,14 +496,14 @@
     copies.finish()
 
 
-def close(pieces, coefs, dks, dvs, keys, values, facts, heads, hp):
+def close(halves, dks, dvs, keys, values, facts, heads, hp):
     rows, width = values.shape
-    args = (coefs, keys, values, facts, *dks, *dvs)
+    args = (keys, values, facts, *dks, *dvs)
     buf = pltpu.VMEM((rows, width), BF16)
     return kernel_call(
-        functools.partial(close_kernel, heads, hp, len(pieces)),
-        (*pieces, *args),
-        [VM] * (len(pieces) + 1) + [HB] * (len(args) - 1),
+        functools.partial(close_kernel, heads, hp),
+        (*halves, *args),
+        [VM, VM] + [HB] * len(args),
         [((rows, width), BF16)] * 2,
         (HB,) * 2,
         [
@@ -532,81 +537,104 @@
         parts.append(lax.ppermute(hidden, "head", ring))
     owners = jnp.stack([(mine + head_size - s) % head_size for s in range(head_size)]).astype(jnp.int32)
 
-    facts, msg, state = prepare(log_decay.T, keys, values, heads, hp, scaling)
-    query, adjoint, amsg = project(parts, owners, w_query, d_out, facts, hp)
-
+    facts, kept, sent, share = prepare(log_decay.T, keys, values, heads, hp, scaling)
+    query, akept, asent = project(parts, owners, w_query, d_out, facts, hp)
+
+    size = width // 2
     wide = lambda factor: factor[:heads, None, :]
-    cube = lambda flat: flat.reshape(heads, HDIM, HDIM)
+    cube = lambda flat: flat[:size].reshape(heads, HDIM // 2, HDIM).astype(F32)
+    flat = lambda cubes: cubes.astype(BF16).reshape(size, HDIM)
     split = lambda f: (f.astype(BF16), (f - f.astype(BF16).astype(F32)).astype(BF16))
-    joined = lambda pair: pair[:hp].astype(F32) + pair[hp:].astype(F32)
+    joined = lambda rows: rows[size : size + hp].astype(F32) + rows[size + hp :].astype(F32)
     stages = (ctx_size - 1).bit_length()
+    uppers = [(me & (1 << stage)) != 0 for stage in range(stages)]
 
     def send(array, stage, up):
-        dist = 1 << stage
-        if stage < stages - 1:
+        dist = 1 << (stage % stages)
+        if stage != stages - 1:
             pairs = [(i, i ^ dist) for i in range(ctx_size)]
         else:
             pairs = [(i, i + dist) if up else (i + dist, i) for i in range(ctx_size) if not i & dist]
         return lax.ppermute(array, "ctx", pairs)
 
-    uppers = [(me & (1 << stage)) != 0 for stage in range(stages)]
-    shares, others = [joined(msg[width:])], []
-    got, agot = [], []
-    before, after = [jnp.ones_like(shares[0])], [jnp.ones_like(shares[0])]
-
-    def fold_state(stage, state):
-        upper, arrived = uppers[stage], cube(got[stage][:width]).astype(F32)
-        theirs = joined(got[stage][width:])
+    shares, others = [share], []
+    before, after = [jnp.ones_like(share)], [jnp.ones_like(share)]
+
+    def fold(stage, total, carried, arrived, up):
+        upper = uppers[stage]
+        first = upper if up else ~upper
+        arrived = cube(arrived)
+        if stage > 0:
+            weight = jnp.where(first, before[stage] if up else after[stage], 0.0)
+            carried = carried + wide(weight) * arrived
+        if stage == stages - 1:
+            lead = uppers[0] if up else ~uppers[0]
+            block, other = total
+            mine = jnp.where(lead, cube(other) + wide(others[0]) * carried, carried)
+            theirs = jnp.where(lead, carried, cube(block) + wide(shares[0]) * carried)
+            return flat(theirs), flat(mine), None
+        own, other = jnp.where(first, 1.0, others[stage]), jnp.where(first, shares[stage], 1.0)
+        total = wide(own) * total + wide(other) * arrived
+        return flat(total), total, carried
+
+    def fold_factors(stage, arrived):
+        theirs = joined(arrived)
         others.append(theirs)
-        own, other = jnp.where(upper, 1.0, theirs), jnp.where(upper, shares[stage], 1.0)
-        state = (wide(own) * cube(state) + wide(other) * arrived).reshape(width, HDIM)
         shares.append(shares[stage] * theirs)
-        before.append(jnp.where(upper, before[stage] * theirs, before[stage]))
-        after.append(jnp.where(upper, after[stage], after[stage] * theirs))
-        msg = state.astype(BF16)
-        if stage + 2 < stages:
-            msg = jnp.concatenate([msg, *split(shares[-1])], axis=0)
-        return msg, state
-
-    def fold_adjoint(stage, adjoint):
-        upper, arrived = uppers[stage], cube(agot[stage]).astype(F32)
-        own, other = jnp.where(upper, others[stage], 1.0), jnp.where(upper, 1.0, shares[stage])
-        adjoint = (wide(own) * cube(adjoint) + wide(other) * arrived).reshape(width, HDIM)
-        return adjoint.astype(BF16), adjoint
-
+        upper = uppers[stage]
+        pair = stage == 0
+        before.append(before[stage] if pair else jnp.where(upper, before[stage] * theirs, before[stage]))
+        after.append(after[stage] if pair else jnp.where(upper, after[stage], after[stage] * theirs))
+
+    class Chain:
+        def __init__(self, kept, sent, up):
+            self.kept, self.sent, self.up = kept, sent, up
+            self.total, self.carried, self.stage, self.arrived = cube(kept), jnp.zeros_like(cube(kept)), 0, None
+
+        def go(self):
+            self.arrived = send(self.sent, self.stage, self.up)
+
+        def take(self):
+            stage, self.stage = self.stage, self.stage + 1
+            if stage == 0:
+                self.first = self.arrived
+            total = self.total if stage < stages - 1 else (self.kept, self.first)
+            if self.up and stage < stages - 1:
+                fold_factors(stage, self.arrived)
+            self.sent, self.total, self.carried = fold(stage, total, self.carried, self.arrived, self.up)
+            if self.up and stage + 2 < stages:
+                self.sent = jnp.concatenate([self.sent, *split(shares[-1])], axis=0)
+
+    states, adjoints = Chain(kept, sent, True), Chain(akept, asent, False)
     half = max(1, heads // 2)
     pending = [(first, first + half) for first in range(0, heads, half)]
     inner_parts = []
-
-    def next_inner():
-        return inner(*pending.pop(0), query, keys, values, d_out, facts, hp)
-
     barrier = lax.optimization_barrier
-    for stage in range(stages):
-        arrived = send(msg if stage < stages - 1 else msg[:width], stage, True)
+    for stage in range(stages + 1):
+        states.go()
         if stage == 0:
-            arrived, query, adjoint, amsg = barrier((arrived, query, adjoint, amsg))
+            states.arrived, query, adjoints.kept, adjoints.sent = barrier(
+                (states.arrived, query, adjoints.kept, adjoints.sent)
+            )
+            adjoints.total = cube(adjoints.kept)
         else:
-            agot.append(send(amsg, stage - 1, False))
-            if pending and (stage == 1 or stage == stages - 1):
-                part = next_inner()
-                arrived, *part = barrier((arrived, *part))
+            adjoints.go()
+            if pending:
+                query, _ = barrier((query, adjoints.sent))
+                part = inner(*pending.pop(0), query, keys, values, d_out, facts, hp)
+                states.arrived, *part = barrier((states.arrived, *part))
                 inner_parts.append(part)
-        got.append(arrived)
-        if stage < stages - 1:
-            msg, state = fold_state(stage, state)
+        if stage < stages:
+            states.take()
         if stage >= 1:
-            agot[-1], _ = barrier((agot[-1], msg))
-            amsg, adjoint = fold_adjoint(stage - 1, adjoint)
+            adjoints.arrived, _ = barrier((adjoints.arrived, states.sent if stage < stages else states.total))
+            adjoints.take()
     while pending:
-        inner_parts.append(next_inner())
-    agot.append(send(amsg, stages - 1, False))
-    got[-1], _ = barrier((got[-1], amsg))
-
-    state_coefs = [jnp.where(u, f, 0.0)[:heads] for u, f in zip(uppers, before)]
-    adjoint_coefs = [jnp.where(u, 0.0, f)[:heads] for u, f in zip(uppers, after)]
-    state_coefs = jnp.concatenate(state_coefs, axis=0)
-    adjoint_coefs = jnp.concatenate(adjoint_coefs, axis=0)
+        inner_parts.append(inner(*pending.pop(0), query, keys, values, d_out, facts, hp))
+    adjoints.go()
+    states.arrived, _ = barrier((states.arrived, adjoints.sent))
+    state_halves = (states.total, states.arrived)
+    adjoint_halves = (adjoints.total, adjoints.arrived)
     dqs, dks, dvs = zip(*inner_parts)
 
     place = lambda shift: ((mine + shift) % head_size).astype(jnp.int32).reshape(1)
@@ -617,12 +645,12 @@
         for first in range(0, feat, count):
             if shift == 1 and first == 0:
                 d_query, term = query_term(
-                    got, state_coefs, dqs, d_out, facts, w_query, place(1), feat, count, heads, hp
+                    state_halves, dqs, d_out, facts, w_query, place(1), feat, count, heads, hp
                 )
             else:
                 term = plain_term(d_query, w_query, place(shift), feat, first, count)
             arrived.append(lax.ppermute(term, "head", ring))
-    d_keys, d_values = close(agot, adjoint_coefs, dks, dvs, keys, values, facts, heads, hp)
+    d_keys, d_values = close(adjoint_halves, dks, dvs, keys, values, facts, heads, hp)
     d_hidden = finish(d_query, w_query, place(0), arrived, feat)
     return (d_hidden, d_keys, d_values)
 

time: 73.4 us -> 66.4 us (0.905)
  waiting for transfers between devices: 17.7 us -> 9.28 us
  starting transfers between devices: 15.2 us -> 17.1 us
    ppermute x8 -> x10, waiting for transfers between devices: 17.7 us -> 9.11 us  [send(): return lax.ppermute(array, 'ctx', pairs)]
    ppermute x8 -> x10, starting transfers between devices: 14.7 us -> 16.5 us  [send(): return lax.ppermute(array, 'ctx', pairs)]
  transfers between devices with their start and end apart: 10 -> 12, of which waited for: 3 -> 4; matrix products, arithmetic and copies ran while one was open for 2% -> 1% of each run, Pallas kernels for 44% -> 49%
where the time goes in v8:
time: 66.4 us; the launch traced here: 66.1 us
  Pallas kernels  37.7 us (57%)
  starting transfers between devices  17.1 us (26%)
  waiting for transfers between devices  9.28 us (14%)
  other arithmetic  1.07 us (2%)
  between operations  0.99 us (1%)
    pallas_call x7, Pallas kernels, kernel_call(): pl.pallas_call(kernel, in_specs=specs, out_specs=tuple(out_specs), out_sh...  37.7 us
    ppermute x10, starting transfers between devices, send(): return lax.ppermute(array, 'ctx', pairs)  16.5 us
    ppermute x10, waiting for transfers between devices, send(): return lax.ppermute(array, 'ctx', pairs)  9.11 us
  transfers between devices with their start and end apart: 12, of which 4 were waited for; matrix products, arithmetic and copies ran while one was open for 1% of the time, Pallas kernels for 49%

profile of v8, /device:TPU:0, one launch (start us, length us, event | category | flops | bytes accessed | tf_op | source)
XLA Modules:
  0.0 66.1 jit_solution(3491713912849087275)
XLA Ops:
  0.6 0.5 collective-permute-start.1
  1.1 3.7 %prepare.1 = (f32[32,512]{1,0:T(8,128)}, bf16[512,128]{1,0:T(8,128)(2,1)S(1)}, bf16[528,128]{1,0:T(8,128)(2,1)S(1)}, f32[8,128]{1,0:T(8,128)S(1)}) custom-call(f32[8,512]{1,0:T(8,128)} %bitcast.126, bf16[512,1024]{1,0:T(8,128)(2,1)} %refs_2_.9, bf16[512,1024]{1,0:T(8,128)(2,1)} %refs_3_.7), custom_call_target="tpu_custom_call" | custom-call | flops 4000000000 | bytes 1 | tf_op jit(solution)/shard_map/prepare/pallas_call | solution.py:34
  4.8 2.6 %collective-permute-start = (bf16[528,128]{1,0:T(8,128)(2,1)S(1)}, bf16[528,128]{1,0:T(8,128)(2,1)S(1)}, u32[]{:S(2)}, u32[]{:S(2)}) collective-permute-start(bf16[528,128]{1,0:T(8,128)(2,1)S(1)} %get-tuple-element.39), channel_id=1, source_target_pairs={{0,2},{2,0},{4,6},{6,4},{8,10},{10,8},{12,14},{14,12},{16,18},{18,... | collective-permute-start | bytes 405512 | tf_op jit(solution)/shard_map/ppermute | solution.py:558
  7.4 0.1 pad_add_fusion.place_ref
  7.5 8.5 %project.1 = (bf16[512,1024]{1,0:T(8,128)(2,1)}, bf16[512,128]{1,0:T(8,128)(2,1)S(1)}, bf16[512,128]{1,0:T(8,128)(2,1)S(1)}) custom-call(s32[2]{0:T(128)S(1)} %pad_add_fusion.place_ref, bf16[512,2048]{1,0:T(8,128)(2,1)} %refs_0_.1, bf16[512,2048]{1,0:T(8,128)(2,1)S(1)} %collective-permute-done.1.refs_1_, bf16[4096,1024]{1,0:T(8,128)(2,1)} %refs_1_.5, ...), custom_call_target="tpu_custom_call" | custom-call | flops 8000000000 | bytes 1 | tf_op jit(solution)/shard_map/project/pallas_call | solution.py:34
  15.9 0.6 collective-permute-start.4
  16.6 0.1 fusion.21
  16.6 1.6 %collective-permute-start.2 = (bf16[528,128]{1,0:T(8,128)(2,1)S(1)}, bf16[528,128]{1,0:T(8,128)(2,1)S(1)}, u32[]{:S(2)}, u32[]{:S(2)}) collective-permute-start(bf16[528,128]{1,0:T(8,128)(2,1)S(1)} %pad_maximum_fusion), channel_id=1, source_target_pairs={{0,4},{2,6},{4,0},{6,2},{8,12},{10,14},{12,8},{14,10},{16,20},{18,... | collective-permute-start | bytes 405512 | tf_op jit(solution)/shard_map/ppermute | solution.py:558
  18.2 5.0 %inner.2 = (bf16[512,512]{1,0:T(8,128)(2,1)}, bf16[512,512]{1,0:T(8,128)(2,1)}, bf16[512,512]{1,0:T(8,128)(2,1)}) custom-call(bf16[512,1024]{1,0:T(8,128)(2,1)} %get-tuple-element.56.refs_0_, bf16[512,1024]{1,0:T(8,128)(2,1)} %refs_2_.9, bf16[512,1024]{1,0:T(8,128)(2,1)} %refs_3_.7, bf16[512,1024]{1,0:T(8,128)(2,1)} %refs_2_.8, ...), custom_call_target="tpu_custom_call" | custom-call | flops 3000000000 | bytes 1 | tf_op jit(solution)/shard_map/inner/pallas_call | solution.py:34
  23.2 0.1 fusion.23
  23.4 0.1 fusion.20
  23.4 0.6 collective-permute-start.7
  24.0 1.6 %collective-permute-start.3 = (bf16[528,128]{1,0:T(8,128)(2,1)S(1)}, bf16[528,128]{1,0:T(8,128)(2,1)S(1)}, u32[]{:S(2)}, u32[]{:S(2)}) collective-permute-start(bf16[528,128]{1,0:T(8,128)(2,1)S(1)} %pad_maximum_fusion.1), channel_id=1, source_target_pairs={{0,8},{2,10},{4,12},{6,14},{8,0},{10,2},{12,4},{14,6},{16,24},{18,... | collective-permute-start | bytes 405512 | tf_op jit(solution)/shard_map/ppermute | solution.py:558
  25.6 5.0 %inner.3 = (bf16[512,512]{1,0:T(8,128)(2,1)}, bf16[512,512]{1,0:T(8,128)(2,1)}, bf16[512,512]{1,0:T(8,128)(2,1)}) custom-call(bf16[512,1024]{1,0:T(8,128)(2,1)} %get-tuple-element.56.refs_0_, bf16[512,1024]{1,0:T(8,128)(2,1)} %refs_2_.9, bf16[512,1024]{1,0:T(8,128)(2,1)} %refs_3_.7, bf16[512,1024]{1,0:T(8,128)(2,1)} %refs_2_.8, ...), custom_call_target="tpu_custom_call" | custom-call | flops 3000000000 | bytes 1 | tf_op jit(solution)/shard_map/inner/pallas_call | solution.py:34
  30.6 0.1 fusion.14
  30.7 4.5 %collective-permute-start.5 = (bf16[512,128]{1,0:T(8,128)(2,1)S(1)}, bf16[512,128]{1,0:T(8,128)(2,1)S(1)}, u32[]{:S(2)}, u32[]{:S(2)}) collective-permute-start(bf16[512,128]{1,0:T(8,128)(2,1)S(1)} %fusion.14), channel_id=1, source_target_pairs={{0,16},{2,18},{4,20},{6,22},{8,24},{10,26},{12,28},{14,30},{1,17},... | collective-permute-start | bytes 393224 | tf_op jit(solution)/shard_map/ppermute | solution.py:558
  35.3 0.1 fusion.22
  35.4 0.5 collective-permute-start.8
  35.9 2.8 %collective-permute-done.5 = bf16[512,128]{1,0:T(8,128)(2,1)S(1)} collective-permute-done((bf16[512,128]{1,0:T(8,128)(2,1)S(1)}, bf16[512,128]{1,0:T(8,128)(2,1)S(1)}, u32[]{:S(2)}, u32[]{:S(2)}) %collective-permute-start.5) | collective-permute-done | bytes 131104 | tf_op jit(solution)/shard_map/ppermute | solution.py:558
  38.7 0.2 fusion.4
  38.9 1.6 %collective-permute-done.8 = bf16[512,128]{1,0:T(8,128)(2,1)S(1)} collective-permute-done((bf16[512,128]{1,0:T(8,128)(2,1)S(1)}, bf16[512,128]{1,0:T(8,128)(2,1)S(1)}, u32[]{:S(2)}, u32[]{:S(2)}) %collective-permute-start.8) | collective-permute-done | bytes 131104 | tf_op jit(solution)/shard_map/ppermute | solution.py:558
  40.4 0.1 fusion.19
  40.6 1.5 %collective-permute-start.9 = (bf16[512,128]{1,0:T(8,128)(2,1)S(1)}, bf16[512,128]{1,0:T(8,128)(2,1)S(1)}, u32[]{:S(2)}, u32[]{:S(2)}) collective-permute-start(bf16[512,128]{1,0:T(8,128)(2,1)S(1)} %fusion.19), channel_id=1, source_target_pairs={{16,0},{18,2},{20,4},{22,6},{24,8},{26,10},{28,12},{30,14},{17,1},... | collective-permute-start | bytes 393224 | tf_op jit(solution)/shard_map/ppermute | solution.py:558
  42.0 1.6 %collective-permute-start.6 = (bf16[512,128]{1,0:T(8,128)(2,1)S(1)}, bf16[512,128]{1,0:T(8,128)(2,1)S(1)}, u32[]{:S(2)}, u32[]{:S(2)}) collective-permute-start(bf16[512,128]{1,0:T(8,128)(2,1)S(1)} %get-tuple-element.85), channel_id=1, source_target_pairs={{0,2},{2,0},{4,6},{6,4},{8,10},{10,8},{12,14},{14,12},{16,18},{18,... | collective-permute-start | bytes 393224 | tf_op jit(solution)/shard_map/ppermute | solution.py:558
  43.6 4.7 %collective-permute-done.9 = bf16[512,128]{1,0:T(8,128)(2,1)S(1)} collective-permute-done((bf16[512,128]{1,0:T(8,128)(2,1)S(1)}, bf16[512,128]{1,0:T(8,128)(2,1)S(1)}, u32[]{:S(2)}, u32[]{:S(2)}) %collective-permute-start.9) | collective-permute-done | bytes 131104 | tf_op jit(solution)/shard_map/ppermute | solution.py:558
  48.3 0.2 fusion.12
  48.5 1.6 %collective-permute-start.11 = (bf16[512,128]{1,0:T(8,128)(2,1)S(1)}, bf16[512,128]{1,0:T(8,128)(2,1)S(1)}, u32[]{:S(2)}, u32[]{:S(2)}) collective-permute-start(bf16[512,128]{1,0:T(8,128)(2,1)S(1)} %get-tuple-element.88), channel_id=1, source_target_pairs={{0,2},{2,0},{4,6},{6,4},{8,10},{10,8},{12,14},{14,12},{16,18},{18,... | collective-permute-start | bytes 393224 | tf_op jit(solution)/shard_map/ppermute | solution.py:558
  50.0 5.9 %query_term.1 = (bf16[512,1024]{1,0:T(8,128)(2,1)}, bf16[512,2048]{1,0:T(8,128)(2,1)}) custom-call(s32[1]{0:T(128)} %bitcast.1.place_ref, bf16[512,128]{1,0:T(8,128)(2,1)S(1)} %get-tuple-element.86.refs_0_, bf16[512,128]{1,0:T(8,128)(2,1)S(1)} %collective-permute-done.6.refs_1_, bf16[512,1024]{1,0:T(8,128)(2,1)} %refs_2_.8, ...), custom_call_target="tpu_custom_call" | custom-call | flops 6000000000 | bytes 1 | tf_op jit(solution)/shard_map/query_term/pallas_call | solution.py:34
  56.0 0.1 collective-permute-start.10
  56.0 4.2 %close.1 = (bf16[512,1024]{1,0:T(8,128)(2,1)}, bf16[512,1024]{1,0:T(8,128)(2,1)}) custom-call(bf16[512,128]{1,0:T(8,128)(2,1)S(1)} %get-tuple-element.87.refs_0_, bf16[512,128]{1,0:T(8,128)(2,1)S(1)} %collective-permute-done.11.refs_1_, bf16[512,1024]{1,0:T(8,128)(2,1)} %refs_2_.9, bf16[512,1024]{1,0:T(8,128)(2,1)} %refs_3_.7, ...), custom_call_target="tpu_custom_call" | custom-call | flops 99999997952 | bytes 1 | tf_op jit(solution)/shard_map/close/pallas_call | solution.py:34
  60.2 0.2 collective-permute-done.10.refs_2_
  60.4 5.5 %finish.1 = bf16[512,2048]{1,0:T(8,128)(2,1)} custom-call(s32[1]{0:T(128)} %bitcast.place_ref, bf16[512,1024]{1,0:T(8,128)(2,1)} %get-tuple-element.67.refs_0_, bf16[4096,1024]{1,0:T(8,128)(2,1)} %refs_1_.5, bf16[512,2048]{1,0:T(8,128)(2,1)S(1)} %collective-permute-done.10.refs_2_), custom_call_target="tpu_custom_call" | custom-call | flops 6000000000 | bytes 1 | tf_op jit(solution)/shard_map/finish/pallas_call | solution.py:34
  (16 shorter events, 0.1 us)
Async XLA Ops:
  0.6 6.8 %collective-permute-start.1 = (bf16[512,2048]{1,0:T(8,128)(2,1)}, bf16[512,2048]{1,0:T(8,128)(2,1)S(1)}, u32[]{:S(2)}, u32[]{:S(2)}) collective-permute-start(bf16[512,2048]{1,0:T(8,128)(2,1)} %refs_0_.1), channel_id=1, source_target_pairs={{0,1},{1,0},{2,3},{3,2},{4,5},{5,4},{6,7},{7,6},{8,9},{9,8},{10,11... | collective-permute-start | bytes 6291464 | tf_op jit(solution)/shard_map/ppermute | solution.py:537
  4.8 11.1 %collective-permute-start = (bf16[528,128]{1,0:T(8,128)(2,1)S(1)}, bf16[528,128]{1,0:T(8,128)(2,1)S(1)}, u32[]{:S(2)}, u32[]{:S(2)}) collective-permute-start(bf16[528,128]{1,0:T(8,128)(2,1)S(1)} %get-tuple-element.39), channel_id=1, source_target_pairs={{0,2},{2,0},{4,6},{6,4},{8,10},{10,8},{12,14},{14,12},{16,18},{18,... | collective-permute-start | bytes 405512 | tf_op jit(solution)/shard_map/ppermute | solution.py:558
  15.9 7.4 %collective-permute-start.4 = (bf16[512,128]{1,0:T(8,128)(2,1)S(1)}, bf16[512,128]{1,0:T(8,128)(2,1)S(1)}, u32[]{:S(2)}, u32[]{:S(2)}) collective-permute-start(bf16[512,128]{1,0:T(8,128)(2,1)S(1)} %get-tuple-element.48), channel_id=1, source_target_pairs={{0,2},{2,0},{4,6},{6,4},{8,10},{10,8},{12,14},{14,12},{16,18},{18,... | collective-permute-start | bytes 393224 | tf_op jit(solution)/shard_map/ppermute | solution.py:558
  16.6 6.6 %collective-permute-start.2 = (bf16[528,128]{1,0:T(8,128)(2,1)S(1)}, bf16[528,128]{1,0:T(8,128)(2,1)S(1)}, u32[]{:S(2)}, u32[]{:S(2)}) collective-permute-start(bf16[528,128]{1,0:T(8,128)(2,1)S(1)} %pad_maximum_fusion), channel_id=1, source_target_pairs={{0,4},{2,6},{4,0},{6,2},{8,12},{10,14},{12,8},{14,10},{16,20},{18,... | collective-permute-start | bytes 405512 | tf_op jit(solution)/shard_map/ppermute | solution.py:558
  23.4 11.8 %collective-permute-start.7 = (bf16[512,128]{1,0:T(8,128)(2,1)S(1)}, bf16[512,128]{1,0:T(8,128)(2,1)S(1)}, u32[]{:S(2)}, u32[]{:S(2)}) collective-permute-start(bf16[512,128]{1,0:T(8,128)(2,1)S(1)} %fusion.20), channel_id=1, source_target_pairs={{0,4},{2,6},{4,0},{6,2},{8,12},{10,14},{12,8},{14,10},{16,20},{18,... | collective-permute-start | bytes 393224 | tf_op jit(solution)/shard_map/ppermute | solution.py:558
  24.0 6.6 %collective-permute-start.3 = (bf16[528,128]{1,0:T(8,128)(2,1)S(1)}, bf16[528,128]{1,0:T(8,128)(2,1)S(1)}, u32[]{:S(2)}, u32[]{:S(2)}) collective-permute-start(bf16[528,128]{1,0:T(8,128)(2,1)S(1)} %pad_maximum_fusion.1), channel_id=1, source_target_pairs={{0,8},{2,10},{4,12},{6,14},{8,0},{10,2},{12,4},{14,6},{16,24},{18,... | collective-permute-start | bytes 405512 | tf_op jit(solution)/shard_map/ppermute | solution.py:558
  30.7 7.9 %collective-permute-start.5 = (bf16[512,128]{1,0:T(8,128)(2,1)S(1)}, bf16[512,128]{1,0:T(8,128)(2,1)S(1)}, u32[]{:S(2)}, u32[]{:S(2)}) collective-permute-start(bf16[512,128]{1,0:T(8,128)(2,1)S(1)} %fusion.14), channel_id=1, source_target_pairs={{0,16},{2,18},{4,20},{6,22},{8,24},{10,26},{12,28},{14,30},{1,17},... | collective-permute-start | bytes 393224 | tf_op jit(solution)/shard_map/ppermute | solution.py:558
  35.4 5.0 %collective-permute-start.8 = (bf16[512,128]{1,0:T(8,128)(2,1)S(1)}, bf16[512,128]{1,0:T(8,128)(2,1)S(1)}, u32[]{:S(2)}, u32[]{:S(2)}) collective-permute-start(bf16[512,128]{1,0:T(8,128)(2,1)S(1)} %fusion.22), channel_id=1, source_target_pairs={{0,8},{2,10},{4,12},{6,14},{8,0},{10,2},{12,4},{14,6},{16,24},{18,... | collective-permute-start | bytes 393224 | tf_op jit(solution)/shard_map/ppermute | solution.py:558
  40.6 7.8 %collective-permute-start.9 = (bf16[512,128]{1,0:T(8,128)(2,1)S(1)}, bf16[512,128]{1,0:T(8,128)(2,1)S(1)}, u32[]{:S(2)}, u32[]{:S(2)}) collective-permute-start(bf16[512,128]{1,0:T(8,128)(2,1)S(1)} %fusion.19), channel_id=1, source_target_pairs={{16,0},{18,2},{20,4},{22,6},{24,8},{26,10},{28,12},{30,14},{17,1},... | collective-permute-start | bytes 393224 | tf_op jit(solution)/shard_map/ppermute | solution.py:558
  42.0 8.0 %collective-permute-start.6 = (bf16[512,128]{1,0:T(8,128)(2,1)S(1)}, bf16[512,128]{1,0:T(8,128)(2,1)S(1)}, u32[]{:S(2)}, u32[]{:S(2)}) collective-permute-start(bf16[512,128]{1,0:T(8,128)(2,1)S(1)} %get-tuple-element.85), channel_id=1, source_target_pairs={{0,2},{2,0},{4,6},{6,4},{8,10},{10,8},{12,14},{14,12},{16,18},{18,... | collective-permute-start | bytes 393224 | tf_op jit(solution)/shard_map/ppermute | solution.py:558
  48.5 7.5 %collective-permute-start.11 = (bf16[512,128]{1,0:T(8,128)(2,1)S(1)}, bf16[512,128]{1,0:T(8,128)(2,1)S(1)}, u32[]{:S(2)}, u32[]{:S(2)}) collective-permute-start(bf16[512,128]{1,0:T(8,128)(2,1)S(1)} %get-tuple-element.88), channel_id=1, source_target_pairs={{0,2},{2,0},{4,6},{6,4},{8,10},{10,8},{12,14},{14,12},{16,18},{18,... | collective-permute-start | bytes 393224 | tf_op jit(solution)/shard_map/ppermute | solution.py:558
  56.0 4.4 %collective-permute-start.10 = (bf16[512,2048]{1,0:T(8,128)(2,1)}, bf16[512,2048]{1,0:T(8,128)(2,1)S(1)}, u32[]{:S(2)}, u32[]{:S(2)}) collective-permute-start(bf16[512,2048]{1,0:T(8,128)(2,1)} %get-tuple-element.68), channel_id=1, source_target_pairs={{0,1},{1,0},{2,3},{3,2},{4,5},{5,4},{6,7},{7,6},{8,9},{9,8},{10,11... | collective-permute-start | bytes 6291464 | tf_op jit(solution)/shard_map/ppermute | solution.py:652

commit v9 on v8

--- a/solution.py
+++ b/solution.py
@@ -74,6 +74,12 @@
     def finish(self):
         for copy in self.out:
             copy.wait()
+
+
+def spans_of(heads):
+    half, quarter = heads // 2, heads // 4
+    edges = sorted({0, half, half + quarter, heads})
+    return list(zip(edges, edges[1:]))
 
 
 def groups(heads):
@@ -165,57 +171,61 @@
     )
 
 
-def project_kernel(hp, nparts, chunk, place_ref, *refs):
+def project_kernel(hp, nparts, chunks, place_ref, *refs):
     parts, (w_hbm, do_hbm, facts_hbm, q_hbm, kept_ref, sent_ref) = refs[:nparts], refs[nparts : nparts + 6]
     hbuf, wbuf, dobuf, facts_ref, qbuf, total, sems = refs[nparts + 6 :]
     rows, feat = parts[0].shape
     width = wbuf.shape[1]
-    heads = width // HDIM
     upper = lax.axis_index("ctx") % 2 == 1
     copies = Copies(sems)
     loads = []
-    for part, ref in enumerate(parts):
-        for first in range(0, feat, chunk):
-            here = pl.ds(part * feat + first, chunk)
-            start = pl.multiple_of(place_ref[part] * feat + first, chunk)
-            loads.append(
-                (
-                    slice(part * feat + first, part * feat + first + chunk),
-                    copies.start(ref.at[:, pl.ds(first, chunk)], hbuf.at[:, here]),
-                    copies.start(w_hbm.at[pl.ds(start, chunk), :], wbuf.at[here, :]),
-                )
+    for part, first, size in chunks:
+        at = part * feat + first
+        start = pl.multiple_of(place_ref[part] * feat + first, math.gcd(feat, first) if first else feat)
+        loads.append(
+            (
+                slice(at, at + size),
+                copies.start(parts[part].at[:, pl.ds(first, size)], hbuf.at[:, pl.ds(at, size)]),
+                copies.start(w_hbm.at[pl.ds(start, size), :], wbuf.at[pl.ds(at, size), :]),
             )
-    late = [copies.start(facts_hbm, facts_ref), copies.start(do_hbm, dobuf)]
+        )
+        if len(loads) == min(4, len(chunks)):
+            late = [copies.start(facts_hbm, facts_ref), copies.start(do_hbm, dobuf)]
     block = min(256, width)
     for order, (here, h_in, w_in) in enumerate(loads):
         h_in.wait()
         w_in.wait()
+        if order == len(loads) - 1:
+            for copy in late:
+                copy.wait()
+            table = turned(facts_ref[...])
         for first in range(0, width, block):
             wide = slice(first, first + block)
             term = dot(hbuf[:, here], wbuf[here, wide], NN)
-            if order == 0:
+            if order > 0:
+                term = total[:, wide] + term
+            if order < len(loads) - 1:
                 total[:, wide] = term
-            elif order < len(loads) - 1:
-                total[:, wide] += term
-            else:
-                qbuf[:, wide] = (total[:, wide] + term).astype(BF16)
-    for copy in late:
-        copy.wait()
-    copies.store(qbuf, q_hbm)
-    table = turned(facts_ref[...])
-    for h in range(heads):
-        cols = slice(h * HDIM, (h + 1) * HDIM)
-        decayed = (column(table, 3 * hp + h) * qbuf[:, cols].astype(F32)).astype(BF16)
-        put_halves(upper, h, dot(decayed, dobuf[:, cols], TN), kept_ref, sent_ref)
+                continue
+            qbuf[:, wide] = term.astype(BF16)
+            copies.store(qbuf.at[:, wide], q_hbm.at[:, wide])
+            for h in range(first // HDIM, (first + block) // HDIM):
+                cols = slice(h * HDIM, (h + 1) * HDIM)
+                decayed = (column(table, 3 * hp + h) * qbuf[:, cols].astype(F32)).astype(BF16)
+                put_halves(upper, h, dot(decayed, dobuf[:, cols], TN), kept_ref, sent_ref)
     copies.finish()
 
 
 def project(parts, owners, w_query, d_out, facts, hp):
     rows, feat = parts[0].shape
     depth, width = w_query.shape
-    chunk = min(512, feat)
+    chunks = []
+    for part in range(len(parts)):
+        sizes = [feat] if feat % 1024 else ([256, 256, 512] + [1024] * (feat // 1024 - 1) if part == 0 else [1024] * (feat // 1024))
+        for order, size in enumerate(sizes):
+            chunks.append((part, sum(sizes[:order]), size))
     return kernel_call(
-        functools.partial(project_kernel, hp, len(parts), chunk),
+        functools.partial(project_kernel, hp, len(parts), chunks),
         (owners, *parts, w_query, d_out, facts),
         [SM, HB] + [AN] * (len(parts) - 1) + [HB] * 3,
         [((rows, width), BF16), ((width // 2, HDIM), BF16), ((width // 2, HDIM), BF16)],
@@ -227,7 +237,7 @@
             pltpu.VMEM(facts.shape, F32),
             pltpu.VMEM((rows, width), BF16),
             pltpu.VMEM((rows, width), F32),
-            pltpu.SemaphoreType.DMA((2 * len(parts) * (feat // chunk) + 3,)),
+            pltpu.SemaphoreType.DMA((2 * len(chunks) + 2 + width // min(256, width),)),
         ],
         28,
         "project",
@@ -294,7 +304,7 @@
         ],
         24,
         "inner",
-        3,
+        1,
     )
 
 
@@ -305,100 +315,86 @@
     return jnp.concatenate([jnp.where(upper, theirs, mine), jnp.where(upper, mine, theirs)], axis=0)
 
 
-def load_weight(copies, place_ref, first, w_hbm, wbuf, feat, block):
-    loads = []
-    for at in range(0, wbuf.shape[0], block):
+def load_weight(copies, place_ref, first, w_hbm, wbuf, feat, blocks):
+    loads, at = [], 0
+    for block in blocks:
         start = pl.multiple_of(place_ref[0] * feat + first + at, block)
-        loads.append((at, copies.start(w_hbm.at[pl.ds(start, block), :], wbuf.at[pl.ds(at, block), :])))
+        loads.append((at, block, copies.start(w_hbm.at[pl.ds(start, block), :], wbuf.at[pl.ds(at, block), :])))
+        at += block
     return loads
 
 
-def query_kernel(heads, hp, feat, block, place_ref, *refs):
+def query_kernel(heads, hp, feat, blocks, place_ref, *refs):
     mine_ref, theirs_ref, do_hbm, facts_hbm, w_hbm = refs[:5]
-    inner_hbm = refs[5:-9]
-    dq_hbm, out_hbm, dobuf, facts_ref, wbuf, local, held, sent, sems = refs[-9:]
+    inner_hbm = refs[5:-7]
+    held, out_ref, dobuf, facts_ref, wbuf, local, sems = refs[-7:]
     upper = lax.axis_index("ctx") % 2 == 1
     copies = Copies(sems)
-    each = heads // len(inner_hbm)
     facts_in = copies.start(facts_hbm, facts_ref)
-    loads = []
-    for part, src in enumerate(inner_hbm):
-        wide = pl.ds(part * each * HDIM, each * HDIM)
-        loads.append(
-            (copies.start(do_hbm.at[:, wide], dobuf.at[:, wide]), copies.start(src, local.at[:, wide]))
-        )
-    w_in = load_weight(copies, place_ref, 0, w_hbm, wbuf, feat, block)
+    loads = {}
+    for (first, last), src in zip(spans_of(heads), inner_hbm):
+        wide = pl.ds(first * HDIM, (last - first) * HDIM)
+        loads[first] = (copies.start(do_hbm.at[:, wide], dobuf.at[:, wide]), copies.start(src, local.at[:, wide]))
+    w_in = load_weight(copies, place_ref, 0, w_hbm, wbuf, feat, blocks)
     facts_in.wait()
     table = turned(facts_ref[...])
     for h in range(heads):
-        if h % each == 0:
-            for copy in loads[h // each]:
-                copy.wait()
+        for copy in loads.get(h, ()):
+            copy.wait()
         cols = slice(h * HDIM, (h + 1) * HDIM)
         state = whole_head(upper, h, mine_ref, theirs_ref)
         carry = dot(dobuf[:, cols], state, NT)
         held[:, cols] = (local[:, cols].astype(F32) + column(table, 3 * hp + h) * carry).astype(BF16)
-    copies.store(held, dq_hbm)
-    send_terms(copies, w_in, held, wbuf, sent, out_hbm, block)
-    copies.finish()
-
-
-def send_terms(copies, w_in, dq_ref, wbuf, sent, out_hbm, block):
-    for at, copy in w_in:
+    put_terms(w_in, held, wbuf, out_ref)
+
+
+def put_terms(w_in, dq_ref, wbuf, out_ref):
+    for at, block, copy in w_in:
         copy.wait()
         wide = slice(at, at + block)
-        sent[:, wide] = dot(dq_ref[...], wbuf[wide, :], NT).astype(BF16)
-        copies.store(sent.at[:, wide], out_hbm.at[:, wide])
+        out_ref[:, wide] = dot(dq_ref[...], wbuf[wide, :], NT).astype(BF16)
 
 
 def query_term(halves, inner_dq, d_out, facts, w_query, place, feat, count, heads, hp):
     rows, width = d_out.shape
-    block = min(512, count)
+    blocks = blocks_of(count)
     args = (d_out, facts, w_query, *inner_dq)
     return kernel_call(
-        functools.partial(query_kernel, heads, hp, feat, block),
+        functools.partial(query_kernel, heads, hp, feat, blocks),
         (place, *halves, *args),
         [SM, VM, VM] + [HB] * len(args),
         [((rows, width), BF16), ((rows, count), BF16)],
-        (HB, HB),
+        (VM, VM),
         [
             pltpu.VMEM((rows, width), BF16),
             pltpu.VMEM(facts.shape, F32),
             pltpu.VMEM((count, width), BF16),
             pltpu.VMEM((rows, width), BF16),
-            pltpu.VMEM((rows, width), BF16),
-            pltpu.VMEM((rows, count), BF16),
-            pltpu.SemaphoreType.DMA((2 + 2 * len(inner_dq) + 2 * (count // block),)),
+            pltpu.SemaphoreType.DMA((1 + 2 * len(inner_dq) + len(blocks),)),
         ],
-        20,
+        16,
         "query_term",
         6,
     )
 
 
-def term_kernel(feat, first, block, place_ref, dq_hbm, w_hbm, out_hbm, held, wbuf, sent, sems):
+def term_kernel(feat, first, blocks, place_ref, dq_ref, w_hbm, out_ref, wbuf, sems):
     copies = Copies(sems)
-    dq_in = copies.start(dq_hbm, held)
-    w_in = load_weight(copies, place_ref, first, w_hbm, wbuf, feat, block)
-    dq_in.wait()
-    send_terms(copies, w_in, held, wbuf, sent, out_hbm, block)
-    copies.finish()
+    put_terms(load_weight(copies, place_ref, first, w_hbm, wbuf, feat, blocks), dq_ref, wbuf, out_ref)
 
 
 def plain_term(d_query, w_query, place, feat, first, count):
     rows, width = d_query.shape
-    block = min(512, count)
+    blocks = blocks_of(count)
     return kernel_call(
-        functools.partial(term_kernel, feat, first, block),
+        functools.partial(term_kernel, feat, first, blocks),
         (place, d_query, w_query),
-        [SM, HB, HB],
+        [SM, VM, HB],
         [((rows, count), BF16)],
-        (HB,),
+        (VM,),
         [
-            pltpu.VMEM((rows, width), BF16),
             pltpu.VMEM((count, width), BF16),
-            pltpu.VMEM((rows, count), BF16),
-            pltpu.SemaphoreType.DMA((1 + 2 * (count // block),)),
+            pltpu.SemaphoreType.DMA((len(blocks),)),
         ],
         16,
         "term",
@@ -406,51 +402,46 @@
     )[0]
 
 
-def finish_kernel(count, block, place_ref, *refs):
-    dq_hbm, w_hbm = refs[:2]
-    arrived, (out_hbm, held, wbuf, extra, sent, sems) = refs[2:-6], refs[-6:]
+def finish_kernel(count, blocks, place_ref, dq_ref, w_hbm, *refs):
+    arrived, (out_hbm, wbuf, sent, sems) = refs[:-4], refs[-4:]
     feat = sent.shape[1]
+    per = feat // count
     copies = Copies(sems)
-    dq_in = copies.start(dq_hbm, held)
-    w_in = load_weight(copies, place_ref, 0, w_hbm, wbuf, feat, block)
-    per = feat // count
-    others = []
-    for index, src in enumerate(arrived):
-        shift, first = divmod(index, per)
-        others.append(copies.start(src, extra.at[shift, :, pl.ds(first * count, count)]))
-    dq_in.wait()
-    for at, copy in w_in:
+    w_in = load_weight(copies, place_ref, 0, w_hbm, wbuf, feat, blocks)
+    for at, block, copy in w_in:
         copy.wait()
         wide = slice(at, at + block)
-        total = dot(held[...], wbuf[wide, :], NT).astype(BF16).astype(F32)
-        for index, other in enumerate(others):
-            if at == index % per * count:
-                other.wait()
-        for shift in range(extra.shape[0]):
-            total = total + extra[shift, :, wide].astype(F32)
+        total = dot(dq_ref[...], wbuf[wide, :], NT).astype(BF16).astype(F32)
+        part, here = at // count, slice(at % count, at % count + block)
+        for shift in range(len(arrived) // per):
+            total = total + arrived[shift * per + part][:, here].astype(F32)
         sent[:, wide] = total.astype(BF16)
         copies.store(sent.at[:, wide], out_hbm.at[:, wide])
     copies.finish()
 
 
+def blocks_of(count):
+    if count % 512 or count < 1024:
+        return [count]
+    return [256, 256] + [512] * (count // 512 - 2) + [256, 256]
+
+
 def finish(d_query, w_query, place, arrived, feat):
     rows, width = d_query.shape
     count = arrived[0].shape[1]
-    block = min(512, count)
+    blocks = blocks_of(feat) if count == feat else [count] * (feat // count)
     return kernel_call(
-        functools.partial(finish_kernel, count, block),
+        functools.partial(finish_kernel, count, blocks),
         (place, d_query, w_query, *arrived),
-        [SM, HB, HB] + [AN] * len(arrived),
+        [SM, VM, HB] + [VM] * len(arrived),
         [((rows, feat), BF16)],
         (HB,),
         [
-            pltpu.VMEM((rows, width), BF16),
             pltpu.VMEM((feat, width), BF16),
-            pltpu.VMEM((len(arrived) * count // feat, rows, feat), BF16),
             pltpu.VMEM((rows, feat), BF16),
-            pltpu.SemaphoreType.DMA((1 + 2 * (feat // block) + len(arrived),)),
+            pltpu.SemaphoreType.DMA((2 * len(blocks),)),
         ],
-        24,
+        16,
         "finish",
         6,
     )[0]
@@ -462,25 +453,27 @@
     upper = lax.axis_index("ctx") % 2 == 1
     dk_hbm, dv_hbm, kbuf, vbuf, facts_ref, dkbuf, dvbuf, kside, vside, sems = refs[-10:]
     dks, dvs = rest[: len(rest) // 2], rest[len(rest) // 2 :]
-    each = heads // len(dks)
+    pair = 2 if all(edge % 2 == 0 for span in spans_of(heads) for edge in span) else 1
     copies = Copies(sems)
     facts_in = copies.start(facts_hbm, facts_ref)
     loads = []
-    for part, (dk, dv) in enumerate(zip(dks, dvs)):
-        wide = pl.ds(part * each * HDIM, each * HDIM)
-        loads.append(
-            (
-                copies.start(v_hbm.at[:, wide], vbuf.at[:, wide]),
-                copies.start(dk, dkbuf.at[:, wide]),
-                copies.start(in_hbm.at[:, wide], kbuf.at[:, wide]),
-                copies.start(dv, dvbuf.at[:, wide]),
+    for (start, last), dk, dv in zip(spans_of(heads), dks, dvs):
+        for h in range(start, last, pair):
+            wide = pl.ds(h * HDIM, pair * HDIM)
+            part = pl.ds((h - start) * HDIM, pair * HDIM)
+            loads.append(
+                (
+                    copies.start(v_hbm.at[:, wide], vbuf.at[:, wide]),
+                    copies.start(dk.at[:, part], dkbuf.at[:, wide]),
+                    copies.start(in_hbm.at[:, wide], kbuf.at[:, wide]),
+                    copies.start(dv.at[:, part], dvbuf.at[:, wide]),
+                )
             )
-        )
     facts_in.wait()
     table = turned(facts_ref[...])
     for h in range(heads):
-        if h % each == 0:
-            for copy in loads[h // each]:
+        if h % pair == 0:
+            for copy in loads[h // pair]:
                 copy.wait()
         cols = slice(h * HDIM, (h + 1) * HDIM)
         adjoint = whole_head(upper, h, mine_ref, theirs_ref)
@@ -489,8 +482,8 @@
         kside[:, cols] = (gain * (dkbuf[:, cols].astype(F32) + tail * carry_k)).astype(BF16)
         carry_v = dot(scaled_keys(table, hp, h, kbuf[:, cols]), adjoint, NN)
         vside[:, cols] = (dvbuf[:, cols].astype(F32) + tail * carry_v).astype(BF16)
-        if (h + 1) % each == 0:
-            wide = slice((h + 1 - each) * HDIM, (h + 1) * HDIM)
+        if (h + 1) % pair == 0:
+            wide = slice((h + 1 - pair) * HDIM, (h + 1) * HDIM)
             copies.store(kside.at[:, wide], dk_hbm.at[:, wide])
             copies.store(vside.at[:, wide], dv_hbm.at[:, wide])
     copies.finish()
@@ -514,7 +507,7 @@
             buf,
             buf,
             buf,
-            pltpu.SemaphoreType.DMA((1 + 6 * len(dks),)),
+            pltpu.SemaphoreType.DMA((1 + 6 * heads,)),
         ],
         20,
         "close",
@@ -549,13 +542,9 @@
     stages = (ctx_size - 1).bit_length()
     uppers = [(me & (1 << stage)) != 0 for stage in range(stages)]
 
-    def send(array, stage, up):
+    def send(array, stage):
         dist = 1 << (stage % stages)
-        if stage != stages - 1:
-            pairs = [(i, i ^ dist) for i in range(ctx_size)]
-        else:
-            pairs = [(i, i + dist) if up else (i + dist, i) for i in range(ctx_size) if not i & dist]
-        return lax.ppermute(array, "ctx", pairs)
+        return lax.ppermute(array, "ctx", [(i, i ^ dist) for i in range(ctx_size)])
 
     shares, others = [share], []
     before, after = [jnp.ones_like(share)], [jnp.ones_like(share)]
@@ -592,7 +581,7 @@
             self.total, self.carried, self.stage, self.arrived = cube(kept), jnp.zeros_like(cube(kept)), 0, None
 
         def go(self):
-            self.arrived = send(self.sent, self.stage, self.up)
+            self.arrived = send(self.sent, self.stage)
 
         def take(self):
             stage, self.stage = self.stage, self.stage + 1
@@ -606,8 +595,8 @@
                 self.sent = jnp.concatenate([self.sent, *split(shares[-1])], axis=0)
 
     states, adjoints = Chain(kept, sent, True), Chain(akept, asent, False)
-    half = max(1, heads // 2)
-    pending = [(first, first + half) for first in range(0, heads, half)]
+    spans = spans_of(heads)
+    pending = list(spans)
     inner_parts = []
     barrier = lax.optimization_barrier
     for stage in range(stages + 1):
@@ -619,7 +608,7 @@
             adjoints.total = cube(adjoints.kept)
         else:
             adjoints.go()
-            if pending:
+            if pending and stage <= len(spans):
                 query, _ = barrier((query, adjoints.sent))
                 part = inner(*pending.pop(0), query, keys, values, d_out, facts, hp)
                 states.arrived, *part = barrier((states.arrived, *part))

time: 66.4 us -> 67.5 us (1.017)
  Pallas kernels: 37.7 us -> 43 us
  starting transfers between devices: 17.1 us -> 14.3 us
  waiting for transfers between devices: 9.28 us -> 7.87 us
    pallas_call x7 -> x8, Pallas kernels: 37.7 us -> 43 us  [kernel_call(): pl.pallas_call(kernel, in_specs=specs, out_specs=tuple(out_specs), out_sh...]
    ppermute x10, starting transfers between devices: 16.5 us -> 13.8 us  [send(): return lax.ppermute(array, 'ctx', [(i, i ^ dist) for i in range(ctx_size)])]
    ppermute x10, waiting for transfers between devices: 9.11 us -> 7.87 us  [send(): return lax.ppermute(array, 'ctx', [(i, i ^ dist) for i in range(ctx_size)])]
  transfers between devices with their start and end apart: 12 -> 12, of which waited for: 4 -> 3; matrix products, arithmetic and copies ran while one was open for 1% -> 1% of each run, Pallas kernels for 49% -> 55%
where the time goes in v9:
time: 67.5 us; the launch traced here: 67.2 us
  Pallas kernels  43 us (64%)
  starting transfers between devices  14.3 us (21%)
  waiting for transfers between devices  7.87 us (12%)
  other arithmetic  1.07 us (2%)
  between operations  0.99 us (1%)
    pallas_call x8, Pallas kernels, kernel_call(): pl.pallas_call(kernel, in_specs=specs, out_specs=tuple(out_specs), out_sh...  43 us
    ppermute x10, starting transfers between devices, send(): return lax.ppermute(array, 'ctx', [(i, i ^ dist) for i in range(ctx_size)])  13.8 us
    ppermute x10, waiting for transfers between devices, send(): return lax.ppermute(array, 'ctx', [(i, i ^ dist) for i in range(ctx_size)])  7.87 us
  transfers between devices with their start and end apart: 12, of which 3 were waited for; matrix products, arithmetic and copies ran while one was open for 1% of the time, Pallas kernels for 55%

profile of v9, /device:TPU:0, one launch (start us, length us, event | category | flops | bytes accessed | tf_op | source)
XLA Modules:
  0.0 67.2 jit_solution(8461138540411837200)
XLA Ops:
  0.6 0.5 collective-permute-start.1
  1.1 3.7 %prepare.1 = (f32[32,512]{1,0:T(8,128)}, bf16[512,128]{1,0:T(8,128)(2,1)S(1)}, bf16[528,128]{1,0:T(8,128)(2,1)S(1)}, f32[8,128]{1,0:T(8,128)S(1)}) custom-call(f32[8,512]{1,0:T(8,128)} %bitcast.126, bf16[512,1024]{1,0:T(8,128)(2,1)} %refs_2_.11, bf16[512,1024]{1,0:T(8,128)(2,1)} %refs_3_.9), custom_call_target="tpu_custom_call" | custom-call | flops 4000000000 | bytes 1 | tf_op jit(solution)/shard_map/prepare/pallas_call | solution.py:34
  4.8 2.6 %collective-permute-start = (bf16[528,128]{1,0:T(8,128)(2,1)S(1)}, bf16[528,128]{1,0:T(8,128)(2,1)S(1)}, u32[]{:S(2)}, u32[]{:S(2)}) collective-permute-start(bf16[528,128]{1,0:T(8,128)(2,1)S(1)} %get-tuple-element.47), channel_id=1, source_target_pairs={{0,2},{2,0},{4,6},{6,4},{8,10},{10,8},{12,14},{14,12},{16,18},{18,... | collective-permute-start | bytes 405512 | tf_op jit(solution)/shard_map/ppermute | solution.py:547
  7.4 0.1 pad_add_fusion.place_ref
  7.5 10.0 %project.1 = (bf16[512,1024]{1,0:T(8,128)(2,1)}, bf16[512,128]{1,0:T(8,128)(2,1)S(1)}, bf16[512,128]{1,0:T(8,128)(2,1)S(1)}) custom-call(s32[2]{0:T(128)S(1)} %pad_add_fusion.place_ref, bf16[512,2048]{1,0:T(8,128)(2,1)} %refs_0_.1, bf16[512,2048]{1,0:T(8,128)(2,1)S(1)} %collective-permute-done.1.refs_1_, bf16[4096,1024]{1,0:T(8,128)(2,1)} %w_hbm.1, ...), custom_call_target="tpu_custom_call" | custom-call | flops 8000000000 | bytes 1 | tf_op jit(solution)/shard_map/project/pallas_call | solution.py:34
  17.5 0.1 fusion.21
  17.6 1.6 %collective-permute-start.2 = (bf16[528,128]{1,0:T(8,128)(2,1)S(1)}, bf16[528,128]{1,0:T(8,128)(2,1)S(1)}, u32[]{:S(2)}, u32[]{:S(2)}) collective-permute-start(bf16[528,128]{1,0:T(8,128)(2,1)S(1)} %pad_maximum_fusion), channel_id=1, source_target_pairs={{0,4},{2,6},{4,0},{6,2},{8,12},{10,14},{12,8},{14,10},{16,20},{18,... | collective-permute-start | bytes 405512 | tf_op jit(solution)/shard_map/ppermute | solution.py:547
  19.2 0.5 collective-permute-start.4
  19.7 5.0 %inner.3 = (bf16[512,512]{1,0:T(8,128)(2,1)}, bf16[512,512]{1,0:T(8,128)(2,1)}, bf16[512,512]{1,0:T(8,128)(2,1)}) custom-call(bf16[512,1024]{1,0:T(8,128)(2,1)} %get-tuple-element.70.refs_0_, bf16[512,1024]{1,0:T(8,128)(2,1)} %refs_2_.11, bf16[512,1024]{1,0:T(8,128)(2,1)} %refs_3_.9, bf16[512,1024]{1,0:T(8,128)(2,1)} %refs_2_.10, ...), custom_call_target="tpu_custom_call" | custom-call | flops 1000000000 | bytes 1 | tf_op jit(solution)/shard_map/inner/pallas_call | solution.py:34
  24.7 0.1 fusion.23
  24.9 1.6 %collective-permute-start.3 = (bf16[528,128]{1,0:T(8,128)(2,1)S(1)}, bf16[528,128]{1,0:T(8,128)(2,1)S(1)}, u32[]{:S(2)}, u32[]{:S(2)}) collective-permute-start(bf16[528,128]{1,0:T(8,128)(2,1)S(1)} %pad_maximum_fusion.1), channel_id=1, source_target_pairs={{0,8},{2,10},{4,12},{6,14},{8,0},{10,2},{12,4},{14,6},{16,24},{18,... | collective-permute-start | bytes 405512 | tf_op jit(solution)/shard_map/ppermute | solution.py:547
  26.5 0.1 fusion.20
  26.6 0.6 collective-permute-start.6
  27.2 3.5 %inner.4 = (bf16[512,256]{1,0:T(8,128)(2,1)}, bf16[512,256]{1,0:T(8,128)(2,1)}, bf16[512,256]{1,0:T(8,128)(2,1)}) custom-call(bf16[512,1024]{1,0:T(8,128)(2,1)} %get-tuple-element.70.refs_0_, bf16[512,1024]{1,0:T(8,128)(2,1)} %refs_2_.11, bf16[512,1024]{1,0:T(8,128)(2,1)} %refs_3_.9, bf16[512,1024]{1,0:T(8,128)(2,1)} %refs_2_.10, ...), custom_call_target="tpu_custom_call" | custom-call | flops 1000000000 | bytes 1 | tf_op jit(solution)/shard_map/inner/pallas_call | solution.py:34
  30.7 0.1 fusion.14
  30.8 2.7 %collective-permute-start.5 = (bf16[512,128]{1,0:T(8,128)(2,1)S(1)}, bf16[512,128]{1,0:T(8,128)(2,1)S(1)}, u32[]{:S(2)}, u32[]{:S(2)}) collective-permute-start(bf16[512,128]{1,0:T(8,128)(2,1)S(1)} %fusion.14), channel_id=1, source_target_pairs={{0,16},{2,18},{4,20},{6,22},{8,24},{10,26},{12,28},{14,30},{16,0},... | collective-permute-start | bytes 393224 | tf_op jit(solution)/shard_map/ppermute | solution.py:547
  33.5 0.1 fusion.22
  33.6 1.0 %collective-permute-start.8 = (bf16[512,128]{1,0:T(8,128)(2,1)S(1)}, bf16[512,128]{1,0:T(8,128)(2,1)S(1)}, u32[]{:S(2)}, u32[]{:S(2)}) collective-permute-start(bf16[512,128]{1,0:T(8,128)(2,1)S(1)} %fusion.22), channel_id=1, source_target_pairs={{0,8},{2,10},{4,12},{6,14},{8,0},{10,2},{12,4},{14,6},{16,24},{18,... | collective-permute-start | bytes 393224 | tf_op jit(solution)/shard_map/ppermute | solution.py:547
  34.6 3.5 %inner.5 = (bf16[512,256]{1,0:T(8,128)(2,1)}, bf16[512,256]{1,0:T(8,128)(2,1)}, bf16[512,256]{1,0:T(8,128)(2,1)}) custom-call(bf16[512,1024]{1,0:T(8,128)(2,1)} %get-tuple-element.70.refs_0_, bf16[512,1024]{1,0:T(8,128)(2,1)} %refs_2_.11, bf16[512,1024]{1,0:T(8,128)(2,1)} %refs_3_.9, bf16[512,1024]{1,0:T(8,128)(2,1)} %refs_2_.10, ...), custom_call_target="tpu_custom_call" | custom-call | flops 1000000000 | bytes 1 | tf_op jit(solution)/shard_map/inner/pallas_call | solution.py:34
  38.2 1.0 %collective-permute-done.5 = bf16[512,128]{1,0:T(8,128)(2,1)S(1)} collective-permute-done((bf16[512,128]{1,0:T(8,128)(2,1)S(1)}, bf16[512,128]{1,0:T(8,128)(2,1)S(1)}, u32[]{:S(2)}, u32[]{:S(2)}) %collective-permute-start.5) | collective-permute-done | bytes 131104 | tf_op jit(solution)/shard_map/ppermute | solution.py:547
  39.2 0.2 fusion.4
  39.4 1.1 %collective-permute-done.8 = bf16[512,128]{1,0:T(8,128)(2,1)S(1)} collective-permute-done((bf16[512,128]{1,0:T(8,128)(2,1)S(1)}, bf16[512,128]{1,0:T(8,128)(2,1)S(1)}, u32[]{:S(2)}, u32[]{:S(2)}) %collective-permute-start.8) | collective-permute-done | bytes 131104 | tf_op jit(solution)/shard_map/ppermute | solution.py:547
  40.5 0.1 fusion.19
  40.6 0.1 collective-permute-start.9
  40.7 1.6 %collective-permute-start.7 = (bf16[512,128]{1,0:T(8,128)(2,1)S(1)}, bf16[512,128]{1,0:T(8,128)(2,1)S(1)}, u32[]{:S(2)}, u32[]{:S(2)}) collective-permute-start(bf16[512,128]{1,0:T(8,128)(2,1)S(1)} %get-tuple-element.101), channel_id=1, source_target_pairs={{0,2},{2,0},{4,6},{6,4},{8,10},{10,8},{12,14},{14,12},{16,18},{18,... | collective-permute-start | bytes 393224 | tf_op jit(solution)/shard_map/ppermute | solution.py:547
  42.3 5.7 %collective-permute-done.9 = bf16[512,128]{1,0:T(8,128)(2,1)S(1)} collective-permute-done((bf16[512,128]{1,0:T(8,128)(2,1)S(1)}, bf16[512,128]{1,0:T(8,128)(2,1)S(1)}, u32[]{:S(2)}, u32[]{:S(2)}) %collective-permute-start.9) | collective-permute-done | bytes 131104 | tf_op jit(solution)/shard_map/ppermute | solution.py:547
  48.0 0.2 fusion.12
  48.1 1.5 %collective-permute-start.11 = (bf16[512,128]{1,0:T(8,128)(2,1)S(1)}, bf16[512,128]{1,0:T(8,128)(2,1)S(1)}, u32[]{:S(2)}, u32[]{:S(2)}) collective-permute-start(bf16[512,128]{1,0:T(8,128)(2,1)S(1)} %get-tuple-element.104), channel_id=1, source_target_pairs={{0,2},{2,0},{4,6},{6,4},{8,10},{10,8},{12,14},{14,12},{16,18},{18,... | collective-permute-start | bytes 393224 | tf_op jit(solution)/shard_map/ppermute | solution.py:547
  49.7 6.8 %query_term.1 = (bf16[512,1024]{1,0:T(8,128)(2,1)S(1)}, bf16[512,2048]{1,0:T(8,128)(2,1)S(1)}) custom-call(s32[1]{0:T(128)} %bitcast.1.place_ref, bf16[512,128]{1,0:T(8,128)(2,1)S(1)} %get-tuple-element.102.refs_0_, bf16[512,128]{1,0:T(8,128)(2,1)S(1)} %collective-permute-done.7.refs_1_, bf16[512,1024]{1,0:T(8,128)(2,1)} %refs_2_.10, ...), custom_call_target="tpu_custom_call" | custom-call | flops 6000000000 | bytes 1 | tf_op jit(solution)/shard_map/query_term/pallas_call | solution.py:34
  56.5 0.1 collective-permute-start.10
  56.6 4.2 %close.1 = (bf16[512,1024]{1,0:T(8,128)(2,1)}, bf16[512,1024]{1,0:T(8,128)(2,1)}) custom-call(bf16[512,128]{1,0:T(8,128)(2,1)S(1)} %get-tuple-element.103.refs_0_, bf16[512,128]{1,0:T(8,128)(2,1)S(1)} %collective-permute-done.11.refs_1_, bf16[512,1024]{1,0:T(8,128)(2,1)} %refs_2_.11, bf16[512,1024]{1,0:T(8,128)(2,1)} %refs_3_.9, ...), custom_call_target="tpu_custom_call" | custom-call | flops 99999997952 | bytes 1 | tf_op jit(solution)/shard_map/close/pallas_call | solution.py:34
  60.8 6.3 %finish.1 = bf16[512,2048]{1,0:T(8,128)(2,1)} custom-call(s32[1]{0:T(128)} %bitcast.place_ref, bf16[512,1024]{1,0:T(8,128)(2,1)S(1)} %get-tuple-element.81.dq_ref, bf16[4096,1024]{1,0:T(8,128)(2,1)} %w_hbm.1, bf16[512,2048]{1,0:T(8,128)(2,1)S(1)} %collective-permute-done.10.refs_0_), custom_call_target="tpu_custom_call" | custom-call | flops 6000000000 | bytes 1 | tf_op jit(solution)/shard_map/finish/pallas_call | solution.py:34
  (17 shorter events, 0.1 us)
Async XLA Ops:
  0.6 6.8 %collective-permute-start.1 = (bf16[512,2048]{1,0:T(8,128)(2,1)}, bf16[512,2048]{1,0:T(8,128)(2,1)S(1)}, u32[]{:S(2)}, u32[]{:S(2)}) collective-permute-start(bf16[512,2048]{1,0:T(8,128)(2,1)} %refs_0_.1), channel_id=1, source_target_pairs={{0,1},{1,0},{2,3},{3,2},{4,5},{5,4},{6,7},{7,6},{8,9},{9,8},{10,11... | collective-permute-start | bytes 6291464 | tf_op jit(solution)/shard_map/ppermute | solution.py:530
  4.8 12.7 %collective-permute-start = (bf16[528,128]{1,0:T(8,128)(2,1)S(1)}, bf16[528,128]{1,0:T(8,128)(2,1)S(1)}, u32[]{:S(2)}, u32[]{:S(2)}) collective-permute-start(bf16[528,128]{1,0:T(8,128)(2,1)S(1)} %get-tuple-element.47), channel_id=1, source_target_pairs={{0,2},{2,0},{4,6},{6,4},{8,10},{10,8},{12,14},{14,12},{16,18},{18,... | collective-permute-start | bytes 405512 | tf_op jit(solution)/shard_map/ppermute | solution.py:547
  17.6 7.1 %collective-permute-start.2 = (bf16[528,128]{1,0:T(8,128)(2,1)S(1)}, bf16[528,128]{1,0:T(8,128)(2,1)S(1)}, u32[]{:S(2)}, u32[]{:S(2)}) collective-permute-start(bf16[528,128]{1,0:T(8,128)(2,1)S(1)} %pad_maximum_fusion), channel_id=1, source_target_pairs={{0,4},{2,6},{4,0},{6,2},{8,12},{10,14},{12,8},{14,10},{16,20},{18,... | collective-permute-start | bytes 405512 | tf_op jit(solution)/shard_map/ppermute | solution.py:547
  19.2 7.3 %collective-permute-start.4 = (bf16[512,128]{1,0:T(8,128)(2,1)S(1)}, bf16[512,128]{1,0:T(8,128)(2,1)S(1)}, u32[]{:S(2)}, u32[]{:S(2)}) collective-permute-start(bf16[512,128]{1,0:T(8,128)(2,1)S(1)} %get-tuple-element.56), channel_id=1, source_target_pairs={{0,2},{2,0},{4,6},{6,4},{8,10},{10,8},{12,14},{14,12},{16,18},{18,... | collective-permute-start | bytes 393224 | tf_op jit(solution)/shard_map/ppermute | solution.py:547
  24.9 5.8 %collective-permute-start.3 = (bf16[528,128]{1,0:T(8,128)(2,1)S(1)}, bf16[528,128]{1,0:T(8,128)(2,1)S(1)}, u32[]{:S(2)}, u32[]{:S(2)}) collective-permute-start(bf16[528,128]{1,0:T(8,128)(2,1)S(1)} %pad_maximum_fusion.1), channel_id=1, source_target_pairs={{0,8},{2,10},{4,12},{6,14},{8,0},{10,2},{12,4},{14,6},{16,24},{18,... | collective-permute-start | bytes 405512 | tf_op jit(solution)/shard_map/ppermute | solution.py:547
  26.6 6.9 %collective-permute-start.6 = (bf16[512,128]{1,0:T(8,128)(2,1)S(1)}, bf16[512,128]{1,0:T(8,128)(2,1)S(1)}, u32[]{:S(2)}, u32[]{:S(2)}) collective-permute-start(bf16[512,128]{1,0:T(8,128)(2,1)S(1)} %fusion.20), channel_id=1, source_target_pairs={{0,4},{2,6},{4,0},{6,2},{8,12},{10,14},{12,8},{14,10},{16,20},{18,... | collective-permute-start | bytes 393224 | tf_op jit(solution)/shard_map/ppermute | solution.py:547
  30.8 8.4 %collective-permute-start.5 = (bf16[512,128]{1,0:T(8,128)(2,1)S(1)}, bf16[512,128]{1,0:T(8,128)(2,1)S(1)}, u32[]{:S(2)}, u32[]{:S(2)}) collective-permute-start(bf16[512,128]{1,0:T(8,128)(2,1)S(1)} %fusion.14), channel_id=1, source_target_pairs={{0,16},{2,18},{4,20},{6,22},{8,24},{10,26},{12,28},{14,30},{16,0},... | collective-permute-start | bytes 393224 | tf_op jit(solution)/shard_map/ppermute | solution.py:547
  33.6 6.9 %collective-permute-start.8 = (bf16[512,128]{1,0:T(8,128)(2,1)S(1)}, bf16[512,128]{1,0:T(8,128)(2,1)S(1)}, u32[]{:S(2)}, u32[]{:S(2)}) collective-permute-start(bf16[512,128]{1,0:T(8,128)(2,1)S(1)} %fusion.22), channel_id=1, source_target_pairs={{0,8},{2,10},{4,12},{6,14},{8,0},{10,2},{12,4},{14,6},{16,24},{18,... | collective-permute-start | bytes 393224 | tf_op jit(solution)/shard_map/ppermute | solution.py:547
  40.6 7.3 %collective-permute-start.9 = (bf16[512,128]{1,0:T(8,128)(2,1)S(1)}, bf16[512,128]{1,0:T(8,128)(2,1)S(1)}, u32[]{:S(2)}, u32[]{:S(2)}) collective-permute-start(bf16[512,128]{1,0:T(8,128)(2,1)S(1)} %fusion.19), channel_id=1, source_target_pairs={{0,16},{2,18},{4,20},{6,22},{8,24},{10,26},{12,28},{14,30},{16,0},... | collective-permute-start | bytes 393224 | tf_op jit(solution)/shard_map/ppermute | solution.py:547
  40.7 8.9 %collective-permute-start.7 = (bf16[512,128]{1,0:T(8,128)(2,1)S(1)}, bf16[512,128]{1,0:T(8,128)(2,1)S(1)}, u32[]{:S(2)}, u32[]{:S(2)}) collective-permute-start(bf16[512,128]{1,0:T(8,128)(2,1)S(1)} %get-tuple-element.101), channel_id=1, source_target_pairs={{0,2},{2,0},{4,6},{6,4},{8,10},{10,8},{12,14},{14,12},{16,18},{18,... | collective-permute-start | bytes 393224 | tf_op jit(solution)/shard_map/ppermute | solution.py:547
  48.1 8.4 %collective-permute-start.11 = (bf16[512,128]{1,0:T(8,128)(2,1)S(1)}, bf16[512,128]{1,0:T(8,128)(2,1)S(1)}, u32[]{:S(2)}, u32[]{:S(2)}) collective-permute-start(bf16[512,128]{1,0:T(8,128)(2,1)S(1)} %get-tuple-element.104), channel_id=1, source_target_pairs={{0,2},{2,0},{4,6},{6,4},{8,10},{10,8},{12,14},{14,12},{16,18},{18,... | collective-permute-start | bytes 393224 | tf_op jit(solution)/shard_map/ppermute | solution.py:547
  56.5 4.3 %collective-permute-start.10 = (bf16[512,2048]{1,0:T(8,128)(2,1)S(1)}, bf16[512,2048]{1,0:T(8,128)(2,1)S(1)}, u32[]{:S(2)}, u32[]{:S(2)}) collective-permute-start(bf16[512,2048]{1,0:T(8,128)(2,1)S(1)} %get-tuple-element.82), channel_id=1, source_target_pairs={{0,1},{1,0},{2,3},{3,2},{4,5},{5,4},{6,7},{7,6},{8,9},{9,8},{10,11... | collective-permute-start | bytes 6291464 | tf_op jit(solution)/shard_map/ppermute | solution.py:641

commit v10 on v9

--- a/solution.py
+++ b/solution.py
@@ -100,8 +100,9 @@
 
 
 def prepare_kernel(
-    heads, hp, scaling, ld_hbm, k_hbm, v_hbm, facts_hbm, kept_ref, sent_ref, share_ref, ld, facts_ref, kbuf, vbuf, sems
+    heads, hp, scaling, ld_hbm, k_hbm, v_hbm, facts_hbm, kept_ref, sent_ref, share_ref, *scratch
 ):
+    ld, facts_ref, kbuf, vbuf, sems = scratch
     upper = lax.axis_index("ctx") % 2 == 1
     rows = kbuf.shape[0]
     copies = Copies(sems)
@@ -156,7 +157,12 @@
         functools.partial(prepare_kernel, heads, hp, scaling),
         (logs, keys, values),
         [HB] * 3,
-        [((4 * hp, rows), F32), ((width // 2, HDIM), BF16), ((width // 2 + 2 * hp, HDIM), BF16), ((hp, LANES), F32)],
+        [
+            ((4 * hp, rows), F32),
+            ((width // 2, HDIM), BF16),
+            ((width // 2 + 2 * hp, HDIM), BF16),
+            ((hp, LANES), F32),
+        ],
         (HB, VM, VM, VM),
         [
             pltpu.VMEM((heads, rows), F32),
@@ -171,61 +177,57 @@
     )
 
 
-def project_kernel(hp, nparts, chunks, place_ref, *refs):
+def project_kernel(hp, nparts, chunk, place_ref, *refs):
     parts, (w_hbm, do_hbm, facts_hbm, q_hbm, kept_ref, sent_ref) = refs[:nparts], refs[nparts : nparts + 6]
     hbuf, wbuf, dobuf, facts_ref, qbuf, total, sems = refs[nparts + 6 :]
     rows, feat = parts[0].shape
     width = wbuf.shape[1]
+    heads = width // HDIM
     upper = lax.axis_index("ctx") % 2 == 1
     copies = Copies(sems)
     loads = []
-    for part, first, size in chunks:
-        at = part * feat + first
-        start = pl.multiple_of(place_ref[part] * feat + first, math.gcd(feat, first) if first else feat)
-        loads.append(
-            (
-                slice(at, at + size),
-                copies.start(parts[part].at[:, pl.ds(first, size)], hbuf.at[:, pl.ds(at, size)]),
-                copies.start(w_hbm.at[pl.ds(start, size), :], wbuf.at[pl.ds(at, size), :]),
+    for part, ref in enumerate(parts):
+        for first in range(0, feat, chunk):
+            here = pl.ds(part * feat + first, chunk)
+            start = pl.multiple_of(place_ref[part] * feat + first, chunk)
+            loads.append(
+                (
+                    slice(part * feat + first, part * feat + first + chunk),
+                    copies.start(ref.at[:, pl.ds(first, chunk)], hbuf.at[:, here]),
+                    copies.start(w_hbm.at[pl.ds(start, chunk), :], wbuf.at[here, :]),
+                )
             )
-        )
-        if len(loads) == min(4, len(chunks)):
-            late = [copies.start(facts_hbm, facts_ref), copies.start(do_hbm, dobuf)]
+    late = [copies.start(facts_hbm, facts_ref), copies.start(do_hbm, dobuf)]
     block = min(256, width)
     for order, (here, h_in, w_in) in enumerate(loads):
         h_in.wait()
         w_in.wait()
-        if order == len(loads) - 1:
-            for copy in late:
-                copy.wait()
-            table = turned(facts_ref[...])
         for first in range(0, width, block):
             wide = slice(first, first + block)
             term = dot(hbuf[:, here], wbuf[here, wide], NN)
-            if order > 0:
-                term = total[:, wide] + term
-            if order < len(loads) - 1:
+            if order == 0:
                 total[:, wide] = term
-                continue
-            qbuf[:, wide] = term.astype(BF16)
-            copies.store(qbuf.at[:, wide], q_hbm.at[:, wide])
-            for h in range(first // HDIM, (first + block) // HDIM):
-                cols = slice(h * HDIM, (h + 1) * HDIM)
-                decayed = (column(table, 3 * hp + h) * qbuf[:, cols].astype(F32)).astype(BF16)
-                put_halves(upper, h, dot(decayed, dobuf[:, cols], TN), kept_ref, sent_ref)
+            elif order < len(loads) - 1:
+                total[:, wide] += term
+            else:
+                qbuf[:, wide] = (total[:, wide] + term).astype(BF16)
+    for copy in late:
+        copy.wait()
+    copies.store(qbuf, q_hbm)
+    table = turned(facts_ref[...])
+    for h in range(heads):
+        cols = slice(h * HDIM, (h + 1) * HDIM)
+        decayed = (column(table, 3 * hp + h) * qbuf[:, cols].astype(F32)).astype(BF16)
+        put_halves(upper, h, dot(decayed, dobuf[:, cols], TN), kept_ref, sent_ref)
     copies.finish()
 
 
 def project(parts, owners, w_query, d_out, facts, hp):
     rows, feat = parts[0].shape
     depth, width = w_query.shape
-    chunks = []
-    for part in range(len(parts)):
-        sizes = [feat] if feat % 1024 else ([256, 256, 512] + [1024] * (feat // 1024 - 1) if part == 0 else [1024] * (feat // 1024))
-        for order, size in enumerate(sizes):
-            chunks.append((part, sum(sizes[:order]), size))
-    return kernel_call(
-        functools.partial(project_kernel, hp, len(parts), chunks),
+    chunk = min(512, feat)
+    return kernel_call(
+        functools.partial(project_kernel, hp, len(parts), chunk),
         (owners, *parts, w_query, d_out, facts),
         [SM, HB] + [AN] * (len(parts) - 1) + [HB] * 3,
         [((rows, width), BF16), ((width // 2, HDIM), BF16), ((width // 2, HDIM), BF16)],
@@ -237,7 +239,7 @@
             pltpu.VMEM(facts.shape, F32),
             pltpu.VMEM((rows, width), BF16),
             pltpu.VMEM((rows, width), F32),
-            pltpu.SemaphoreType.DMA((2 * len(chunks) + 2 + width // min(256, width),)),
+            pltpu.SemaphoreType.DMA((2 * len(parts) * (feat // chunk) + 3,)),
         ],
         28,
         "project",
@@ -315,19 +317,35 @@
     return jnp.concatenate([jnp.where(upper, theirs, mine), jnp.where(upper, mine, theirs)], axis=0)
 
 
-def load_weight(copies, place_ref, first, w_hbm, wbuf, feat, blocks):
-    loads, at = [], 0
-    for block in blocks:
-        start = pl.multiple_of(place_ref[0] * feat + first + at, block)
-        loads.append((at, block, copies.start(w_hbm.at[pl.ds(start, block), :], wbuf.at[pl.ds(at, block), :])))
-        at += block
-    return loads
-
-
-def query_kernel(heads, hp, feat, blocks, place_ref, *refs):
-    mine_ref, theirs_ref, do_hbm, facts_hbm, w_hbm = refs[:5]
-    inner_hbm = refs[5:-7]
-    held, out_ref, dobuf, facts_ref, wbuf, local, sems = refs[-7:]
+def fetch_kernel(place_ref, w_hbm, *refs):
+    outs, sems = refs[:-1], refs[-1]
+    copies = Copies(sems)
+    for index, out in enumerate(outs):
+        feat = out.shape[0]
+        start = pl.multiple_of(place_ref[index] * feat, feat)
+        copies.store(w_hbm.at[pl.ds(start, feat), :], out)
+    copies.finish()
+
+
+def fetch(places, w_query, feat):
+    count = places.shape[0]
+    return kernel_call(
+        fetch_kernel,
+        (places, w_query),
+        [SM, HB],
+        [((feat, w_query.shape[1]), BF16)] * count,
+        (VM,) * count,
+        [pltpu.SemaphoreType.DMA((count,))],
+        2,
+        "fetch",
+        4,
+    )
+
+
+def query_kernel(heads, hp, *refs):
+    mine_ref, theirs_ref, w_ref, do_hbm, facts_hbm = refs[:5]
+    inner_hbm = refs[5:-6]
+    held, out_ref, dobuf, facts_ref, local, sems = refs[-6:]
     upper = lax.axis_index("ctx") % 2 == 1
     copies = Copies(sems)
     facts_in = copies.start(facts_hbm, facts_ref)
@@ -335,7 +353,6 @@
     for (first, last), src in zip(spans_of(heads), inner_hbm):
         wide = pl.ds(first * HDIM, (last - first) * HDIM)
         loads[first] = (copies.start(do_hbm.at[:, wide], dobuf.at[:, wide]), copies.start(src, local.at[:, wide]))
-    w_in = load_weight(copies, place_ref, 0, w_hbm, wbuf, feat, blocks)
     facts_in.wait()
     table = turned(facts_ref[...])
     for h in range(heads):
@@ -345,103 +362,78 @@
         state = whole_head(upper, h, mine_ref, theirs_ref)
         carry = dot(dobuf[:, cols], state, NT)
         held[:, cols] = (local[:, cols].astype(F32) + column(table, 3 * hp + h) * carry).astype(BF16)
-    put_terms(w_in, held, wbuf, out_ref)
-
-
-def put_terms(w_in, dq_ref, wbuf, out_ref):
-    for at, block, copy in w_in:
-        copy.wait()
-        wide = slice(at, at + block)
-        out_ref[:, wide] = dot(dq_ref[...], wbuf[wide, :], NT).astype(BF16)
-
-
-def query_term(halves, inner_dq, d_out, facts, w_query, place, feat, count, heads, hp):
+    put_terms(held, w_ref, out_ref)
+
+
+def put_terms(dq_ref, w_ref, out_ref):
+    block = min(512, out_ref.shape[1])
+    for at in range(0, out_ref.shape[1], block):
+        out_ref[:, at : at + block] = dot(dq_ref[...], w_ref[at : at + block, :], NT).astype(BF16)
+
+
+def query_term(halves, inner_dq, d_out, facts, weight, heads, hp):
     rows, width = d_out.shape
-    blocks = blocks_of(count)
-    args = (d_out, facts, w_query, *inner_dq)
-    return kernel_call(
-        functools.partial(query_kernel, heads, hp, feat, blocks),
-        (place, *halves, *args),
-        [SM, VM, VM] + [HB] * len(args),
-        [((rows, width), BF16), ((rows, count), BF16)],
+    args = (d_out, facts, *inner_dq)
+    return kernel_call(
+        functools.partial(query_kernel, heads, hp),
+        (*halves, weight, *args),
+        [VM, VM, VM] + [HB] * len(args),
+        [((rows, width), BF16), ((rows, weight.shape[0]), BF16)],
         (VM, VM),
         [
             pltpu.VMEM((rows, width), BF16),
             pltpu.VMEM(facts.shape, F32),
-            pltpu.VMEM((count, width), BF16),
             pltpu.VMEM((rows, width), BF16),
-            pltpu.SemaphoreType.DMA((1 + 2 * len(inner_dq) + len(blocks),)),
+            pltpu.SemaphoreType.DMA((1 + 2 * len(inner_dq),)),
         ],
-        16,
+        12,
         "query_term",
         6,
     )
 
 
-def term_kernel(feat, first, blocks, place_ref, dq_ref, w_hbm, out_ref, wbuf, sems):
-    copies = Copies(sems)
-    put_terms(load_weight(copies, place_ref, first, w_hbm, wbuf, feat, blocks), dq_ref, wbuf, out_ref)
-
-
-def plain_term(d_query, w_query, place, feat, first, count):
-    rows, width = d_query.shape
-    blocks = blocks_of(count)
-    return kernel_call(
-        functools.partial(term_kernel, feat, first, blocks),
-        (place, d_query, w_query),
-        [SM, VM, HB],
-        [((rows, count), BF16)],
+def plain_term(d_query, weight):
+    return kernel_call(
+        put_terms,
+        (d_query, weight),
+        [VM, VM],
+        [((d_query.shape[0], weight.shape[0]), BF16)],
         (VM,),
-        [
-            pltpu.VMEM((count, width), BF16),
-            pltpu.SemaphoreType.DMA((len(blocks),)),
-        ],
-        16,
+        [],
+        12,
         "term",
         4,
     )[0]
 
 
-def finish_kernel(count, blocks, place_ref, dq_ref, w_hbm, *refs):
-    arrived, (out_hbm, wbuf, sent, sems) = refs[:-4], refs[-4:]
+def finish_kernel(dq_ref, w_ref, *refs):
+    arrived, (out_hbm, sent, sems) = refs[:-3], refs[-3:]
     feat = sent.shape[1]
-    per = feat // count
     copies = Copies(sems)
-    w_in = load_weight(copies, place_ref, 0, w_hbm, wbuf, feat, blocks)
-    for at, block, copy in w_in:
-        copy.wait()
+    block = min(512, feat)
+    for at in range(0, feat, block):
         wide = slice(at, at + block)
-        total = dot(dq_ref[...], wbuf[wide, :], NT).astype(BF16).astype(F32)
-        part, here = at // count, slice(at % count, at % count + block)
-        for shift in range(len(arrived) // per):
-            total = total + arrived[shift * per + part][:, here].astype(F32)
+        total = dot(dq_ref[...], w_ref[wide, :], NT).astype(BF16).astype(F32)
+        for other in arrived:
+            total = total + other[:, wide].astype(F32)
         sent[:, wide] = total.astype(BF16)
         copies.store(sent.at[:, wide], out_hbm.at[:, wide])
     copies.finish()
 
 
-def blocks_of(count):
-    if count % 512 or count < 1024:
-        return [count]
-    return [256, 256] + [512] * (count // 512 - 2) + [256, 256]
-
-
-def finish(d_query, w_query, place, arrived, feat):
-    rows, width = d_query.shape
-    count = arrived[0].shape[1]
-    blocks = blocks_of(feat) if count == feat else [count] * (feat // count)
-    return kernel_call(
-        functools.partial(finish_kernel, count, blocks),
-        (place, d_query, w_query, *arrived),
-        [SM, VM, HB] + [VM] * len(arrived),
+def finish(d_query, weight, arrived):
+    rows, feat = d_query.shape[0], weight.shape[0]
+    return kernel_call(
+        finish_kernel,
+        (d_query, weight, *arrived),
+        [VM, VM] + [VM] * len(arrived),
         [((rows, feat), BF16)],
         (HB,),
         [
-            pltpu.VMEM((feat, width), BF16),
             pltpu.VMEM((rows, feat), BF16),
-            pltpu.SemaphoreType.DMA((2 * len(blocks),)),
+            pltpu.SemaphoreType.DMA((feat // min(512, feat),)),
         ],
-        16,
+        12,
         "finish",
         6,
     )[0]
@@ -599,7 +591,11 @@
     pending = list(spans)
     inner_parts = []
     barrier = lax.optimization_barrier
+    places = jnp.stack([(mine + shift) % head_size for shift in range(head_size)]).astype(jnp.int32)
     for stage in range(stages + 1):
+        if stage == stages:
+            places, _ = barrier((places, adjoints.sent))
+            weights = fetch(places, w_query, feat)
         states.go()
         if stage == 0:
             states.arrived, query, adjoints.kept, adjoints.sent = barrier(
@@ -626,21 +622,16 @@
     adjoint_halves = (adjoints.total, adjoints.arrived)
     dqs, dks, dvs = zip(*inner_parts)
 
-    place = lambda shift: ((mine + shift) % head_size).astype(jnp.int32).reshape(1)
-    count = feat
     arrived = []
     for shift in range(1, head_size):
         ring = [(i, (i + shift) % head_size) for i in range(head_size)]
-        for first in range(0, feat, count):
-            if shift == 1 and first == 0:
-                d_query, term = query_term(
-                    state_halves, dqs, d_out, facts, w_query, place(1), feat, count, heads, hp
-                )
-            else:
-                term = plain_term(d_query, w_query, place(shift), feat, first, count)
-            arrived.append(lax.ppermute(term, "head", ring))
+        if shift == 1:
+            d_query, term = query_term(state_halves, dqs, d_out, facts, weights[shift], heads, hp)
+        else:
+            term = plain_term(d_query, weights[shift])
+        arrived.append(lax.ppermute(term, "head", ring))
     d_keys, d_values = close(adjoint_halves, dks, dvs, keys, values, facts, heads, hp)
-    d_hidden = finish(d_query, w_query, place(0), arrived, feat)
+    d_hidden = finish(d_query, weights[0], arrived)
     return (d_hidden, d_keys, d_values)
 
 

time: 67.5 us -> 60.7 us (0.90)
  waiting for transfers between devices: 7.87 us -> 2.67 us
  Pallas kernels: 43 us -> 40.2 us
  starting transfers between devices: 14.3 us -> 15.5 us
    ppermute x10, waiting for transfers between devices: 7.87 us -> 2.66 us  [send(): return lax.ppermute(array, 'ctx', [(i, i ^ dist) for i in range(ctx_size)])]
    pallas_call x8 -> x9, Pallas kernels: 43 us -> 40.2 us  [kernel_call(): pl.pallas_call(kernel, in_specs=specs, out_specs=tuple(out_specs), out_sh...]
    ppermute x10, starting transfers between devices: 13.8 us -> 14.9 us  [send(): return lax.ppermute(array, 'ctx', [(i, i ^ dist) for i in range(ctx_size)])]
  transfers between devices with their start and end apart: 12 -> 12, of which waited for: 3 -> 2; matrix products, arithmetic and copies ran while one was open for 1% -> 2% of each run, Pallas kernels for 55% -> 61%
where the time goes in v10:
time: 60.7 us; the launch traced here: 60.5 us
  Pallas kernels  40.2 us (66%)
  starting transfers between devices  15.5 us (26%)
  waiting for transfers between devices  2.67 us (4%)
  other arithmetic  1.12 us (2%)
  between operations  1.02 us (2%)
    pallas_call x9, Pallas kernels, kernel_call(): pl.pallas_call(kernel, in_specs=specs, out_specs=tuple(out_specs), out_sh...  40.2 us
    ppermute x10, starting transfers between devices, send(): return lax.ppermute(array, 'ctx', [(i, i ^ dist) for i in range(ctx_size)])  14.9 us
    ppermute x10, waiting for transfers between devices, send(): return lax.ppermute(array, 'ctx', [(i, i ^ dist) for i in range(ctx_size)])  2.66 us
  transfers between devices with their start and end apart: 12, of which 2 were waited for; matrix products, arithmetic and copies ran while one was open for 2% of the time, Pallas kernels for 61%

profile of v10, /device:TPU:0, one launch (start us, length us, event | category | flops | bytes accessed | tf_op | source)
XLA Modules:
  0.0 60.5 jit_solution(6674849488513763412)
XLA Ops:
  0.6 0.5 collective-permute-start.1
  1.1 3.7 %prepare.1 = (f32[32,512]{1,0:T(8,128)}, bf16[512,128]{1,0:T(8,128)(2,1)S(1)}, bf16[528,128]{1,0:T(8,128)(2,1)S(1)}, f32[8,128]{1,0:T(8,128)S(1)}) custom-call(f32[8,512]{1,0:T(8,128)} %bitcast.126, bf16[512,1024]{1,0:T(8,128)(2,1)} %refs_2_.9, bf16[512,1024]{1,0:T(8,128)(2,1)} %refs_3_.11), custom_call_target="tpu_custom_call" | custom-call | flops 4000000000 | bytes 1 | tf_op jit(solution)/shard_map/prepare/pallas_call | solution.py:34
  4.8 2.6 %collective-permute-start = (bf16[528,128]{1,0:T(8,128)(2,1)S(1)}, bf16[528,128]{1,0:T(8,128)(2,1)S(1)}, u32[]{:S(2)}, u32[]{:S(2)}) collective-permute-start(bf16[528,128]{1,0:T(8,128)(2,1)S(1)} %get-tuple-element.50), channel_id=1, source_target_pairs={{0,2},{2,0},{4,6},{6,4},{8,10},{10,8},{12,14},{14,12},{16,18},{18,... | collective-permute-start | bytes 405512 | tf_op jit(solution)/shard_map/ppermute | solution.py:539
  7.4 0.1 pad_add_fusion.place_ref
  7.5 8.5 %project.1 = (bf16[512,1024]{1,0:T(8,128)(2,1)}, bf16[512,128]{1,0:T(8,128)(2,1)S(1)}, bf16[512,128]{1,0:T(8,128)(2,1)S(1)}) custom-call(s32[2]{0:T(128)S(1)} %pad_add_fusion.place_ref, bf16[512,2048]{1,0:T(8,128)(2,1)} %refs_0_.1, bf16[512,2048]{1,0:T(8,128)(2,1)S(1)} %collective-permute-done.1.refs_1_, bf16[4096,1024]{1,0:T(8,128)(2,1)} %w_hbm.1, ...), custom_call_target="tpu_custom_call" | custom-call | flops 8000000000 | bytes 1 | tf_op jit(solution)/shard_map/project/pallas_call | solution.py:34
  16.0 0.1 fusion.21
  16.1 1.6 %collective-permute-start.2 = (bf16[528,128]{1,0:T(8,128)(2,1)S(1)}, bf16[528,128]{1,0:T(8,128)(2,1)S(1)}, u32[]{:S(2)}, u32[]{:S(2)}) collective-permute-start(bf16[528,128]{1,0:T(8,128)(2,1)S(1)} %pad_maximum_fusion), channel_id=1, source_target_pairs={{0,4},{2,6},{4,0},{6,2},{8,12},{10,14},{12,8},{14,10},{16,20},{18,... | collective-permute-start | bytes 405512 | tf_op jit(solution)/shard_map/ppermute | solution.py:539
  17.6 0.5 collective-permute-start.4
  18.2 5.0 %inner.3 = (bf16[512,512]{1,0:T(8,128)(2,1)}, bf16[512,512]{1,0:T(8,128)(2,1)}, bf16[512,512]{1,0:T(8,128)(2,1)}) custom-call(bf16[512,1024]{1,0:T(8,128)(2,1)} %get-tuple-element.73.refs_0_, bf16[512,1024]{1,0:T(8,128)(2,1)} %refs_2_.9, bf16[512,1024]{1,0:T(8,128)(2,1)} %refs_3_.11, bf16[512,1024]{1,0:T(8,128)(2,1)} %refs_3_.10, ...), custom_call_target="tpu_custom_call" | custom-call | flops 1000000000 | bytes 1 | tf_op jit(solution)/shard_map/inner/pallas_call | solution.py:34
  23.2 0.1 fusion.23
  23.3 1.6 %collective-permute-start.3 = (bf16[528,128]{1,0:T(8,128)(2,1)S(1)}, bf16[528,128]{1,0:T(8,128)(2,1)S(1)}, u32[]{:S(2)}, u32[]{:S(2)}) collective-permute-start(bf16[528,128]{1,0:T(8,128)(2,1)S(1)} %pad_maximum_fusion.1), channel_id=1, source_target_pairs={{0,8},{2,10},{4,12},{6,14},{8,0},{10,2},{12,4},{14,6},{16,24},{18,... | collective-permute-start | bytes 405512 | tf_op jit(solution)/shard_map/ppermute | solution.py:539
  25.0 0.6 collective-permute-start.6
  25.6 3.5 %inner.4 = (bf16[512,256]{1,0:T(8,128)(2,1)}, bf16[512,256]{1,0:T(8,128)(2,1)}, bf16[512,256]{1,0:T(8,128)(2,1)}) custom-call(bf16[512,1024]{1,0:T(8,128)(2,1)} %get-tuple-element.73.refs_0_, bf16[512,1024]{1,0:T(8,128)(2,1)} %refs_2_.9, bf16[512,1024]{1,0:T(8,128)(2,1)} %refs_3_.11, bf16[512,1024]{1,0:T(8,128)(2,1)} %refs_3_.10, ...), custom_call_target="tpu_custom_call" | custom-call | flops 1000000000 | bytes 1 | tf_op jit(solution)/shard_map/inner/pallas_call | solution.py:34
  29.1 0.1 fusion.14
  29.3 2.7 %collective-permute-start.5 = (bf16[512,128]{1,0:T(8,128)(2,1)S(1)}, bf16[512,128]{1,0:T(8,128)(2,1)S(1)}, u32[]{:S(2)}, u32[]{:S(2)}) collective-permute-start(bf16[512,128]{1,0:T(8,128)(2,1)S(1)} %fusion.14), channel_id=1, source_target_pairs={{0,16},{2,18},{4,20},{6,22},{8,24},{10,26},{12,28},{14,30},{16,0},... | collective-permute-start | bytes 393224 | tf_op jit(solution)/shard_map/ppermute | solution.py:539
  32.0 0.1 fusion.22
  32.1 1.0 %collective-permute-start.8 = (bf16[512,128]{1,0:T(8,128)(2,1)S(1)}, bf16[512,128]{1,0:T(8,128)(2,1)S(1)}, u32[]{:S(2)}, u32[]{:S(2)}) collective-permute-start(bf16[512,128]{1,0:T(8,128)(2,1)S(1)} %fusion.22), channel_id=1, source_target_pairs={{0,8},{2,10},{4,12},{6,14},{8,0},{10,2},{12,4},{14,6},{16,24},{18,... | collective-permute-start | bytes 393224 | tf_op jit(solution)/shard_map/ppermute | solution.py:539
  33.1 0.1 pad_add_fusion.1.place_ref
  33.2 3.5 %inner.5 = (bf16[512,256]{1,0:T(8,128)(2,1)}, bf16[512,256]{1,0:T(8,128)(2,1)}, bf16[512,256]{1,0:T(8,128)(2,1)}) custom-call(bf16[512,1024]{1,0:T(8,128)(2,1)} %get-tuple-element.73.refs_0_, bf16[512,1024]{1,0:T(8,128)(2,1)} %refs_2_.9, bf16[512,1024]{1,0:T(8,128)(2,1)} %refs_3_.11, bf16[512,1024]{1,0:T(8,128)(2,1)} %refs_3_.10, ...), custom_call_target="tpu_custom_call" | custom-call | flops 1000000000 | bytes 1 | tf_op jit(solution)/shard_map/inner/pallas_call | solution.py:34
  36.7 1.0 %collective-permute-done.5 = bf16[512,128]{1,0:T(8,128)(2,1)S(1)} collective-permute-done((bf16[512,128]{1,0:T(8,128)(2,1)S(1)}, bf16[512,128]{1,0:T(8,128)(2,1)S(1)}, u32[]{:S(2)}, u32[]{:S(2)}) %collective-permute-start.5) | collective-permute-done | bytes 131104 | tf_op jit(solution)/shard_map/ppermute | solution.py:539
  37.7 0.2 fusion.4
  37.8 1.5 %collective-permute-start.7 = (bf16[512,128]{1,0:T(8,128)(2,1)S(1)}, bf16[512,128]{1,0:T(8,128)(2,1)S(1)}, u32[]{:S(2)}, u32[]{:S(2)}) collective-permute-start(bf16[512,128]{1,0:T(8,128)(2,1)S(1)} %get-tuple-element.107), channel_id=1, source_target_pairs={{0,2},{2,0},{4,6},{6,4},{8,10},{10,8},{12,14},{14,12},{16,18},{18,... | collective-permute-start | bytes 393224 | tf_op jit(solution)/shard_map/ppermute | solution.py:539
  39.4 0.1 fusion.19
  39.5 1.3 %collective-permute-start.9 = (bf16[512,128]{1,0:T(8,128)(2,1)S(1)}, bf16[512,128]{1,0:T(8,128)(2,1)S(1)}, u32[]{:S(2)}, u32[]{:S(2)}) collective-permute-start(bf16[512,128]{1,0:T(8,128)(2,1)S(1)} %fusion.19), channel_id=1, source_target_pairs={{0,16},{2,18},{4,20},{6,22},{8,24},{10,26},{12,28},{14,30},{16,0},... | collective-permute-start | bytes 393224 | tf_op jit(solution)/shard_map/ppermute | solution.py:539
  40.8 4.0 %fetch.1 = (bf16[2048,1024]{1,0:T(8,128)(2,1)S(1)}, bf16[2048,1024]{1,0:T(8,128)(2,1)S(1)}) custom-call(s32[2]{0:T(128)S(1)} %pad_add_fusion.1.place_ref, bf16[4096,1024]{1,0:T(8,128)(2,1)} %w_hbm.1), custom_call_target="tpu_custom_call" | custom-call | flops 4000000000 | bytes 1 | tf_op jit(solution)/shard_map/fetch/pallas_call | solution.py:34
  44.8 1.6 %collective-permute-done.9 = bf16[512,128]{1,0:T(8,128)(2,1)S(1)} collective-permute-done((bf16[512,128]{1,0:T(8,128)(2,1)S(1)}, bf16[512,128]{1,0:T(8,128)(2,1)S(1)}, u32[]{:S(2)}, u32[]{:S(2)}) %collective-permute-start.9) | collective-permute-done | bytes 131104 | tf_op jit(solution)/shard_map/ppermute | solution.py:539
  46.5 0.2 fusion.12
  46.6 1.5 %collective-permute-start.11 = (bf16[512,128]{1,0:T(8,128)(2,1)S(1)}, bf16[512,128]{1,0:T(8,128)(2,1)S(1)}, u32[]{:S(2)}, u32[]{:S(2)}) collective-permute-start(bf16[512,128]{1,0:T(8,128)(2,1)S(1)} %get-tuple-element.110), channel_id=1, source_target_pairs={{0,2},{2,0},{4,6},{6,4},{8,10},{10,8},{12,14},{14,12},{16,18},{18,... | collective-permute-start | bytes 393224 | tf_op jit(solution)/shard_map/ppermute | solution.py:539
  48.1 4.6 %query_term.1 = (bf16[512,1024]{1,0:T(8,128)(2,1)S(1)}, bf16[512,2048]{1,0:T(8,128)(2,1)S(1)}) custom-call(bf16[512,128]{1,0:T(8,128)(2,1)S(1)} %get-tuple-element.108.refs_0_, bf16[512,128]{1,0:T(8,128)(2,1)S(1)} %collective-permute-done.7.refs_1_, bf16[2048,1024]{1,0:T(8,128)(2,1)S(1)} %get-tuple-element.82.refs_2_, bf16[512,1024]{1,0:T(8,128)(2,1)} %refs_3_.10, ...), custom_call_target="tpu_custom_call" | custom-call | flops 6000000000 | bytes 1 | tf_op jit(solution)/shard_map/query_term/pallas_call | solution.py:34
  52.7 0.1 collective-permute-start.10
  52.8 4.2 %close.1 = (bf16[512,1024]{1,0:T(8,128)(2,1)}, bf16[512,1024]{1,0:T(8,128)(2,1)}) custom-call(bf16[512,128]{1,0:T(8,128)(2,1)S(1)} %get-tuple-element.109.refs_0_, bf16[512,128]{1,0:T(8,128)(2,1)S(1)} %collective-permute-done.11.refs_1_, bf16[512,1024]{1,0:T(8,128)(2,1)} %refs_2_.9, bf16[512,1024]{1,0:T(8,128)(2,1)} %refs_3_.11, ...), custom_call_target="tpu_custom_call" | custom-call | flops 99999997952 | bytes 1 | tf_op jit(solution)/shard_map/close/pallas_call | solution.py:34
  57.0 3.3 %finish.1 = bf16[512,2048]{1,0:T(8,128)(2,1)} custom-call(bf16[512,1024]{1,0:T(8,128)(2,1)S(1)} %get-tuple-element.86.dq_ref, bf16[2048,1024]{1,0:T(8,128)(2,1)S(1)} %get-tuple-element.87.w_ref, bf16[512,2048]{1,0:T(8,128)(2,1)S(1)} %collective-permute-done.10.refs_0_), custom_call_target="tpu_custom_call" | custom-call | flops 6000000000 | bytes 1 | tf_op jit(solution)/shard_map/finish/pallas_call | solution.py:34
  (19 shorter events, 0.2 us)
Async XLA Ops:
  0.6 6.8 %collective-permute-start.1 = (bf16[512,2048]{1,0:T(8,128)(2,1)}, bf16[512,2048]{1,0:T(8,128)(2,1)S(1)}, u32[]{:S(2)}, u32[]{:S(2)}) collective-permute-start(bf16[512,2048]{1,0:T(8,128)(2,1)} %refs_0_.1), channel_id=1, source_target_pairs={{0,1},{1,0},{2,3},{3,2},{4,5},{5,4},{6,7},{7,6},{8,9},{9,8},{10,11... | collective-permute-start | bytes 6291464 | tf_op jit(solution)/shard_map/ppermute | solution.py:522
  4.8 11.1 %collective-permute-start = (bf16[528,128]{1,0:T(8,128)(2,1)S(1)}, bf16[528,128]{1,0:T(8,128)(2,1)S(1)}, u32[]{:S(2)}, u32[]{:S(2)}) collective-permute-start(bf16[528,128]{1,0:T(8,128)(2,1)S(1)} %get-tuple-element.50), channel_id=1, source_target_pairs={{0,2},{2,0},{4,6},{6,4},{8,10},{10,8},{12,14},{14,12},{16,18},{18,... | collective-permute-start | bytes 405512 | tf_op jit(solution)/shard_map/ppermute | solution.py:539
  16.1 7.1 %collective-permute-start.2 = (bf16[528,128]{1,0:T(8,128)(2,1)S(1)}, bf16[528,128]{1,0:T(8,128)(2,1)S(1)}, u32[]{:S(2)}, u32[]{:S(2)}) collective-permute-start(bf16[528,128]{1,0:T(8,128)(2,1)S(1)} %pad_maximum_fusion), channel_id=1, source_target_pairs={{0,4},{2,6},{4,0},{6,2},{8,12},{10,14},{12,8},{14,10},{16,20},{18,... | collective-permute-start | bytes 405512 | tf_op jit(solution)/shard_map/ppermute | solution.py:539
  17.6 7.3 %collective-permute-start.4 = (bf16[512,128]{1,0:T(8,128)(2,1)S(1)}, bf16[512,128]{1,0:T(8,128)(2,1)S(1)}, u32[]{:S(2)}, u32[]{:S(2)}) collective-permute-start(bf16[512,128]{1,0:T(8,128)(2,1)S(1)} %get-tuple-element.59), channel_id=1, source_target_pairs={{0,2},{2,0},{4,6},{6,4},{8,10},{10,8},{12,14},{14,12},{16,18},{18,... | collective-permute-start | bytes 393224 | tf_op jit(solution)/shard_map/ppermute | solution.py:539
  23.3 5.8 %collective-permute-start.3 = (bf16[528,128]{1,0:T(8,128)(2,1)S(1)}, bf16[528,128]{1,0:T(8,128)(2,1)S(1)}, u32[]{:S(2)}, u32[]{:S(2)}) collective-permute-start(bf16[528,128]{1,0:T(8,128)(2,1)S(1)} %pad_maximum_fusion.1), channel_id=1, source_target_pairs={{0,8},{2,10},{4,12},{6,14},{8,0},{10,2},{12,4},{14,6},{16,24},{18,... | collective-permute-start | bytes 405512 | tf_op jit(solution)/shard_map/ppermute | solution.py:539
  25.0 6.9 %collective-permute-start.6 = (bf16[512,128]{1,0:T(8,128)(2,1)S(1)}, bf16[512,128]{1,0:T(8,128)(2,1)S(1)}, u32[]{:S(2)}, u32[]{:S(2)}) collective-permute-start(bf16[512,128]{1,0:T(8,128)(2,1)S(1)} %fusion.20), channel_id=1, source_target_pairs={{0,4},{2,6},{4,0},{6,2},{8,12},{10,14},{12,8},{14,10},{16,20},{18,... | collective-permute-start | bytes 393224 | tf_op jit(solution)/shard_map/ppermute | solution.py:539
  29.3 8.4 %collective-permute-start.5 = (bf16[512,128]{1,0:T(8,128)(2,1)S(1)}, bf16[512,128]{1,0:T(8,128)(2,1)S(1)}, u32[]{:S(2)}, u32[]{:S(2)}) collective-permute-start(bf16[512,128]{1,0:T(8,128)(2,1)S(1)} %fusion.14), channel_id=1, source_target_pairs={{0,16},{2,18},{4,20},{6,22},{8,24},{10,26},{12,28},{14,30},{16,0},... | collective-permute-start | bytes 393224 | tf_op jit(solution)/shard_map/ppermute | solution.py:539
  32.1 7.3 %collective-permute-start.8 = (bf16[512,128]{1,0:T(8,128)(2,1)S(1)}, bf16[512,128]{1,0:T(8,128)(2,1)S(1)}, u32[]{:S(2)}, u32[]{:S(2)}) collective-permute-start(bf16[512,128]{1,0:T(8,128)(2,1)S(1)} %fusion.22), channel_id=1, source_target_pairs={{0,8},{2,10},{4,12},{6,14},{8,0},{10,2},{12,4},{14,6},{16,24},{18,... | collective-permute-start | bytes 393224 | tf_op jit(solution)/shard_map/ppermute | solution.py:539
  37.8 10.3 %collective-permute-start.7 = (bf16[512,128]{1,0:T(8,128)(2,1)S(1)}, bf16[512,128]{1,0:T(8,128)(2,1)S(1)}, u32[]{:S(2)}, u32[]{:S(2)}) collective-permute-start(bf16[512,128]{1,0:T(8,128)(2,1)S(1)} %get-tuple-element.107), channel_id=1, source_target_pairs={{0,2},{2,0},{4,6},{6,4},{8,10},{10,8},{12,14},{14,12},{16,18},{18,... | collective-permute-start | bytes 393224 | tf_op jit(solution)/shard_map/ppermute | solution.py:539
  39.5 7.0 %collective-permute-start.9 = (bf16[512,128]{1,0:T(8,128)(2,1)S(1)}, bf16[512,128]{1,0:T(8,128)(2,1)S(1)}, u32[]{:S(2)}, u32[]{:S(2)}) collective-permute-start(bf16[512,128]{1,0:T(8,128)(2,1)S(1)} %fusion.19), channel_id=1, source_target_pairs={{0,16},{2,18},{4,20},{6,22},{8,24},{10,26},{12,28},{14,30},{16,0},... | collective-permute-start | bytes 393224 | tf_op jit(solution)/shard_map/ppermute | solution.py:539
  46.6 6.2 %collective-permute-start.11 = (bf16[512,128]{1,0:T(8,128)(2,1)S(1)}, bf16[512,128]{1,0:T(8,128)(2,1)S(1)}, u32[]{:S(2)}, u32[]{:S(2)}) collective-permute-start(bf16[512,128]{1,0:T(8,128)(2,1)S(1)} %get-tuple-element.110), channel_id=1, source_target_pairs={{0,2},{2,0},{4,6},{6,4},{8,10},{10,8},{12,14},{14,12},{16,18},{18,... | collective-permute-start | bytes 393224 | tf_op jit(solution)/shard_map/ppermute | solution.py:539
  52.7 4.3 %collective-permute-start.10 = (bf16[512,2048]{1,0:T(8,128)(2,1)S(1)}, bf16[512,2048]{1,0:T(8,128)(2,1)S(1)}, u32[]{:S(2)}, u32[]{:S(2)}) collective-permute-start(bf16[512,2048]{1,0:T(8,128)(2,1)S(1)} %get-tuple-element.88), channel_id=1, source_target_pairs={{0,1},{1,0},{2,3},{3,2},{4,5},{5,4},{6,7},{7,6},{8,9},{9,8},{10,11... | collective-permute-start | bytes 6291464 | tf_op jit(solution)/shard_map/ppermute | solution.py:632

commit v11 on v10

--- a/solution.py
+++ b/solution.py
@@ -77,8 +77,7 @@
 
 
 def spans_of(heads):
-    half, quarter = heads // 2, heads // 4
-    edges = sorted({0, half, half + quarter, heads})
+    edges = sorted({0, heads // 4, heads // 2, heads})
     return list(zip(edges, edges[1:]))
 
 
@@ -177,7 +176,7 @@
     )
 
 
-def project_kernel(hp, nparts, chunk, place_ref, *refs):
+def project_kernel(hp, nparts, chunk, *refs):
     parts, (w_hbm, do_hbm, facts_hbm, q_hbm, kept_ref, sent_ref) = refs[:nparts], refs[nparts : nparts + 6]
     hbuf, wbuf, dobuf, facts_ref, qbuf, total, sems = refs[nparts + 6 :]
     rows, feat = parts[0].shape
@@ -189,7 +188,8 @@
     for part, ref in enumerate(parts):
         for first in range(0, feat, chunk):
             here = pl.ds(part * feat + first, chunk)
-            start = pl.multiple_of(place_ref[part] * feat + first, chunk)
+            owner = lax.rem(lax.axis_index("head") + nparts - part, nparts)
+            start = pl.multiple_of(owner * feat + first, chunk)
             loads.append(
                 (
                     slice(part * feat + first, part * feat + first + chunk),
@@ -222,14 +222,14 @@
     copies.finish()
 
 
-def project(parts, owners, w_query, d_out, facts, hp):
+def project(parts, w_query, d_out, facts, hp):
     rows, feat = parts[0].shape
     depth, width = w_query.shape
     chunk = min(512, feat)
     return kernel_call(
         functools.partial(project_kernel, hp, len(parts), chunk),
-        (owners, *parts, w_query, d_out, facts),
-        [SM, HB] + [AN] * (len(parts) - 1) + [HB] * 3,
+        (*parts, w_query, d_out, facts),
+        [HB] + [AN] * (len(parts) - 1) + [HB] * 3,
         [((rows, width), BF16), ((width // 2, HDIM), BF16), ((width // 2, HDIM), BF16)],
         (HB, VM, VM),
         [
@@ -317,25 +317,27 @@
     return jnp.concatenate([jnp.where(upper, theirs, mine), jnp.where(upper, mine, theirs)], axis=0)
 
 
-def fetch_kernel(place_ref, w_hbm, *refs):
+def rows_of(w_hbm, shift, count, feat):
+    owner = lax.rem(lax.axis_index("head") + shift, count)
+    return w_hbm.at[pl.ds(pl.multiple_of(owner * feat, feat), feat), :]
+
+
+def fetch_kernel(count, w_hbm, *refs):
     outs, sems = refs[:-1], refs[-1]
     copies = Copies(sems)
     for index, out in enumerate(outs):
-        feat = out.shape[0]
-        start = pl.multiple_of(place_ref[index] * feat, feat)
-        copies.store(w_hbm.at[pl.ds(start, feat), :], out)
+        copies.store(rows_of(w_hbm, index + 1, count, out.shape[0]), out)
     copies.finish()
 
 
-def fetch(places, w_query, feat):
-    count = places.shape[0]
-    return kernel_call(
-        fetch_kernel,
-        (places, w_query),
-        [SM, HB],
-        [((feat, w_query.shape[1]), BF16)] * count,
-        (VM,) * count,
-        [pltpu.SemaphoreType.DMA((count,))],
+def fetch(count, w_query, feat):
+    return kernel_call(
+        functools.partial(fetch_kernel, count),
+        (w_query,),
+        [HB],
+        [((feat, w_query.shape[1]), BF16)] * (count - 1),
+        (VM,) * (count - 1),
+        [pltpu.SemaphoreType.DMA((count - 1,))],
         2,
         "fetch",
         4,
@@ -439,11 +441,11 @@
     )[0]
 
 
-def close_kernel(heads, hp, *refs):
-    mine_ref, theirs_ref, in_hbm, v_hbm, facts_hbm = refs[:5]
-    rest = refs[5:-10]
+def close_kernel(heads, hp, count, *refs):
+    mine_ref, theirs_ref, in_hbm, v_hbm, facts_hbm, w_hbm = refs[:6]
+    rest = refs[6:-11]
     upper = lax.axis_index("ctx") % 2 == 1
-    dk_hbm, dv_hbm, kbuf, vbuf, facts_ref, dkbuf, dvbuf, kside, vside, sems = refs[-10:]
+    dk_hbm, dv_hbm, own_ref, kbuf, vbuf, facts_ref, dkbuf, dvbuf, kside, vside, sems = refs[-11:]
     dks, dvs = rest[: len(rest) // 2], rest[len(rest) // 2 :]
     pair = 2 if all(edge % 2 == 0 for span in spans_of(heads) for edge in span) else 1
     copies = Copies(sems)
@@ -461,6 +463,7 @@
                     copies.start(dv.at[:, part], dvbuf.at[:, wide]),
                 )
             )
+    copies.store(rows_of(w_hbm, 0, count, own_ref.shape[0]), own_ref)
     facts_in.wait()
     table = turned(facts_ref[...])
     for h in range(heads):
@@ -481,16 +484,16 @@
     copies.finish()
 
 
-def close(halves, dks, dvs, keys, values, facts, heads, hp):
+def close(halves, dks, dvs, keys, values, facts, w_query, feat, count, heads, hp):
     rows, width = values.shape
-    args = (keys, values, facts, *dks, *dvs)
+    args = (keys, values, facts, w_query, *dks, *dvs)
     buf = pltpu.VMEM((rows, width), BF16)
     return kernel_call(
-        functools.partial(close_kernel, heads, hp),
+        functools.partial(close_kernel, heads, hp, count),
         (*halves, *args),
         [VM, VM] + [HB] * len(args),
-        [((rows, width), BF16)] * 2,
-        (HB,) * 2,
+        [((rows, width), BF16)] * 2 + [((feat, width), BF16)],
+        (HB, HB, VM),
         [
             buf,
             buf,
@@ -499,7 +502,7 @@
             buf,
             buf,
             buf,
-            pltpu.SemaphoreType.DMA((1 + 6 * heads,)),
+            pltpu.SemaphoreType.DMA((2 + 6 * heads,)),
         ],
         20,
         "close",
@@ -514,16 +517,14 @@
     hp = sublanes(heads)
     scaling = HDIM ** (-0.5)
     me = lax.axis_index("ctx")
-    mine = lax.axis_index("head")
 
     parts = [hidden]
     for shift in range(1, head_size):
         ring = [(i, (i + shift) % head_size) for i in range(head_size)]
         parts.append(lax.ppermute(hidden, "head", ring))
-    owners = jnp.stack([(mine + head_size - s) % head_size for s in range(head_size)]).astype(jnp.int32)
 
     facts, kept, sent, share = prepare(log_decay.T, keys, values, heads, hp, scaling)
-    query, akept, asent = project(parts, owners, w_query, d_out, facts, hp)
+    query, akept, asent = project(parts, w_query, d_out, facts, hp)
 
     size = width // 2
     wide = lambda factor: factor[:heads, None, :]
@@ -591,11 +592,10 @@
     pending = list(spans)
     inner_parts = []
     barrier = lax.optimization_barrier
-    places = jnp.stack([(mine + shift) % head_size for shift in range(head_size)]).astype(jnp.int32)
     for stage in range(stages + 1):
         if stage == stages:
-            places, _ = barrier((places, adjoints.sent))
-            weights = fetch(places, w_query, feat)
+            weight, _ = barrier((w_query, adjoints.sent))
+            weights = fetch(head_size, weight, feat)
         states.go()
         if stage == 0:
             states.arrived, query, adjoints.kept, adjoints.sent = barrier(
@@ -609,6 +609,11 @@
                 part = inner(*pending.pop(0), query, keys, values, d_out, facts, hp)
                 states.arrived, *part = barrier((states.arrived, *part))
                 inner_parts.append(part)
+        if stage == stages - 1:
+            adjoints.take()
+            states.arrived, _ = barrier((states.arrived, adjoints.sent))
+            states.take()
+            continue
         if stage < stages:
             states.take()
         if stage >= 1:
@@ -626,12 +631,14 @@
     for shift in range(1, head_size):
         ring = [(i, (i + shift) % head_size) for i in range(head_size)]
         if shift == 1:
-            d_query, term = query_term(state_halves, dqs, d_out, facts, weights[shift], heads, hp)
+            d_query, term = query_term(state_halves, dqs, d_out, facts, weights[0], heads, hp)
         else:
-            term = plain_term(d_query, weights[shift])
+            term = plain_term(d_query, weights[shift - 1])
         arrived.append(lax.ppermute(term, "head", ring))
-    d_keys, d_values = close(adjoint_halves, dks, dvs, keys, values, facts, heads, hp)
-    d_hidden = finish(d_query, weights[0], arrived)
+    d_keys, d_values, own = close(
+        adjoint_halves, dks, dvs, keys, values, facts, w_query, feat, head_size, heads, hp
+    )
+    d_hidden = finish(d_query, own, arrived)
     return (d_hidden, d_keys, d_values)
 
 

time: 60.7 us -> 58.4 us (0.962)
  Pallas kernels: 40.2 us -> 38.2 us
  starting transfers between devices: 15.5 us -> 14.2 us
  waiting for transfers between devices: 2.67 us -> 3.68 us
    pallas_call x9, Pallas kernels: 40.2 us -> 38.2 us  [kernel_call(): pl.pallas_call(kernel, in_specs=specs, out_specs=tuple(out_specs), out_sh...]
    ppermute x10, starting transfers between devices: 14.9 us -> 13.7 us  [send(): return lax.ppermute(array, 'ctx', [(i, i ^ dist) for i in range(ctx_size)])]
    ppermute x10, waiting for transfers between devices: 2.66 us -> 3.68 us  [send(): return lax.ppermute(array, 'ctx', [(i, i ^ dist) for i in range(ctx_size)])]
  transfers between devices with their start and end apart: 12 -> 12, of which waited for: 2 -> 1; matrix products, arithmetic and copies ran while one was open for 2% -> 1% of each run, Pallas kernels for 61% -> 60%
where the time goes in v11:
time: 58.4 us; the launch traced here: 58.1 us
  Pallas kernels  38.2 us (65%)
  starting transfers between devices  14.2 us (24%)
  waiting for transfers between devices  3.68 us (6%)
  between operations  1.02 us (2%)
  other arithmetic  0.98 us (2%)
    pallas_call x9, Pallas kernels, kernel_call(): pl.pallas_call(kernel, in_specs=specs, out_specs=tuple(out_specs), out_sh...  38.2 us
    ppermute x10, starting transfers between devices, send(): return lax.ppermute(array, 'ctx', [(i, i ^ dist) for i in range(ctx_size)])  13.7 us
    ppermute x10, waiting for transfers between devices, send(): return lax.ppermute(array, 'ctx', [(i, i ^ dist) for i in range(ctx_size)])  3.68 us
  transfers between devices with their start and end apart: 12, of which 1 were waited for; matrix products, arithmetic and copies ran while one was open for 1% of the time, Pallas kernels for 60%

profile of v11, /device:TPU:0, one launch (start us, length us, event | category | flops | bytes accessed | tf_op | source)
XLA Modules:
  0.0 58.1 jit_solution(3451166984918745707)
XLA Ops:
  0.6 0.5 collective-permute-start.1
  1.1 3.7 %prepare.1 = (f32[32,512]{1,0:T(8,128)}, bf16[512,128]{1,0:T(8,128)(2,1)S(1)}, bf16[528,128]{1,0:T(8,128)(2,1)S(1)}, f32[8,128]{1,0:T(8,128)S(1)}) custom-call(f32[8,512]{1,0:T(8,128)} %bitcast.123, bf16[512,1024]{1,0:T(8,128)(2,1)} %refs_2_.9, bf16[512,1024]{1,0:T(8,128)(2,1)} %refs_3_.11), custom_call_target="tpu_custom_call" | custom-call | flops 4000000000 | bytes 1 | tf_op jit(solution)/shard_map/prepare/pallas_call | solution.py:34
  4.8 2.6 %collective-permute-start = (bf16[528,128]{1,0:T(8,128)(2,1)S(1)}, bf16[528,128]{1,0:T(8,128)(2,1)S(1)}, u32[]{:S(2)}, u32[]{:S(2)}) collective-permute-start(bf16[528,128]{1,0:T(8,128)(2,1)S(1)} %get-tuple-element.49), channel_id=1, source_target_pairs={{0,2},{2,0},{4,6},{6,4},{8,10},{10,8},{12,14},{14,12},{16,18},{18,... | collective-permute-start | bytes 405512 | tf_op jit(solution)/shard_map/ppermute | solution.py:540
  7.4 0.0 collective-permute-done.1.refs_1_
  7.4 7.9 %project.1 = (bf16[512,1024]{1,0:T(8,128)(2,1)}, bf16[512,128]{1,0:T(8,128)(2,1)S(1)}, bf16[512,128]{1,0:T(8,128)(2,1)S(1)}) custom-call(bf16[512,2048]{1,0:T(8,128)(2,1)} %refs_0_.1, bf16[512,2048]{1,0:T(8,128)(2,1)S(1)} %collective-permute-done.1.refs_1_, bf16[4096,1024]{1,0:T(8,128)(2,1)} %refs_5_.1, bf16[512,1024]{1,0:T(8,128)(2,1)} %refs_3_.10, ...), custom_call_target="tpu_custom_call" | custom-call | flops 8000000000 | bytes 1 | tf_op jit(solution)/shard_map/project/pallas_call | solution.py:34
  15.4 0.1 fusion.21
  15.4 1.6 %collective-permute-start.2 = (bf16[528,128]{1,0:T(8,128)(2,1)S(1)}, bf16[528,128]{1,0:T(8,128)(2,1)S(1)}, u32[]{:S(2)}, u32[]{:S(2)}) collective-permute-start(bf16[528,128]{1,0:T(8,128)(2,1)S(1)} %pad_maximum_fusion), channel_id=1, source_target_pairs={{0,4},{2,6},{4,0},{6,2},{8,12},{10,14},{12,8},{14,10},{16,20},{18,... | collective-permute-start | bytes 405512 | tf_op jit(solution)/shard_map/ppermute | solution.py:540
  17.0 0.6 %collective-permute-start.4 = (bf16[512,128]{1,0:T(8,128)(2,1)S(1)}, bf16[512,128]{1,0:T(8,128)(2,1)S(1)}, u32[]{:S(2)}, u32[]{:S(2)}) collective-permute-start(bf16[512,128]{1,0:T(8,128)(2,1)S(1)} %get-tuple-element.58), channel_id=1, source_target_pairs={{0,2},{2,0},{4,6},{6,4},{8,10},{10,8},{12,14},{14,12},{16,18},{18,... | collective-permute-start | bytes 393224 | tf_op jit(solution)/shard_map/ppermute | solution.py:540
  17.6 3.5 %inner.3 = (bf16[512,256]{1,0:T(8,128)(2,1)}, bf16[512,256]{1,0:T(8,128)(2,1)}, bf16[512,256]{1,0:T(8,128)(2,1)}) custom-call(bf16[512,1024]{1,0:T(8,128)(2,1)} %get-tuple-element.72.refs_0_, bf16[512,1024]{1,0:T(8,128)(2,1)} %refs_2_.9, bf16[512,1024]{1,0:T(8,128)(2,1)} %refs_3_.11, bf16[512,1024]{1,0:T(8,128)(2,1)} %refs_3_.10, ...), custom_call_target="tpu_custom_call" | custom-call | flops 1000000000 | bytes 1 | tf_op jit(solution)/shard_map/inner/pallas_call | solution.py:34
  21.2 0.0 collective-permute-done.2
  21.2 0.1 fusion.23
  21.3 1.6 %collective-permute-start.3 = (bf16[528,128]{1,0:T(8,128)(2,1)S(1)}, bf16[528,128]{1,0:T(8,128)(2,1)S(1)}, u32[]{:S(2)}, u32[]{:S(2)}) collective-permute-start(bf16[528,128]{1,0:T(8,128)(2,1)S(1)} %pad_maximum_fusion.1), channel_id=1, source_target_pairs={{0,8},{2,10},{4,12},{6,14},{8,0},{10,2},{12,4},{14,6},{16,24},{18,... | collective-permute-start | bytes 405512 | tf_op jit(solution)/shard_map/ppermute | solution.py:540
  23.0 0.1 fusion.20
  23.0 1.6 %collective-permute-start.6 = (bf16[512,128]{1,0:T(8,128)(2,1)S(1)}, bf16[512,128]{1,0:T(8,128)(2,1)S(1)}, u32[]{:S(2)}, u32[]{:S(2)}) collective-permute-start(bf16[512,128]{1,0:T(8,128)(2,1)S(1)} %fusion.20), channel_id=1, source_target_pairs={{0,4},{2,6},{4,0},{6,2},{8,12},{10,14},{12,8},{14,10},{16,20},{18,... | collective-permute-start | bytes 393224 | tf_op jit(solution)/shard_map/ppermute | solution.py:540
  24.6 3.5 %inner.4 = (bf16[512,256]{1,0:T(8,128)(2,1)}, bf16[512,256]{1,0:T(8,128)(2,1)}, bf16[512,256]{1,0:T(8,128)(2,1)}) custom-call(bf16[512,1024]{1,0:T(8,128)(2,1)} %get-tuple-element.72.refs_0_, bf16[512,1024]{1,0:T(8,128)(2,1)} %refs_2_.9, bf16[512,1024]{1,0:T(8,128)(2,1)} %refs_3_.11, bf16[512,1024]{1,0:T(8,128)(2,1)} %refs_3_.10, ...), custom_call_target="tpu_custom_call" | custom-call | flops 1000000000 | bytes 1 | tf_op jit(solution)/shard_map/inner/pallas_call | solution.py:34
  28.2 0.1 fusion.14
  28.4 0.1 fusion.22
  28.5 0.7 %collective-permute-start.7 = (bf16[512,128]{1,0:T(8,128)(2,1)S(1)}, bf16[512,128]{1,0:T(8,128)(2,1)S(1)}, u32[]{:S(2)}, u32[]{:S(2)}) collective-permute-start(bf16[512,128]{1,0:T(8,128)(2,1)S(1)} %fusion.22), channel_id=1, source_target_pairs={{0,8},{2,10},{4,12},{6,14},{8,0},{10,2},{12,4},{14,6},{16,24},{18,... | collective-permute-start | bytes 393224 | tf_op jit(solution)/shard_map/ppermute | solution.py:540
  29.2 2.6 %collective-permute-start.5 = (bf16[512,128]{1,0:T(8,128)(2,1)S(1)}, bf16[512,128]{1,0:T(8,128)(2,1)S(1)}, u32[]{:S(2)}, u32[]{:S(2)}) collective-permute-start(bf16[512,128]{1,0:T(8,128)(2,1)S(1)} %fusion.14), channel_id=1, source_target_pairs={{0,16},{2,18},{4,20},{6,22},{8,24},{10,26},{12,28},{14,30},{16,0},... | collective-permute-start | bytes 393224 | tf_op jit(solution)/shard_map/ppermute | solution.py:540
  31.8 5.0 %inner.5 = (bf16[512,512]{1,0:T(8,128)(2,1)}, bf16[512,512]{1,0:T(8,128)(2,1)}, bf16[512,512]{1,0:T(8,128)(2,1)}) custom-call(bf16[512,1024]{1,0:T(8,128)(2,1)} %get-tuple-element.72.refs_0_, bf16[512,1024]{1,0:T(8,128)(2,1)} %refs_2_.9, bf16[512,1024]{1,0:T(8,128)(2,1)} %refs_3_.11, bf16[512,1024]{1,0:T(8,128)(2,1)} %refs_3_.10, ...), custom_call_target="tpu_custom_call" | custom-call | flops 1000000000 | bytes 1 | tf_op jit(solution)/shard_map/inner/pallas_call | solution.py:34
  36.8 0.1 fusion.19
  36.9 0.4 collective-permute-start.9
  37.3 0.2 fusion.4
  37.5 1.0 %collective-permute-start.8 = (bf16[512,128]{1,0:T(8,128)(2,1)S(1)}, bf16[512,128]{1,0:T(8,128)(2,1)S(1)}, u32[]{:S(2)}, u32[]{:S(2)}) collective-permute-start(bf16[512,128]{1,0:T(8,128)(2,1)S(1)} %get-tuple-element.105), channel_id=1, source_target_pairs={{0,2},{2,0},{4,6},{6,4},{8,10},{10,8},{12,14},{14,12},{16,18},{18,... | collective-permute-start | bytes 393224 | tf_op jit(solution)/shard_map/ppermute | solution.py:540
  38.5 2.2 %fetch.1.refs_2_ = bf16[2048,1024]{1,0:T(8,128)(2,1)S(1)} custom-call(bf16[4096,1024]{1,0:T(8,128)(2,1)} %refs_5_.1), custom_call_target="tpu_custom_call" | custom-call | flops 4000000000 | bytes 1 | tf_op jit(solution)/shard_map/fetch/pallas_call | solution.py:34
  40.7 3.6 %collective-permute-done.9 = bf16[512,128]{1,0:T(8,128)(2,1)S(1)} collective-permute-done((bf16[512,128]{1,0:T(8,128)(2,1)S(1)}, bf16[512,128]{1,0:T(8,128)(2,1)S(1)}, u32[]{:S(2)}, u32[]{:S(2)}) %collective-permute-start.9) | collective-permute-done | bytes 131104 | tf_op jit(solution)/shard_map/ppermute | solution.py:540
  44.3 0.2 fusion.12
  44.4 1.0 %collective-permute-start.10 = (bf16[512,128]{1,0:T(8,128)(2,1)S(1)}, bf16[512,128]{1,0:T(8,128)(2,1)S(1)}, u32[]{:S(2)}, u32[]{:S(2)}) collective-permute-start(bf16[512,128]{1,0:T(8,128)(2,1)S(1)} %get-tuple-element.108), channel_id=1, source_target_pairs={{0,2},{2,0},{4,6},{6,4},{8,10},{10,8},{12,14},{14,12},{16,18},{18,... | collective-permute-start | bytes 393224 | tf_op jit(solution)/shard_map/ppermute | solution.py:540
  45.4 4.4 %query_term.1 = (bf16[512,1024]{1,0:T(8,128)(2,1)S(1)}, bf16[512,2048]{1,0:T(8,128)(2,1)S(1)}) custom-call(bf16[512,128]{1,0:T(8,128)(2,1)S(1)} %get-tuple-element.106.refs_0_, bf16[512,128]{1,0:T(8,128)(2,1)S(1)} %collective-permute-done.8.refs_1_, bf16[2048,1024]{1,0:T(8,128)(2,1)S(1)} %fetch.1.refs_2_, bf16[512,1024]{1,0:T(8,128)(2,1)} %refs_3_.10, ...), custom_call_target="tpu_custom_call" | custom-call | flops 6000000000 | bytes 1 | tf_op jit(solution)/shard_map/query_term/pallas_call | solution.py:34
  49.8 0.1 collective-permute-start.11
  49.9 4.8 %close.1 = (bf16[512,1024]{1,0:T(8,128)(2,1)}, bf16[512,1024]{1,0:T(8,128)(2,1)}, bf16[2048,1024]{1,0:T(8,128)(2,1)S(1)}) custom-call(bf16[512,128]{1,0:T(8,128)(2,1)S(1)} %get-tuple-element.107.refs_0_, bf16[512,128]{1,0:T(8,128)(2,1)S(1)} %collective-permute-done.10.refs_1_, bf16[512,1024]{1,0:T(8,128)(2,1)} %refs_2_.9, bf16[512,1024]{1,0:T(8,128)(2,1)} %refs_3_.11, ...), custom_call_target="tpu_custom_call" | custom-call | flops 99999997952 | bytes 1 | tf_op jit(solution)/shard_map/close/pallas_call | solution.py:34
  54.7 3.3 %finish.1 = bf16[512,2048]{1,0:T(8,128)(2,1)} custom-call(bf16[512,1024]{1,0:T(8,128)(2,1)S(1)} %get-tuple-element.84.dq_ref, bf16[2048,1024]{1,0:T(8,128)(2,1)S(1)} %get-tuple-element.91.w_ref, bf16[512,2048]{1,0:T(8,128)(2,1)S(1)} %collective-permute-done.11.refs_0_), custom_call_target="tpu_custom_call" | custom-call | flops 6000000000 | bytes 1 | tf_op jit(solution)/shard_map/finish/pallas_call | solution.py:34
  (17 shorter events, 0.1 us)
Async XLA Ops:
  0.6 6.8 %collective-permute-start.1 = (bf16[512,2048]{1,0:T(8,128)(2,1)}, bf16[512,2048]{1,0:T(8,128)(2,1)S(1)}, u32[]{:S(2)}, u32[]{:S(2)}) collective-permute-start(bf16[512,2048]{1,0:T(8,128)(2,1)} %refs_0_.1), channel_id=1, source_target_pairs={{0,1},{1,0},{2,3},{3,2},{4,5},{5,4},{6,7},{7,6},{8,9},{9,8},{10,11... | collective-permute-start | bytes 6291464 | tf_op jit(solution)/shard_map/ppermute | solution.py:524
  4.8 10.5 %collective-permute-start = (bf16[528,128]{1,0:T(8,128)(2,1)S(1)}, bf16[528,128]{1,0:T(8,128)(2,1)S(1)}, u32[]{:S(2)}, u32[]{:S(2)}) collective-permute-start(bf16[528,128]{1,0:T(8,128)(2,1)S(1)} %get-tuple-element.49), channel_id=1, source_target_pairs={{0,2},{2,0},{4,6},{6,4},{8,10},{10,8},{12,14},{14,12},{16,18},{18,... | collective-permute-start | bytes 405512 | tf_op jit(solution)/shard_map/ppermute | solution.py:540
  15.4 5.8 %collective-permute-start.2 = (bf16[528,128]{1,0:T(8,128)(2,1)S(1)}, bf16[528,128]{1,0:T(8,128)(2,1)S(1)}, u32[]{:S(2)}, u32[]{:S(2)}) collective-permute-start(bf16[528,128]{1,0:T(8,128)(2,1)S(1)} %pad_maximum_fusion), channel_id=1, source_target_pairs={{0,4},{2,6},{4,0},{6,2},{8,12},{10,14},{12,8},{14,10},{16,20},{18,... | collective-permute-start | bytes 405512 | tf_op jit(solution)/shard_map/ppermute | solution.py:540
  17.0 6.0 %collective-permute-start.4 = (bf16[512,128]{1,0:T(8,128)(2,1)S(1)}, bf16[512,128]{1,0:T(8,128)(2,1)S(1)}, u32[]{:S(2)}, u32[]{:S(2)}) collective-permute-start(bf16[512,128]{1,0:T(8,128)(2,1)S(1)} %get-tuple-element.58), channel_id=1, source_target_pairs={{0,2},{2,0},{4,6},{6,4},{8,10},{10,8},{12,14},{14,12},{16,18},{18,... | collective-permute-start | bytes 393224 | tf_op jit(solution)/shard_map/ppermute | solution.py:540
  21.3 6.8 %collective-permute-start.3 = (bf16[528,128]{1,0:T(8,128)(2,1)S(1)}, bf16[528,128]{1,0:T(8,128)(2,1)S(1)}, u32[]{:S(2)}, u32[]{:S(2)}) collective-permute-start(bf16[528,128]{1,0:T(8,128)(2,1)S(1)} %pad_maximum_fusion.1), channel_id=1, source_target_pairs={{0,8},{2,10},{4,12},{6,14},{8,0},{10,2},{12,4},{14,6},{16,24},{18,... | collective-permute-start | bytes 405512 | tf_op jit(solution)/shard_map/ppermute | solution.py:540
  23.0 5.3 %collective-permute-start.6 = (bf16[512,128]{1,0:T(8,128)(2,1)S(1)}, bf16[512,128]{1,0:T(8,128)(2,1)S(1)}, u32[]{:S(2)}, u32[]{:S(2)}) collective-permute-start(bf16[512,128]{1,0:T(8,128)(2,1)S(1)} %fusion.20), channel_id=1, source_target_pairs={{0,4},{2,6},{4,0},{6,2},{8,12},{10,14},{12,8},{14,10},{16,20},{18,... | collective-permute-start | bytes 393224 | tf_op jit(solution)/shard_map/ppermute | solution.py:540
  28.5 8.3 %collective-permute-start.7 = (bf16[512,128]{1,0:T(8,128)(2,1)S(1)}, bf16[512,128]{1,0:T(8,128)(2,1)S(1)}, u32[]{:S(2)}, u32[]{:S(2)}) collective-permute-start(bf16[512,128]{1,0:T(8,128)(2,1)S(1)} %fusion.22), channel_id=1, source_target_pairs={{0,8},{2,10},{4,12},{6,14},{8,0},{10,2},{12,4},{14,6},{16,24},{18,... | collective-permute-start | bytes 393224 | tf_op jit(solution)/shard_map/ppermute | solution.py:540
  29.2 8.1 %collective-permute-start.5 = (bf16[512,128]{1,0:T(8,128)(2,1)S(1)}, bf16[512,128]{1,0:T(8,128)(2,1)S(1)}, u32[]{:S(2)}, u32[]{:S(2)}) collective-permute-start(bf16[512,128]{1,0:T(8,128)(2,1)S(1)} %fusion.14), channel_id=1, source_target_pairs={{0,16},{2,18},{4,20},{6,22},{8,24},{10,26},{12,28},{14,30},{16,0},... | collective-permute-start | bytes 393224 | tf_op jit(solution)/shard_map/ppermute | solution.py:540
  36.9 7.3 %collective-permute-start.9 = (bf16[512,128]{1,0:T(8,128)(2,1)S(1)}, bf16[512,128]{1,0:T(8,128)(2,1)S(1)}, u32[]{:S(2)}, u32[]{:S(2)}) collective-permute-start(bf16[512,128]{1,0:T(8,128)(2,1)S(1)} %fusion.19), channel_id=1, source_target_pairs={{0,16},{2,18},{4,20},{6,22},{8,24},{10,26},{12,28},{14,30},{16,0},... | collective-permute-start | bytes 393224 | tf_op jit(solution)/shard_map/ppermute | solution.py:540
  37.5 7.9 %collective-permute-start.8 = (bf16[512,128]{1,0:T(8,128)(2,1)S(1)}, bf16[512,128]{1,0:T(8,128)(2,1)S(1)}, u32[]{:S(2)}, u32[]{:S(2)}) collective-permute-start(bf16[512,128]{1,0:T(8,128)(2,1)S(1)} %get-tuple-element.105), channel_id=1, source_target_pairs={{0,2},{2,0},{4,6},{6,4},{8,10},{10,8},{12,14},{14,12},{16,18},{18,... | collective-permute-start | bytes 393224 | tf_op jit(solution)/shard_map/ppermute | solution.py:540
  44.4 5.5 %collective-permute-start.10 = (bf16[512,128]{1,0:T(8,128)(2,1)S(1)}, bf16[512,128]{1,0:T(8,128)(2,1)S(1)}, u32[]{:S(2)}, u32[]{:S(2)}) collective-permute-start(bf16[512,128]{1,0:T(8,128)(2,1)S(1)} %get-tuple-element.108), channel_id=1, source_target_pairs={{0,2},{2,0},{4,6},{6,4},{8,10},{10,8},{12,14},{14,12},{16,18},{18,... | collective-permute-start | bytes 393224 | tf_op jit(solution)/shard_map/ppermute | solution.py:540
  49.8 4.9 %collective-permute-start.11 = (bf16[512,2048]{1,0:T(8,128)(2,1)S(1)}, bf16[512,2048]{1,0:T(8,128)(2,1)S(1)}, u32[]{:S(2)}, u32[]{:S(2)}) collective-permute-start(bf16[512,2048]{1,0:T(8,128)(2,1)S(1)} %get-tuple-element.92), channel_id=1, source_target_pairs={{0,1},{1,0},{2,3},{3,2},{4,5},{5,4},{6,7},{7,6},{8,9},{9,8},{10,11... | collective-permute-start | bytes 6291464 | tf_op jit(solution)/shard_map/ppermute | solution.py:637

commit v12 on v11

--- a/solution.py
+++ b/solution.py
@@ -322,49 +322,62 @@
     return w_hbm.at[pl.ds(pl.multiple_of(owner * feat, feat), feat), :]
 
 
-def fetch_kernel(count, w_hbm, *refs):
-    outs, sems = refs[:-1], refs[-1]
+def fetch_kernel(heads, count, w_hbm, do_hbm, facts_hbm, *refs):
+    inner_hbm, refs = refs[: len(spans_of(heads))], refs[len(spans_of(heads)) :]
+    do_ref, local_ref, table_ref, outs, (facts_ref, sems) = refs[0], refs[1], refs[2], refs[3:-2], refs[-2:]
     copies = Copies(sems)
+    facts_in = copies.start(facts_hbm, facts_ref)
     for index, out in enumerate(outs):
         copies.store(rows_of(w_hbm, index + 1, count, out.shape[0]), out)
+    copies.store(do_hbm, do_ref)
+    for (first, last), src in zip(spans_of(heads), inner_hbm):
+        copies.store(src, local_ref.at[:, pl.ds(first * HDIM, (last - first) * HDIM)])
+    facts_in.wait()
+    table_ref[...] = turned(facts_ref[...])
     copies.finish()
 
 
-def fetch(count, w_query, feat):
-    return kernel_call(
-        functools.partial(fetch_kernel, count),
-        (w_query,),
-        [HB],
-        [((feat, w_query.shape[1]), BF16)] * (count - 1),
-        (VM,) * (count - 1),
-        [pltpu.SemaphoreType.DMA((count - 1,))],
-        2,
+def fetch(count, w_query, d_out, facts, inner_dq, feat, heads):
+    rows, width = d_out.shape
+    return kernel_call(
+        functools.partial(fetch_kernel, heads, count),
+        (w_query, d_out, facts, *inner_dq),
+        [HB] * (3 + len(inner_dq)),
+        [((rows, width), BF16)] * 2 + [((rows, LANES), F32)] + [((feat, width), BF16)] * (count - 1),
+        (VM,) * (count + 2),
+        [pltpu.VMEM(facts.shape, F32), pltpu.SemaphoreType.DMA((count + 1 + len(inner_dq),))],
+        4,
         "fetch",
         4,
     )
 
 
-def query_kernel(heads, hp, *refs):
-    mine_ref, theirs_ref, w_ref, do_hbm, facts_hbm = refs[:5]
-    inner_hbm = refs[5:-6]
-    held, out_ref, dobuf, facts_ref, local, sems = refs[-6:]
+def query_kernel(heads, hp, count, *refs):
+    mine_ref, theirs_ref, w_ref, do_ref, local_ref, table_ref, k_hbm, v_hbm, w_hbm = refs[:9]
+    parts = len(spans_of(heads))
+    dks, dvs, refs = refs[9 : 9 + parts], refs[9 + parts : 9 + 2 * parts], refs[9 + 2 * parts :]
+    held, out_ref, k_ref, v_ref, dk_ref, dv_ref, next_table, own_first, own_second, sems = refs
     upper = lax.axis_index("ctx") % 2 == 1
     copies = Copies(sems)
-    facts_in = copies.start(facts_hbm, facts_ref)
-    loads = {}
-    for (first, last), src in zip(spans_of(heads), inner_hbm):
+    copies.store(k_hbm, k_ref)
+    copies.store(v_hbm, v_ref)
+    for (first, last), dk, dv in zip(spans_of(heads), dks, dvs):
         wide = pl.ds(first * HDIM, (last - first) * HDIM)
-        loads[first] = (copies.start(do_hbm.at[:, wide], dobuf.at[:, wide]), copies.start(src, local.at[:, wide]))
-    facts_in.wait()
-    table = turned(facts_ref[...])
+        copies.store(dk, dk_ref.at[:, wide])
+        copies.store(dv, dv_ref.at[:, wide])
+    half = own_first.shape[0]
+    rows = rows_of(w_hbm, 0, count, 2 * half)
+    copies.store(rows.at[pl.ds(0, half), :], own_first)
+    copies.store(rows.at[pl.ds(half, half), :], own_second)
+    table = table_ref[...]
+    next_table[...] = table
     for h in range(heads):
-        for copy in loads.get(h, ()):
-            copy.wait()
         cols = slice(h * HDIM, (h + 1) * HDIM)
         state = whole_head(upper, h, mine_ref, theirs_ref)
-        carry = dot(dobuf[:, cols], state, NT)
-        held[:, cols] = (local[:, cols].astype(F32) + column(table, 3 * hp + h) * carry).astype(BF16)
+        carry = dot(do_ref[:, cols], state, NT)
+        held[:, cols] = (local_ref[:, cols].astype(F32) + column(table, 3 * hp + h) * carry).astype(BF16)
     put_terms(held, w_ref, out_ref)
+    copies.finish()
 
 
 def put_terms(dq_ref, w_ref, out_ref):
@@ -373,22 +386,21 @@
         out_ref[:, at : at + block] = dot(dq_ref[...], w_ref[at : at + block, :], NT).astype(BF16)
 
 
-def query_term(halves, inner_dq, d_out, facts, weight, heads, hp):
-    rows, width = d_out.shape
-    args = (d_out, facts, *inner_dq)
-    return kernel_call(
-        functools.partial(query_kernel, heads, hp),
-        (*halves, weight, *args),
-        [VM, VM, VM] + [HB] * len(args),
-        [((rows, width), BF16), ((rows, weight.shape[0]), BF16)],
-        (VM, VM),
-        [
-            pltpu.VMEM((rows, width), BF16),
-            pltpu.VMEM(facts.shape, F32),
-            pltpu.VMEM((rows, width), BF16),
-            pltpu.SemaphoreType.DMA((1 + 2 * len(inner_dq),)),
-        ],
-        12,
+def query_term(halves, weight, fetched, keys, values, w_query, dks, dvs, count, heads, hp):
+    rows, width = keys.shape
+    feat = weight.shape[0]
+    vm_args, hbm_args = (*halves, weight, *fetched), (keys, values, w_query, *dks, *dvs)
+    return kernel_call(
+        functools.partial(query_kernel, heads, hp, count),
+        (*vm_args, *hbm_args),
+        [VM] * len(vm_args) + [HB] * len(hbm_args),
+        [((rows, width), BF16), ((rows, feat), BF16)]
+        + [((rows, width), BF16)] * 4
+        + [((rows, LANES), F32)]
+        + [((feat // 2, width), BF16)] * 2,
+        (VM,) * 9,
+        [pltpu.SemaphoreType.DMA((4 + 2 * len(dks),))],
+        8,
         "query_term",
         6,
     )
@@ -408,14 +420,17 @@
     )[0]
 
 
-def finish_kernel(dq_ref, w_ref, *refs):
+def finish_kernel(dq_ref, w_ref, early_ref, *refs):
     arrived, (out_hbm, sent, sems) = refs[:-3], refs[-3:]
-    feat = sent.shape[1]
+    half = w_ref.shape[0]
     copies = Copies(sems)
-    block = min(512, feat)
-    for at in range(0, feat, block):
+    block = min(512, half)
+    for at in range(0, 2 * half, block):
         wide = slice(at, at + block)
-        total = dot(dq_ref[...], w_ref[wide, :], NT).astype(BF16).astype(F32)
+        if at < half:
+            total = early_ref[:, wide].astype(F32)
+        else:
+            total = dot(dq_ref[...], w_ref[at - half : at - half + block, :], NT).astype(BF16).astype(F32)
         for other in arrived:
             total = total + other[:, wide].astype(F32)
         sent[:, wide] = total.astype(BF16)
@@ -423,17 +438,17 @@
     copies.finish()
 
 
-def finish(d_query, weight, arrived):
-    rows, feat = d_query.shape[0], weight.shape[0]
+def finish(d_query, weight, early, arrived):
+    rows, feat = arrived[0].shape
     return kernel_call(
         finish_kernel,
-        (d_query, weight, *arrived),
-        [VM, VM] + [VM] * len(arrived),
+        (d_query, weight, early, *arrived),
+        [VM] * (3 + len(arrived)),
         [((rows, feat), BF16)],
         (HB,),
         [
             pltpu.VMEM((rows, feat), BF16),
-            pltpu.SemaphoreType.DMA((feat // min(512, feat),)),
+            pltpu.SemaphoreType.DMA((feat // min(512, feat // 2),)),
         ],
         12,
         "finish",
@@ -441,70 +456,41 @@
     )[0]
 
 
-def close_kernel(heads, hp, count, *refs):
-    mine_ref, theirs_ref, in_hbm, v_hbm, facts_hbm, w_hbm = refs[:6]
-    rest = refs[6:-11]
+def close_kernel(
+    heads, hp, mine_ref, theirs_ref, k_ref, v_ref, dk_ref, dv_ref, table_ref, dq_ref, own_ref, dk_hbm, dv_hbm, early_ref, kside, vside, sems
+):
     upper = lax.axis_index("ctx") % 2 == 1
-    dk_hbm, dv_hbm, own_ref, kbuf, vbuf, facts_ref, dkbuf, dvbuf, kside, vside, sems = refs[-11:]
-    dks, dvs = rest[: len(rest) // 2], rest[len(rest) // 2 :]
-    pair = 2 if all(edge % 2 == 0 for span in spans_of(heads) for edge in span) else 1
+    pair = min(2, heads)
     copies = Copies(sems)
-    facts_in = copies.start(facts_hbm, facts_ref)
-    loads = []
-    for (start, last), dk, dv in zip(spans_of(heads), dks, dvs):
-        for h in range(start, last, pair):
-            wide = pl.ds(h * HDIM, pair * HDIM)
-            part = pl.ds((h - start) * HDIM, pair * HDIM)
-            loads.append(
-                (
-                    copies.start(v_hbm.at[:, wide], vbuf.at[:, wide]),
-                    copies.start(dk.at[:, part], dkbuf.at[:, wide]),
-                    copies.start(in_hbm.at[:, wide], kbuf.at[:, wide]),
-                    copies.start(dv.at[:, part], dvbuf.at[:, wide]),
-                )
-            )
-    copies.store(rows_of(w_hbm, 0, count, own_ref.shape[0]), own_ref)
-    facts_in.wait()
-    table = turned(facts_ref[...])
+    table = table_ref[...]
     for h in range(heads):
-        if h % pair == 0:
-            for copy in loads[h // pair]:
-                copy.wait()
         cols = slice(h * HDIM, (h + 1) * HDIM)
         adjoint = whole_head(upper, h, mine_ref, theirs_ref)
         tail, gain = column(table, 2 * hp + h), column(table, hp + h)
-        carry_k = dot(vbuf[:, cols], adjoint, NT)
-        kside[:, cols] = (gain * (dkbuf[:, cols].astype(F32) + tail * carry_k)).astype(BF16)
-        carry_v = dot(scaled_keys(table, hp, h, kbuf[:, cols]), adjoint, NN)
-        vside[:, cols] = (dvbuf[:, cols].astype(F32) + tail * carry_v).astype(BF16)
+        carry_k = dot(v_ref[:, cols], adjoint, NT)
+        kside[:, cols] = (gain * (dk_ref[:, cols].astype(F32) + tail * carry_k)).astype(BF16)
+        carry_v = dot(scaled_keys(table, hp, h, k_ref[:, cols]), adjoint, NN)
+        vside[:, cols] = (dv_ref[:, cols].astype(F32) + tail * carry_v).astype(BF16)
         if (h + 1) % pair == 0:
             wide = slice((h + 1 - pair) * HDIM, (h + 1) * HDIM)
             copies.store(kside.at[:, wide], dk_hbm.at[:, wide])
             copies.store(vside.at[:, wide], dv_hbm.at[:, wide])
+    put_terms(dq_ref, own_ref, early_ref)
     copies.finish()
 
 
-def close(halves, dks, dvs, keys, values, facts, w_query, feat, count, heads, hp):
-    rows, width = values.shape
-    args = (keys, values, facts, w_query, *dks, *dvs)
+def close(halves, held, d_query, own, heads, hp):
+    rows, width = d_query.shape
+    args = (*halves, *held, d_query, own)
     buf = pltpu.VMEM((rows, width), BF16)
     return kernel_call(
-        functools.partial(close_kernel, heads, hp, count),
-        (*halves, *args),
-        [VM, VM] + [HB] * len(args),
-        [((rows, width), BF16)] * 2 + [((feat, width), BF16)],
+        functools.partial(close_kernel, heads, hp),
+        args,
+        [VM] * len(args),
+        [((rows, width), BF16)] * 2 + [((rows, own.shape[0]), BF16)],
         (HB, HB, VM),
-        [
-            buf,
-            buf,
-            pltpu.VMEM(facts.shape, F32),
-            buf,
-            buf,
-            buf,
-            buf,
-            pltpu.SemaphoreType.DMA((2 + 6 * heads,)),
-        ],
-        20,
+        [buf, buf, pltpu.SemaphoreType.DMA((2 * (heads // min(2, heads)),))],
+        12,
         "close",
         100,
     )
@@ -595,7 +581,9 @@
     for stage in range(stages + 1):
         if stage == stages:
             weight, _ = barrier((w_query, adjoints.sent))
-            weights = fetch(head_size, weight, feat)
+            dqs, dks, dvs = zip(*inner_parts)
+            *fetched, = fetch(head_size, weight, d_out, facts, dqs, feat, heads)
+            fetched, weights = fetched[:3], fetched[3:]
         states.go()
         if stage == 0:
             states.arrived, query, adjoints.kept, adjoints.sent = barrier(
@@ -619,26 +607,22 @@
         if stage >= 1:
             adjoints.arrived, _ = barrier((adjoints.arrived, states.sent if stage < stages else states.total))
             adjoints.take()
-    while pending:
-        inner_parts.append(inner(*pending.pop(0), query, keys, values, d_out, facts, hp))
     adjoints.go()
     states.arrived, _ = barrier((states.arrived, adjoints.sent))
     state_halves = (states.total, states.arrived)
     adjoint_halves = (adjoints.total, adjoints.arrived)
-    dqs, dks, dvs = zip(*inner_parts)
-
     arrived = []
     for shift in range(1, head_size):
         ring = [(i, (i + shift) % head_size) for i in range(head_size)]
         if shift == 1:
-            d_query, term = query_term(state_halves, dqs, d_out, facts, weights[0], heads, hp)
+            d_query, term, *held, own_first, own_second = query_term(
+                state_halves, weights[0], fetched, keys, values, w_query, dks, dvs, head_size, heads, hp
+            )
         else:
             term = plain_term(d_query, weights[shift - 1])
         arrived.append(lax.ppermute(term, "head", ring))
-    d_keys, d_values, own = close(
-        adjoint_halves, dks, dvs, keys, values, facts, w_query, feat, head_size, heads, hp
-    )
-    d_hidden = finish(d_query, own, arrived)
+    d_keys, d_values, early = close(adjoint_halves, held, d_query, own_first, heads, hp)
+    d_hidden = finish(d_query, own_second, early, arrived)
     return (d_hidden, d_keys, d_values)
 
 

time: 58.4 us -> 56.5 us (0.967)
  Pallas kernels: 38.2 us -> 35.9 us
    pallas_call x9, Pallas kernels: 38.2 us -> 35.9 us  [kernel_call(): pl.pallas_call(kernel, in_specs=specs, out_specs=tuple(out_specs), out_sh...]
    ppermute x1, waiting for transfers between devices: 0.01 us -> 0.95 us  [body(): arrived.append(lax.ppermute(term, 'head', ring))]
  transfers between devices with their start and end apart: 12 -> 12, of which waited for: 1 -> 3; matrix products, arithmetic and copies ran while one was open for 1% -> 1% of each run, Pallas kernels for 60% -> 59%
where the time goes in v12:
time: 56.5 us; the launch traced here: 56.2 us
  Pallas kernels  35.9 us (64%)
  starting transfers between devices  14.2 us (25%)
  waiting for transfers between devices  4.15 us (7%)
  between operations  1 us (2%)
  other arithmetic  0.98 us (2%)
    pallas_call x9, Pallas kernels, kernel_call(): pl.pallas_call(kernel, in_specs=specs, out_specs=tuple(out_specs), out_sh...  35.9 us
    ppermute x10, starting transfers between devices, send(): return lax.ppermute(array, 'ctx', [(i, i ^ dist) for i in range(ctx_size)])  13.7 us
    ppermute x10, waiting for transfers between devices, send(): return lax.ppermute(array, 'ctx', [(i, i ^ dist) for i in range(ctx_size)])  3.2 us
  transfers between devices with their start and end apart: 12, of which 3 were waited for; matrix products, arithmetic and copies ran while one was open for 1% of the time, Pallas kernels for 59%

profile of v12, /device:TPU:0, one launch (start us, length us, event | category | flops | bytes accessed | tf_op | source)
XLA Modules:
  0.0 56.2 jit_solution(9389953653435532216)
XLA Ops:
  0.6 0.5 collective-permute-start.1
  1.1 3.7 %prepare.1 = (f32[32,512]{1,0:T(8,128)}, bf16[512,128]{1,0:T(8,128)(2,1)S(1)}, bf16[528,128]{1,0:T(8,128)(2,1)S(1)}, f32[8,128]{1,0:T(8,128)S(1)}) custom-call(f32[8,512]{1,0:T(8,128)} %bitcast.123, bf16[512,1024]{1,0:T(8,128)(2,1)} %refs_6_.1, bf16[512,1024]{1,0:T(8,128)(2,1)} %refs_7_.1), custom_call_target="tpu_custom_call" | custom-call | flops 4000000000 | bytes 1 | tf_op jit(solution)/shard_map/prepare/pallas_call | solution.py:34
  4.8 2.6 %collective-permute-start = (bf16[528,128]{1,0:T(8,128)(2,1)S(1)}, bf16[528,128]{1,0:T(8,128)(2,1)S(1)}, u32[]{:S(2)}, u32[]{:S(2)}) collective-permute-start(bf16[528,128]{1,0:T(8,128)(2,1)S(1)} %get-tuple-element.60), channel_id=1, source_target_pairs={{0,2},{2,0},{4,6},{6,4},{8,10},{10,8},{12,14},{14,12},{16,18},{18,... | collective-permute-start | bytes 405512 | tf_op jit(solution)/shard_map/ppermute | solution.py:526
  7.4 7.9 %project.1 = (bf16[512,1024]{1,0:T(8,128)(2,1)}, bf16[512,128]{1,0:T(8,128)(2,1)S(1)}, bf16[512,128]{1,0:T(8,128)(2,1)S(1)}) custom-call(bf16[512,2048]{1,0:T(8,128)(2,1)} %refs_0_.1, bf16[512,2048]{1,0:T(8,128)(2,1)S(1)} %collective-permute-done.1.refs_1_, bf16[4096,1024]{1,0:T(8,128)(2,1)} %refs_8_.1, bf16[512,1024]{1,0:T(8,128)(2,1)} %do_hbm.1, ...), custom_call_target="tpu_custom_call" | custom-call | flops 8000000000 | bytes 1 | tf_op jit(solution)/shard_map/project/pallas_call | solution.py:34
  15.4 0.1 fusion.21
  15.4 1.6 %collective-permute-start.2 = (bf16[528,128]{1,0:T(8,128)(2,1)S(1)}, bf16[528,128]{1,0:T(8,128)(2,1)S(1)}, u32[]{:S(2)}, u32[]{:S(2)}) collective-permute-start(bf16[528,128]{1,0:T(8,128)(2,1)S(1)} %pad_maximum_fusion), channel_id=1, source_target_pairs={{0,4},{2,6},{4,0},{6,2},{8,12},{10,14},{12,8},{14,10},{16,20},{18,... | collective-permute-start | bytes 405512 | tf_op jit(solution)/shard_map/ppermute | solution.py:526
  17.0 0.6 %collective-permute-start.4 = (bf16[512,128]{1,0:T(8,128)(2,1)S(1)}, bf16[512,128]{1,0:T(8,128)(2,1)S(1)}, u32[]{:S(2)}, u32[]{:S(2)}) collective-permute-start(bf16[512,128]{1,0:T(8,128)(2,1)S(1)} %get-tuple-element.69), channel_id=1, source_target_pairs={{0,2},{2,0},{4,6},{6,4},{8,10},{10,8},{12,14},{14,12},{16,18},{18,... | collective-permute-start | bytes 393224 | tf_op jit(solution)/shard_map/ppermute | solution.py:526
  17.6 3.5 %inner.3 = (bf16[512,256]{1,0:T(8,128)(2,1)}, bf16[512,256]{1,0:T(8,128)(2,1)}, bf16[512,256]{1,0:T(8,128)(2,1)}) custom-call(bf16[512,1024]{1,0:T(8,128)(2,1)} %get-tuple-element.83.refs_0_, bf16[512,1024]{1,0:T(8,128)(2,1)} %refs_6_.1, bf16[512,1024]{1,0:T(8,128)(2,1)} %refs_7_.1, bf16[512,1024]{1,0:T(8,128)(2,1)} %do_hbm.1, ...), custom_call_target="tpu_custom_call" | custom-call | flops 1000000000 | bytes 1 | tf_op jit(solution)/shard_map/inner/pallas_call | solution.py:34
  21.2 0.1 fusion.23
  21.3 1.6 %collective-permute-start.3 = (bf16[528,128]{1,0:T(8,128)(2,1)S(1)}, bf16[528,128]{1,0:T(8,128)(2,1)S(1)}, u32[]{:S(2)}, u32[]{:S(2)}) collective-permute-start(bf16[528,128]{1,0:T(8,128)(2,1)S(1)} %pad_maximum_fusion.1), channel_id=1, source_target_pairs={{0,8},{2,10},{4,12},{6,14},{8,0},{10,2},{12,4},{14,6},{16,24},{18,... | collective-permute-start | bytes 405512 | tf_op jit(solution)/shard_map/ppermute | solution.py:526
  23.0 0.1 fusion.20
  23.0 1.6 %collective-permute-start.6 = (bf16[512,128]{1,0:T(8,128)(2,1)S(1)}, bf16[512,128]{1,0:T(8,128)(2,1)S(1)}, u32[]{:S(2)}, u32[]{:S(2)}) collective-permute-start(bf16[512,128]{1,0:T(8,128)(2,1)S(1)} %fusion.20), channel_id=1, source_target_pairs={{0,4},{2,6},{4,0},{6,2},{8,12},{10,14},{12,8},{14,10},{16,20},{18,... | collective-permute-start | bytes 393224 | tf_op jit(solution)/shard_map/ppermute | solution.py:526
  24.6 3.5 %inner.4 = (bf16[512,256]{1,0:T(8,128)(2,1)}, bf16[512,256]{1,0:T(8,128)(2,1)}, bf16[512,256]{1,0:T(8,128)(2,1)}) custom-call(bf16[512,1024]{1,0:T(8,128)(2,1)} %get-tuple-element.83.refs_0_, bf16[512,1024]{1,0:T(8,128)(2,1)} %refs_6_.1, bf16[512,1024]{1,0:T(8,128)(2,1)} %refs_7_.1, bf16[512,1024]{1,0:T(8,128)(2,1)} %do_hbm.1, ...), custom_call_target="tpu_custom_call" | custom-call | flops 1000000000 | bytes 1 | tf_op jit(solution)/shard_map/inner/pallas_call | solution.py:34
  28.2 0.1 fusion.14
  28.3 0.1 fusion.22
  28.4 0.8 %collective-permute-start.7 = (bf16[512,128]{1,0:T(8,128)(2,1)S(1)}, bf16[512,128]{1,0:T(8,128)(2,1)S(1)}, u32[]{:S(2)}, u32[]{:S(2)}) collective-permute-start(bf16[512,128]{1,0:T(8,128)(2,1)S(1)} %fusion.22), channel_id=1, source_target_pairs={{0,8},{2,10},{4,12},{6,14},{8,0},{10,2},{12,4},{14,6},{16,24},{18,... | collective-permute-start | bytes 393224 | tf_op jit(solution)/shard_map/ppermute | solution.py:526
  29.2 2.6 %collective-permute-start.5 = (bf16[512,128]{1,0:T(8,128)(2,1)S(1)}, bf16[512,128]{1,0:T(8,128)(2,1)S(1)}, u32[]{:S(2)}, u32[]{:S(2)}) collective-permute-start(bf16[512,128]{1,0:T(8,128)(2,1)S(1)} %fusion.14), channel_id=1, source_target_pairs={{0,16},{2,18},{4,20},{6,22},{8,24},{10,26},{12,28},{14,30},{16,0},... | collective-permute-start | bytes 393224 | tf_op jit(solution)/shard_map/ppermute | solution.py:526
  31.8 5.0 %inner.5 = (bf16[512,512]{1,0:T(8,128)(2,1)}, bf16[512,512]{1,0:T(8,128)(2,1)}, bf16[512,512]{1,0:T(8,128)(2,1)}) custom-call(bf16[512,1024]{1,0:T(8,128)(2,1)} %get-tuple-element.83.refs_0_, bf16[512,1024]{1,0:T(8,128)(2,1)} %refs_6_.1, bf16[512,1024]{1,0:T(8,128)(2,1)} %refs_7_.1, bf16[512,1024]{1,0:T(8,128)(2,1)} %do_hbm.1, ...), custom_call_target="tpu_custom_call" | custom-call | flops 1000000000 | bytes 1 | tf_op jit(solution)/shard_map/inner/pallas_call | solution.py:34
  36.8 0.1 fusion.19
  36.9 0.4 collective-permute-start.9
  37.3 0.2 fusion.4
  37.5 1.0 %collective-permute-start.8 = (bf16[512,128]{1,0:T(8,128)(2,1)S(1)}, bf16[512,128]{1,0:T(8,128)(2,1)S(1)}, u32[]{:S(2)}, u32[]{:S(2)}) collective-permute-start(bf16[512,128]{1,0:T(8,128)(2,1)S(1)} %get-tuple-element.127), channel_id=1, source_target_pairs={{0,2},{2,0},{4,6},{6,4},{8,10},{10,8},{12,14},{14,12},{16,18},{18,... | collective-permute-start | bytes 393224 | tf_op jit(solution)/shard_map/ppermute | solution.py:526
  38.4 2.9 %fetch.1 = (bf16[512,1024]{1,0:T(8,128)(2,1)S(1)}, bf16[512,1024]{1,0:T(8,128)(2,1)S(1)}, f32[512,128]{1,0:T(8,128)S(1)}, bf16[2048,1024]{1,0:T(8,128)(2,1)S(1)}) custom-call(bf16[4096,1024]{1,0:T(8,128)(2,1)} %refs_8_.1, bf16[512,1024]{1,0:T(8,128)(2,1)} %do_hbm.1, f32[32,512]{1,0:T(8,128)} %get-tuple-element.61.refs_4_.facts_hbm, ...), custom_call_target="tpu_custom_call" | custom-call | flops 4000000000 | bytes 1 | tf_op jit(solution)/shard_map/fetch/pallas_call | solution.py:34
  41.3 3.0 %collective-permute-done.9 = bf16[512,128]{1,0:T(8,128)(2,1)S(1)} collective-permute-done((bf16[512,128]{1,0:T(8,128)(2,1)S(1)}, bf16[512,128]{1,0:T(8,128)(2,1)S(1)}, u32[]{:S(2)}, u32[]{:S(2)}) %collective-permute-start.9) | collective-permute-done | bytes 131104 | tf_op jit(solution)/shard_map/ppermute | solution.py:526
  44.2 0.2 fusion.12
  44.4 1.0 %collective-permute-start.10 = (bf16[512,128]{1,0:T(8,128)(2,1)S(1)}, bf16[512,128]{1,0:T(8,128)(2,1)S(1)}, u32[]{:S(2)}, u32[]{:S(2)}) collective-permute-start(bf16[512,128]{1,0:T(8,128)(2,1)S(1)} %get-tuple-element.130), channel_id=1, source_target_pairs={{0,2},{2,0},{4,6},{6,4},{8,10},{10,8},{12,14},{14,12},{16,18},{18,... | collective-permute-start | bytes 393224 | tf_op jit(solution)/shard_map/ppermute | solution.py:526
  45.4 3.8 %query_term.1 = (bf16[512,1024]{1,0:T(8,128)(2,1)S(1)}, bf16[512,2048]{1,0:T(8,128)(2,1)S(1)}, bf16[512,1024]{1,0:T(8,128)(2,1)S(1)}, bf16[512,1024]{1,0:T(8,128...) custom-call(bf16[512,128]{1,0:T(8,128)(2,1)S(1)} %get-tuple-element., ...), custom_call_target="tpu_custom_call" | custom-call | flops 6000000000 | bytes 1 | tf_op jit(solution)/shard_map/query_term/pallas_call | solution.py:34
  49.2 0.1 collective-permute-start.11
  49.3 0.2 collective-permute-done.10.theirs_ref
  49.4 3.0 %close.1 = (bf16[512,1024]{1,0:T(8,128)(2,1)}, bf16[512,1024]{1,0:T(8,128)(2,1)}, bf16[512,1024]{1,0:T(8,128)(2,1)S(1)}) custom-call(bf16[512,128]{1,0:T(8,128)(2,1)S(1)} %get-tuple-element.129.mine_ref, bf16[512,128]{1,0:T(8,128)(2,1)S(1)} %collective-permute-done.10.theirs_ref, bf16[512,1024]{1,0:T(8,128)(2,1)S(1)} %get-tuple-element.107.k_ref, ...), custom_call_target="tpu_custom_call" | custom-call | flops 99999997952 | bytes 1 | tf_op jit(solution)/shard_map/close/pallas_call | solution.py:34
  52.5 0.9 %collective-permute-done.11.refs_0_ = bf16[512,2048]{1,0:T(8,128)(2,1)S(1)} collective-permute-done((bf16[512,2048]{1,0:T(8,128)(2,1)S(1)}, bf16[512,2048]{1,0:T(8,128)(2,1)S(1)}, u32[]{:S(2)}, u32[]{:S(2)}) %collective-permute-start.11) | collective-permute-done | bytes 2097184 | tf_op jit(solution)/shard_map/ppermute | solution.py:623
  53.4 2.6 %finish.1 = bf16[512,2048]{1,0:T(8,128)(2,1)} custom-call(bf16[512,1024]{1,0:T(8,128)(2,1)S(1)} %get-tuple-element.105.dq_ref, bf16[1024,1024]{1,0:T(8,128)(2,1)S(1)} %get-tuple-element.106.w_ref, bf16[512,1024]{1,0:T(8,128)(2,1)S(1)} %get-tuple-element.113.early_ref, bf16[512,2048]{1,0:T(8,128)(2,1)S(1)} %collective-permute-done.11.refs_0_), custom_call_target="tpu_custom_call" | custom-call | flops 6000000000 | bytes 1 | tf_op jit(solution)/shard_map/finish/pallas_call | solution.py:34
  (17 shorter events, 0.1 us)
Async XLA Ops:
  0.6 6.8 %collective-permute-start.1 = (bf16[512,2048]{1,0:T(8,128)(2,1)}, bf16[512,2048]{1,0:T(8,128)(2,1)S(1)}, u32[]{:S(2)}, u32[]{:S(2)}) collective-permute-start(bf16[512,2048]{1,0:T(8,128)(2,1)} %refs_0_.1), channel_id=1, source_target_pairs={{0,1},{1,0},{2,3},{3,2},{4,5},{5,4},{6,7},{7,6},{8,9},{9,8},{10,11... | collective-permute-start | bytes 6291464 | tf_op jit(solution)/shard_map/ppermute | solution.py:510
  4.8 10.5 %collective-permute-start = (bf16[528,128]{1,0:T(8,128)(2,1)S(1)}, bf16[528,128]{1,0:T(8,128)(2,1)S(1)}, u32[]{:S(2)}, u32[]{:S(2)}) collective-permute-start(bf16[528,128]{1,0:T(8,128)(2,1)S(1)} %get-tuple-element.60), channel_id=1, source_target_pairs={{0,2},{2,0},{4,6},{6,4},{8,10},{10,8},{12,14},{14,12},{16,18},{18,... | collective-permute-start | bytes 405512 | tf_op jit(solution)/shard_map/ppermute | solution.py:526
  15.4 5.8 %collective-permute-start.2 = (bf16[528,128]{1,0:T(8,128)(2,1)S(1)}, bf16[528,128]{1,0:T(8,128)(2,1)S(1)}, u32[]{:S(2)}, u32[]{:S(2)}) collective-permute-start(bf16[528,128]{1,0:T(8,128)(2,1)S(1)} %pad_maximum_fusion), channel_id=1, source_target_pairs={{0,4},{2,6},{4,0},{6,2},{8,12},{10,14},{12,8},{14,10},{16,20},{18,... | collective-permute-start | bytes 405512 | tf_op jit(solution)/shard_map/ppermute | solution.py:526
  17.0 6.0 %collective-permute-start.4 = (bf16[512,128]{1,0:T(8,128)(2,1)S(1)}, bf16[512,128]{1,0:T(8,128)(2,1)S(1)}, u32[]{:S(2)}, u32[]{:S(2)}) collective-permute-start(bf16[512,128]{1,0:T(8,128)(2,1)S(1)} %get-tuple-element.69), channel_id=1, source_target_pairs={{0,2},{2,0},{4,6},{6,4},{8,10},{10,8},{12,14},{14,12},{16,18},{18,... | collective-permute-start | bytes 393224 | tf_op jit(solution)/shard_map/ppermute | solution.py:526
  21.3 6.8 %collective-permute-start.3 = (bf16[528,128]{1,0:T(8,128)(2,1)S(1)}, bf16[528,128]{1,0:T(8,128)(2,1)S(1)}, u32[]{:S(2)}, u32[]{:S(2)}) collective-permute-start(bf16[528,128]{1,0:T(8,128)(2,1)S(1)} %pad_maximum_fusion.1), channel_id=1, source_target_pairs={{0,8},{2,10},{4,12},{6,14},{8,0},{10,2},{12,4},{14,6},{16,24},{18,... | collective-permute-start | bytes 405512 | tf_op jit(solution)/shard_map/ppermute | solution.py:526
  23.0 5.3 %collective-permute-start.6 = (bf16[512,128]{1,0:T(8,128)(2,1)S(1)}, bf16[512,128]{1,0:T(8,128)(2,1)S(1)}, u32[]{:S(2)}, u32[]{:S(2)}) collective-permute-start(bf16[512,128]{1,0:T(8,128)(2,1)S(1)} %fusion.20), channel_id=1, source_target_pairs={{0,4},{2,6},{4,0},{6,2},{8,12},{10,14},{12,8},{14,10},{16,20},{18,... | collective-permute-start | bytes 393224 | tf_op jit(solution)/shard_map/ppermute | solution.py:526
  28.4 8.3 %collective-permute-start.7 = (bf16[512,128]{1,0:T(8,128)(2,1)S(1)}, bf16[512,128]{1,0:T(8,128)(2,1)S(1)}, u32[]{:S(2)}, u32[]{:S(2)}) collective-permute-start(bf16[512,128]{1,0:T(8,128)(2,1)S(1)} %fusion.22), channel_id=1, source_target_pairs={{0,8},{2,10},{4,12},{6,14},{8,0},{10,2},{12,4},{14,6},{16,24},{18,... | collective-permute-start | bytes 393224 | tf_op jit(solution)/shard_map/ppermute | solution.py:526
  29.2 8.1 %collective-permute-start.5 = (bf16[512,128]{1,0:T(8,128)(2,1)S(1)}, bf16[512,128]{1,0:T(8,128)(2,1)S(1)}, u32[]{:S(2)}, u32[]{:S(2)}) collective-permute-start(bf16[512,128]{1,0:T(8,128)(2,1)S(1)} %fusion.14), channel_id=1, source_target_pairs={{0,16},{2,18},{4,20},{6,22},{8,24},{10,26},{12,28},{14,30},{16,0},... | collective-permute-start | bytes 393224 | tf_op jit(solution)/shard_map/ppermute | solution.py:526
  36.9 7.3 %collective-permute-start.9 = (bf16[512,128]{1,0:T(8,128)(2,1)S(1)}, bf16[512,128]{1,0:T(8,128)(2,1)S(1)}, u32[]{:S(2)}, u32[]{:S(2)}) collective-permute-start(bf16[512,128]{1,0:T(8,128)(2,1)S(1)} %fusion.19), channel_id=1, source_target_pairs={{0,16},{2,18},{4,20},{6,22},{8,24},{10,26},{12,28},{14,30},{16,0},... | collective-permute-start | bytes 393224 | tf_op jit(solution)/shard_map/ppermute | solution.py:526
  37.5 7.9 %collective-permute-start.8 = (bf16[512,128]{1,0:T(8,128)(2,1)S(1)}, bf16[512,128]{1,0:T(8,128)(2,1)S(1)}, u32[]{:S(2)}, u32[]{:S(2)}) collective-permute-start(bf16[512,128]{1,0:T(8,128)(2,1)S(1)} %get-tuple-element.127), channel_id=1, source_target_pairs={{0,2},{2,0},{4,6},{6,4},{8,10},{10,8},{12,14},{14,12},{16,18},{18,... | collective-permute-start | bytes 393224 | tf_op jit(solution)/shard_map/ppermute | solution.py:526
  44.4 5.0 %collective-permute-start.10 = (bf16[512,128]{1,0:T(8,128)(2,1)S(1)}, bf16[512,128]{1,0:T(8,128)(2,1)S(1)}, u32[]{:S(2)}, u32[]{:S(2)}) collective-permute-start(bf16[512,128]{1,0:T(8,128)(2,1)S(1)} %get-tuple-element.130), channel_id=1, source_target_pairs={{0,2},{2,0},{4,6},{6,4},{8,10},{10,8},{12,14},{14,12},{16,18},{18,... | collective-permute-start | bytes 393224 | tf_op jit(solution)/shard_map/ppermute | solution.py:526
  49.2 4.2 %collective-permute-start.11 = (bf16[512,2048]{1,0:T(8,128)(2,1)S(1)}, bf16[512,2048]{1,0:T(8,128)(2,1)S(1)}, u32[]{:S(2)}, u32[]{:S(2)}) collective-permute-start(bf16[512,2048]{1,0:T(8,128)(2,1)S(1)} %get-tuple-element.114), channel_id=1, source_target_pairs={{0,1},{1,0},{2,3},{3,2},{4,5},{5,4},{6,7},{7,6},{8,9},{9,8},{10,11... | collective-permute-start | bytes 6291464 | tf_op jit(solution)/shard_map/ppermute | solution.py:623

commit v13 on v12

--- a/solution.py
+++ b/solution.py
@@ -356,7 +356,7 @@
     mine_ref, theirs_ref, w_ref, do_ref, local_ref, table_ref, k_hbm, v_hbm, w_hbm = refs[:9]
     parts = len(spans_of(heads))
     dks, dvs, refs = refs[9 : 9 + parts], refs[9 + parts : 9 + 2 * parts], refs[9 + 2 * parts :]
-    held, out_ref, k_ref, v_ref, dk_ref, dv_ref, next_table, own_first, own_second, sems = refs
+    held, out_ref, k_ref, v_ref, dk_ref, dv_ref, next_table, *owns, sems = refs
     upper = lax.axis_index("ctx") % 2 == 1
     copies = Copies(sems)
     copies.store(k_hbm, k_ref)
@@ -365,10 +365,11 @@
         wide = pl.ds(first * HDIM, (last - first) * HDIM)
         copies.store(dk, dk_ref.at[:, wide])
         copies.store(dv, dv_ref.at[:, wide])
-    half = own_first.shape[0]
-    rows = rows_of(w_hbm, 0, count, 2 * half)
-    copies.store(rows.at[pl.ds(0, half), :], own_first)
-    copies.store(rows.at[pl.ds(half, half), :], own_second)
+    at, rows = 0, rows_of(w_hbm, 0, count, w_ref.shape[0])
+    for own in owns:
+        size = own.shape[0]
+        copies.store(rows.at[pl.ds(at, size), :], own)
+        at += size
     table = table_ref[...]
     next_table[...] = table
     for h in range(heads):
@@ -380,10 +381,10 @@
     copies.finish()
 
 
-def put_terms(dq_ref, w_ref, out_ref):
-    block = min(512, out_ref.shape[1])
-    for at in range(0, out_ref.shape[1], block):
-        out_ref[:, at : at + block] = dot(dq_ref[...], w_ref[at : at + block, :], NT).astype(BF16)
+def put_terms(dq_ref, w_ref, out_ref, first=0):
+    block = min(512, w_ref.shape[0])
+    for at in range(0, w_ref.shape[0], block):
+        out_ref[:, first + at : first + at + block] = dot(dq_ref[...], w_ref[at : at + block, :], NT).astype(BF16)
 
 
 def query_term(halves, weight, fetched, keys, values, w_query, dks, dvs, count, heads, hp):
@@ -397,7 +398,7 @@
         [((rows, width), BF16), ((rows, feat), BF16)]
         + [((rows, width), BF16)] * 4
         + [((rows, LANES), F32)]
-        + [((feat // 2, width), BF16)] * 2,
+        + [((size, width), BF16) for size in (feat // 2, feat // 2)],
         (VM,) * 9,
         [pltpu.SemaphoreType.DMA((4 + 2 * len(dks),))],
         8,
@@ -420,35 +421,32 @@
     )[0]
 
 
-def finish_kernel(dq_ref, w_ref, early_ref, *refs):
-    arrived, (out_hbm, sent, sems) = refs[:-3], refs[-3:]
-    half = w_ref.shape[0]
+def finish_kernel(*refs):
+    terms, (out_hbm, sent, sems) = refs[:-3], refs[-3:]
+    feat = sent.shape[1]
     copies = Copies(sems)
-    block = min(512, half)
-    for at in range(0, 2 * half, block):
+    block = min(512, feat)
+    for at in range(0, feat, block):
         wide = slice(at, at + block)
-        if at < half:
-            total = early_ref[:, wide].astype(F32)
-        else:
-            total = dot(dq_ref[...], w_ref[at - half : at - half + block, :], NT).astype(BF16).astype(F32)
-        for other in arrived:
+        total = terms[0][:, wide].astype(F32)
+        for other in terms[1:]:
             total = total + other[:, wide].astype(F32)
         sent[:, wide] = total.astype(BF16)
         copies.store(sent.at[:, wide], out_hbm.at[:, wide])
     copies.finish()
 
 
-def finish(d_query, weight, early, arrived):
-    rows, feat = arrived[0].shape
+def finish(terms):
+    rows, feat = terms[0].shape
     return kernel_call(
         finish_kernel,
-        (d_query, weight, early, *arrived),
-        [VM] * (3 + len(arrived)),
+        terms,
+        [VM] * len(terms),
         [((rows, feat), BF16)],
         (HB,),
         [
             pltpu.VMEM((rows, feat), BF16),
-            pltpu.SemaphoreType.DMA((feat // min(512, feat // 2),)),
+            pltpu.SemaphoreType.DMA((feat // min(512, feat),)),
         ],
         12,
         "finish",
@@ -457,8 +455,9 @@
 
 
 def close_kernel(
-    heads, hp, mine_ref, theirs_ref, k_ref, v_ref, dk_ref, dv_ref, table_ref, dq_ref, own_ref, dk_hbm, dv_hbm, early_ref, kside, vside, sems
+    heads, hp, mine_ref, theirs_ref, k_ref, v_ref, dk_ref, dv_ref, table_ref, dq_ref, own_ref, second_ref, *refs
 ):
+    dk_hbm, dv_hbm, term_ref, kside, vside, sems = refs
     upper = lax.axis_index("ctx") % 2 == 1
     pair = min(2, heads)
     copies = Copies(sems)
@@ -475,19 +474,20 @@
             wide = slice((h + 1 - pair) * HDIM, (h + 1) * HDIM)
             copies.store(kside.at[:, wide], dk_hbm.at[:, wide])
             copies.store(vside.at[:, wide], dv_hbm.at[:, wide])
-    put_terms(dq_ref, own_ref, early_ref)
+    put_terms(dq_ref, own_ref, term_ref)
+    put_terms(dq_ref, second_ref, term_ref, own_ref.shape[0])
     copies.finish()
 
 
-def close(halves, held, d_query, own, heads, hp):
+def close(halves, held, d_query, owns, heads, hp):
     rows, width = d_query.shape
-    args = (*halves, *held, d_query, own)
+    args = (*halves, *held, d_query, *owns)
     buf = pltpu.VMEM((rows, width), BF16)
     return kernel_call(
         functools.partial(close_kernel, heads, hp),
         args,
         [VM] * len(args),
-        [((rows, width), BF16)] * 2 + [((rows, own.shape[0]), BF16)],
+        [((rows, width), BF16)] * 2 + [((rows, sum(own.shape[0] for own in owns)), BF16)],
         (HB, HB, VM),
         [buf, buf, pltpu.SemaphoreType.DMA((2 * (heads // min(2, heads)),))],
         12,
@@ -615,14 +615,14 @@
     for shift in range(1, head_size):
         ring = [(i, (i + shift) % head_size) for i in range(head_size)]
         if shift == 1:
-            d_query, term, *held, own_first, own_second = query_term(
+            d_query, term, *held, first, second = query_term(
                 state_halves, weights[0], fetched, keys, values, w_query, dks, dvs, head_size, heads, hp
             )
         else:
             term = plain_term(d_query, weights[shift - 1])
         arrived.append(lax.ppermute(term, "head", ring))
-    d_keys, d_values, early = close(adjoint_halves, held, d_query, own_first, heads, hp)
-    d_hidden = finish(d_query, own_second, early, arrived)
+    d_keys, d_values, own = close(adjoint_halves, held, d_query, (first, second), heads, hp)
+    d_hidden = finish((own, *arrived))
     return (d_hidden, d_keys, d_values)
 
 

time: 56.5 us -> 55.3 us (0.979)
  Pallas kernels: 35.9 us -> 35.2 us
    pallas_call x9, Pallas kernels: 35.9 us -> 35.2 us  [kernel_call(): pl.pallas_call(kernel, in_specs=specs, out_specs=tuple(out_specs), out_sh...]
  transfers between devices with their start and end apart: 12 -> 12, of which waited for: 3 -> 3; matrix products, arithmetic and copies ran while one was open for 1% -> 1% of each run, Pallas kernels for 59% -> 61%
where the time goes in v13:
time: 55.3 us; the launch traced here: 55.1 us
  Pallas kernels  35.2 us (64%)
  starting transfers between devices  14.2 us (26%)
  waiting for transfers between devices  3.64 us (7%)
  between operations  1 us (2%)
  other arithmetic  0.97 us (2%)
    pallas_call x9, Pallas kernels, kernel_call(): pl.pallas_call(kernel, in_specs=specs, out_specs=tuple(out_specs), out_sh...  35.2 us
    ppermute x10, starting transfers between devices, send(): return lax.ppermute(array, 'ctx', [(i, i ^ dist) for i in range(ctx_size)])  13.7 us
    ppermute x10, waiting for transfers between devices, send(): return lax.ppermute(array, 'ctx', [(i, i ^ dist) for i in range(ctx_size)])  3.2 us
  transfers between devices with their start and end apart: 12, of which 3 were waited for; matrix products, arithmetic and copies ran while one was open for 1% of the time, Pallas kernels for 61%

profile of v13, /device:TPU:0, one launch (start us, length us, event | category | flops | bytes accessed | tf_op | source)
XLA Modules:
  0.0 55.1 jit_solution(16049816611325566113)
XLA Ops:
  0.6 0.5 collective-permute-start.1
  1.1 3.7 %prepare.1 = (f32[32,512]{1,0:T(8,128)}, bf16[512,128]{1,0:T(8,128)(2,1)S(1)}, bf16[528,128]{1,0:T(8,128)(2,1)S(1)}, f32[8,128]{1,0:T(8,128)S(1)}) custom-call(f32[8,512]{1,0:T(8,128)} %bitcast.123, bf16[512,1024]{1,0:T(8,128)(2,1)} %refs_6_.1, bf16[512,1024]{1,0:T(8,128)(2,1)} %refs_7_.1), custom_call_target="tpu_custom_call" | custom-call | flops 4000000000 | bytes 1 | tf_op jit(solution)/shard_map/prepare/pallas_call | solution.py:34
  4.8 2.6 %collective-permute-start = (bf16[528,128]{1,0:T(8,128)(2,1)S(1)}, bf16[528,128]{1,0:T(8,128)(2,1)S(1)}, u32[]{:S(2)}, u32[]{:S(2)}) collective-permute-start(bf16[528,128]{1,0:T(8,128)(2,1)S(1)} %get-tuple-element.60), channel_id=1, source_target_pairs={{0,2},{2,0},{4,6},{6,4},{8,10},{10,8},{12,14},{14,12},{16,18},{18,... | collective-permute-start | bytes 405512 | tf_op jit(solution)/shard_map/ppermute | solution.py:526
  7.4 7.9 %project.1 = (bf16[512,1024]{1,0:T(8,128)(2,1)}, bf16[512,128]{1,0:T(8,128)(2,1)S(1)}, bf16[512,128]{1,0:T(8,128)(2,1)S(1)}) custom-call(bf16[512,2048]{1,0:T(8,128)(2,1)} %refs_0_.1, bf16[512,2048]{1,0:T(8,128)(2,1)S(1)} %collective-permute-done.1.refs_1_, bf16[4096,1024]{1,0:T(8,128)(2,1)} %refs_8_.1, bf16[512,1024]{1,0:T(8,128)(2,1)} %do_hbm.1, ...), custom_call_target="tpu_custom_call" | custom-call | flops 8000000000 | bytes 1 | tf_op jit(solution)/shard_map/project/pallas_call | solution.py:34
  15.4 0.1 fusion.21
  15.4 1.6 %collective-permute-start.3 = (bf16[528,128]{1,0:T(8,128)(2,1)S(1)}, bf16[528,128]{1,0:T(8,128)(2,1)S(1)}, u32[]{:S(2)}, u32[]{:S(2)}) collective-permute-start(bf16[528,128]{1,0:T(8,128)(2,1)S(1)} %pad_maximum_fusion), channel_id=1, source_target_pairs={{0,4},{2,6},{4,0},{6,2},{8,12},{10,14},{12,8},{14,10},{16,20},{18,... | collective-permute-start | bytes 405512 | tf_op jit(solution)/shard_map/ppermute | solution.py:526
  17.0 0.6 %collective-permute-start.2 = (bf16[512,128]{1,0:T(8,128)(2,1)S(1)}, bf16[512,128]{1,0:T(8,128)(2,1)S(1)}, u32[]{:S(2)}, u32[]{:S(2)}) collective-permute-start(bf16[512,128]{1,0:T(8,128)(2,1)S(1)} %get-tuple-element.65), channel_id=1, source_target_pairs={{0,2},{2,0},{4,6},{6,4},{8,10},{10,8},{12,14},{14,12},{16,18},{18,... | collective-permute-start | bytes 393224 | tf_op jit(solution)/shard_map/ppermute | solution.py:526
  17.6 3.5 %inner.3 = (bf16[512,256]{1,0:T(8,128)(2,1)}, bf16[512,256]{1,0:T(8,128)(2,1)}, bf16[512,256]{1,0:T(8,128)(2,1)}) custom-call(bf16[512,1024]{1,0:T(8,128)(2,1)} %get-tuple-element.83.refs_0_, bf16[512,1024]{1,0:T(8,128)(2,1)} %refs_6_.1, bf16[512,1024]{1,0:T(8,128)(2,1)} %refs_7_.1, bf16[512,1024]{1,0:T(8,128)(2,1)} %do_hbm.1, ...), custom_call_target="tpu_custom_call" | custom-call | flops 1000000000 | bytes 1 | tf_op jit(solution)/shard_map/inner/pallas_call | solution.py:34
  21.2 0.1 fusion.23
  21.3 1.6 %collective-permute-start.5 = (bf16[528,128]{1,0:T(8,128)(2,1)S(1)}, bf16[528,128]{1,0:T(8,128)(2,1)S(1)}, u32[]{:S(2)}, u32[]{:S(2)}) collective-permute-start(bf16[528,128]{1,0:T(8,128)(2,1)S(1)} %pad_maximum_fusion.1), channel_id=1, source_target_pairs={{0,8},{2,10},{4,12},{6,14},{8,0},{10,2},{12,4},{14,6},{16,24},{18,... | collective-permute-start | bytes 405512 | tf_op jit(solution)/shard_map/ppermute | solution.py:526
  23.0 0.1 fusion.20
  23.0 1.6 %collective-permute-start.4 = (bf16[512,128]{1,0:T(8,128)(2,1)S(1)}, bf16[512,128]{1,0:T(8,128)(2,1)S(1)}, u32[]{:S(2)}, u32[]{:S(2)}) collective-permute-start(bf16[512,128]{1,0:T(8,128)(2,1)S(1)} %fusion.20), channel_id=1, source_target_pairs={{0,4},{2,6},{4,0},{6,2},{8,12},{10,14},{12,8},{14,10},{16,20},{18,... | collective-permute-start | bytes 393224 | tf_op jit(solution)/shard_map/ppermute | solution.py:526
  24.6 3.5 %inner.4 = (bf16[512,256]{1,0:T(8,128)(2,1)}, bf16[512,256]{1,0:T(8,128)(2,1)}, bf16[512,256]{1,0:T(8,128)(2,1)}) custom-call(bf16[512,1024]{1,0:T(8,128)(2,1)} %get-tuple-element.83.refs_0_, bf16[512,1024]{1,0:T(8,128)(2,1)} %refs_6_.1, bf16[512,1024]{1,0:T(8,128)(2,1)} %refs_7_.1, bf16[512,1024]{1,0:T(8,128)(2,1)} %do_hbm.1, ...), custom_call_target="tpu_custom_call" | custom-call | flops 1000000000 | bytes 1 | tf_op jit(solution)/shard_map/inner/pallas_call | solution.py:34
  28.2 0.1 fusion.14
  28.3 0.1 fusion.22
  28.4 0.8 %collective-permute-start.6 = (bf16[512,128]{1,0:T(8,128)(2,1)S(1)}, bf16[512,128]{1,0:T(8,128)(2,1)S(1)}, u32[]{:S(2)}, u32[]{:S(2)}) collective-permute-start(bf16[512,128]{1,0:T(8,128)(2,1)S(1)} %fusion.22), channel_id=1, source_target_pairs={{0,8},{2,10},{4,12},{6,14},{8,0},{10,2},{12,4},{14,6},{16,24},{18,... | collective-permute-start | bytes 393224 | tf_op jit(solution)/shard_map/ppermute | solution.py:526
  29.2 2.6 %collective-permute-start.8 = (bf16[512,128]{1,0:T(8,128)(2,1)S(1)}, bf16[512,128]{1,0:T(8,128)(2,1)S(1)}, u32[]{:S(2)}, u32[]{:S(2)}) collective-permute-start(bf16[512,128]{1,0:T(8,128)(2,1)S(1)} %fusion.14), channel_id=1, source_target_pairs={{0,16},{2,18},{4,20},{6,22},{8,24},{10,26},{12,28},{14,30},{16,0},... | collective-permute-start | bytes 393224 | tf_op jit(solution)/shard_map/ppermute | solution.py:526
  31.8 5.0 %inner.5 = (bf16[512,512]{1,0:T(8,128)(2,1)}, bf16[512,512]{1,0:T(8,128)(2,1)}, bf16[512,512]{1,0:T(8,128)(2,1)}) custom-call(bf16[512,1024]{1,0:T(8,128)(2,1)} %get-tuple-element.83.refs_0_, bf16[512,1024]{1,0:T(8,128)(2,1)} %refs_6_.1, bf16[512,1024]{1,0:T(8,128)(2,1)} %refs_7_.1, bf16[512,1024]{1,0:T(8,128)(2,1)} %do_hbm.1, ...), custom_call_target="tpu_custom_call" | custom-call | flops 1000000000 | bytes 1 | tf_op jit(solution)/shard_map/inner/pallas_call | solution.py:34
  36.8 0.1 fusion.19
  36.9 0.4 collective-permute-start.7
  37.3 0.2 fusion.2
  37.5 1.0 %collective-permute-start.10 = (bf16[512,128]{1,0:T(8,128)(2,1)S(1)}, bf16[512,128]{1,0:T(8,128)(2,1)S(1)}, u32[]{:S(2)}, u32[]{:S(2)}) collective-permute-start(bf16[512,128]{1,0:T(8,128)(2,1)S(1)} %get-tuple-element.127), channel_id=1, source_target_pairs={{0,2},{2,0},{4,6},{6,4},{8,10},{10,8},{12,14},{14,12},{16,18},{18,... | collective-permute-start | bytes 393224 | tf_op jit(solution)/shard_map/ppermute | solution.py:526
  38.4 2.9 %fetch.1 = (bf16[512,1024]{1,0:T(8,128)(2,1)S(1)}, bf16[512,1024]{1,0:T(8,128)(2,1)S(1)}, f32[512,128]{1,0:T(8,128)S(1)}, bf16[2048,1024]{1,0:T(8,128)(2,1)S(1)}) custom-call(bf16[4096,1024]{1,0:T(8,128)(2,1)} %refs_8_.1, bf16[512,1024]{1,0:T(8,128)(2,1)} %do_hbm.1, f32[32,512]{1,0:T(8,128)} %get-tuple-element.61.refs_4_.facts_hbm, ...), custom_call_target="tpu_custom_call" | custom-call | flops 4000000000 | bytes 1 | tf_op jit(solution)/shard_map/fetch/pallas_call | solution.py:34
  41.3 3.0 %collective-permute-done.7 = bf16[512,128]{1,0:T(8,128)(2,1)S(1)} collective-permute-done((bf16[512,128]{1,0:T(8,128)(2,1)S(1)}, bf16[512,128]{1,0:T(8,128)(2,1)S(1)}, u32[]{:S(2)}, u32[]{:S(2)}) %collective-permute-start.7) | collective-permute-done | bytes 131104 | tf_op jit(solution)/shard_map/ppermute | solution.py:526
  44.2 0.2 fusion.12
  44.4 1.0 %collective-permute-start.9 = (bf16[512,128]{1,0:T(8,128)(2,1)S(1)}, bf16[512,128]{1,0:T(8,128)(2,1)S(1)}, u32[]{:S(2)}, u32[]{:S(2)}) collective-permute-start(bf16[512,128]{1,0:T(8,128)(2,1)S(1)} %get-tuple-element.129), channel_id=1, source_target_pairs={{0,2},{2,0},{4,6},{6,4},{8,10},{10,8},{12,14},{14,12},{16,18},{18,... | collective-permute-start | bytes 393224 | tf_op jit(solution)/shard_map/ppermute | solution.py:526
  45.4 3.8 %query_term.1 = (bf16[512,1024]{1,0:T(8,128)(2,1)S(1)}, bf16[512,2048]{1,0:T(8,128)(2,1)S(1)}, bf16[512,1024]{1,0:T(8,128)(2,1)S(1)}, bf16[512,1024]{1,0:T(8,128...) custom-call(bf16[512,128]{1,0:T(8,128)(2,1)S(1)} %get-tuple-element., ...), custom_call_target="tpu_custom_call" | custom-call | flops 6000000000 | bytes 1 | tf_op jit(solution)/shard_map/query_term/pallas_call | solution.py:34
  49.2 0.1 collective-permute-start.11
  49.3 0.2 collective-permute-done.9.theirs_ref
  49.4 3.5 %close.1 = (bf16[512,1024]{1,0:T(8,128)(2,1)}, bf16[512,1024]{1,0:T(8,128)(2,1)}, bf16[512,2048]{1,0:T(8,128)(2,1)S(1)}) custom-call(bf16[512,128]{1,0:T(8,128)(2,1)S(1)} %get-tuple-element.130.mine_ref, bf16[512,128]{1,0:T(8,128)(2,1)S(1)} %collective-permute-done.9.theirs_ref, bf16[512,1024]{1,0:T(8,128)(2,1)S(1)} %get-tuple-element.105.k_ref, ...), custom_call_target="tpu_custom_call" | custom-call | flops 99999997952 | bytes 1 | tf_op jit(solution)/shard_map/close/pallas_call | solution.py:34
  53.0 0.4 collective-permute-done.11.refs_1_
  53.4 1.5 %finish.1 = bf16[512,2048]{1,0:T(8,128)(2,1)} custom-call(bf16[512,2048]{1,0:T(8,128)(2,1)S(1)} %get-tuple-element.113.refs_0_, bf16[512,2048]{1,0:T(8,128)(2,1)S(1)} %collective-permute-done.11.refs_1_), custom_call_target="tpu_custom_call" | custom-call | flops 6000000000 | bytes 1 | tf_op jit(solution)/shard_map/finish/pallas_call | solution.py:34
  (17 shorter events, 0.1 us)
Async XLA Ops:
  0.6 6.8 %collective-permute-start.1 = (bf16[512,2048]{1,0:T(8,128)(2,1)}, bf16[512,2048]{1,0:T(8,128)(2,1)S(1)}, u32[]{:S(2)}, u32[]{:S(2)}) collective-permute-start(bf16[512,2048]{1,0:T(8,128)(2,1)} %refs_0_.1), channel_id=1, source_target_pairs={{0,1},{1,0},{2,3},{3,2},{4,5},{5,4},{6,7},{7,6},{8,9},{9,8},{10,11... | collective-permute-start | bytes 6291464 | tf_op jit(solution)/shard_map/ppermute | solution.py:510
  4.8 10.5 %collective-permute-start = (bf16[528,128]{1,0:T(8,128)(2,1)S(1)}, bf16[528,128]{1,0:T(8,128)(2,1)S(1)}, u32[]{:S(2)}, u32[]{:S(2)}) collective-permute-start(bf16[528,128]{1,0:T(8,128)(2,1)S(1)} %get-tuple-element.60), channel_id=1, source_target_pairs={{0,2},{2,0},{4,6},{6,4},{8,10},{10,8},{12,14},{14,12},{16,18},{18,... | collective-permute-start | bytes 405512 | tf_op jit(solution)/shard_map/ppermute | solution.py:526
  15.4 5.8 %collective-permute-start.3 = (bf16[528,128]{1,0:T(8,128)(2,1)S(1)}, bf16[528,128]{1,0:T(8,128)(2,1)S(1)}, u32[]{:S(2)}, u32[]{:S(2)}) collective-permute-start(bf16[528,128]{1,0:T(8,128)(2,1)S(1)} %pad_maximum_fusion), channel_id=1, source_target_pairs={{0,4},{2,6},{4,0},{6,2},{8,12},{10,14},{12,8},{14,10},{16,20},{18,... | collective-permute-start | bytes 405512 | tf_op jit(solution)/shard_map/ppermute | solution.py:526
  17.0 6.0 %collective-permute-start.2 = (bf16[512,128]{1,0:T(8,128)(2,1)S(1)}, bf16[512,128]{1,0:T(8,128)(2,1)S(1)}, u32[]{:S(2)}, u32[]{:S(2)}) collective-permute-start(bf16[512,128]{1,0:T(8,128)(2,1)S(1)} %get-tuple-element.65), channel_id=1, source_target_pairs={{0,2},{2,0},{4,6},{6,4},{8,10},{10,8},{12,14},{14,12},{16,18},{18,... | collective-permute-start | bytes 393224 | tf_op jit(solution)/shard_map/ppermute | solution.py:526
  21.3 6.8 %collective-permute-start.5 = (bf16[528,128]{1,0:T(8,128)(2,1)S(1)}, bf16[528,128]{1,0:T(8,128)(2,1)S(1)}, u32[]{:S(2)}, u32[]{:S(2)}) collective-permute-start(bf16[528,128]{1,0:T(8,128)(2,1)S(1)} %pad_maximum_fusion.1), channel_id=1, source_target_pairs={{0,8},{2,10},{4,12},{6,14},{8,0},{10,2},{12,4},{14,6},{16,24},{18,... | collective-permute-start | bytes 405512 | tf_op jit(solution)/shard_map/ppermute | solution.py:526
  23.0 5.3 %collective-permute-start.4 = (bf16[512,128]{1,0:T(8,128)(2,1)S(1)}, bf16[512,128]{1,0:T(8,128)(2,1)S(1)}, u32[]{:S(2)}, u32[]{:S(2)}) collective-permute-start(bf16[512,128]{1,0:T(8,128)(2,1)S(1)} %fusion.20), channel_id=1, source_target_pairs={{0,4},{2,6},{4,0},{6,2},{8,12},{10,14},{12,8},{14,10},{16,20},{18,... | collective-permute-start | bytes 393224 | tf_op jit(solution)/shard_map/ppermute | solution.py:526
  28.4 8.3 %collective-permute-start.6 = (bf16[512,128]{1,0:T(8,128)(2,1)S(1)}, bf16[512,128]{1,0:T(8,128)(2,1)S(1)}, u32[]{:S(2)}, u32[]{:S(2)}) collective-permute-start(bf16[512,128]{1,0:T(8,128)(2,1)S(1)} %fusion.22), channel_id=1, source_target_pairs={{0,8},{2,10},{4,12},{6,14},{8,0},{10,2},{12,4},{14,6},{16,24},{18,... | collective-permute-start | bytes 393224 | tf_op jit(solution)/shard_map/ppermute | solution.py:526
  29.2 8.1 %collective-permute-start.8 = (bf16[512,128]{1,0:T(8,128)(2,1)S(1)}, bf16[512,128]{1,0:T(8,128)(2,1)S(1)}, u32[]{:S(2)}, u32[]{:S(2)}) collective-permute-start(bf16[512,128]{1,0:T(8,128)(2,1)S(1)} %fusion.14), channel_id=1, source_target_pairs={{0,16},{2,18},{4,20},{6,22},{8,24},{10,26},{12,28},{14,30},{16,0},... | collective-permute-start | bytes 393224 | tf_op jit(solution)/shard_map/ppermute | solution.py:526
  36.9 7.3 %collective-permute-start.7 = (bf16[512,128]{1,0:T(8,128)(2,1)S(1)}, bf16[512,128]{1,0:T(8,128)(2,1)S(1)}, u32[]{:S(2)}, u32[]{:S(2)}) collective-permute-start(bf16[512,128]{1,0:T(8,128)(2,1)S(1)} %fusion.19), channel_id=1, source_target_pairs={{0,16},{2,18},{4,20},{6,22},{8,24},{10,26},{12,28},{14,30},{16,0},... | collective-permute-start | bytes 393224 | tf_op jit(solution)/shard_map/ppermute | solution.py:526
  37.5 7.9 %collective-permute-start.10 = (bf16[512,128]{1,0:T(8,128)(2,1)S(1)}, bf16[512,128]{1,0:T(8,128)(2,1)S(1)}, u32[]{:S(2)}, u32[]{:S(2)}) collective-permute-start(bf16[512,128]{1,0:T(8,128)(2,1)S(1)} %get-tuple-element.127), channel_id=1, source_target_pairs={{0,2},{2,0},{4,6},{6,4},{8,10},{10,8},{12,14},{14,12},{16,18},{18,... | collective-permute-start | bytes 393224 | tf_op jit(solution)/shard_map/ppermute | solution.py:526
  44.4 5.0 %collective-permute-start.9 = (bf16[512,128]{1,0:T(8,128)(2,1)S(1)}, bf16[512,128]{1,0:T(8,128)(2,1)S(1)}, u32[]{:S(2)}, u32[]{:S(2)}) collective-permute-start(bf16[512,128]{1,0:T(8,128)(2,1)S(1)} %get-tuple-element.129), channel_id=1, source_target_pairs={{0,2},{2,0},{4,6},{6,4},{8,10},{10,8},{12,14},{14,12},{16,18},{18,... | collective-permute-start | bytes 393224 | tf_op jit(solution)/shard_map/ppermute | solution.py:526
  49.2 4.2 %collective-permute-start.11 = (bf16[512,2048]{1,0:T(8,128)(2,1)S(1)}, bf16[512,2048]{1,0:T(8,128)(2,1)S(1)}, u32[]{:S(2)}, u32[]{:S(2)}) collective-permute-start(bf16[512,2048]{1,0:T(8,128)(2,1)S(1)} %get-tuple-element.114), channel_id=1, source_target_pairs={{0,1},{1,0},{2,3},{3,2},{4,5},{5,4},{6,7},{7,6},{8,9},{9,8},{10,11... | collective-permute-start | bytes 6291464 | tf_op jit(solution)/shard_map/ppermute | solution.py:623

commit v14 on v13

--- a/solution.py
+++ b/solution.py
@@ -96,6 +96,16 @@
     at = slice(h * half, (h + 1) * half)
     kept_ref[at, :] = jnp.where(upper, local[half:], local[:half]).astype(BF16)
     sent_ref[at, :] = jnp.where(upper, local[:half], local[half:]).astype(BF16)
+
+
+def put_pairs(upper, first, last, left_ref, right_ref, kept_ref, sent_ref):
+    for h in range(first, last, 2):
+        count = min(2, last - h)
+        cols = slice(h * HDIM, (h + count) * HDIM)
+        both = dot(left_ref[:, cols], right_ref[:, cols], TN)
+        for own in range(count):
+            at = slice(own * HDIM, (own + 1) * HDIM)
+            put_halves(upper, h + own, both[at, at], kept_ref, sent_ref)
 
 
 def prepare_kernel(
@@ -140,8 +150,8 @@
         for h in range(first, last):
             cols = slice(h * HDIM, (h + 1) * HDIM)
             scaled = scaled_keys(table, hp, h, kbuf[:, cols])
-            decayed = (column(table, 2 * hp + h) * scaled.astype(F32)).astype(BF16)
-            put_halves(upper, h, dot(decayed, vbuf[:, cols], TN), kept_ref, sent_ref)
+            kbuf[:, cols] = (column(table, 2 * hp + h) * scaled.astype(F32)).astype(BF16)
+        put_pairs(upper, first, last, kbuf, vbuf, kept_ref, sent_ref)
     copies.finish()
 
 
@@ -178,7 +188,7 @@
 
 def project_kernel(hp, nparts, chunk, *refs):
     parts, (w_hbm, do_hbm, facts_hbm, q_hbm, kept_ref, sent_ref) = refs[:nparts], refs[nparts : nparts + 6]
-    hbuf, wbuf, dobuf, facts_ref, qbuf, total, sems = refs[nparts + 6 :]
+    hbuf, wbuf, dobuf, facts_ref, qbuf, decayed, total, sems = refs[nparts + 6 :]
     rows, feat = parts[0].shape
     width = wbuf.shape[1]
     heads = width // HDIM
@@ -217,8 +227,8 @@
     table = turned(facts_ref[...])
     for h in range(heads):
         cols = slice(h * HDIM, (h + 1) * HDIM)
-        decayed = (column(table, 3 * hp + h) * qbuf[:, cols].astype(F32)).astype(BF16)
-        put_halves(upper, h, dot(decayed, dobuf[:, cols], TN), kept_ref, sent_ref)
+        decayed[:, cols] = (column(table, 3 * hp + h) * qbuf[:, cols].astype(F32)).astype(BF16)
+    put_pairs(upper, 0, heads, decayed, dobuf, kept_ref, sent_ref)
     copies.finish()
 
 
@@ -237,6 +247,7 @@
             pltpu.VMEM((depth, width), BF16),
             pltpu.VMEM((rows, width), BF16),
             pltpu.VMEM(facts.shape, F32),
+            pltpu.VMEM((rows, width), BF16),
             pltpu.VMEM((rows, width), BF16),
             pltpu.VMEM((rows, width), F32),
             pltpu.SemaphoreType.DMA((2 * len(parts) * (feat // chunk) + 3,)),
@@ -324,7 +335,7 @@
 
 def fetch_kernel(heads, count, w_hbm, do_hbm, facts_hbm, *refs):
     inner_hbm, refs = refs[: len(spans_of(heads))], refs[len(spans_of(heads)) :]
-    do_ref, local_ref, table_ref, outs, (facts_ref, sems) = refs[0], refs[1], refs[2], refs[3:-2], refs[-2:]
+    do_ref, local_ref, table_ref, own_ref, outs, (facts_ref, sems) = *refs[:4], refs[4:-2], refs[-2:]
     copies = Copies(sems)
     facts_in = copies.start(facts_hbm, facts_ref)
     for index, out in enumerate(outs):
@@ -332,6 +343,7 @@
     copies.store(do_hbm, do_ref)
     for (first, last), src in zip(spans_of(heads), inner_hbm):
         copies.store(src, local_ref.at[:, pl.ds(first * HDIM, (last - first) * HDIM)])
+    copies.store(rows_of(w_hbm, 0, count, own_ref.shape[0]), own_ref)
     facts_in.wait()
     table_ref[...] = turned(facts_ref[...])
     copies.finish()
@@ -343,20 +355,22 @@
         functools.partial(fetch_kernel, heads, count),
         (w_query, d_out, facts, *inner_dq),
         [HB] * (3 + len(inner_dq)),
-        [((rows, width), BF16)] * 2 + [((rows, LANES), F32)] + [((feat, width), BF16)] * (count - 1),
-        (VM,) * (count + 2),
-        [pltpu.VMEM(facts.shape, F32), pltpu.SemaphoreType.DMA((count + 1 + len(inner_dq),))],
+        [((rows, width), BF16)] * 2
+        + [((rows, LANES), F32), ((feat, width), BF16)]
+        + [((feat, width), BF16)] * (count - 1),
+        (VM,) * (count + 3),
+        [pltpu.VMEM(facts.shape, F32), pltpu.SemaphoreType.DMA((count + 2 + len(inner_dq),))],
         4,
         "fetch",
         4,
     )
 
 
-def query_kernel(heads, hp, count, *refs):
-    mine_ref, theirs_ref, w_ref, do_ref, local_ref, table_ref, k_hbm, v_hbm, w_hbm = refs[:9]
+def query_kernel(heads, hp, *refs):
+    mine_ref, theirs_ref, w_ref, do_ref, local_ref, table_ref, k_hbm, v_hbm = refs[:8]
     parts = len(spans_of(heads))
-    dks, dvs, refs = refs[9 : 9 + parts], refs[9 + parts : 9 + 2 * parts], refs[9 + 2 * parts :]
-    held, out_ref, k_ref, v_ref, dk_ref, dv_ref, next_table, *owns, sems = refs
+    dks, dvs, refs = refs[8 : 8 + parts], refs[8 + parts : 8 + 2 * parts], refs[8 + 2 * parts :]
+    held, out_ref, k_ref, v_ref, dk_ref, dv_ref, next_table, sems = refs
     upper = lax.axis_index("ctx") % 2 == 1
     copies = Copies(sems)
     copies.store(k_hbm, k_ref)
@@ -365,11 +379,6 @@
         wide = pl.ds(first * HDIM, (last - first) * HDIM)
         copies.store(dk, dk_ref.at[:, wide])
         copies.store(dv, dv_ref.at[:, wide])
-    at, rows = 0, rows_of(w_hbm, 0, count, w_ref.shape[0])
-    for own in owns:
-        size = own.shape[0]
-        copies.store(rows.at[pl.ds(at, size), :], own)
-        at += size
     table = table_ref[...]
     next_table[...] = table
     for h in range(heads):
@@ -381,26 +390,25 @@
     copies.finish()
 
 
-def put_terms(dq_ref, w_ref, out_ref, first=0):
+def put_terms(dq_ref, w_ref, out_ref):
     block = min(512, w_ref.shape[0])
     for at in range(0, w_ref.shape[0], block):
-        out_ref[:, first + at : first + at + block] = dot(dq_ref[...], w_ref[at : at + block, :], NT).astype(BF16)
-
-
-def query_term(halves, weight, fetched, keys, values, w_query, dks, dvs, count, heads, hp):
+        out_ref[:, at : at + block] = dot(dq_ref[...], w_ref[at : at + block, :], NT).astype(BF16)
+
+
+def query_term(halves, weight, fetched, keys, values, dks, dvs, heads, hp):
     rows, width = keys.shape
     feat = weight.shape[0]
-    vm_args, hbm_args = (*halves, weight, *fetched), (keys, values, w_query, *dks, *dvs)
-    return kernel_call(
-        functools.partial(query_kernel, heads, hp, count),
+    vm_args, hbm_args = (*halves, weight, *fetched), (keys, values, *dks, *dvs)
+    return kernel_call(
+        functools.partial(query_kernel, heads, hp),
         (*vm_args, *hbm_args),
         [VM] * len(vm_args) + [HB] * len(hbm_args),
         [((rows, width), BF16), ((rows, feat), BF16)]
         + [((rows, width), BF16)] * 4
-        + [((rows, LANES), F32)]
-        + [((size, width), BF16) for size in (feat // 2, feat // 2)],
-        (VM,) * 9,
-        [pltpu.SemaphoreType.DMA((4 + 2 * len(dks),))],
+        + [((rows, LANES), F32)],
+        (VM,) * 7,
+        [pltpu.SemaphoreType.DMA((2 + 2 * len(dks),))],
         8,
         "query_term",
         6,
@@ -455,7 +463,7 @@
 
 
 def close_kernel(
-    heads, hp, mine_ref, theirs_ref, k_ref, v_ref, dk_ref, dv_ref, table_ref, dq_ref, own_ref, second_ref, *refs
+    heads, hp, mine_ref, theirs_ref, k_ref, v_ref, dk_ref, dv_ref, table_ref, dq_ref, own_ref, *refs
 ):
     dk_hbm, dv_hbm, term_ref, kside, vside, sems = refs
     upper = lax.axis_index("ctx") % 2 == 1
@@ -475,19 +483,18 @@
             copies.store(kside.at[:, wide], dk_hbm.at[:, wide])
             copies.store(vside.at[:, wide], dv_hbm.at[:, wide])
     put_terms(dq_ref, own_ref, term_ref)
-    put_terms(dq_ref, second_ref, term_ref, own_ref.shape[0])
     copies.finish()
 
 
-def close(halves, held, d_query, owns, heads, hp):
+def close(halves, held, d_query, own, heads, hp):
     rows, width = d_query.shape
-    args = (*halves, *held, d_query, *owns)
+    args = (*halves, *held, d_query, own)
     buf = pltpu.VMEM((rows, width), BF16)
     return kernel_call(
         functools.partial(close_kernel, heads, hp),
         args,
         [VM] * len(args),
-        [((rows, width), BF16)] * 2 + [((rows, sum(own.shape[0] for own in owns)), BF16)],
+        [((rows, width), BF16)] * 2 + [((rows, own.shape[0]), BF16)],
         (HB, HB, VM),
         [buf, buf, pltpu.SemaphoreType.DMA((2 * (heads // min(2, heads)),))],
         12,
@@ -583,7 +590,7 @@
             weight, _ = barrier((w_query, adjoints.sent))
             dqs, dks, dvs = zip(*inner_parts)
             *fetched, = fetch(head_size, weight, d_out, facts, dqs, feat, heads)
-            fetched, weights = fetched[:3], fetched[3:]
+            fetched, own, weights = fetched[:3], fetched[3], fetched[4:]
         states.go()
         if stage == 0:
             states.arrived, query, adjoints.kept, adjoints.sent = barrier(
@@ -615,13 +622,13 @@
     for shift in range(1, head_size):
         ring = [(i, (i + shift) % head_size) for i in range(head_size)]
         if shift == 1:
-            d_query, term, *held, first, second = query_term(
-                state_halves, weights[0], fetched, keys, values, w_query, dks, dvs, head_size, heads, hp
+            d_query, term, *held = query_term(
+                state_halves, weights[0], fetched, keys, values, dks, dvs, heads, hp
             )
         else:
             term = plain_term(d_query, weights[shift - 1])
         arrived.append(lax.ppermute(term, "head", ring))
-    d_keys, d_values, own = close(adjoint_halves, held, d_query, (first, second), heads, hp)
+    d_keys, d_values, own = close(adjoint_halves, held, d_query, own, heads, hp)
     d_hidden = finish((own, *arrived))
     return (d_hidden, d_keys, d_values)
 

time: 55.3 us -> 54.6 us (0.987)
  waiting for transfers between devices: 3.64 us -> 2.61 us
    ppermute x10, waiting for transfers between devices: 3.2 us -> 2.61 us  [send(): return lax.ppermute(array, 'ctx', [(i, i ^ dist) for i in range(ctx_size)])]
  transfers between devices with their start and end apart: 12 -> 12, of which waited for: 3 -> 2; matrix products, arithmetic and copies ran while one was open for 1% -> 1% of each run, Pallas kernels for 61% -> 63%
where the time goes in v14:
time: 54.6 us; the launch traced here: 54.3 us
  Pallas kernels  35.4 us (65%)
  starting transfers between devices  14.3 us (26%)
  waiting for transfers between devices  2.61 us (5%)
  between operations  1.01 us (2%)
  other arithmetic  0.98 us (2%)
    pallas_call x9, Pallas kernels, kernel_call(): pl.pallas_call(kernel, in_specs=specs, out_specs=tuple(out_specs), out_sh...  35.4 us
    ppermute x10, starting transfers between devices, send(): return lax.ppermute(array, 'ctx', [(i, i ^ dist) for i in range(ctx_size)])  13.7 us
    ppermute x10, waiting for transfers between devices, send(): return lax.ppermute(array, 'ctx', [(i, i ^ dist) for i in range(ctx_size)])  2.61 us
  transfers between devices with their start and end apart: 12, of which 2 were waited for; matrix products, arithmetic and copies ran while one was open for 1% of the time, Pallas kernels for 63%

profile of v14, /device:TPU:0, one launch (start us, length us, event | category | flops | bytes accessed | tf_op | source)
XLA Modules:
  0.0 54.3 jit_solution(1929753401709914833)
XLA Ops:
  0.6 0.5 collective-permute-start.1
  1.1 3.5 %prepare.1 = (f32[32,512]{1,0:T(8,128)}, bf16[512,128]{1,0:T(8,128)(2,1)S(1)}, bf16[528,128]{1,0:T(8,128)(2,1)S(1)}, f32[8,128]{1,0:T(8,128)S(1)}) custom-call(f32[8,512]{1,0:T(8,128)} %bitcast.123, bf16[512,1024]{1,0:T(8,128)(2,1)} %refs_6_.1, bf16[512,1024]{1,0:T(8,128)(2,1)} %refs_7_.1), custom_call_target="tpu_custom_call" | custom-call | flops 4000000000 | bytes 1 | tf_op jit(solution)/shard_map/prepare/pallas_call | solution.py:34
  4.7 2.6 %collective-permute-start = (bf16[528,128]{1,0:T(8,128)(2,1)S(1)}, bf16[528,128]{1,0:T(8,128)(2,1)S(1)}, u32[]{:S(2)}, u32[]{:S(2)}) collective-permute-start(bf16[528,128]{1,0:T(8,128)(2,1)S(1)} %get-tuple-element.59), channel_id=1, source_target_pairs={{0,2},{2,0},{4,6},{6,4},{8,10},{10,8},{12,14},{14,12},{16,18},{18,... | collective-permute-start | bytes 405512 | tf_op jit(solution)/shard_map/ppermute | solution.py:533
  7.3 0.0 collective-permute-done.1.refs_1_
  7.3 7.8 %project.1 = (bf16[512,1024]{1,0:T(8,128)(2,1)}, bf16[512,128]{1,0:T(8,128)(2,1)S(1)}, bf16[512,128]{1,0:T(8,128)(2,1)S(1)}) custom-call(bf16[512,2048]{1,0:T(8,128)(2,1)} %refs_0_.1, bf16[512,2048]{1,0:T(8,128)(2,1)S(1)} %collective-permute-done.1.refs_1_, bf16[4096,1024]{1,0:T(8,128)(2,1)} %w_hbm, bf16[512,1024]{1,0:T(8,128)(2,1)} %do_hbm.1, ...), custom_call_target="tpu_custom_call" | custom-call | flops 8000000000 | bytes 1 | tf_op jit(solution)/shard_map/project/pallas_call | solution.py:34
  15.1 0.1 fusion.21
  15.2 1.6 %collective-permute-start.3 = (bf16[528,128]{1,0:T(8,128)(2,1)S(1)}, bf16[528,128]{1,0:T(8,128)(2,1)S(1)}, u32[]{:S(2)}, u32[]{:S(2)}) collective-permute-start(bf16[528,128]{1,0:T(8,128)(2,1)S(1)} %pad_maximum_fusion), channel_id=1, source_target_pairs={{0,4},{2,6},{4,0},{6,2},{8,12},{10,14},{12,8},{14,10},{16,20},{18,... | collective-permute-start | bytes 405512 | tf_op jit(solution)/shard_map/ppermute | solution.py:533
  16.8 0.7 %collective-permute-start.2 = (bf16[512,128]{1,0:T(8,128)(2,1)S(1)}, bf16[512,128]{1,0:T(8,128)(2,1)S(1)}, u32[]{:S(2)}, u32[]{:S(2)}) collective-permute-start(bf16[512,128]{1,0:T(8,128)(2,1)S(1)} %get-tuple-element.64), channel_id=1, source_target_pairs={{0,2},{2,0},{4,6},{6,4},{8,10},{10,8},{12,14},{14,12},{16,18},{18,... | collective-permute-start | bytes 393224 | tf_op jit(solution)/shard_map/ppermute | solution.py:533
  17.5 3.5 %inner.3 = (bf16[512,256]{1,0:T(8,128)(2,1)}, bf16[512,256]{1,0:T(8,128)(2,1)}, bf16[512,256]{1,0:T(8,128)(2,1)}) custom-call(bf16[512,1024]{1,0:T(8,128)(2,1)} %get-tuple-element.82.refs_0_, bf16[512,1024]{1,0:T(8,128)(2,1)} %refs_6_.1, bf16[512,1024]{1,0:T(8,128)(2,1)} %refs_7_.1, bf16[512,1024]{1,0:T(8,128)(2,1)} %do_hbm.1, ...), custom_call_target="tpu_custom_call" | custom-call | flops 1000000000 | bytes 1 | tf_op jit(solution)/shard_map/inner/pallas_call | solution.py:34
  21.1 0.1 fusion.23
  21.2 1.6 %collective-permute-start.5 = (bf16[528,128]{1,0:T(8,128)(2,1)S(1)}, bf16[528,128]{1,0:T(8,128)(2,1)S(1)}, u32[]{:S(2)}, u32[]{:S(2)}) collective-permute-start(bf16[528,128]{1,0:T(8,128)(2,1)S(1)} %pad_maximum_fusion.1), channel_id=1, source_target_pairs={{0,8},{2,10},{4,12},{6,14},{8,0},{10,2},{12,4},{14,6},{16,24},{18,... | collective-permute-start | bytes 405512 | tf_op jit(solution)/shard_map/ppermute | solution.py:533
  22.8 0.1 fusion.20
  22.9 1.5 %collective-permute-start.4 = (bf16[512,128]{1,0:T(8,128)(2,1)S(1)}, bf16[512,128]{1,0:T(8,128)(2,1)S(1)}, u32[]{:S(2)}, u32[]{:S(2)}) collective-permute-start(bf16[512,128]{1,0:T(8,128)(2,1)S(1)} %fusion.20), channel_id=1, source_target_pairs={{0,4},{2,6},{4,0},{6,2},{8,12},{10,14},{12,8},{14,10},{16,20},{18,... | collective-permute-start | bytes 393224 | tf_op jit(solution)/shard_map/ppermute | solution.py:533
  24.4 3.5 %inner.4 = (bf16[512,256]{1,0:T(8,128)(2,1)}, bf16[512,256]{1,0:T(8,128)(2,1)}, bf16[512,256]{1,0:T(8,128)(2,1)}) custom-call(bf16[512,1024]{1,0:T(8,128)(2,1)} %get-tuple-element.82.refs_0_, bf16[512,1024]{1,0:T(8,128)(2,1)} %refs_6_.1, bf16[512,1024]{1,0:T(8,128)(2,1)} %refs_7_.1, bf16[512,1024]{1,0:T(8,128)(2,1)} %do_hbm.1, ...), custom_call_target="tpu_custom_call" | custom-call | flops 1000000000 | bytes 1 | tf_op jit(solution)/shard_map/inner/pallas_call | solution.py:34
  27.9 0.1 fusion.14
  28.1 0.1 fusion.22
  28.2 0.8 %collective-permute-start.6 = (bf16[512,128]{1,0:T(8,128)(2,1)S(1)}, bf16[512,128]{1,0:T(8,128)(2,1)S(1)}, u32[]{:S(2)}, u32[]{:S(2)}) collective-permute-start(bf16[512,128]{1,0:T(8,128)(2,1)S(1)} %fusion.22), channel_id=1, source_target_pairs={{0,8},{2,10},{4,12},{6,14},{8,0},{10,2},{12,4},{14,6},{16,24},{18,... | collective-permute-start | bytes 393224 | tf_op jit(solution)/shard_map/ppermute | solution.py:533
  28.9 2.6 %collective-permute-start.8 = (bf16[512,128]{1,0:T(8,128)(2,1)S(1)}, bf16[512,128]{1,0:T(8,128)(2,1)S(1)}, u32[]{:S(2)}, u32[]{:S(2)}) collective-permute-start(bf16[512,128]{1,0:T(8,128)(2,1)S(1)} %fusion.14), channel_id=1, source_target_pairs={{0,16},{2,18},{4,20},{6,22},{8,24},{10,26},{12,28},{14,30},{16,0},... | collective-permute-start | bytes 393224 | tf_op jit(solution)/shard_map/ppermute | solution.py:533
  31.5 5.0 %inner.5 = (bf16[512,512]{1,0:T(8,128)(2,1)}, bf16[512,512]{1,0:T(8,128)(2,1)}, bf16[512,512]{1,0:T(8,128)(2,1)}) custom-call(bf16[512,1024]{1,0:T(8,128)(2,1)} %get-tuple-element.82.refs_0_, bf16[512,1024]{1,0:T(8,128)(2,1)} %refs_6_.1, bf16[512,1024]{1,0:T(8,128)(2,1)} %refs_7_.1, bf16[512,1024]{1,0:T(8,128)(2,1)} %do_hbm.1, ...), custom_call_target="tpu_custom_call" | custom-call | flops 1000000000 | bytes 1 | tf_op jit(solution)/shard_map/inner/pallas_call | solution.py:34
  36.5 0.1 fusion.19
  36.6 0.4 collective-permute-start.7
  37.1 0.2 fusion.2
  37.2 1.0 %collective-permute-start.10 = (bf16[512,128]{1,0:T(8,128)(2,1)S(1)}, bf16[512,128]{1,0:T(8,128)(2,1)S(1)}, u32[]{:S(2)}, u32[]{:S(2)}) collective-permute-start(bf16[512,128]{1,0:T(8,128)(2,1)S(1)} %get-tuple-element.125), channel_id=1, source_target_pairs={{0,2},{2,0},{4,6},{6,4},{8,10},{10,8},{12,14},{14,12},{16,18},{18,... | collective-permute-start | bytes 393224 | tf_op jit(solution)/shard_map/ppermute | solution.py:533
  38.2 4.2 %fetch.1 = (bf16[512,1024]{1,0:T(8,128)(2,1)S(1)}, bf16[512,1024]{1,0:T(8,128)(2,1)S(1)}, f32[512,128]{1,0:T(8,128)S(1)}, bf16[2048,1024]{1,0:T(8,128)(2,1)S(1)}, bf16[2048,1024]{1,0:T(8,128)(2,1)S(1)}) custom-call(bf16[4096,1024]{1,0:T(8,128)(2,1)} %w_hbm, bf16[512,1024]{1,0:T(8,128)(2,1)} %do_hbm.1, f32[32,512]{1,0:T(8,128)} %get-tuple-element.60.refs_4_.facts_hbm, ...), custom_call_target="tpu_custom_call" | custom-call | flops 4000000000 | bytes 1 | tf_op jit(solution)/shard_map/fetch/pallas_call | solution.py:34
  42.4 1.6 %collective-permute-done.7 = bf16[512,128]{1,0:T(8,128)(2,1)S(1)} collective-permute-done((bf16[512,128]{1,0:T(8,128)(2,1)S(1)}, bf16[512,128]{1,0:T(8,128)(2,1)S(1)}, u32[]{:S(2)}, u32[]{:S(2)}) %collective-permute-start.7) | collective-permute-done | bytes 131104 | tf_op jit(solution)/shard_map/ppermute | solution.py:533
  44.0 0.2 fusion.12
  44.1 1.0 %collective-permute-start.9 = (bf16[512,128]{1,0:T(8,128)(2,1)S(1)}, bf16[512,128]{1,0:T(8,128)(2,1)S(1)}, u32[]{:S(2)}, u32[]{:S(2)}) collective-permute-start(bf16[512,128]{1,0:T(8,128)(2,1)S(1)} %get-tuple-element.127), channel_id=1, source_target_pairs={{0,2},{2,0},{4,6},{6,4},{8,10},{10,8},{12,14},{14,12},{16,18},{18,... | collective-permute-start | bytes 393224 | tf_op jit(solution)/shard_map/ppermute | solution.py:533
  45.1 3.0 %query_term.1 = (bf16[512,1024]{1,0:T(8,128)(2,1)S(1)}, bf16[512,2048]{1,0:T(8,128)(2,1)S(1)}, bf16[512,1024]{1,0:T(8,128)(2,1)S(1)}, bf16[512,1024]{1,0:T(8,128...) custom-call(bf16[512,128]{1,0:T(8,128)(2,1)S(1)} %get-tuple-element.126.refs_0_, ...), custom_call_target="tpu_custom_call" | custom-call | flops 6000000000 | bytes 1 | tf_op jit(solution)/shard_map/query_term/pallas_call | solution.py:34
  48.1 0.1 collective-permute-start.11
  48.2 1.0 %collective-permute-done.9.theirs_ref = bf16[512,128]{1,0:T(8,128)(2,1)S(1)} collective-permute-done((bf16[512,128]{1,0:T(8,128)(2,1)S(1)}, bf16[512,128]{1,0:T(8,128)(2,1)S(1)}, u32[]{:S(2)}, u32[]{:S(2)}) %collective-permute-start.9) | collective-permute-done | bytes 131104 | tf_op jit(solution)/shard_map/ppermute | solution.py:533
  49.2 3.5 %close.1 = (bf16[512,1024]{1,0:T(8,128)(2,1)}, bf16[512,1024]{1,0:T(8,128)(2,1)}, bf16[512,2048]{1,0:T(8,128)(2,1)S(1)}) custom-call(bf16[512,128]{1,0:T(8,128)(2,1)S(1)} %get-tuple-element.128.mine_ref, bf16[512,128]{1,0:T(8,128)(2,1)S(1)} %collective-permute-done.9.theirs_ref, bf16[512,1024]{1,0:T(8,128)(2,1)S(1)} %get-tuple-element.104.k_ref, ...), custom_call_target="tpu_custom_call" | custom-call | flops 99999997952 | bytes 1 | tf_op jit(solution)/shard_map/close/pallas_call | solution.py:34
  52.7 1.5 %finish.1 = bf16[512,2048]{1,0:T(8,128)(2,1)} custom-call(bf16[512,2048]{1,0:T(8,128)(2,1)S(1)} %get-tuple-element.111.refs_0_, bf16[512,2048]{1,0:T(8,128)(2,1)S(1)} %collective-permute-done.11.refs_1_), custom_call_target="tpu_custom_call" | custom-call | flops 6000000000 | bytes 1 | tf_op jit(solution)/shard_map/finish/pallas_call | solution.py:34
  (17 shorter events, 0.1 us)
Async XLA Ops:
  0.6 6.6 %collective-permute-start.1 = (bf16[512,2048]{1,0:T(8,128)(2,1)}, bf16[512,2048]{1,0:T(8,128)(2,1)S(1)}, u32[]{:S(2)}, u32[]{:S(2)}) collective-permute-start(bf16[512,2048]{1,0:T(8,128)(2,1)} %refs_0_.1), channel_id=1, source_target_pairs={{0,1},{1,0},{2,3},{3,2},{4,5},{5,4},{6,7},{7,6},{8,9},{9,8},{10,11... | collective-permute-start | bytes 6291464 | tf_op jit(solution)/shard_map/ppermute | solution.py:517
  4.7 10.4 %collective-permute-start = (bf16[528,128]{1,0:T(8,128)(2,1)S(1)}, bf16[528,128]{1,0:T(8,128)(2,1)S(1)}, u32[]{:S(2)}, u32[]{:S(2)}) collective-permute-start(bf16[528,128]{1,0:T(8,128)(2,1)S(1)} %get-tuple-element.59), channel_id=1, source_target_pairs={{0,2},{2,0},{4,6},{6,4},{8,10},{10,8},{12,14},{14,12},{16,18},{18,... | collective-permute-start | bytes 405512 | tf_op jit(solution)/shard_map/ppermute | solution.py:533
  15.2 5.8 %collective-permute-start.3 = (bf16[528,128]{1,0:T(8,128)(2,1)S(1)}, bf16[528,128]{1,0:T(8,128)(2,1)S(1)}, u32[]{:S(2)}, u32[]{:S(2)}) collective-permute-start(bf16[528,128]{1,0:T(8,128)(2,1)S(1)} %pad_maximum_fusion), channel_id=1, source_target_pairs={{0,4},{2,6},{4,0},{6,2},{8,12},{10,14},{12,8},{14,10},{16,20},{18,... | collective-permute-start | bytes 405512 | tf_op jit(solution)/shard_map/ppermute | solution.py:533
  16.8 6.1 %collective-permute-start.2 = (bf16[512,128]{1,0:T(8,128)(2,1)S(1)}, bf16[512,128]{1,0:T(8,128)(2,1)S(1)}, u32[]{:S(2)}, u32[]{:S(2)}) collective-permute-start(bf16[512,128]{1,0:T(8,128)(2,1)S(1)} %get-tuple-element.64), channel_id=1, source_target_pairs={{0,2},{2,0},{4,6},{6,4},{8,10},{10,8},{12,14},{14,12},{16,18},{18,... | collective-permute-start | bytes 393224 | tf_op jit(solution)/shard_map/ppermute | solution.py:533
  21.2 6.7 %collective-permute-start.5 = (bf16[528,128]{1,0:T(8,128)(2,1)S(1)}, bf16[528,128]{1,0:T(8,128)(2,1)S(1)}, u32[]{:S(2)}, u32[]{:S(2)}) collective-permute-start(bf16[528,128]{1,0:T(8,128)(2,1)S(1)} %pad_maximum_fusion.1), channel_id=1, source_target_pairs={{0,8},{2,10},{4,12},{6,14},{8,0},{10,2},{12,4},{14,6},{16,24},{18,... | collective-permute-start | bytes 405512 | tf_op jit(solution)/shard_map/ppermute | solution.py:533
  22.9 5.2 %collective-permute-start.4 = (bf16[512,128]{1,0:T(8,128)(2,1)S(1)}, bf16[512,128]{1,0:T(8,128)(2,1)S(1)}, u32[]{:S(2)}, u32[]{:S(2)}) collective-permute-start(bf16[512,128]{1,0:T(8,128)(2,1)S(1)} %fusion.20), channel_id=1, source_target_pairs={{0,4},{2,6},{4,0},{6,2},{8,12},{10,14},{12,8},{14,10},{16,20},{18,... | collective-permute-start | bytes 393224 | tf_op jit(solution)/shard_map/ppermute | solution.py:533
  28.2 8.3 %collective-permute-start.6 = (bf16[512,128]{1,0:T(8,128)(2,1)S(1)}, bf16[512,128]{1,0:T(8,128)(2,1)S(1)}, u32[]{:S(2)}, u32[]{:S(2)}) collective-permute-start(bf16[512,128]{1,0:T(8,128)(2,1)S(1)} %fusion.22), channel_id=1, source_target_pairs={{0,8},{2,10},{4,12},{6,14},{8,0},{10,2},{12,4},{14,6},{16,24},{18,... | collective-permute-start | bytes 393224 | tf_op jit(solution)/shard_map/ppermute | solution.py:533
  28.9 8.1 %collective-permute-start.8 = (bf16[512,128]{1,0:T(8,128)(2,1)S(1)}, bf16[512,128]{1,0:T(8,128)(2,1)S(1)}, u32[]{:S(2)}, u32[]{:S(2)}) collective-permute-start(bf16[512,128]{1,0:T(8,128)(2,1)S(1)} %fusion.14), channel_id=1, source_target_pairs={{0,16},{2,18},{4,20},{6,22},{8,24},{10,26},{12,28},{14,30},{16,0},... | collective-permute-start | bytes 393224 | tf_op jit(solution)/shard_map/ppermute | solution.py:533
  36.6 7.3 %collective-permute-start.7 = (bf16[512,128]{1,0:T(8,128)(2,1)S(1)}, bf16[512,128]{1,0:T(8,128)(2,1)S(1)}, u32[]{:S(2)}, u32[]{:S(2)}) collective-permute-start(bf16[512,128]{1,0:T(8,128)(2,1)S(1)} %fusion.19), channel_id=1, source_target_pairs={{0,16},{2,18},{4,20},{6,22},{8,24},{10,26},{12,28},{14,30},{16,0},... | collective-permute-start | bytes 393224 | tf_op jit(solution)/shard_map/ppermute | solution.py:533
  37.2 7.9 %collective-permute-start.10 = (bf16[512,128]{1,0:T(8,128)(2,1)S(1)}, bf16[512,128]{1,0:T(8,128)(2,1)S(1)}, u32[]{:S(2)}, u32[]{:S(2)}) collective-permute-start(bf16[512,128]{1,0:T(8,128)(2,1)S(1)} %get-tuple-element.125), channel_id=1, source_target_pairs={{0,2},{2,0},{4,6},{6,4},{8,10},{10,8},{12,14},{14,12},{16,18},{18,... | collective-permute-start | bytes 393224 | tf_op jit(solution)/shard_map/ppermute | solution.py:533
  44.1 5.0 %collective-permute-start.9 = (bf16[512,128]{1,0:T(8,128)(2,1)S(1)}, bf16[512,128]{1,0:T(8,128)(2,1)S(1)}, u32[]{:S(2)}, u32[]{:S(2)}) collective-permute-start(bf16[512,128]{1,0:T(8,128)(2,1)S(1)} %get-tuple-element.127), channel_id=1, source_target_pairs={{0,2},{2,0},{4,6},{6,4},{8,10},{10,8},{12,14},{14,12},{16,18},{18,... | collective-permute-start | bytes 393224 | tf_op jit(solution)/shard_map/ppermute | solution.py:533
  48.1 4.6 %collective-permute-start.11 = (bf16[512,2048]{1,0:T(8,128)(2,1)S(1)}, bf16[512,2048]{1,0:T(8,128)(2,1)S(1)}, u32[]{:S(2)}, u32[]{:S(2)}) collective-permute-start(bf16[512,2048]{1,0:T(8,128)(2,1)S(1)} %get-tuple-element.112), channel_id=1, source_target_pairs={{0,1},{1,0},{2,3},{3,2},{4,5},{5,4},{6,7},{7,6},{8,9},{9,8},{10,11... | collective-permute-start | bytes 6291464 | tf_op jit(solution)/shard_map/ppermute | solution.py:630

commit v15 on v14

--- a/solution.py
+++ b/solution.py
@@ -82,7 +82,7 @@
 
 
 def groups(heads):
-    size = min(4, heads)
+    size = min(8, heads)
     return [(f, f + size, slice(f * HDIM, (f + size) * HDIM)) for f in range(0, heads, size)]
 
 

time: 54.6 us -> 54.4 us (level)
  transfers between devices with their start and end apart: 12 -> 12, of which waited for: 2 -> 2; matrix products, arithmetic and copies ran while one was open for 1% -> 1% of each run, Pallas kernels for 63% -> 62%
where the time goes in v15:
time: 54.4 us; the launch traced here: 54.2 us
  Pallas kernels  35.3 us (65%)
  starting transfers between devices  14.3 us (26%)
  waiting for transfers between devices  2.64 us (5%)
  between operations  1 us (2%)
  other arithmetic  0.98 us (2%)
    pallas_call x9, Pallas kernels, kernel_call(): pl.pallas_call(kernel, in_specs=specs, out_specs=tuple(out_specs), out_sh...  35.3 us
    ppermute x10, starting transfers between devices, send(): return lax.ppermute(array, 'ctx', [(i, i ^ dist) for i in range(ctx_size)])  13.7 us
    ppermute x10, waiting for transfers between devices, send(): return lax.ppermute(array, 'ctx', [(i, i ^ dist) for i in range(ctx_size)])  2.63 us
  transfers between devices with their start and end apart: 12, of which 2 were waited for; matrix products, arithmetic and copies ran while one was open for 1% of the time, Pallas kernels for 62%

profile of v15, /device:TPU:0, one launch (start us, length us, event | category | flops | bytes accessed | tf_op | source)
XLA Modules:
  0.0 54.2 jit_solution(11435937883503926704)
XLA Ops:
  0.6 0.5 collective-permute-start.1
  1.1 3.4 %prepare.1 = (f32[32,512]{1,0:T(8,128)}, bf16[512,128]{1,0:T(8,128)(2,1)S(1)}, bf16[528,128]{1,0:T(8,128)(2,1)S(1)}, f32[8,128]{1,0:T(8,128)S(1)}) custom-call(f32[8,512]{1,0:T(8,128)} %bitcast.123, bf16[512,1024]{1,0:T(8,128)(2,1)} %refs_6_.1, bf16[512,1024]{1,0:T(8,128)(2,1)} %refs_7_.1), custom_call_target="tpu_custom_call" | custom-call | flops 4000000000 | bytes 1 | tf_op jit(solution)/shard_map/prepare/pallas_call | solution.py:34
  4.5 2.6 %collective-permute-start = (bf16[528,128]{1,0:T(8,128)(2,1)S(1)}, bf16[528,128]{1,0:T(8,128)(2,1)S(1)}, u32[]{:S(2)}, u32[]{:S(2)}) collective-permute-start(bf16[528,128]{1,0:T(8,128)(2,1)S(1)} %get-tuple-element.59), channel_id=1, source_target_pairs={{0,2},{2,0},{4,6},{6,4},{8,10},{10,8},{12,14},{14,12},{16,18},{18,... | collective-permute-start | bytes 405512 | tf_op jit(solution)/shard_map/ppermute | solution.py:533
  7.1 7.8 %project.1 = (bf16[512,1024]{1,0:T(8,128)(2,1)}, bf16[512,128]{1,0:T(8,128)(2,1)S(1)}, bf16[512,128]{1,0:T(8,128)(2,1)S(1)}) custom-call(bf16[512,2048]{1,0:T(8,128)(2,1)} %refs_0_.1, bf16[512,2048]{1,0:T(8,128)(2,1)S(1)} %collective-permute-done.1.refs_1_, bf16[4096,1024]{1,0:T(8,128)(2,1)} %w_hbm, bf16[512,1024]{1,0:T(8,128)(2,1)} %do_hbm.1, ...), custom_call_target="tpu_custom_call" | custom-call | flops 8000000000 | bytes 1 | tf_op jit(solution)/shard_map/project/pallas_call | solution.py:34
  14.9 0.1 fusion.21
  15.0 1.6 %collective-permute-start.3 = (bf16[528,128]{1,0:T(8,128)(2,1)S(1)}, bf16[528,128]{1,0:T(8,128)(2,1)S(1)}, u32[]{:S(2)}, u32[]{:S(2)}) collective-permute-start(bf16[528,128]{1,0:T(8,128)(2,1)S(1)} %pad_maximum_fusion), channel_id=1, source_target_pairs={{0,4},{2,6},{4,0},{6,2},{8,12},{10,14},{12,8},{14,10},{16,20},{18,... | collective-permute-start | bytes 405512 | tf_op jit(solution)/shard_map/ppermute | solution.py:533
  16.6 0.9 %collective-permute-start.2 = (bf16[512,128]{1,0:T(8,128)(2,1)S(1)}, bf16[512,128]{1,0:T(8,128)(2,1)S(1)}, u32[]{:S(2)}, u32[]{:S(2)}) collective-permute-start(bf16[512,128]{1,0:T(8,128)(2,1)S(1)} %get-tuple-element.64), channel_id=1, source_target_pairs={{0,2},{2,0},{4,6},{6,4},{8,10},{10,8},{12,14},{14,12},{16,18},{18,... | collective-permute-start | bytes 393224 | tf_op jit(solution)/shard_map/ppermute | solution.py:533
  17.5 3.5 %inner.3 = (bf16[512,256]{1,0:T(8,128)(2,1)}, bf16[512,256]{1,0:T(8,128)(2,1)}, bf16[512,256]{1,0:T(8,128)(2,1)}) custom-call(bf16[512,1024]{1,0:T(8,128)(2,1)} %get-tuple-element.82.refs_0_, bf16[512,1024]{1,0:T(8,128)(2,1)} %refs_6_.1, bf16[512,1024]{1,0:T(8,128)(2,1)} %refs_7_.1, bf16[512,1024]{1,0:T(8,128)(2,1)} %do_hbm.1, ...), custom_call_target="tpu_custom_call" | custom-call | flops 1000000000 | bytes 1 | tf_op jit(solution)/shard_map/inner/pallas_call | solution.py:34
  21.1 0.1 fusion.23
  21.2 1.6 %collective-permute-start.5 = (bf16[528,128]{1,0:T(8,128)(2,1)S(1)}, bf16[528,128]{1,0:T(8,128)(2,1)S(1)}, u32[]{:S(2)}, u32[]{:S(2)}) collective-permute-start(bf16[528,128]{1,0:T(8,128)(2,1)S(1)} %pad_maximum_fusion.1), channel_id=1, source_target_pairs={{0,8},{2,10},{4,12},{6,14},{8,0},{10,2},{12,4},{14,6},{16,24},{18,... | collective-permute-start | bytes 405512 | tf_op jit(solution)/shard_map/ppermute | solution.py:533
  22.8 0.1 fusion.20
  22.9 1.3 %collective-permute-start.4 = (bf16[512,128]{1,0:T(8,128)(2,1)S(1)}, bf16[512,128]{1,0:T(8,128)(2,1)S(1)}, u32[]{:S(2)}, u32[]{:S(2)}) collective-permute-start(bf16[512,128]{1,0:T(8,128)(2,1)S(1)} %fusion.20), channel_id=1, source_target_pairs={{0,4},{2,6},{4,0},{6,2},{8,12},{10,14},{12,8},{14,10},{16,20},{18,... | collective-permute-start | bytes 393224 | tf_op jit(solution)/shard_map/ppermute | solution.py:533
  24.2 3.5 %inner.4 = (bf16[512,256]{1,0:T(8,128)(2,1)}, bf16[512,256]{1,0:T(8,128)(2,1)}, bf16[512,256]{1,0:T(8,128)(2,1)}) custom-call(bf16[512,1024]{1,0:T(8,128)(2,1)} %get-tuple-element.82.refs_0_, bf16[512,1024]{1,0:T(8,128)(2,1)} %refs_6_.1, bf16[512,1024]{1,0:T(8,128)(2,1)} %refs_7_.1, bf16[512,1024]{1,0:T(8,128)(2,1)} %do_hbm.1, ...), custom_call_target="tpu_custom_call" | custom-call | flops 1000000000 | bytes 1 | tf_op jit(solution)/shard_map/inner/pallas_call | solution.py:34
  27.7 0.1 fusion.14
  27.9 0.0 collective-permute-done.4
  27.9 0.1 fusion.22
  28.0 0.7 %collective-permute-start.6 = (bf16[512,128]{1,0:T(8,128)(2,1)S(1)}, bf16[512,128]{1,0:T(8,128)(2,1)S(1)}, u32[]{:S(2)}, u32[]{:S(2)}) collective-permute-start(bf16[512,128]{1,0:T(8,128)(2,1)S(1)} %fusion.22), channel_id=1, source_target_pairs={{0,8},{2,10},{4,12},{6,14},{8,0},{10,2},{12,4},{14,6},{16,24},{18,... | collective-permute-start | bytes 393224 | tf_op jit(solution)/shard_map/ppermute | solution.py:533
  28.8 2.6 %collective-permute-start.8 = (bf16[512,128]{1,0:T(8,128)(2,1)S(1)}, bf16[512,128]{1,0:T(8,128)(2,1)S(1)}, u32[]{:S(2)}, u32[]{:S(2)}) collective-permute-start(bf16[512,128]{1,0:T(8,128)(2,1)S(1)} %fusion.14), channel_id=1, source_target_pairs={{0,16},{2,18},{4,20},{6,22},{8,24},{10,26},{12,28},{14,30},{16,0},... | collective-permute-start | bytes 393224 | tf_op jit(solution)/shard_map/ppermute | solution.py:533
  31.3 5.0 %inner.5 = (bf16[512,512]{1,0:T(8,128)(2,1)}, bf16[512,512]{1,0:T(8,128)(2,1)}, bf16[512,512]{1,0:T(8,128)(2,1)}) custom-call(bf16[512,1024]{1,0:T(8,128)(2,1)} %get-tuple-element.82.refs_0_, bf16[512,1024]{1,0:T(8,128)(2,1)} %refs_6_.1, bf16[512,1024]{1,0:T(8,128)(2,1)} %refs_7_.1, bf16[512,1024]{1,0:T(8,128)(2,1)} %do_hbm.1, ...), custom_call_target="tpu_custom_call" | custom-call | flops 1000000000 | bytes 1 | tf_op jit(solution)/shard_map/inner/pallas_call | solution.py:34
  36.3 0.1 fusion.19
  36.5 0.4 collective-permute-start.7
  36.9 0.2 fusion.2
  37.0 1.0 %collective-permute-start.10 = (bf16[512,128]{1,0:T(8,128)(2,1)S(1)}, bf16[512,128]{1,0:T(8,128)(2,1)S(1)}, u32[]{:S(2)}, u32[]{:S(2)}) collective-permute-start(bf16[512,128]{1,0:T(8,128)(2,1)S(1)} %get-tuple-element.125), channel_id=1, source_target_pairs={{0,2},{2,0},{4,6},{6,4},{8,10},{10,8},{12,14},{14,12},{16,18},{18,... | collective-permute-start | bytes 393224 | tf_op jit(solution)/shard_map/ppermute | solution.py:533
  38.0 4.2 %fetch.1 = (bf16[512,1024]{1,0:T(8,128)(2,1)S(1)}, bf16[512,1024]{1,0:T(8,128)(2,1)S(1)}, f32[512,128]{1,0:T(8,128)S(1)}, bf16[2048,1024]{1,0:T(8,128)(2,1)S(1)}, bf16[2048,1024]{1,0:T(8,128)(2,1)S(1)}) custom-call(bf16[4096,1024]{1,0:T(8,128)(2,1)} %w_hbm, bf16[512,1024]{1,0:T(8,128)(2,1)} %do_hbm.1, f32[32,512]{1,0:T(8,128)} %get-tuple-element.60.refs_4_.facts_hbm, ...), custom_call_target="tpu_custom_call" | custom-call | flops 4000000000 | bytes 1 | tf_op jit(solution)/shard_map/fetch/pallas_call | solution.py:34
  42.2 1.6 %collective-permute-done.7 = bf16[512,128]{1,0:T(8,128)(2,1)S(1)} collective-permute-done((bf16[512,128]{1,0:T(8,128)(2,1)S(1)}, bf16[512,128]{1,0:T(8,128)(2,1)S(1)}, u32[]{:S(2)}, u32[]{:S(2)}) %collective-permute-start.7) | collective-permute-done | bytes 131104 | tf_op jit(solution)/shard_map/ppermute | solution.py:533
  43.8 0.2 fusion.12
  44.0 1.0 %collective-permute-start.9 = (bf16[512,128]{1,0:T(8,128)(2,1)S(1)}, bf16[512,128]{1,0:T(8,128)(2,1)S(1)}, u32[]{:S(2)}, u32[]{:S(2)}) collective-permute-start(bf16[512,128]{1,0:T(8,128)(2,1)S(1)} %get-tuple-element.127), channel_id=1, source_target_pairs={{0,2},{2,0},{4,6},{6,4},{8,10},{10,8},{12,14},{14,12},{16,18},{18,... | collective-permute-start | bytes 393224 | tf_op jit(solution)/shard_map/ppermute | solution.py:533
  44.9 3.0 %query_term.1 = (bf16[512,1024]{1,0:T(8,128)(2,1)S(1)}, bf16[512,2048]{1,0:T(8,128)(2,1)S(1)}, bf16[512,1024]{1,0:T(8,128)(2,1)S(1)}, bf16[512,1024]{1,0:T(8,128...) custom-call(bf16[512,128]{1,0:T(8,128)(2,1)S(1)} %get-tuple-element.126.refs_0_, ...), custom_call_target="tpu_custom_call" | custom-call | flops 6000000000 | bytes 1 | tf_op jit(solution)/shard_map/query_term/pallas_call | solution.py:34
  48.0 0.1 collective-permute-start.11
  48.0 1.0 %collective-permute-done.9.theirs_ref = bf16[512,128]{1,0:T(8,128)(2,1)S(1)} collective-permute-done((bf16[512,128]{1,0:T(8,128)(2,1)S(1)}, bf16[512,128]{1,0:T(8,128)(2,1)S(1)}, u32[]{:S(2)}, u32[]{:S(2)}) %collective-permute-start.9) | collective-permute-done | bytes 131104 | tf_op jit(solution)/shard_map/ppermute | solution.py:533
  49.0 3.5 %close.1 = (bf16[512,1024]{1,0:T(8,128)(2,1)}, bf16[512,1024]{1,0:T(8,128)(2,1)}, bf16[512,2048]{1,0:T(8,128)(2,1)S(1)}) custom-call(bf16[512,128]{1,0:T(8,128)(2,1)S(1)} %get-tuple-element.128.mine_ref, bf16[512,128]{1,0:T(8,128)(2,1)S(1)} %collective-permute-done.9.theirs_ref, bf16[512,1024]{1,0:T(8,128)(2,1)S(1)} %get-tuple-element.104.k_ref, ...), custom_call_target="tpu_custom_call" | custom-call | flops 99999997952 | bytes 1 | tf_op jit(solution)/shard_map/close/pallas_call | solution.py:34
  52.5 1.5 %finish.1 = bf16[512,2048]{1,0:T(8,128)(2,1)} custom-call(bf16[512,2048]{1,0:T(8,128)(2,1)S(1)} %get-tuple-element.111.refs_0_, bf16[512,2048]{1,0:T(8,128)(2,1)S(1)} %collective-permute-done.11.refs_1_), custom_call_target="tpu_custom_call" | custom-call | flops 6000000000 | bytes 1 | tf_op jit(solution)/shard_map/finish/pallas_call | solution.py:34
  (17 shorter events, 0.1 us)
Async XLA Ops:
  0.6 6.5 %collective-permute-start.1 = (bf16[512,2048]{1,0:T(8,128)(2,1)}, bf16[512,2048]{1,0:T(8,128)(2,1)S(1)}, u32[]{:S(2)}, u32[]{:S(2)}) collective-permute-start(bf16[512,2048]{1,0:T(8,128)(2,1)} %refs_0_.1), channel_id=1, source_target_pairs={{0,1},{1,0},{2,3},{3,2},{4,5},{5,4},{6,7},{7,6},{8,9},{9,8},{10,11... | collective-permute-start | bytes 6291464 | tf_op jit(solution)/shard_map/ppermute | solution.py:517
  4.5 10.4 %collective-permute-start = (bf16[528,128]{1,0:T(8,128)(2,1)S(1)}, bf16[528,128]{1,0:T(8,128)(2,1)S(1)}, u32[]{:S(2)}, u32[]{:S(2)}) collective-permute-start(bf16[528,128]{1,0:T(8,128)(2,1)S(1)} %get-tuple-element.59), channel_id=1, source_target_pairs={{0,2},{2,0},{4,6},{6,4},{8,10},{10,8},{12,14},{14,12},{16,18},{18,... | collective-permute-start | bytes 405512 | tf_op jit(solution)/shard_map/ppermute | solution.py:533
  15.0 6.0 %collective-permute-start.3 = (bf16[528,128]{1,0:T(8,128)(2,1)S(1)}, bf16[528,128]{1,0:T(8,128)(2,1)S(1)}, u32[]{:S(2)}, u32[]{:S(2)}) collective-permute-start(bf16[528,128]{1,0:T(8,128)(2,1)S(1)} %pad_maximum_fusion), channel_id=1, source_target_pairs={{0,4},{2,6},{4,0},{6,2},{8,12},{10,14},{12,8},{14,10},{16,20},{18,... | collective-permute-start | bytes 405512 | tf_op jit(solution)/shard_map/ppermute | solution.py:533
  16.6 6.2 %collective-permute-start.2 = (bf16[512,128]{1,0:T(8,128)(2,1)S(1)}, bf16[512,128]{1,0:T(8,128)(2,1)S(1)}, u32[]{:S(2)}, u32[]{:S(2)}) collective-permute-start(bf16[512,128]{1,0:T(8,128)(2,1)S(1)} %get-tuple-element.64), channel_id=1, source_target_pairs={{0,2},{2,0},{4,6},{6,4},{8,10},{10,8},{12,14},{14,12},{16,18},{18,... | collective-permute-start | bytes 393224 | tf_op jit(solution)/shard_map/ppermute | solution.py:533
  21.2 6.5 %collective-permute-start.5 = (bf16[528,128]{1,0:T(8,128)(2,1)S(1)}, bf16[528,128]{1,0:T(8,128)(2,1)S(1)}, u32[]{:S(2)}, u32[]{:S(2)}) collective-permute-start(bf16[528,128]{1,0:T(8,128)(2,1)S(1)} %pad_maximum_fusion.1), channel_id=1, source_target_pairs={{0,8},{2,10},{4,12},{6,14},{8,0},{10,2},{12,4},{14,6},{16,24},{18,... | collective-permute-start | bytes 405512 | tf_op jit(solution)/shard_map/ppermute | solution.py:533
  22.9 5.0 %collective-permute-start.4 = (bf16[512,128]{1,0:T(8,128)(2,1)S(1)}, bf16[512,128]{1,0:T(8,128)(2,1)S(1)}, u32[]{:S(2)}, u32[]{:S(2)}) collective-permute-start(bf16[512,128]{1,0:T(8,128)(2,1)S(1)} %fusion.20), channel_id=1, source_target_pairs={{0,4},{2,6},{4,0},{6,2},{8,12},{10,14},{12,8},{14,10},{16,20},{18,... | collective-permute-start | bytes 393224 | tf_op jit(solution)/shard_map/ppermute | solution.py:533
  28.0 8.3 %collective-permute-start.6 = (bf16[512,128]{1,0:T(8,128)(2,1)S(1)}, bf16[512,128]{1,0:T(8,128)(2,1)S(1)}, u32[]{:S(2)}, u32[]{:S(2)}) collective-permute-start(bf16[512,128]{1,0:T(8,128)(2,1)S(1)} %fusion.22), channel_id=1, source_target_pairs={{0,8},{2,10},{4,12},{6,14},{8,0},{10,2},{12,4},{14,6},{16,24},{18,... | collective-permute-start | bytes 393224 | tf_op jit(solution)/shard_map/ppermute | solution.py:533
  28.8 8.1 %collective-permute-start.8 = (bf16[512,128]{1,0:T(8,128)(2,1)S(1)}, bf16[512,128]{1,0:T(8,128)(2,1)S(1)}, u32[]{:S(2)}, u32[]{:S(2)}) collective-permute-start(bf16[512,128]{1,0:T(8,128)(2,1)S(1)} %fusion.14), channel_id=1, source_target_pairs={{0,16},{2,18},{4,20},{6,22},{8,24},{10,26},{12,28},{14,30},{16,0},... | collective-permute-start | bytes 393224 | tf_op jit(solution)/shard_map/ppermute | solution.py:533
  36.5 7.3 %collective-permute-start.7 = (bf16[512,128]{1,0:T(8,128)(2,1)S(1)}, bf16[512,128]{1,0:T(8,128)(2,1)S(1)}, u32[]{:S(2)}, u32[]{:S(2)}) collective-permute-start(bf16[512,128]{1,0:T(8,128)(2,1)S(1)} %fusion.19), channel_id=1, source_target_pairs={{0,16},{2,18},{4,20},{6,22},{8,24},{10,26},{12,28},{14,30},{16,0},... | collective-permute-start | bytes 393224 | tf_op jit(solution)/shard_map/ppermute | solution.py:533
  37.0 7.9 %collective-permute-start.10 = (bf16[512,128]{1,0:T(8,128)(2,1)S(1)}, bf16[512,128]{1,0:T(8,128)(2,1)S(1)}, u32[]{:S(2)}, u32[]{:S(2)}) collective-permute-start(bf16[512,128]{1,0:T(8,128)(2,1)S(1)} %get-tuple-element.125), channel_id=1, source_target_pairs={{0,2},{2,0},{4,6},{6,4},{8,10},{10,8},{12,14},{14,12},{16,18},{18,... | collective-permute-start | bytes 393224 | tf_op jit(solution)/shard_map/ppermute | solution.py:533
  44.0 5.0 %collective-permute-start.9 = (bf16[512,128]{1,0:T(8,128)(2,1)S(1)}, bf16[512,128]{1,0:T(8,128)(2,1)S(1)}, u32[]{:S(2)}, u32[]{:S(2)}) collective-permute-start(bf16[512,128]{1,0:T(8,128)(2,1)S(1)} %get-tuple-element.127), channel_id=1, source_target_pairs={{0,2},{2,0},{4,6},{6,4},{8,10},{10,8},{12,14},{14,12},{16,18},{18,... | collective-permute-start | bytes 393224 | tf_op jit(solution)/shard_map/ppermute | solution.py:533
  48.0 4.6 %collective-permute-start.11 = (bf16[512,2048]{1,0:T(8,128)(2,1)S(1)}, bf16[512,2048]{1,0:T(8,128)(2,1)S(1)}, u32[]{:S(2)}, u32[]{:S(2)}) collective-permute-start(bf16[512,2048]{1,0:T(8,128)(2,1)S(1)} %get-tuple-element.112), channel_id=1, source_target_pairs={{0,1},{1,0},{2,3},{3,2},{4,5},{5,4},{6,7},{7,6},{8,9},{9,8},{10,11... | collective-permute-start | bytes 6291464 | tf_op jit(solution)/shard_map/ppermute | solution.py:630

commit v16 on v15

--- a/solution.py
+++ b/solution.py
@@ -429,15 +429,33 @@
     )[0]
 
 
-def finish_kernel(*refs):
+def early_kernel(dq_ref, w_ref, out_ref):
+    put_terms(dq_ref, w_ref.at[: out_ref.shape[1]], out_ref)
+
+
+def early_term(d_query, own):
+    return kernel_call(
+        early_kernel,
+        (d_query, own),
+        [VM, VM],
+        [((d_query.shape[0], own.shape[0] // 4), BF16)],
+        (VM,),
+        [],
+        8,
+        "early",
+        1,
+    )[0]
+
+
+def finish_kernel(early_ref, rest_ref, *refs):
     terms, (out_hbm, sent, sems) = refs[:-3], refs[-3:]
     feat = sent.shape[1]
     copies = Copies(sems)
-    block = min(512, feat)
+    block = early_ref.shape[1]
     for at in range(0, feat, block):
         wide = slice(at, at + block)
-        total = terms[0][:, wide].astype(F32)
-        for other in terms[1:]:
+        total = (rest_ref[:, at - block : at] if at else early_ref[...]).astype(F32)
+        for other in terms:
             total = total + other[:, wide].astype(F32)
         sent[:, wide] = total.astype(BF16)
         copies.store(sent.at[:, wide], out_hbm.at[:, wide])
@@ -445,7 +463,7 @@
 
 
 def finish(terms):
-    rows, feat = terms[0].shape
+    rows, feat = terms[-1].shape
     return kernel_call(
         finish_kernel,
         terms,
@@ -454,7 +472,7 @@
         (HB,),
         [
             pltpu.VMEM((rows, feat), BF16),
-            pltpu.SemaphoreType.DMA((feat // min(512, feat),)),
+            pltpu.SemaphoreType.DMA((feat // terms[0].shape[1],)),
         ],
         12,
         "finish",
@@ -482,7 +500,7 @@
             wide = slice((h + 1 - pair) * HDIM, (h + 1) * HDIM)
             copies.store(kside.at[:, wide], dk_hbm.at[:, wide])
             copies.store(vside.at[:, wide], dv_hbm.at[:, wide])
-    put_terms(dq_ref, own_ref, term_ref)
+    put_terms(dq_ref, own_ref.at[own_ref.shape[0] - term_ref.shape[1] :], term_ref)
     copies.finish()
 
 
@@ -494,7 +512,7 @@
         functools.partial(close_kernel, heads, hp),
         args,
         [VM] * len(args),
-        [((rows, width), BF16)] * 2 + [((rows, own.shape[0]), BF16)],
+        [((rows, width), BF16)] * 2 + [((rows, own.shape[0] * 3 // 4), BF16)],
         (HB, HB, VM),
         [buf, buf, pltpu.SemaphoreType.DMA((2 * (heads // min(2, heads)),))],
         12,
@@ -628,8 +646,9 @@
         else:
             term = plain_term(d_query, weights[shift - 1])
         arrived.append(lax.ppermute(term, "head", ring))
-    d_keys, d_values, own = close(adjoint_halves, held, d_query, own, heads, hp)
-    d_hidden = finish((own, *arrived))
+    early = early_term(d_query, own)
+    d_keys, d_values, rest = close(adjoint_halves, held, d_query, own, heads, hp)
+    d_hidden = finish((early, rest, *arrived))
     return (d_hidden, d_keys, d_values)
 
 

time: 54.4 us -> 54.1 us (level)
    ppermute x10, waiting for transfers between devices: 2.63 us -> 1.87 us  [send(): return lax.ppermute(array, 'ctx', [(i, i ^ dist) for i in range(ctx_size)])]
    pallas_call x9 -> x10, Pallas kernels: 35.3 us -> 35.5 us  [kernel_call(): pl.pallas_call(kernel, in_specs=specs, out_specs=tuple(out_specs), out_sh...]
  transfers between devices with their start and end apart: 12 -> 12, of which waited for: 2 -> 3; matrix products, arithmetic and copies ran while one was open for 1% -> 1% of each run, Pallas kernels for 62% -> 63%
where the time goes in v16:
time: 54.1 us; the launch traced here: 53.8 us
  Pallas kernels  35.5 us (66%)
  starting transfers between devices  14.3 us (26%)
  waiting for transfers between devices  2.1 us (4%)
  between operations  1 us (2%)
  other arithmetic  0.98 us (2%)
    pallas_call x10, Pallas kernels, kernel_call(): pl.pallas_call(kernel, in_specs=specs, out_specs=tuple(out_specs), out_sh...  35.5 us
    ppermute x10, starting transfers between devices, send(): return lax.ppermute(array, 'ctx', [(i, i ^ dist) for i in range(ctx_size)])  13.7 us
    ppermute x10, waiting for transfers between devices, send(): return lax.ppermute(array, 'ctx', [(i, i ^ dist) for i in range(ctx_size)])  1.87 us
  transfers between devices with their start and end apart: 12, of which 3 were waited for; matrix products, arithmetic and copies ran while one was open for 1% of the time, Pallas kernels for 63%

profile of v16, /device:TPU:0, one launch (start us, length us, event | category | flops | bytes accessed | tf_op | source)
XLA Modules:
  0.0 53.8 jit_solution(4808556659730104700)
XLA Ops:
  0.6 0.5 collective-permute-start.1
  1.1 3.4 %prepare.1 = (f32[32,512]{1,0:T(8,128)}, bf16[512,128]{1,0:T(8,128)(2,1)S(1)}, bf16[528,128]{1,0:T(8,128)(2,1)S(1)}, f32[8,128]{1,0:T(8,128)S(1)}) custom-call(f32[8,512]{1,0:T(8,128)} %bitcast.123, bf16[512,1024]{1,0:T(8,128)(2,1)} %refs_6_.1, bf16[512,1024]{1,0:T(8,128)(2,1)} %refs_7_.1), custom_call_target="tpu_custom_call" | custom-call | flops 4000000000 | bytes 1 | tf_op jit(solution)/shard_map/prepare/pallas_call | solution.py:34
  4.5 2.6 %collective-permute-start = (bf16[528,128]{1,0:T(8,128)(2,1)S(1)}, bf16[528,128]{1,0:T(8,128)(2,1)S(1)}, u32[]{:S(2)}, u32[]{:S(2)}) collective-permute-start(bf16[528,128]{1,0:T(8,128)(2,1)S(1)} %get-tuple-element.59), channel_id=1, source_target_pairs={{0,2},{2,0},{4,6},{6,4},{8,10},{10,8},{12,14},{14,12},{16,18},{18,... | collective-permute-start | bytes 405512 | tf_op jit(solution)/shard_map/ppermute | solution.py:551
  7.1 7.8 %project.1 = (bf16[512,1024]{1,0:T(8,128)(2,1)}, bf16[512,128]{1,0:T(8,128)(2,1)S(1)}, bf16[512,128]{1,0:T(8,128)(2,1)S(1)}) custom-call(bf16[512,2048]{1,0:T(8,128)(2,1)} %refs_0_.1, bf16[512,2048]{1,0:T(8,128)(2,1)S(1)} %collective-permute-done.1.refs_1_, bf16[4096,1024]{1,0:T(8,128)(2,1)} %w_hbm, bf16[512,1024]{1,0:T(8,128)(2,1)} %do_hbm.1, ...), custom_call_target="tpu_custom_call" | custom-call | flops 8000000000 | bytes 1 | tf_op jit(solution)/shard_map/project/pallas_call | solution.py:34
  15.0 1.6 %collective-permute-start.2 = (bf16[528,128]{1,0:T(8,128)(2,1)S(1)}, bf16[528,128]{1,0:T(8,128)(2,1)S(1)}, u32[]{:S(2)}, u32[]{:S(2)}) collective-permute-start(bf16[528,128]{1,0:T(8,128)(2,1)S(1)} %pad_maximum_fusion), channel_id=1, source_target_pairs={{0,4},{2,6},{4,0},{6,2},{8,12},{10,14},{12,8},{14,10},{16,20},{18,... | collective-permute-start | bytes 405512 | tf_op jit(solution)/shard_map/ppermute | solution.py:551
  16.6 0.9 %collective-permute-start.4 = (bf16[512,128]{1,0:T(8,128)(2,1)S(1)}, bf16[512,128]{1,0:T(8,128)(2,1)S(1)}, u32[]{:S(2)}, u32[]{:S(2)}) collective-permute-start(bf16[512,128]{1,0:T(8,128)(2,1)S(1)} %get-tuple-element.68), channel_id=1, source_target_pairs={{0,2},{2,0},{4,6},{6,4},{8,10},{10,8},{12,14},{14,12},{16,18},{18,... | collective-permute-start | bytes 393224 | tf_op jit(solution)/shard_map/ppermute | solution.py:551
  17.5 3.5 %inner.3 = (bf16[512,256]{1,0:T(8,128)(2,1)}, bf16[512,256]{1,0:T(8,128)(2,1)}, bf16[512,256]{1,0:T(8,128)(2,1)}) custom-call(bf16[512,1024]{1,0:T(8,128)(2,1)} %get-tuple-element.82.refs_0_, bf16[512,1024]{1,0:T(8,128)(2,1)} %refs_6_.1, bf16[512,1024]{1,0:T(8,128)(2,1)} %refs_7_.1, bf16[512,1024]{1,0:T(8,128)(2,1)} %do_hbm.1, ...), custom_call_target="tpu_custom_call" | custom-call | flops 1000000000 | bytes 1 | tf_op jit(solution)/shard_map/inner/pallas_call | solution.py:34
  21.1 0.1 fusion.23
  21.2 1.6 %collective-permute-start.3 = (bf16[528,128]{1,0:T(8,128)(2,1)S(1)}, bf16[528,128]{1,0:T(8,128)(2,1)S(1)}, u32[]{:S(2)}, u32[]{:S(2)}) collective-permute-start(bf16[528,128]{1,0:T(8,128)(2,1)S(1)} %pad_maximum_fusion.1), channel_id=1, source_target_pairs={{0,8},{2,10},{4,12},{6,14},{8,0},{10,2},{12,4},{14,6},{16,24},{18,... | collective-permute-start | bytes 405512 | tf_op jit(solution)/shard_map/ppermute | solution.py:551
  22.8 0.1 fusion.20
  22.9 1.3 %collective-permute-start.6 = (bf16[512,128]{1,0:T(8,128)(2,1)S(1)}, bf16[512,128]{1,0:T(8,128)(2,1)S(1)}, u32[]{:S(2)}, u32[]{:S(2)}) collective-permute-start(bf16[512,128]{1,0:T(8,128)(2,1)S(1)} %fusion.20), channel_id=1, source_target_pairs={{0,4},{2,6},{4,0},{6,2},{8,12},{10,14},{12,8},{14,10},{16,20},{18,... | collective-permute-start | bytes 393224 | tf_op jit(solution)/shard_map/ppermute | solution.py:551
  24.2 3.5 %inner.4 = (bf16[512,256]{1,0:T(8,128)(2,1)}, bf16[512,256]{1,0:T(8,128)(2,1)}, bf16[512,256]{1,0:T(8,128)(2,1)}) custom-call(bf16[512,1024]{1,0:T(8,128)(2,1)} %get-tuple-element.82.refs_0_, bf16[512,1024]{1,0:T(8,128)(2,1)} %refs_6_.1, bf16[512,1024]{1,0:T(8,128)(2,1)} %refs_7_.1, bf16[512,1024]{1,0:T(8,128)(2,1)} %do_hbm.1, ...), custom_call_target="tpu_custom_call" | custom-call | flops 1000000000 | bytes 1 | tf_op jit(solution)/shard_map/inner/pallas_call | solution.py:34
  27.7 0.1 fusion.14
  27.9 0.1 fusion.22
  28.0 0.7 %collective-permute-start.7 = (bf16[512,128]{1,0:T(8,128)(2,1)S(1)}, bf16[512,128]{1,0:T(8,128)(2,1)S(1)}, u32[]{:S(2)}, u32[]{:S(2)}) collective-permute-start(bf16[512,128]{1,0:T(8,128)(2,1)S(1)} %fusion.22), channel_id=1, source_target_pairs={{0,8},{2,10},{4,12},{6,14},{8,0},{10,2},{12,4},{14,6},{16,24},{18,... | collective-permute-start | bytes 393224 | tf_op jit(solution)/shard_map/ppermute | solution.py:551
  28.8 2.6 %collective-permute-start.5 = (bf16[512,128]{1,0:T(8,128)(2,1)S(1)}, bf16[512,128]{1,0:T(8,128)(2,1)S(1)}, u32[]{:S(2)}, u32[]{:S(2)}) collective-permute-start(bf16[512,128]{1,0:T(8,128)(2,1)S(1)} %fusion.14), channel_id=1, source_target_pairs={{0,16},{2,18},{4,20},{6,22},{8,24},{10,26},{12,28},{14,30},{16,0},... | collective-permute-start | bytes 393224 | tf_op jit(solution)/shard_map/ppermute | solution.py:551
  31.3 5.0 %inner.5 = (bf16[512,512]{1,0:T(8,128)(2,1)}, bf16[512,512]{1,0:T(8,128)(2,1)}, bf16[512,512]{1,0:T(8,128)(2,1)}) custom-call(bf16[512,1024]{1,0:T(8,128)(2,1)} %get-tuple-element.82.refs_0_, bf16[512,1024]{1,0:T(8,128)(2,1)} %refs_6_.1, bf16[512,1024]{1,0:T(8,128)(2,1)} %refs_7_.1, bf16[512,1024]{1,0:T(8,128)(2,1)} %do_hbm.1, ...), custom_call_target="tpu_custom_call" | custom-call | flops 1000000000 | bytes 1 | tf_op jit(solution)/shard_map/inner/pallas_call | solution.py:34
  36.3 0.1 fusion.19
  36.5 0.4 collective-permute-start.9
  36.9 0.2 fusion.4
  37.0 1.0 %collective-permute-start.8 = (bf16[512,128]{1,0:T(8,128)(2,1)S(1)}, bf16[512,128]{1,0:T(8,128)(2,1)S(1)}, u32[]{:S(2)}, u32[]{:S(2)}) collective-permute-start(bf16[512,128]{1,0:T(8,128)(2,1)S(1)} %get-tuple-element.125), channel_id=1, source_target_pairs={{0,2},{2,0},{4,6},{6,4},{8,10},{10,8},{12,14},{14,12},{16,18},{18,... | collective-permute-start | bytes 393224 | tf_op jit(solution)/shard_map/ppermute | solution.py:551
  38.0 4.2 %fetch.1 = (bf16[512,1024]{1,0:T(8,128)(2,1)S(1)}, bf16[512,1024]{1,0:T(8,128)(2,1)S(1)}, f32[512,128]{1,0:T(8,128)S(1)}, bf16[2048,1024]{1,0:T(8,128)(2,1)S(1)}, bf16[2048,1024]{1,0:T(8,128)(2,1)S(1)}) custom-call(bf16[4096,1024]{1,0:T(8,128)(2,1)} %w_hbm, bf16[512,1024]{1,0:T(8,128)(2,1)} %do_hbm.1, f32[32,512]{1,0:T(8,128)} %get-tuple-element.60.refs_4_.facts_hbm, ...), custom_call_target="tpu_custom_call" | custom-call | flops 4000000000 | bytes 1 | tf_op jit(solution)/shard_map/fetch/pallas_call | solution.py:34
  42.2 1.6 %collective-permute-done.9 = bf16[512,128]{1,0:T(8,128)(2,1)S(1)} collective-permute-done((bf16[512,128]{1,0:T(8,128)(2,1)S(1)}, bf16[512,128]{1,0:T(8,128)(2,1)S(1)}, u32[]{:S(2)}, u32[]{:S(2)}) %collective-permute-start.9) | collective-permute-done | bytes 131104 | tf_op jit(solution)/shard_map/ppermute | solution.py:551
  43.8 0.2 fusion.12
  44.0 1.0 %collective-permute-start.10 = (bf16[512,128]{1,0:T(8,128)(2,1)S(1)}, bf16[512,128]{1,0:T(8,128)(2,1)S(1)}, u32[]{:S(2)}, u32[]{:S(2)}) collective-permute-start(bf16[512,128]{1,0:T(8,128)(2,1)S(1)} %get-tuple-element.128), channel_id=1, source_target_pairs={{0,2},{2,0},{4,6},{6,4},{8,10},{10,8},{12,14},{14,12},{16,18},{18,... | collective-permute-start | bytes 393224 | tf_op jit(solution)/shard_map/ppermute | solution.py:551
  44.9 3.0 %query_term.1 = (bf16[512,1024]{1,0:T(8,128)(2,1)S(1)}, bf16[512,2048]{1,0:T(8,128)(2,1)S(1)}, bf16[512,1024]{1,0:T(8,128)(2,1)S(1)}, bf16[512,1024]{1,0:T(8,128...) custom-call(bf16[512,128]{1,0:T(8,128)(2,1)S(1)} %get-tuple-element.126.refs_0_, ...), custom_call_target="tpu_custom_call" | custom-call | flops 6000000000 | bytes 1 | tf_op jit(solution)/shard_map/query_term/pallas_call | solution.py:34
  48.0 0.1 collective-permute-start.11
  48.1 0.7 %early.1.early_ref = bf16[512,512]{1,0:T(8,128)(2,1)S(1)} custom-call(bf16[512,1024]{1,0:T(8,128)(2,1)S(1)} %get-tuple-element.104.dq_ref, bf16[2048,1024]{1,0:T(8,128)(2,1)S(1)} %get-tuple-element.105.w_ref.own_ref), custom_call_target="tpu_custom_call" | custom-call | flops 1000000000 | bytes 1 | tf_op jit(solution)/shard_map/early/pallas_call | solution.py:34
  48.8 0.2 collective-permute-done.10.theirs_ref
  49.0 3.0 %close.1 = (bf16[512,1024]{1,0:T(8,128)(2,1)}, bf16[512,1024]{1,0:T(8,128)(2,1)}, bf16[512,1536]{1,0:T(8,128)(2,1)S(1)}) custom-call(bf16[512,128]{1,0:T(8,128)(2,1)S(1)} %get-tuple-element.127.mine_ref, bf16[512,128]{1,0:T(8,128)(2,1)S(1)} %collective-permute-done.10.theirs_ref, bf16[512,1024]{1,0:T(8,128)(2,1)S(1)} %get-tuple-element.106.k_ref, ...), custom_call_target="tpu_custom_call" | custom-call | flops 99999997952 | bytes 1 | tf_op jit(solution)/shard_map/close/pallas_call | solution.py:34
  52.0 0.2 collective-permute-done.11.refs_0_
  52.2 1.5 %finish.1 = bf16[512,2048]{1,0:T(8,128)(2,1)} custom-call(bf16[512,512]{1,0:T(8,128)(2,1)S(1)} %early.1.early_ref, bf16[512,1536]{1,0:T(8,128)(2,1)S(1)} %get-tuple-element.111.rest_ref, bf16[512,2048]{1,0:T(8,128)(2,1)S(1)} %collective-permute-done.11.refs_0_), custom_call_target="tpu_custom_call" | custom-call | flops 6000000000 | bytes 1 | tf_op jit(solution)/shard_map/finish/pallas_call | solution.py:34
  (18 shorter events, 0.2 us)
Async XLA Ops:
  0.6 6.5 %collective-permute-start.1 = (bf16[512,2048]{1,0:T(8,128)(2,1)}, bf16[512,2048]{1,0:T(8,128)(2,1)S(1)}, u32[]{:S(2)}, u32[]{:S(2)}) collective-permute-start(bf16[512,2048]{1,0:T(8,128)(2,1)} %refs_0_.1), channel_id=1, source_target_pairs={{0,1},{1,0},{2,3},{3,2},{4,5},{5,4},{6,7},{7,6},{8,9},{9,8},{10,11... | collective-permute-start | bytes 6291464 | tf_op jit(solution)/shard_map/ppermute | solution.py:535
  4.5 10.4 %collective-permute-start = (bf16[528,128]{1,0:T(8,128)(2,1)S(1)}, bf16[528,128]{1,0:T(8,128)(2,1)S(1)}, u32[]{:S(2)}, u32[]{:S(2)}) collective-permute-start(bf16[528,128]{1,0:T(8,128)(2,1)S(1)} %get-tuple-element.59), channel_id=1, source_target_pairs={{0,2},{2,0},{4,6},{6,4},{8,10},{10,8},{12,14},{14,12},{16,18},{18,... | collective-permute-start | bytes 405512 | tf_op jit(solution)/shard_map/ppermute | solution.py:551
  15.0 6.0 %collective-permute-start.2 = (bf16[528,128]{1,0:T(8,128)(2,1)S(1)}, bf16[528,128]{1,0:T(8,128)(2,1)S(1)}, u32[]{:S(2)}, u32[]{:S(2)}) collective-permute-start(bf16[528,128]{1,0:T(8,128)(2,1)S(1)} %pad_maximum_fusion), channel_id=1, source_target_pairs={{0,4},{2,6},{4,0},{6,2},{8,12},{10,14},{12,8},{14,10},{16,20},{18,... | collective-permute-start | bytes 405512 | tf_op jit(solution)/shard_map/ppermute | solution.py:551
  16.6 6.2 %collective-permute-start.4 = (bf16[512,128]{1,0:T(8,128)(2,1)S(1)}, bf16[512,128]{1,0:T(8,128)(2,1)S(1)}, u32[]{:S(2)}, u32[]{:S(2)}) collective-permute-start(bf16[512,128]{1,0:T(8,128)(2,1)S(1)} %get-tuple-element.68), channel_id=1, source_target_pairs={{0,2},{2,0},{4,6},{6,4},{8,10},{10,8},{12,14},{14,12},{16,18},{18,... | collective-permute-start | bytes 393224 | tf_op jit(solution)/shard_map/ppermute | solution.py:551
  21.2 6.5 %collective-permute-start.3 = (bf16[528,128]{1,0:T(8,128)(2,1)S(1)}, bf16[528,128]{1,0:T(8,128)(2,1)S(1)}, u32[]{:S(2)}, u32[]{:S(2)}) collective-permute-start(bf16[528,128]{1,0:T(8,128)(2,1)S(1)} %pad_maximum_fusion.1), channel_id=1, source_target_pairs={{0,8},{2,10},{4,12},{6,14},{8,0},{10,2},{12,4},{14,6},{16,24},{18,... | collective-permute-start | bytes 405512 | tf_op jit(solution)/shard_map/ppermute | solution.py:551
  22.9 5.0 %collective-permute-start.6 = (bf16[512,128]{1,0:T(8,128)(2,1)S(1)}, bf16[512,128]{1,0:T(8,128)(2,1)S(1)}, u32[]{:S(2)}, u32[]{:S(2)}) collective-permute-start(bf16[512,128]{1,0:T(8,128)(2,1)S(1)} %fusion.20), channel_id=1, source_target_pairs={{0,4},{2,6},{4,0},{6,2},{8,12},{10,14},{12,8},{14,10},{16,20},{18,... | collective-permute-start | bytes 393224 | tf_op jit(solution)/shard_map/ppermute | solution.py:551
  28.0 8.3 %collective-permute-start.7 = (bf16[512,128]{1,0:T(8,128)(2,1)S(1)}, bf16[512,128]{1,0:T(8,128)(2,1)S(1)}, u32[]{:S(2)}, u32[]{:S(2)}) collective-permute-start(bf16[512,128]{1,0:T(8,128)(2,1)S(1)} %fusion.22), channel_id=1, source_target_pairs={{0,8},{2,10},{4,12},{6,14},{8,0},{10,2},{12,4},{14,6},{16,24},{18,... | collective-permute-start | bytes 393224 | tf_op jit(solution)/shard_map/ppermute | solution.py:551
  28.8 8.1 %collective-permute-start.5 = (bf16[512,128]{1,0:T(8,128)(2,1)S(1)}, bf16[512,128]{1,0:T(8,128)(2,1)S(1)}, u32[]{:S(2)}, u32[]{:S(2)}) collective-permute-start(bf16[512,128]{1,0:T(8,128)(2,1)S(1)} %fusion.14), channel_id=1, source_target_pairs={{0,16},{2,18},{4,20},{6,22},{8,24},{10,26},{12,28},{14,30},{16,0},... | collective-permute-start | bytes 393224 | tf_op jit(solution)/shard_map/ppermute | solution.py:551
  36.5 7.3 %collective-permute-start.9 = (bf16[512,128]{1,0:T(8,128)(2,1)S(1)}, bf16[512,128]{1,0:T(8,128)(2,1)S(1)}, u32[]{:S(2)}, u32[]{:S(2)}) collective-permute-start(bf16[512,128]{1,0:T(8,128)(2,1)S(1)} %fusion.19), channel_id=1, source_target_pairs={{0,16},{2,18},{4,20},{6,22},{8,24},{10,26},{12,28},{14,30},{16,0},... | collective-permute-start | bytes 393224 | tf_op jit(solution)/shard_map/ppermute | solution.py:551
  37.0 7.9 %collective-permute-start.8 = (bf16[512,128]{1,0:T(8,128)(2,1)S(1)}, bf16[512,128]{1,0:T(8,128)(2,1)S(1)}, u32[]{:S(2)}, u32[]{:S(2)}) collective-permute-start(bf16[512,128]{1,0:T(8,128)(2,1)S(1)} %get-tuple-element.125), channel_id=1, source_target_pairs={{0,2},{2,0},{4,6},{6,4},{8,10},{10,8},{12,14},{14,12},{16,18},{18,... | collective-permute-start | bytes 393224 | tf_op jit(solution)/shard_map/ppermute | solution.py:551
  44.0 5.0 %collective-permute-start.10 = (bf16[512,128]{1,0:T(8,128)(2,1)S(1)}, bf16[512,128]{1,0:T(8,128)(2,1)S(1)}, u32[]{:S(2)}, u32[]{:S(2)}) collective-permute-start(bf16[512,128]{1,0:T(8,128)(2,1)S(1)} %get-tuple-element.128), channel_id=1, source_target_pairs={{0,2},{2,0},{4,6},{6,4},{8,10},{10,8},{12,14},{14,12},{16,18},{18,... | collective-permute-start | bytes 393224 | tf_op jit(solution)/shard_map/ppermute | solution.py:551
  48.0 4.2 %collective-permute-start.11 = (bf16[512,2048]{1,0:T(8,128)(2,1)S(1)}, bf16[512,2048]{1,0:T(8,128)(2,1)S(1)}, u32[]{:S(2)}, u32[]{:S(2)}) collective-permute-start(bf16[512,2048]{1,0:T(8,128)(2,1)S(1)} %get-tuple-element.112), channel_id=1, source_target_pairs={{0,1},{1,0},{2,3},{3,2},{4,5},{5,4},{6,7},{7,6},{8,9},{9,8},{10,11... | collective-permute-start | bytes 6291464 | tf_op jit(solution)/shard_map/ppermute | solution.py:648
